TPU v7x, 32 devices: a whole 2x2x4 slice. The times are simulated.
32 devices in a mesh: clips: 2 (over y), tm: 4 (over z), rows: 4 (over x, core).
Axes of the slice: x: 2, y: 2, z: 4, core: 2. Of those that a mesh axis runs over, the one named last changes fastest.
Arguments:
- latents: bfloat16 [32, 8, 192, 128], P(('clips', 'tm'), 'rows'), parts along dimension 0, may hold values from -6 to 6
- conv_weight: bfloat16 [3, 27, 192, 192], replicated, may hold values from -0.078125 to 0.078125
- norm_gains: float32 [3, 192], replicated, may hold values from 0.5 to 1.5
- biases: float32 [3, 192], replicated, may hold values from -3 to 3
Outputs:
- decoded: bfloat16 [32, 8, 192, 128], P(('clips', 'tm'), 'rows'), parts along dimension 0
There are 2 independent parts, one for each index of `clips`. A program takes and returns all parts, laid end to end along the dimension named above; an argument that names none is the same for every part. Nothing has to cross between parts.
All inputs are finite; a program needn't handle non-finite values.
Results may differ from a plain program's by a relative error of at most 0.011.
Values may be sent and summed in bfloat16 or wider, within the bound.
No kernel may reach another device: no remote copies, remote signals or barrier semaphores. Data moves between devices by JAX's collectives and lax.ppermute only.
A program may use at most 64 MiB of HBM per device.

v0:
```python
import functools

import jax
import jax.numpy as jnp
from jax import lax
from jax.experimental import pallas as pl
from jax.experimental.pallas import tpu as pltpu
from jax.sharding import PartitionSpec as P

EPSILON = 1e-06
PAIR = 2
LANES = 128
TILE = 256
VMEM = pl.BlockSpec(memory_space=pltpu.VMEM)
SMEM = pl.BlockSpec(memory_space=pltpu.SMEM)
LIMIT = 24 * 1024 * 1024


def rounded(lanes):
    return -(-lanes // LANES) * LANES


def column(row):
    return jnp.transpose(jnp.broadcast_to(row, (LANES, row.shape[1])))


def lane_of(lanes):
    return lax.broadcasted_iota(jnp.int32, (1, lanes), 1)


def filled(lanes, pitch):
    lane = lane_of(lanes)
    gaps = lane < 0
    for end in range(pitch - 1, lanes, pitch):
        gaps = gaps | (lane == end)
    return jnp.where(gaps, 0.0, 1.0)


def activated(values, gain, mask):
    squares = jnp.mean(values * values, axis=0, keepdims=True)
    halved = values * (lax.rsqrt(squares + EPSILON) * (0.5 * mask)) * gain
    return (halved + halved * jnp.tanh(halved)).astype(jnp.bfloat16)


def weights_kernel(place_ref, w_ref, gains_ref, biases_ref, *refs):
    layers, _, outs, ins = w_ref.shape
    flipped = place_ref[1]
    for layer in range(layers):
        for time_tap in range(3):
            for row_tap in range(3):
                source = 9 * time_tap + 3 * (row_tap + flipped * (2 - 2 * row_tap))
                at = (3 * time_tap + row_tap) * ins
                refs[layer][:, at : at + ins] = w_ref[layer, pl.ds(source, 3)].reshape(3 * outs, ins)
        refs[-1][layer, 0] = column(gains_ref[layer : layer + 1, :])
        refs[-1][layer, 1] = column(biases_ref[layer : layer + 1, :])


def weights(place, conv_weight, gains, biases):
    layers, _, outs, ins = conv_weight.shape
    one = jax.ShapeDtypeStruct((3 * outs, 9 * ins), conv_weight.dtype)
    results = pl.pallas_call(
        weights_kernel,
        out_shape=(one,) * layers + (jax.ShapeDtypeStruct((layers, 2, outs, LANES), jnp.float32),),
        in_specs=[SMEM] + [VMEM] * 3,
        out_specs=(VMEM,) * (layers + 1),
        compiler_params=pltpu.CompilerParams(vmem_limit_bytes=LIMIT),
        cost_estimate=pl.CostEstimate(flops=0, bytes_accessed=4 * conv_weight.size, transcendentals=0),
        name="weights",
    )(place, conv_weight, gains, biases)
    return results[:-1], results[-1]


def placed(blocks, place_ref, row, window, line):
    pitch, width = window + 1, line.shape[1]
    lane = lane_of(LANES)
    block, low = divmod(row * pitch, LANES)
    shift = lax.rem(low + LANES - place_ref[0] * (width - window), LANES)
    turned = pltpu.roll(line, shift, 1)
    here = (lane >= low) & (lane < low + window)
    blocks[block] = blocks.get(block, 0.0) + jnp.where(here, turned, 0.0)
    if low + window > LANES:
        blocks[block + 1] = blocks.get(block + 1, 0.0) + jnp.where(lane < low + window - LANES, turned, 0.0)


def near_kernel(halo, place_ref, own_ref, mate_ref, gains_ref, values_ref, *act_refs):
    frames, rows, _, width = own_ref.shape
    window = width // 2 + halo
    group, outer = place_ref[1], place_ref[2] == 1
    gain = column(gains_ref[0:1, :])
    done = act_refs[0].shape[2]
    mask = filled(done, window + 1)
    for f in range(frames):
        blocks = {}
        for row in range(2 * rows):
            at = row % rows
            index = at + group * (rows - 1 - 2 * at)
            one, two = (own_ref, mate_ref) if row < rows else (mate_ref, own_ref)
            line = jnp.where(outer, one[f, index], two[f, index]).astype(jnp.float32)
            placed(blocks, place_ref, row, window, line)
        for b in blocks:
            part = slice(b * LANES, (b + 1) * LANES)
            values_ref[f, :, part] = blocks[b].astype(jnp.bfloat16)
            if part.stop <= done:
                act_refs[f // PAIR][f % PAIR, :, part] = activated(blocks[b], gain, mask[:, part])


def near(halo, place, own, mate, gains):
    frames, rows, channels, width = own.shape
    lanes = 2 * rows * (width // 2 + halo + 1)
    pairs = frames // PAIR
    outs = pl.pallas_call(
        functools.partial(near_kernel, halo),
        out_shape=(jax.ShapeDtypeStruct((frames, channels, rounded(lanes)), jnp.bfloat16),)
        + (jax.ShapeDtypeStruct((PAIR, channels, lanes // LANES * LANES), jnp.bfloat16),) * pairs,
        in_specs=[SMEM] + [VMEM] * 3,
        out_specs=(VMEM,) * (1 + pairs),
        compiler_params=pltpu.CompilerParams(vmem_limit_bytes=LIMIT),
        cost_estimate=pl.CostEstimate(flops=40 * own.size, bytes_accessed=8 * own.size, transcendentals=2 * own.size),
        name="near",
    )(place, own, mate, gains)
    return outs[0], outs[1:]


def far_kernel(halo, pairs, place_ref, far_ref, mate_ref, near_ref, columns_ref, *refs):
    act_refs, value_refs, out_refs, send_ref = refs[:pairs], refs[pairs : 2 * pairs], refs[2 * pairs : -1], refs[-1]
    frames, rows, _, width = far_ref.shape
    window = width // 2 + halo
    group, outer = place_ref[1], place_ref[2] == 1
    lanes, done = out_refs[0].shape[2], act_refs[0].shape[2]
    mask = filled(lanes, window + 1)
    for f in range(frames):
        p, t = divmod(f, PAIR)
        value_refs[p][t, :, :done] = near_ref[f, :, :done]
        out_refs[p][t, :, :done] = act_refs[p][t]
        blocks = {done // LANES: near_ref[f, :, done:].astype(jnp.float32)}
        for row in range(2 * rows, 2 * rows + halo):
            local = 4 * rows - 1 - row
            at = local % rows
            index = at + (1 - group) * (rows - 1 - 2 * at)
            one, two = (mate_ref, far_ref) if local < rows else (far_ref, mate_ref)
            line = jnp.where(outer, one[f, index], two[f, index]).astype(jnp.float32)
            placed(blocks, place_ref, row, window, line)
        for b in blocks:
            part = slice(b * LANES, (b + 1) * LANES)
            value_refs[p][t, :, part] = blocks[b].astype(jnp.bfloat16)
            act = activated(blocks[b], columns_ref[0, 0], mask[:, part])
            out_refs[p][t, :, part] = act
            if p == pairs - 1:
                send_ref[t, :, part.start - done : part.stop - done] = act


def beyond(halo, place, far, mate, near_values, near_act, columns):
    frames, rows, channels, width = far.shape
    lanes = rounded((2 * rows + halo) * (width // 2 + halo + 1))
    out = jax.ShapeDtypeStruct((PAIR, channels, lanes), jnp.bfloat16)
    send = jax.ShapeDtypeStruct((PAIR, channels, lanes - near_act[0].shape[2]), jnp.bfloat16)
    pairs = frames // PAIR
    outs = pl.pallas_call(
        functools.partial(far_kernel, halo, pairs),
        out_shape=(out,) * (2 * pairs) + (send,),
        in_specs=[SMEM] + [VMEM] * (4 + pairs),
        out_specs=(VMEM,) * (2 * pairs + 1),
        compiler_params=pltpu.CompilerParams(vmem_limit_bytes=LIMIT),
        cost_estimate=pl.CostEstimate(flops=40 * far.size, bytes_accessed=8 * far.size, transcendentals=2 * far.size),
        name="beyond",
    )(place, far, mate, near_values, columns, *near_act)
    return outs[:pairs], outs[pairs : 2 * pairs], outs[-1]


def conv_kernel(layer, last, pitch, half, place_ref, act_ref, values_ref, w_ref, columns_ref, *refs):
    earlier_refs, outs, x_ref = refs[:-3], refs[-3:-1], refs[-1]
    _, channels, lanes_in = act_ref.shape
    lanes = x_ref.shape[3] // PAIR
    chunks = lanes // LANES
    lane = lane_of(LANES)
    for j in range(2 * PAIR):
        parts = [ref[j % PAIR] for ref in (earlier_refs if j < PAIR else (act_ref,))]
        middle = parts[0] if len(parts) == 1 else jnp.concatenate(parts, axis=1)
        above = pltpu.roll(middle, pitch, 1)
        edge = jnp.where(lane < pitch, 0.0, above[:, :LANES].astype(jnp.float32)).astype(jnp.bfloat16)
        below = pltpu.roll(middle, lanes_in - pitch, 1)
        for t in range(PAIR):
            if 0 <= j - t < 3:
                for tap, lines in enumerate((above, middle, below)):
                    x_ref[j - t, tap, :, t * lanes : (t + 1) * lanes] = lines[:, :lanes]
                x_ref[j - t, 0, :, t * lanes : t * lanes + LANES] = edge
    tiles = [
        jnp.dot(
            w_ref[...],
            x_ref[:, :, :, at : at + TILE].reshape(9 * channels, TILE),
            preferred_element_type=jnp.float32,
        )
        for at in range(0, PAIR * lanes, TILE)
    ]
    bias = columns_ref[layer, 1]
    if not last:
        mask = filled(lanes, pitch)
        gain = columns_ref[layer + 1, 0]
    for t in range(PAIR):

        def sums(tap, b):
            tile, at = divmod((t * chunks + b) * LANES, TILE)
            return tiles[tile][tap * channels : (tap + 1) * channels, at : at + LANES]

        totals = []
        from_left = 0.0
        from_right = pltpu.roll(sums(2, 0), LANES - 1, 1)
        for b in range(chunks):
            at = slice(b * LANES, (b + 1) * LANES)
            left = pltpu.roll(sums(0, b), 1, 1)
            right = pltpu.roll(sums(2, b + 1), LANES - 1, 1) if b + 1 < chunks else 0.0
            summed = (
                jnp.where(lane == 0, from_left, left) + sums(1, b) + jnp.where(lane == LANES - 1, right, from_right)
            )
            from_left, from_right = left, right
            total = (values_ref[t, :, at].astype(jnp.float32) + summed + bias).astype(jnp.bfloat16)
            totals.append(total.astype(jnp.float32))
            if not last:
                outs[0][t, :, at] = total
                outs[1][t, :, at] = activated(totals[-1], gain, mask[:, at])
        if last:
            whole = jnp.concatenate(totals, axis=1)
            halo = pitch - 1 - half
            whole = jnp.where(place_ref[0] == 1, pltpu.roll(whole, lanes - halo, 1), whole)
            left_half = lane < half

            def rows_of(row):
                one = whole if row == 0 else pltpu.roll(whole, lanes - row * pitch, 1)
                two = pltpu.roll(whole, lanes - (row + 1) * pitch + half, 1)
                return jnp.where(left_half, one[:, :LANES], two[:, :LANES])

            outermost, inner = rows_of(0), rows_of(2)
            outer = place_ref[2] == 1
            outs[0][t] = jnp.where(outer, outermost, inner).astype(jnp.bfloat16)
            outs[1][t] = jnp.where(outer, inner, outermost).astype(jnp.bfloat16)


def conv(layer, last, pitch, rows_left, half, place, earlier, act, values, weight, columns):
    _, channels, _ = act.shape
    lanes = rounded(rows_left * pitch)
    out = jax.ShapeDtypeStruct((PAIR, channels, LANES if last else lanes), jnp.bfloat16)
    return pl.pallas_call(
        functools.partial(conv_kernel, layer, last, pitch, half),
        out_shape=(out, out),
        in_specs=[SMEM] + [VMEM] * (4 + len(earlier)),
        out_specs=(VMEM, VMEM),
        scratch_shapes=[pltpu.VMEM((3, 3, channels, PAIR * lanes), jnp.bfloat16)],
        compiler_params=pltpu.CompilerParams(vmem_limit_bytes=LIMIT),
        cost_estimate=pl.CostEstimate(
            flops=54 * channels * channels * PAIR * lanes,
            bytes_accessed=2 * weight.size,
            transcendentals=PAIR * channels * lanes,
        ),
        name=f"conv_{layer}",
    )(place, act, values, weight, columns, *earlier)


def join_kernel(place_ref, *refs):
    out_ref = refs[-1]
    kept, got = refs[: len(refs) // 2], refs[len(refs) // 2 : -1]
    _, rows, _, width = out_ref.shape
    half = width // 2
    first, group = place_ref[0] == 0, place_ref[1]
    left_half = lane_of(width) < half
    for p in range(len(kept)):
        for t in range(PAIR):
            mine, theirs = kept[p][t].astype(jnp.float32), got[p][t].astype(jnp.float32)
            left, right = jnp.where(first, mine, theirs), jnp.where(first, theirs, mine)
            lines = (
                jnp.where(left_half, left, pltpu.roll(right, half, 1)),
                jnp.where(left_half, pltpu.roll(left, half, 1), right),
            )
            for j in range(rows):
                out_ref[PAIR * p + t, j + group * (rows - 1 - 2 * j)] = lines[j].astype(jnp.bfloat16)


def join(place, kept, got, shape):
    return pl.pallas_call(
        join_kernel,
        out_shape=jax.ShapeDtypeStruct(shape, jnp.bfloat16),
        in_specs=[SMEM] + [VMEM] * (2 * len(kept)),
        out_specs=VMEM,
        compiler_params=pltpu.CompilerParams(vmem_limit_bytes=LIMIT),
        name="join",
    )(place, *kept, *got)


def on_device(latents, conv_weight, norm_gains, biases):
    layers = conv_weight.shape[0]
    frames, rows, channels, width = latents.shape
    strips, blocks = lax.axis_size("rows"), lax.axis_size("tm")
    assert strips == 4 and rows == 2 and frames % PAIR == 0 and width == LANES
    strip = lax.axis_index("rows").astype(jnp.int32)
    core, group = strip & 1, strip >> 1
    place = jnp.stack([core, group, (core == group).astype(jnp.int32)])

    def mate_of(block):
        return lax.ppermute(block, "rows", [(i, i ^ 1) for i in range(strips)])

    def earlier_of(block):
        return lax.ppermute(block, "tm", [(i, i + 1) for i in range(blocks - 1)])

    far = lax.ppermute(latents, "rows", [(i, i ^ 2) for i in range(strips)])
    mate = mate_of(latents)
    weight, columns = weights(place, conv_weight, norm_gains, biases)
    near_values, near_act = near(layers, place, latents, mate, norm_gains)
    halo_near = earlier_of(near_act[-1])
    far, weight, columns, near_values, near_act, halo_near = lax.optimization_barrier(
        (far, weight, columns, near_values, near_act, halo_near)
    )
    values, act, send = beyond(layers, place, far, mate_of(far), near_values, near_act, columns)
    halo = (halo_near, earlier_of(send))
    pitch = width // 2 + layers + 1
    pairs = frames // PAIR
    for layer in range(layers):
        last = layer == layers - 1
        rows_left = 2 * rows + layers - 1 - layer
        if layer:
            halo = (earlier_of(act[-1]),)
        results = [None] * pairs
        for p in reversed(range(pairs)):
            earlier = (act[p - 1],) if p else halo
            results[p] = conv(
                layer, last, pitch, rows_left, width // 2, place, earlier, act[p], values[p], weight[layer], columns
            )
        values, act = [r[0] for r in results], [r[1] for r in results]
    got = [mate_of(send) for send in act]
    return join(place, values, got, latents.shape)


def solution(mesh):
    in_specs = (P(("clips", "tm"), "rows", None, None), P(), P(), P())
    out_specs = P(("clips", "tm"), "rows", None, None)
    return jax.shard_map(on_device, mesh=mesh, in_specs=in_specs, out_specs=out_specs, check_vma=False)
```

profile of v0, /device:TPU:0, one launch (start us, length us, event | category | flops | bytes accessed | tf_op | source)
XLA Modules:
  0.0 49.9 jit_solution(4578362165727866129)
XLA Ops:
  0.0 0.5 collective-permute-start.1
  0.5 2.5 %collective-permute-start = (bf16[4,2,192,128]{3,2,1,0:T(8,128)(2,1)}, bf16[4,2,192,128]{3,2,1,0:T(8,128)(2,1)S(1)}, u32[]{:S(2)}, u32[]{:S(2)}) collective-permute-start(bf16[4,2,192,128]{3,2,1,0:T(8,128)(2,1)} %own_ref.1), channel_id=1, source_target_pairs={{0,2},{1,3},{2,0},{3,1},{4,6},{5,7},{6,4},{7,5},{8,10},{9,11},{10,... | collective-permute-start | bytes 1179656 | tf_op jit(solution)/shard_map/ppermute | solution.py:303
  2.9 0.1 pad_add_fusion.place_ref
  3.0 0.0 collective-permute-done.1.mate_ref
  3.0 1.0 %copy-done.1 = bf16[4,2,192,128]{3,2,1,0:T(8,128)(2,1)S(1)} copy-done((bf16[4,2,192,128]{3,2,1,0:T(8,128)(2,1)S(1)}, bf16[4,2,192,128]{3,2,1,0:T(8,128)(2,1)}, u32[]{:S(2)}) %copy-start.1) | copy-done | bytes 393240
  4.0 0.7 %copy-done.2 = f32[3,192]{1,0:T(4,128)S(1)} copy-done((f32[3,192]{1,0:T(4,128)S(1)}, f32[3,192]{1,0:T(4,128)}, u32[]{:S(2)}) %copy-start.2) | copy-done | bytes 2328
  4.7 1.2 %near.1 = (bf16[4,192,384]{2,1,0:T(8,128)(2,1)S(1)}, bf16[2,192,256]{2,1,0:T(8,128)(2,1)S(1)}, bf16[2,192,256]{2,1,0:T(8,128)(2,1)S(1)}) custom-call(s32[3]{0:T(128)S(1)} %pad_add_fusion.place_ref, bf16[4,2,192,128]{3,2,1,0:T(8,128)(2,1)S(1)} %copy-done.1, bf16[4,2,192,128]{3,2,1,0:T(8,128)(2,1)S(1)} %collective-permute-done.1.mate_ref, f32[3,192]{1,0:T(4,128)S(1)} %copy-done.2), custom_call_target="tpu_custom_call" | custom-call | flops 7864320 | bytes 1572864 | tf_op jit(solution)/shard_map/near/pallas_call | solution.py:111
  5.9 3.9 %collective-permute-start.2 = (bf16[2,192,256]{2,1,0:T(8,128)(2,1)S(1)}, bf16[2,192,256]{2,1,0:T(8,128)(2,1)S(1)}, u32[]{:S(2)}, u32[]{:S(2)}) collective-permute-start(bf16[2,192,256]{2,1,0:T(8,128)(2,1)S(1)} %get-tuple-element.49.refs_1_), channel_id=1, source_target_pairs={{0,4},{4,8},{8,12},{1,5},{5,9},{9,13},{2,6},{6,10},{10,14},{3,7},{... | collective-permute-start | bytes 589832 | tf_op jit(solution)/shard_map/ppermute | solution.py:301
  9.8 0.0 copy-start
  9.8 3.3 %copy-done = bf16[3,27,192,192]{3,2,1,0:T(8,128)(2,1)S(1)} copy-done((bf16[3,27,192,192]{3,2,1,0:T(8,128)(2,1)S(1)}, bf16[3,27,192,192]{3,2,1,0:T(8,128)(2,1)}, u32[]{:S(2)}) %copy-start) | copy-done | bytes 5971992
  13.0 0.7 %copy-done.3 = f32[3,192]{1,0:T(4,128)S(1)} copy-done((f32[3,192]{1,0:T(4,128)S(1)}, f32[3,192]{1,0:T(4,128)}, u32[]{:S(2)}) %copy-start.3) | copy-done | bytes 2328
  13.7 0.7 %copy-done.4 = f32[3,192]{1,0:T(4,128)S(1)} copy-done((f32[3,192]{1,0:T(4,128)S(1)}, f32[3,192]{1,0:T(4,128)}, u32[]{:S(2)}) %copy-start.4) | copy-done | bytes 2328
  14.4 1.7 %weights.1 = (bf16[576,1728]{1,0:T(8,128)(2,1)S(1)}, bf16[576,1728]{1,0:T(8,128)(2,1)S(1)}, bf16[576,1728]{1,0:T(8,128)(2,1)S(1)}, f32[3,2,192,128]{3,2,1,0:T(8,128)S(1)}) custom-call(s32[3]{0:T(128)S(1)} %pad_add_fusion.place_ref, bf16[3,27,192,192]{3,2,1,0:T(8,128)(2,1)S(1)} %copy-done, f32[3,192]{1,0:T(4,128)S(1)} %copy-done.3, f32[3,192]{1,0:T(4,128)S(1)} %copy-done.4), custom_call_target="tpu_custom_call" | custom-call | bytes 11943936 | tf_op jit(solution)/shard_map/weights/pallas_call | solution.py:61
  16.1 0.0 collective-permute-done.far_ref
  16.1 0.0 collective-permute-done.2.refs_0_
  16.1 0.1 collective-permute-start.3
  16.2 1.7 %collective-permute-done.3.mate_ref = bf16[4,2,192,128]{3,2,1,0:T(8,128)(2,1)S(1)} collective-permute-done((bf16[4,2,192,128]{3,2,1,0:T(8,128)(2,1)S(1)}, bf16[4,2,192,128]{3,2,1,0:T(8,128)(2,1)S(1)}, u32[]{:S(2)}, u32[]{:S(2)}) %collective-permute-start.3) | collective-permute-done | bytes 393248 | tf_op jit(solution)/shard_map/ppermute | solution.py:298
  17.9 1.1 %beyond.1 = (bf16[2,192,512]{2,1,0:T(8,128)(2,1)S(1)}, bf16[2,192,512]{2,1,0:T(8,128)(2,1)S(1)}, bf16[2,192,512]{2,1,0:T(8,128)(2,1)S(1)}, bf16[2,192,512]{2,1,0:T(8,128)(2,1)S(1)}, bf16[2,192,256]{2,1,0:T(8,128)(2,1)S(1)}) custom-call(s32[3]{0:T(128)S(1)} %pad_add_fusion.place_ref, bf16[4,2,192,128]{3,2,1,0:T(8,128)(2,1)S(1)} %collective-permute-done.far_ref, ...), custom_call_target="tpu_custom_call" | custom-call | flops 7864320 | bytes 1572864 | tf_op jit(solution)/shard_map/beyond/pallas_call | solution.py:158
  19.0 3.5 %collective-permute-start.4 = (bf16[2,192,256]{2,1,0:T(8,128)(2,1)S(1)}, bf16[2,192,256]{2,1,0:T(8,128)(2,1)S(1)}, u32[]{:S(2)}, u32[]{:S(2)}) collective-permute-start(bf16[2,192,256]{2,1,0:T(8,128)(2,1)S(1)} %get-tuple-element.54), channel_id=1, source_target_pairs={{0,4},{4,8},{8,12},{1,5},{5,9},{9,13},{2,6},{6,10},{10,14},{3,7},{... | collective-permute-start | bytes 589832 | tf_op jit(solution)/shard_map/ppermute | solution.py:301
  22.5 3.4 %conv_0.3 = (bf16[2,192,512]{2,1,0:T(8,128)(2,1)S(1)}, bf16[2,192,512]{2,1,0:T(8,128)(2,1)S(1)}) custom-call(s32[3]{0:T(128)S(1)} %pad_add_fusion.place_ref, bf16[2,192,512]{2,1,0:T(8,128)(2,1)S(1)} %get-tuple-element.58.act_ref, bf16[2,192,512]{2,1,0:T(8,128)(2,1)S(1)} %get-tuple-element.59.values_ref, bf16[576,1728]{1,0:T(8,128)(2,1)S(1)} %get-tuple-element.52.w_ref, ...), custom_call_target="tpu_custom_call" | custom-call | flops 2038431744 | bytes 1990656 | tf_op jit(solution)/shard_map/conv_0/pallas_call | solution.py:242
  25.9 3.5 %collective-permute-start.5 = (bf16[2,192,512]{2,1,0:T(8,128)(2,1)S(1)}, bf16[2,192,512]{2,1,0:T(8,128)(2,1)S(1)}, u32[]{:S(2)}, u32[]{:S(2)}) collective-permute-start(bf16[2,192,512]{2,1,0:T(8,128)(2,1)S(1)} %get-tuple-element.60.act_ref), channel_id=1, source_target_pairs={{0,4},{4,8},{8,12},{1,5},{5,9},{9,13},{2,6},{6,10},{10,14},{3,7},{... | collective-permute-start | bytes 1179656 | tf_op jit(solution)/shard_map/ppermute | solution.py:301
  29.4 3.4 %conv_0.2 = (bf16[2,192,512]{2,1,0:T(8,128)(2,1)S(1)}, bf16[2,192,512]{2,1,0:T(8,128)(2,1)S(1)}) custom-call(s32[3]{0:T(128)S(1)} %pad_add_fusion.place_ref, bf16[2,192,512]{2,1,0:T(8,128)(2,1)S(1)} %get-tuple-element.50.act_ref.refs_0_, bf16[2,192,512]{2,1,0:T(8,128)(2,1)S(1)} %get-tuple-element.51.values_ref, ...), custom_call_target="tpu_custom_call" | custom-call | flops 2038431744 | bytes 1990656 | tf_op jit(solution)/shard_map/conv_0/pallas_call | solution.py:242
  32.8 2.8 %conv_1.3 = (bf16[2,192,384]{2,1,0:T(8,128)(2,1)S(1)}, bf16[2,192,384]{2,1,0:T(8,128)(2,1)S(1)}) custom-call(s32[3]{0:T(128)S(1)} %pad_add_fusion.place_ref, bf16[2,192,512]{2,1,0:T(8,128)(2,1)S(1)} %get-tuple-element.60.act_ref, bf16[2,192,512]{2,1,0:T(8,128)(2,1)S(1)} %get-tuple-element.64.values_ref, bf16[576,1728]{1,0:T(8,128)(2,1)S(1)} %get-tuple-element.57.w_ref, ...), custom_call_target="tpu_custom_call" | custom-call | flops 1528823808 | bytes 1990656 | tf_op jit(solution)/shard_map/conv_1/pallas_call | solution.py:242
  35.7 2.6 %collective-permute-start.6 = (bf16[2,192,384]{2,1,0:T(8,128)(2,1)S(1)}, bf16[2,192,384]{2,1,0:T(8,128)(2,1)S(1)}, u32[]{:S(2)}, u32[]{:S(2)}) collective-permute-start(bf16[2,192,384]{2,1,0:T(8,128)(2,1)S(1)} %get-tuple-element.65.act_ref), channel_id=1, source_target_pairs={{0,4},{4,8},{8,12},{1,5},{5,9},{9,13},{2,6},{6,10},{10,14},{3,7},{... | collective-permute-start | bytes 884744 | tf_op jit(solution)/shard_map/ppermute | solution.py:301
  38.2 2.8 %conv_1.2 = (bf16[2,192,384]{2,1,0:T(8,128)(2,1)S(1)}, bf16[2,192,384]{2,1,0:T(8,128)(2,1)S(1)}) custom-call(s32[3]{0:T(128)S(1)} %pad_add_fusion.place_ref, bf16[2,192,512]{2,1,0:T(8,128)(2,1)S(1)} %get-tuple-element.55.act_ref.refs_0_, bf16[2,192,512]{2,1,0:T(8,128)(2,1)S(1)} %get-tuple-element.56.values_ref, ...), custom_call_target="tpu_custom_call" | custom-call | flops 1528823808 | bytes 1990656 | tf_op jit(solution)/shard_map/conv_1/pallas_call | solution.py:242
  41.1 2.9 %conv_2.3 = (bf16[2,192,128]{2,1,0:T(8,128)(2,1)S(1)}, bf16[2,192,128]{2,1,0:T(8,128)(2,1)S(1)}) custom-call(s32[3]{0:T(128)S(1)} %pad_add_fusion.place_ref, bf16[2,192,384]{2,1,0:T(8,128)(2,1)S(1)} %get-tuple-element.65.act_ref, bf16[2,192,384]{2,1,0:T(8,128)(2,1)S(1)} %get-tuple-element.67.values_ref, bf16[576,1728]{1,0:T(8,128)(2,1)S(1)} %get-tuple-element.63.w_ref, ...), custom_call_target="tpu_custom_call" | custom-call | flops 1528823808 | bytes 1990656 | tf_op jit(solution)/shard_map/conv_2/pallas_call | solution.py:242
  44.0 0.1 collective-permute-start.8
  44.1 0.0 collective-permute-done.6.refs_0_
  44.1 2.9 %conv_2.2 = (bf16[2,192,128]{2,1,0:T(8,128)(2,1)S(1)}, bf16[2,192,128]{2,1,0:T(8,128)(2,1)S(1)}) custom-call(s32[3]{0:T(128)S(1)} %pad_add_fusion.place_ref, bf16[2,192,384]{2,1,0:T(8,128)(2,1)S(1)} %get-tuple-element.61.act_ref.refs_0_, bf16[2,192,384]{2,1,0:T(8,128)(2,1)S(1)} %get-tuple-element.62.values_ref, ...), custom_call_target="tpu_custom_call" | custom-call | flops 1528823808 | bytes 1990656 | tf_op jit(solution)/shard_map/conv_2/pallas_call | solution.py:242
  47.0 0.5 %collective-permute-start.7 = (bf16[2,192,128]{2,1,0:T(8,128)(2,1)S(1)}, bf16[2,192,128]{2,1,0:T(8,128)(2,1)S(1)}, u32[]{:S(2)}, u32[]{:S(2)}) collective-permute-start(bf16[2,192,128]{2,1,0:T(8,128)(2,1)S(1)} %get-tuple-element.69), channel_id=1, source_target_pairs={{0,1},{1,0},{2,3},{3,2},{4,5},{5,4},{6,7},{7,6},{8,9},{9,8},{10,11... | collective-permute-start | bytes 294920 | tf_op jit(solution)/shard_map/ppermute | solution.py:298
  47.5 0.9 %collective-permute-done.7.refs_2_ = bf16[2,192,128]{2,1,0:T(8,128)(2,1)S(1)} collective-permute-done((bf16[2,192,128]{2,1,0:T(8,128)(2,1)S(1)}, bf16[2,192,128]{2,1,0:T(8,128)(2,1)S(1)}, u32[]{:S(2)}, u32[]{:S(2)}) %collective-permute-start.7) | collective-permute-done | bytes 98336 | tf_op jit(solution)/shard_map/ppermute | solution.py:298
  48.5 1.5 %join.1 = bf16[4,2,192,128]{3,2,1,0:T(8,128)(2,1)} custom-call(s32[3]{0:T(128)S(1)} %pad_add_fusion.place_ref, bf16[2,192,128]{2,1,0:T(8,128)(2,1)S(1)} %get-tuple-element.66.refs_0_, bf16[2,192,128]{2,1,0:T(8,128)(2,1)S(1)} %get-tuple-element.68.refs_1_, bf16[2,192,128]{2,1,0:T(8,128)(2,1)S(1)} %collective-permute-done.7.refs_2_, ...), custom_call_target="tpu_custom_call" | custom-call | tf_op jit(solution)/shard_map/join/pallas_call | solution.py:278
  (7 shorter events, 0.0 us)
Async XLA Ops:
  0.0 3.0 %collective-permute-start.1 = (bf16[4,2,192,128]{3,2,1,0:T(8,128)(2,1)}, bf16[4,2,192,128]{3,2,1,0:T(8,128)(2,1)S(1)}, u32[]{:S(2)}, u32[]{:S(2)}) collective-permute-start(bf16[4,2,192,128]{3,2,1,0:T(8,128)(2,1)} %own_ref.1), channel_id=1, source_target_pairs={{0,1},{1,0},{2,3},{3,2},{4,5},{5,4},{6,7},{7,6},{8,9},{9,8},{10,11... | collective-permute-start | bytes 1179656 | tf_op jit(solution)/shard_map/ppermute | solution.py:298
  0.5 15.7 %collective-permute-start = (bf16[4,2,192,128]{3,2,1,0:T(8,128)(2,1)}, bf16[4,2,192,128]{3,2,1,0:T(8,128)(2,1)S(1)}, u32[]{:S(2)}, u32[]{:S(2)}) collective-permute-start(bf16[4,2,192,128]{3,2,1,0:T(8,128)(2,1)} %own_ref.1), channel_id=1, source_target_pairs={{0,2},{1,3},{2,0},{3,1},{4,6},{5,7},{6,4},{7,5},{8,10},{9,11},{10,... | collective-permute-start | bytes 1179656 | tf_op jit(solution)/shard_map/ppermute | solution.py:303
  3.0 1.0 %copy-start.1 = (bf16[4,2,192,128]{3,2,1,0:T(8,128)(2,1)S(1)}, bf16[4,2,192,128]{3,2,1,0:T(8,128)(2,1)}, u32[]{:S(2)}) copy-start(bf16[4,2,192,128]{3,2,1,0:T(8,128)(2,1)} %own_ref.1) | copy-start | bytes 1179652
  4.0 0.7 %copy-start.2 = (f32[3,192]{1,0:T(4,128)S(1)}, f32[3,192]{1,0:T(4,128)}, u32[]{:S(2)}) copy-start(f32[3,192]{1,0:T(4,128)} %gains_ref.3) | copy-start | bytes 6916
  5.9 10.2 %collective-permute-start.2 = (bf16[2,192,256]{2,1,0:T(8,128)(2,1)S(1)}, bf16[2,192,256]{2,1,0:T(8,128)(2,1)S(1)}, u32[]{:S(2)}, u32[]{:S(2)}) collective-permute-start(bf16[2,192,256]{2,1,0:T(8,128)(2,1)S(1)} %get-tuple-element.49.refs_1_), channel_id=1, source_target_pairs={{0,4},{4,8},{8,12},{1,5},{5,9},{9,13},{2,6},{6,10},{10,14},{3,7},{... | collective-permute-start | bytes 589832 | tf_op jit(solution)/shard_map/ppermute | solution.py:301
  9.8 3.3 %copy-start = (bf16[3,27,192,192]{3,2,1,0:T(8,128)(2,1)S(1)}, bf16[3,27,192,192]{3,2,1,0:T(8,128)(2,1)}, u32[]{:S(2)}) copy-start(bf16[3,27,192,192]{3,2,1,0:T(8,128)(2,1)} %w_ref.1) | copy-start | bytes 17915908
  13.0 0.7 %copy-start.3 = (f32[3,192]{1,0:T(4,128)S(1)}, f32[3,192]{1,0:T(4,128)}, u32[]{:S(2)}) copy-start(f32[3,192]{1,0:T(4,128)} %gains_ref.3) | copy-start | bytes 6916
  13.7 0.7 %copy-start.4 = (f32[3,192]{1,0:T(4,128)S(1)}, f32[3,192]{1,0:T(4,128)}, u32[]{:S(2)}) copy-start(f32[3,192]{1,0:T(4,128)} %biases_ref.1) | copy-start | bytes 6916
  16.1 1.8 %collective-permute-start.3 = (bf16[4,2,192,128]{3,2,1,0:T(8,128)(2,1)S(1)}, bf16[4,2,192,128]{3,2,1,0:T(8,128)(2,1)S(1)}, u32[]{:S(2)}, u32[]{:S(2)}) collective-permute-start(bf16[4,2,192,128]{3,2,1,0:T(8,128)(2,1)S(1)} %collective-permute-done.far_ref), channel_id=1, source_target_pairs={{0,1},{1,0},{2,3},{3,2},{4,5},{5,4},{6,7},{7,6},{8,9},{9,8},{10,11... | collective-permute-start | bytes 1179656 | tf_op jit(solution)/shard_map/ppermute | solution.py:298
  19.0 10.4 %collective-permute-start.4 = (bf16[2,192,256]{2,1,0:T(8,128)(2,1)S(1)}, bf16[2,192,256]{2,1,0:T(8,128)(2,1)S(1)}, u32[]{:S(2)}, u32[]{:S(2)}) collective-permute-start(bf16[2,192,256]{2,1,0:T(8,128)(2,1)S(1)} %get-tuple-element.54), channel_id=1, source_target_pairs={{0,4},{4,8},{8,12},{1,5},{5,9},{9,13},{2,6},{6,10},{10,14},{3,7},{... | collective-permute-start | bytes 589832 | tf_op jit(solution)/shard_map/ppermute | solution.py:301
  25.9 12.3 %collective-permute-start.5 = (bf16[2,192,512]{2,1,0:T(8,128)(2,1)S(1)}, bf16[2,192,512]{2,1,0:T(8,128)(2,1)S(1)}, u32[]{:S(2)}, u32[]{:S(2)}) collective-permute-start(bf16[2,192,512]{2,1,0:T(8,128)(2,1)S(1)} %get-tuple-element.60.act_ref), channel_id=1, source_target_pairs={{0,4},{4,8},{8,12},{1,5},{5,9},{9,13},{2,6},{6,10},{10,14},{3,7},{... | collective-permute-start | bytes 1179656 | tf_op jit(solution)/shard_map/ppermute | solution.py:301
  35.7 8.4 %collective-permute-start.6 = (bf16[2,192,384]{2,1,0:T(8,128)(2,1)S(1)}, bf16[2,192,384]{2,1,0:T(8,128)(2,1)S(1)}, u32[]{:S(2)}, u32[]{:S(2)}) collective-permute-start(bf16[2,192,384]{2,1,0:T(8,128)(2,1)S(1)} %get-tuple-element.65.act_ref), channel_id=1, source_target_pairs={{0,4},{4,8},{8,12},{1,5},{5,9},{9,13},{2,6},{6,10},{10,14},{3,7},{... | collective-permute-start | bytes 884744 | tf_op jit(solution)/shard_map/ppermute | solution.py:301
  44.0 3.5 %collective-permute-start.8 = (bf16[2,192,128]{2,1,0:T(8,128)(2,1)S(1)}, bf16[2,192,128]{2,1,0:T(8,128)(2,1)S(1)}, u32[]{:S(2)}, u32[]{:S(2)}) collective-permute-start(bf16[2,192,128]{2,1,0:T(8,128)(2,1)S(1)} %get-tuple-element.70), channel_id=1, source_target_pairs={{0,1},{1,0},{2,3},{3,2},{4,5},{5,4},{6,7},{7,6},{8,9},{9,8},{10,11... | collective-permute-start | bytes 294920 | tf_op jit(solution)/shard_map/ppermute | solution.py:298
  47.0 1.5 %collective-permute-start.7 = (bf16[2,192,128]{2,1,0:T(8,128)(2,1)S(1)}, bf16[2,192,128]{2,1,0:T(8,128)(2,1)S(1)}, u32[]{:S(2)}, u32[]{:S(2)}) collective-permute-start(bf16[2,192,128]{2,1,0:T(8,128)(2,1)S(1)} %get-tuple-element.69), channel_id=1, source_target_pairs={{0,1},{1,0},{2,3},{3,2},{4,5},{5,4},{6,7},{7,6},{8,9},{9,8},{10,11... | collective-permute-start | bytes 294920 | tf_op jit(solution)/shard_map/ppermute | solution.py:298
where the time goes:
time: 50.3 us; the launch traced here: 49.9 us
  Pallas kernels  23.7 us (47%)
  starting transfers between devices  17 us (34%)
  local copies, waits for them, and re-layouts  6.31 us (13%)
  waiting for transfers between devices  2.71 us (5%)
    pallas_call x6, Pallas kernels, conv(): pl.pallas_call(functools.partial(conv_kernel, layer, last, pitch, half),...  18.2 us
    ppermute x4, starting transfers between devices, earlier_of(): return lax.ppermute(block, 'tm', [(i, i + 1) for i in range(blocks - 1)])  13.4 us
    unnamed x10, local copies, waits for them, and re-layouts  6.31 us
    ppermute x4, waiting for transfers between devices, mate_of(): return lax.ppermute(block, 'rows', [(i, i ^ 1) for i in range(strips)])  2.66 us
    ppermute x1, starting transfers between devices, on_device(): far = lax.ppermute(latents, 'rows', [(i, i ^ 2) for i in range(strips)])  2.49 us
    pallas_call x1, Pallas kernels, weights(): pl.pallas_call(weights_kernel, out_shape=(one,) * layers + (jax.ShapeDtyp...  1.73 us
    pallas_call x1, Pallas kernels, join(): pl.pallas_call(join_kernel, out_shape=jax.ShapeDtypeStruct(shape, jnp.bfl...  1.48 us
    pallas_call x1, Pallas kernels, near(): pl.pallas_call(functools.partial(near_kernel, halo), out_shape=(jax.Shape...  1.18 us
  transfers between devices with their start and end apart: 9, of which 2 were waited for; matrix products, arithmetic and copies ran while one was open for 0% of the time, Pallas kernels for 42%

commit v1 on v0

--- a/solution.py
+++ b/solution.py
@@ -13,7 +13,9 @@
 TILE = 256
 VMEM = pl.BlockSpec(memory_space=pltpu.VMEM)
 SMEM = pl.BlockSpec(memory_space=pltpu.SMEM)
+ANY = pl.BlockSpec(memory_space=pl.ANY)
 LIMIT = 24 * 1024 * 1024
+LARGE = 48 * 1024 * 1024
 
 
 def rounded(lanes):
@@ -42,32 +44,64 @@
     return (halved + halved * jnp.tanh(halved)).astype(jnp.bfloat16)
 
 
-def weights_kernel(place_ref, w_ref, gains_ref, biases_ref, *refs):
-    layers, _, outs, ins = w_ref.shape
+def fetched(pairs, sems):
+    copies = [pltpu.make_async_copy(source, to, sems.at[i]) for i, (source, to) in enumerate(pairs)]
+    for copy in copies:
+        copy.start()
+    return copies
+
+
+def weights_kernel(first, columns, place_ref, w_ref, *refs):
+    outs, held_ref, sems = refs[columns:-2], refs[-2], refs[-1]
+    count, _, channels_out, ins = held_ref.shape
+    copies = fetched([(w_ref.at[first + i], held_ref.at[i]) for i in range(count)], sems)
     flipped = place_ref[1]
-    for layer in range(layers):
+    if columns:
+        rows_ref = refs[0]
+        layers = rows_ref.shape[0] // 2
+        for layer in range(layers):
+            outs[-1][layer, 0] = column(rows_ref[layer : layer + 1, :])
+            outs[-1][layer, 1] = column(rows_ref[layers + layer : layers + layer + 1, :])
+    for i in range(count):
+        copies[i].wait()
         for time_tap in range(3):
             for row_tap in range(3):
                 source = 9 * time_tap + 3 * (row_tap + flipped * (2 - 2 * row_tap))
                 at = (3 * time_tap + row_tap) * ins
-                refs[layer][:, at : at + ins] = w_ref[layer, pl.ds(source, 3)].reshape(3 * outs, ins)
-        refs[-1][layer, 0] = column(gains_ref[layer : layer + 1, :])
-        refs[-1][layer, 1] = column(biases_ref[layer : layer + 1, :])
-
-
-def weights(place, conv_weight, gains, biases):
-    layers, _, outs, ins = conv_weight.shape
+                outs[i][:, at : at + ins] = held_ref[i, pl.ds(source, 3)].reshape(3 * channels_out, ins)
+
+
+def weights(first, count, place, conv_weight, *rows):
+    layers, taps, outs, ins = conv_weight.shape
     one = jax.ShapeDtypeStruct((3 * outs, 9 * ins), conv_weight.dtype)
+    columns = len(rows)
     results = pl.pallas_call(
-        weights_kernel,
-        out_shape=(one,) * layers + (jax.ShapeDtypeStruct((layers, 2, outs, LANES), jnp.float32),),
-        in_specs=[SMEM] + [VMEM] * 3,
-        out_specs=(VMEM,) * (layers + 1),
-        compiler_params=pltpu.CompilerParams(vmem_limit_bytes=LIMIT),
-        cost_estimate=pl.CostEstimate(flops=0, bytes_accessed=4 * conv_weight.size, transcendentals=0),
+        functools.partial(weights_kernel, first, columns),
+        out_shape=(one,) * count + (jax.ShapeDtypeStruct((layers, 2, outs, LANES), jnp.float32),) * columns,
+        in_specs=[SMEM, ANY] + [VMEM] * columns,
+        out_specs=(VMEM,) * (count + columns),
+        scratch_shapes=[
+            pltpu.VMEM((count, taps, outs, ins), conv_weight.dtype),
+            pltpu.SemaphoreType.DMA((count,)),
+        ],
+        compiler_params=pltpu.CompilerParams(vmem_limit_bytes=LARGE),
+        cost_estimate=pl.CostEstimate(
+            flops=0, bytes_accessed=4 * conv_weight.size * count // layers, transcendentals=0
+        ),
         name="weights",
-    )(place, conv_weight, gains, biases)
-    return results[:-1], results[-1]
+    )(place, conv_weight, *rows)
+    return list(results[:count]), results[count:]
+
+
+def spread(out_ref, index, act, pitch):
+    lanes = out_ref.shape[3]
+    above = pltpu.roll(act, pitch, 1)
+    below = pltpu.roll(act, act.shape[1] - pitch, 1)
+    edge = jnp.where(lane_of(LANES) < pitch, 0.0, above[:, :LANES].astype(jnp.float32))
+    out_ref[index, 0, :, :LANES] = edge.astype(jnp.bfloat16)
+    out_ref[index, 0, :, LANES:] = above[:, LANES:lanes]
+    out_ref[index, 1] = act[:, :lanes]
+    out_ref[index, 2] = below[:, :lanes]
 
 
 def placed(blocks, place_ref, row, window, line):
@@ -126,12 +160,12 @@
     frames, rows, _, width = far_ref.shape
     window = width // 2 + halo
     group, outer = place_ref[1], place_ref[2] == 1
-    lanes, done = out_refs[0].shape[2], act_refs[0].shape[2]
+    lanes, done = value_refs[0].shape[2], act_refs[0].shape[2]
     mask = filled(lanes, window + 1)
     for f in range(frames):
         p, t = divmod(f, PAIR)
         value_refs[p][t, :, :done] = near_ref[f, :, :done]
-        out_refs[p][t, :, :done] = act_refs[p][t]
+        acts = [act_refs[p][t]]
         blocks = {done // LANES: near_ref[f, :, done:].astype(jnp.float32)}
         for row in range(2 * rows, 2 * rows + halo):
             local = 4 * rows - 1 - row
@@ -140,24 +174,26 @@
             one, two = (mate_ref, far_ref) if local < rows else (far_ref, mate_ref)
             line = jnp.where(outer, one[f, index], two[f, index]).astype(jnp.float32)
             placed(blocks, place_ref, row, window, line)
-        for b in blocks:
+        for b in sorted(blocks):
             part = slice(b * LANES, (b + 1) * LANES)
             value_refs[p][t, :, part] = blocks[b].astype(jnp.bfloat16)
             act = activated(blocks[b], columns_ref[0, 0], mask[:, part])
-            out_refs[p][t, :, part] = act
+            acts.append(act)
             if p == pairs - 1:
                 send_ref[t, :, part.start - done : part.stop - done] = act
+        spread(out_refs[p], t, jnp.concatenate(acts, axis=1), window + 1)
 
 
 def beyond(halo, place, far, mate, near_values, near_act, columns):
     frames, rows, channels, width = far.shape
     lanes = rounded((2 * rows + halo) * (width // 2 + halo + 1))
     out = jax.ShapeDtypeStruct((PAIR, channels, lanes), jnp.bfloat16)
+    shifted = jax.ShapeDtypeStruct((PAIR, 3, channels, rounded((2 * rows + halo - 1) * (width // 2 + halo + 1))), jnp.bfloat16)
     send = jax.ShapeDtypeStruct((PAIR, channels, lanes - near_act[0].shape[2]), jnp.bfloat16)
     pairs = frames // PAIR
     outs = pl.pallas_call(
         functools.partial(far_kernel, halo, pairs),
-        out_shape=(out,) * (2 * pairs) + (send,),
+        out_shape=(out,) * pairs + (shifted,) * pairs + (send,),
         in_specs=[SMEM] + [VMEM] * (4 + pairs),
         out_specs=(VMEM,) * (2 * pairs + 1),
         compiler_params=pltpu.CompilerParams(vmem_limit_bytes=LIMIT),
@@ -167,31 +203,33 @@
     return outs[:pairs], outs[pairs : 2 * pairs], outs[-1]
 
 
-def conv_kernel(layer, last, pitch, half, place_ref, act_ref, values_ref, w_ref, columns_ref, *refs):
-    earlier_refs, outs, x_ref = refs[:-3], refs[-3:-1], refs[-1]
-    _, channels, lanes_in = act_ref.shape
-    lanes = x_ref.shape[3] // PAIR
+def conv_kernel(
+    layer, last, sends, received, pitch, half, place_ref, shifted_ref, values_ref, w_ref, columns_ref, *refs
+):
+    scratch = refs[-1:] if received else ()
+    outs = refs[received or 1 : len(refs) - len(scratch)]
+    if received:
+        earlier_ref = scratch[0]
+        for t in range(PAIR):
+            parts = [ref[t] for ref in refs[:received]]
+            spread(earlier_ref, t, parts[0] if received == 1 else jnp.concatenate(parts, axis=1), pitch)
+    else:
+        earlier_ref = refs[0]
+    _, _, channels, lanes = shifted_ref.shape
     chunks = lanes // LANES
     lane = lane_of(LANES)
-    for j in range(2 * PAIR):
-        parts = [ref[j % PAIR] for ref in (earlier_refs if j < PAIR else (act_ref,))]
-        middle = parts[0] if len(parts) == 1 else jnp.concatenate(parts, axis=1)
-        above = pltpu.roll(middle, pitch, 1)
-        edge = jnp.where(lane < pitch, 0.0, above[:, :LANES].astype(jnp.float32)).astype(jnp.bfloat16)
-        below = pltpu.roll(middle, lanes_in - pitch, 1)
-        for t in range(PAIR):
-            if 0 <= j - t < 3:
-                for tap, lines in enumerate((above, middle, below)):
-                    x_ref[j - t, tap, :, t * lanes : (t + 1) * lanes] = lines[:, :lanes]
-                x_ref[j - t, 0, :, t * lanes : t * lanes + LANES] = edge
-    tiles = [
-        jnp.dot(
-            w_ref[...],
-            x_ref[:, :, :, at : at + TILE].reshape(9 * channels, TILE),
-            preferred_element_type=jnp.float32,
-        )
-        for at in range(0, PAIR * lanes, TILE)
-    ]
+
+    def window(t, b):
+        taken = [(earlier_ref, t + a) if t + a < PAIR else (shifted_ref, t + a - PAIR) for a in range(3)]
+        at = slice(b * LANES, (b + 1) * LANES)
+        return jnp.concatenate([ref[j, :, :, at].reshape(3 * channels, LANES) for ref, j in taken], axis=0)
+
+    places = [(t, b) for t in range(PAIR) for b in range(chunks)]
+    side = TILE // LANES
+    tiles = []
+    for n in range(0, len(places), side):
+        rhs = jnp.concatenate([window(t, b) for t, b in places[n : n + side]], axis=1)
+        tiles.append(jnp.dot(w_ref[...], rhs, preferred_element_type=jnp.float32))
     bias = columns_ref[layer, 1]
     if not last:
         mask = filled(lanes, pitch)
@@ -202,7 +240,7 @@
             tile, at = divmod((t * chunks + b) * LANES, TILE)
             return tiles[tile][tap * channels : (tap + 1) * channels, at : at + LANES]
 
-        totals = []
+        totals, acts = [], []
         from_left = 0.0
         from_right = pltpu.roll(sums(2, 0), LANES - 1, 1)
         for b in range(chunks):
@@ -217,8 +255,12 @@
             totals.append(total.astype(jnp.float32))
             if not last:
                 outs[0][t, :, at] = total
-                outs[1][t, :, at] = activated(totals[-1], gain, mask[:, at])
-        if last:
+                acts.append(activated(totals[-1], gain, mask[:, at]))
+                if sends:
+                    outs[2][t, :, at] = acts[-1]
+        if not last:
+            spread(outs[1], t, jnp.concatenate(acts, axis=1), pitch)
+        else:
             whole = jnp.concatenate(totals, axis=1)
             halo = pitch - 1 - half
             whole = jnp.where(place_ref[0] == 1, pltpu.roll(whole, lanes - halo, 1), whole)
@@ -235,16 +277,22 @@
             outs[1][t] = jnp.where(outer, inner, outermost).astype(jnp.bfloat16)
 
 
-def conv(layer, last, pitch, rows_left, half, place, earlier, act, values, weight, columns):
-    _, channels, _ = act.shape
-    lanes = rounded(rows_left * pitch)
-    out = jax.ShapeDtypeStruct((PAIR, channels, LANES if last else lanes), jnp.bfloat16)
+def conv(layer, last, sends, received, pitch, rows_left, half, place, earlier, shifted, values, weight, columns):
+    _, _, channels, lanes = shifted.shape
+    if last:
+        out_shape = (jax.ShapeDtypeStruct((PAIR, channels, LANES), jnp.bfloat16),) * 2
+    else:
+        out_shape = (
+            jax.ShapeDtypeStruct((PAIR, channels, lanes), jnp.bfloat16),
+            jax.ShapeDtypeStruct((PAIR, 3, channels, rounded((rows_left - 1) * pitch)), jnp.bfloat16),
+        )
+        out_shape += out_shape[:1] * sends
     return pl.pallas_call(
-        functools.partial(conv_kernel, layer, last, pitch, half),
-        out_shape=(out, out),
+        functools.partial(conv_kernel, layer, last, sends, received, pitch, half),
+        out_shape=out_shape,
         in_specs=[SMEM] + [VMEM] * (4 + len(earlier)),
-        out_specs=(VMEM, VMEM),
-        scratch_shapes=[pltpu.VMEM((3, 3, channels, PAIR * lanes), jnp.bfloat16)],
+        out_specs=(VMEM,) * len(out_shape),
+        scratch_shapes=[pltpu.VMEM((PAIR, 3, channels, lanes), jnp.bfloat16)] * (received > 0),
         compiler_params=pltpu.CompilerParams(vmem_limit_bytes=LIMIT),
         cost_estimate=pl.CostEstimate(
             flops=54 * channels * channels * PAIR * lanes,
@@ -252,7 +300,7 @@
             transcendentals=PAIR * channels * lanes,
         ),
         name=f"conv_{layer}",
-    )(place, act, values, weight, columns, *earlier)
+    )(place, shifted, values, weight, columns, *earlier)
 
 
 def join_kernel(place_ref, *refs):
@@ -302,29 +350,45 @@
 
     far = lax.ppermute(latents, "rows", [(i, i ^ 2) for i in range(strips)])
     mate = mate_of(latents)
-    weight, columns = weights(place, conv_weight, norm_gains, biases)
-    near_values, near_act = near(layers, place, latents, mate, norm_gains)
+    row_values = jnp.concatenate([norm_gains, biases], axis=0)
+    weight, (columns,) = weights(0, layers - 1, place, conv_weight, row_values)
+    near_values, near_act = near(layers, place, latents, mate, row_values)
     halo_near = earlier_of(near_act[-1])
     far, weight, columns, near_values, near_act, halo_near = lax.optimization_barrier(
         (far, weight, columns, near_values, near_act, halo_near)
     )
-    values, act, send = beyond(layers, place, far, mate_of(far), near_values, near_act, columns)
+    last_weight, _ = weights(layers - 1, 1, place, conv_weight)
+    far_mate, last_weight = lax.optimization_barrier((mate_of(far), last_weight))
+    weight = weight + last_weight
+    values, shifted, send = beyond(layers, place, far, far_mate, near_values, near_act, columns)
     halo = (halo_near, earlier_of(send))
     pitch = width // 2 + layers + 1
     pairs = frames // PAIR
     for layer in range(layers):
         last = layer == layers - 1
         rows_left = 2 * rows + layers - 1 - layer
-        if layer:
-            halo = (earlier_of(act[-1]),)
         results = [None] * pairs
         for p in reversed(range(pairs)):
-            earlier = (act[p - 1],) if p else halo
+            earlier, received = ((shifted[p - 1],), 0) if p else (halo, len(halo))
             results[p] = conv(
-                layer, last, pitch, rows_left, width // 2, place, earlier, act[p], values[p], weight[layer], columns
+                layer,
+                last,
+                p == pairs - 1,
+                received,
+                pitch,
+                rows_left,
+                width // 2,
+                place,
+                earlier,
+                shifted[p],
+                values[p],
+                weight[layer],
+                columns,
             )
-        values, act = [r[0] for r in results], [r[1] for r in results]
-    got = [mate_of(send) for send in act]
+        values, shifted = [r[0] for r in results], [r[1] for r in results]
+        if not last:
+            halo = (earlier_of(results[-1][2]),)
+    got = [mate_of(send) for send in shifted]
     return join(place, values, got, latents.shape)
 
 

time: 50.3 us -> 51.5 us (1.024)
  local copies, waits for them, and re-layouts: 6.31 us -> 0.99 us
  Pallas kernels: 23.7 us -> 28.4 us
  starting transfers between devices: 17 us -> 18.2 us
  other arithmetic: 0.08 us -> 0.79 us
    unnamed x10 -> x2, local copies, waits for them, and re-layouts: 6.31 us -> 0.99 us
    pallas_call x7 -> x8, Pallas kernels: 19.9 us -> 24.2 us  [the longest x6 18 us: conv(): pl.pallas_call(functools.partial(conv_kernel, layer, last, sends, receive...]
    ppermute x4, starting transfers between devices: 13.4 us -> 15 us  [earlier_of(): return lax.ppermute(block, 'tm', [(i, i + 1) for i in range(blocks - 1)])]
    ppermute x4, waiting for transfers between devices: 2.66 us -> 1.23 us  [mate_of(): return lax.ppermute(block, 'rows', [(i, i ^ 1) for i in range(strips)])]
    ppermute x4, waiting for transfers between devices: 0.05 us -> 1.44 us  [earlier_of(): return lax.ppermute(block, 'tm', [(i, i + 1) for i in range(blocks - 1)])]
    concatenate x0 -> x1, other arithmetic: none -> 0.71 us  [on_device(): row_values = jnp.concatenate([norm_gains, biases], axis=0)]
  transfers between devices with their start and end apart: 9 -> 9, of which waited for: 2 -> 3; matrix products, arithmetic and copies ran while one was open for 0% -> 2% of each run, Pallas kernels for 42% -> 50%
where the time goes in v1:
time: 51.5 us; the launch traced here: 51.2 us
  Pallas kernels  28.4 us (55%)
  starting transfers between devices  18.2 us (35%)
  waiting for transfers between devices  2.68 us (5%)
  local copies, waits for them, and re-layouts  0.99 us (2%)
  other arithmetic  0.79 us (2%)
    pallas_call x6, Pallas kernels, conv(): pl.pallas_call(functools.partial(conv_kernel, layer, last, sends, receive...  18 us
    ppermute x4, starting transfers between devices, earlier_of(): return lax.ppermute(block, 'tm', [(i, i + 1) for i in range(blocks - 1)])  15 us
    pallas_call x2, Pallas kernels, weights(): pl.pallas_call(functools.partial(weights_kernel, first, columns), out_sha...  6.19 us
    ppermute x1, starting transfers between devices, on_device(): far = lax.ppermute(latents, 'rows', [(i, i ^ 2) for i in range(strips)])  2.49 us
    pallas_call x1, Pallas kernels, beyond(): pl.pallas_call(functools.partial(far_kernel, halo, pairs), out_shape=(out...  1.55 us
    pallas_call x1, Pallas kernels, join(): pl.pallas_call(join_kernel, out_shape=jax.ShapeDtypeStruct(shape, jnp.bfl...  1.48 us
    ppermute x4, waiting for transfers between devices, earlier_of(): return lax.ppermute(block, 'tm', [(i, i + 1) for i in range(blocks - 1)])  1.44 us
    ppermute x4, waiting for transfers between devices, mate_of(): return lax.ppermute(block, 'rows', [(i, i ^ 1) for i in range(strips)])  1.23 us
  transfers between devices with their start and end apart: 9, of which 3 were waited for; matrix products, arithmetic and copies ran while one was open for 2% of the time, Pallas kernels for 50%

profile of v1, /device:TPU:0, one launch (start us, length us, event | category | flops | bytes accessed | tf_op | source)
XLA Modules:
  0.0 51.2 jit_solution(5905291593720897361)
XLA Ops:
  0.0 0.5 collective-permute-start.1
  0.5 2.5 %collective-permute-start = (bf16[4,2,192,128]{3,2,1,0:T(8,128)(2,1)}, bf16[4,2,192,128]{3,2,1,0:T(8,128)(2,1)S(1)}, u32[]{:S(2)}, u32[]{:S(2)}) collective-permute-start(bf16[4,2,192,128]{3,2,1,0:T(8,128)(2,1)} %own_ref.1), channel_id=1, source_target_pairs={{0,2},{1,3},{2,0},{3,1},{4,6},{5,7},{6,4},{7,5},{8,10},{9,11},{10,... | collective-permute-start | bytes 1179656 | tf_op jit(solution)/shard_map/ppermute | solution.py:351
  2.9 0.1 pad_add_fusion.place_ref
  3.0 0.7 %pad_maximum_fusion.refs_0_.gains_ref = f32[6,192]{1,0:T(8,128)S(1)} fusion(f32[3,192]{1,0:T(4,128)} %param.7, f32[3,192]{1,0:T(4,128)} %param.6), kind=kLoop, calls=%fused_computation | loop fusion | flops 1152 | bytes 9216 | tf_op jit(solution)/shard_map/concatenate | solution.py:353
  3.7 0.0 collective-permute-done.1.mate_ref
  3.7 0.0 copy-start
  3.7 1.0 %copy-done = bf16[4,2,192,128]{3,2,1,0:T(8,128)(2,1)S(1)} copy-done((bf16[4,2,192,128]{3,2,1,0:T(8,128)(2,1)S(1)}, bf16[4,2,192,128]{3,2,1,0:T(8,128)(2,1)}, u32[]{:S(2)}) %copy-start) | copy-done | bytes 393240
  4.7 1.2 %near.1 = (bf16[4,192,384]{2,1,0:T(8,128)(2,1)S(1)}, bf16[2,192,256]{2,1,0:T(8,128)(2,1)S(1)}, bf16[2,192,256]{2,1,0:T(8,128)(2,1)S(1)}) custom-call(s32[3]{0:T(128)S(1)} %pad_add_fusion.place_ref, bf16[4,2,192,128]{3,2,1,0:T(8,128)(2,1)S(1)} %copy-done, bf16[4,2,192,128]{3,2,1,0:T(8,128)(2,1)S(1)} %collective-permute-done.1.mate_ref, ...), custom_call_target="tpu_custom_call" | custom-call | flops 7864320 | bytes 1572864 | tf_op jit(solution)/shard_map/near/pallas_call | solution.py:145
  5.9 3.5 %collective-permute-start.2 = (bf16[2,192,256]{2,1,0:T(8,128)(2,1)S(1)}, bf16[2,192,256]{2,1,0:T(8,128)(2,1)S(1)}, u32[]{:S(2)}, u32[]{:S(2)}) collective-permute-start(bf16[2,192,256]{2,1,0:T(8,128)(2,1)S(1)} %get-tuple-element.51.refs_1_), channel_id=1, source_target_pairs={{0,4},{4,8},{8,12},{1,5},{5,9},{9,13},{2,6},{6,10},{10,14},{3,7},{... | collective-permute-start | bytes 589832 | tf_op jit(solution)/shard_map/ppermute | solution.py:349
  9.4 3.5 %weights.2 = (bf16[576,1728]{1,0:T(8,128)(2,1)S(1)}, bf16[576,1728]{1,0:T(8,128)(2,1)S(1)}, f32[3,2,192,128]{3,2,1,0:T(8,128)S(1)}) custom-call(s32[3]{0:T(128)S(1)} %pad_add_fusion.place_ref, bf16[3,27,192,192]{3,2,1,0:T(8,128)(2,1)} %w_ref.3, f32[6,192]{1,0:T(8,128)S(1)} %pad_maximum_fusion.refs_0_.gains_ref), custom_call_target="tpu_custom_call" | custom-call | bytes 7962624 | tf_op jit(solution)/shard_map/weights/pallas_call | solution.py:78
  12.9 0.0 collective-permute-done.far_ref
  12.9 1.0 %collective-permute-done.2.refs_0_ = bf16[2,192,256]{2,1,0:T(8,128)(2,1)S(1)} collective-permute-done((bf16[2,192,256]{2,1,0:T(8,128)(2,1)S(1)}, bf16[2,192,256]{2,1,0:T(8,128)(2,1)S(1)}, u32[]{:S(2)}, u32[]{:S(2)}) %collective-permute-start.2) | collective-permute-done | bytes 196640 | tf_op jit(solution)/shard_map/ppermute | solution.py:349
  13.9 0.0 collective-permute-start.3
  14.0 2.7 %weights.3.w_ref = bf16[576,1728]{1,0:T(8,128)(2,1)S(1)} custom-call(s32[3]{0:T(128)S(1)} %pad_add_fusion.place_ref, bf16[3,27,192,192]{3,2,1,0:T(8,128)(2,1)} %w_ref.3), custom_call_target="tpu_custom_call" | custom-call | bytes 3981312 | tf_op jit(solution)/shard_map/weights/pallas_call | solution.py:78
  16.6 0.0 collective-permute-done.3.mate_ref
  16.7 1.6 %beyond.1 = (bf16[2,192,512]{2,1,0:T(8,128)(2,1)S(1)}, bf16[2,192,512]{2,1,0:T(8,128)(2,1)S(1)}, bf16[2,3,192,512]{3,2,1,0:T(8,128)(2,1)S(1)}, bf16[2,3,192,512]...) custom-call(s32[3]{0:T(128)S(1)} %pad_add_fusion.place_ref, bf16[4,2,192,128]{3,2,1,0:T(8,128)(2,1)S(1)} %collective-permute-done.far_ref, ...), custom_call_target="tpu_custom_call" | custom-call | flops 7864320 | bytes 1572864 | tf_op jit(solution)/shard_map/beyond/pallas_call | solution.py:194
  18.2 4.4 %collective-permute-start.4 = (bf16[2,192,256]{2,1,0:T(8,128)(2,1)S(1)}, bf16[2,192,256]{2,1,0:T(8,128)(2,1)S(1)}, u32[]{:S(2)}, u32[]{:S(2)}) collective-permute-start(bf16[2,192,256]{2,1,0:T(8,128)(2,1)S(1)} %get-tuple-element.56), channel_id=1, source_target_pairs={{0,4},{4,8},{8,12},{1,5},{5,9},{9,13},{2,6},{6,10},{10,14},{3,7},{... | collective-permute-start | bytes 589832 | tf_op jit(solution)/shard_map/ppermute | solution.py:349
  22.6 3.3 %conv_0.3 = (bf16[2,192,512]{2,1,0:T(8,128)(2,1)S(1)}, bf16[2,3,192,384]{3,2,1,0:T(8,128)(2,1)S(1)}, bf16[2,192,512]{2,1,0:T(8,128)(2,1)S(1)}) custom-call(s32[3]{0:T(128)S(1)} %pad_add_fusion.place_ref, bf16[2,3,192,512]{3,2,1,0:T(8,128)(2,1)S(1)} %get-tuple-element.60.shifted_ref, bf16[2,192,512]{2,1,0:T(8,128)(2,1)S(1)} %get-tuple-element.61.values_ref, ...), custom_call_target="tpu_custom_call" | custom-call | flops 2038431744 | bytes 1990656 | tf_op jit(solution)/shard_map/conv_0/pallas_call | solution.py:290
  25.9 3.5 %collective-permute-start.5 = (bf16[2,192,512]{2,1,0:T(8,128)(2,1)S(1)}, bf16[2,192,512]{2,1,0:T(8,128)(2,1)S(1)}, u32[]{:S(2)}, u32[]{:S(2)}) collective-permute-start(bf16[2,192,512]{2,1,0:T(8,128)(2,1)S(1)} %get-tuple-element.62), channel_id=1, source_target_pairs={{0,4},{4,8},{8,12},{1,5},{5,9},{9,13},{2,6},{6,10},{10,14},{3,7},{... | collective-permute-start | bytes 1179656 | tf_op jit(solution)/shard_map/ppermute | solution.py:349
  29.4 0.0 collective-permute-done.4.refs_1_
  29.5 3.5 %conv_0.2 = (bf16[2,192,512]{2,1,0:T(8,128)(2,1)S(1)}, bf16[2,3,192,384]{3,2,1,0:T(8,128)(2,1)S(1)}) custom-call(s32[3]{0:T(128)S(1)} %pad_add_fusion.place_ref, bf16[2,3,192,512]{3,2,1,0:T(8,128)(2,1)S(1)} %get-tuple-element.52.shifted_ref.refs_0_, bf16[2,192,512]{2,1,0:T(8,128)(2,1)S(1)} %get-tuple-element.53.values_ref, ...), custom_call_target="tpu_custom_call" | custom-call | flops 2038431744 | bytes 1990656 | tf_op jit(solution)/shard_map/conv_0/pallas_call | solution.py:290
  32.9 2.8 %conv_1.3 = (bf16[2,192,384]{2,1,0:T(8,128)(2,1)S(1)}, bf16[2,3,192,384]{3,2,1,0:T(8,128)(2,1)S(1)}, bf16[2,192,384]{2,1,0:T(8,128)(2,1)S(1)}) custom-call(s32[3]{0:T(128)S(1)} %pad_add_fusion.place_ref, bf16[2,3,192,384]{3,2,1,0:T(8,128)(2,1)S(1)} %get-tuple-element.66.shifted_ref, bf16[2,192,512]{2,1,0:T(8,128)(2,1)S(1)} %get-tuple-element.67.values_ref, ...), custom_call_target="tpu_custom_call" | custom-call | flops 1528823808 | bytes 1990656 | tf_op jit(solution)/shard_map/conv_1/pallas_call | solution.py:290
  35.7 3.7 %collective-permute-start.6 = (bf16[2,192,384]{2,1,0:T(8,128)(2,1)S(1)}, bf16[2,192,384]{2,1,0:T(8,128)(2,1)S(1)}, u32[]{:S(2)}, u32[]{:S(2)}) collective-permute-start(bf16[2,192,384]{2,1,0:T(8,128)(2,1)S(1)} %get-tuple-element.68), channel_id=1, source_target_pairs={{0,4},{4,8},{8,12},{1,5},{5,9},{9,13},{2,6},{6,10},{10,14},{3,7},{... | collective-permute-start | bytes 884744 | tf_op jit(solution)/shard_map/ppermute | solution.py:349
  39.4 2.9 %conv_1.2 = (bf16[2,192,384]{2,1,0:T(8,128)(2,1)S(1)}, bf16[2,3,192,384]{3,2,1,0:T(8,128)(2,1)S(1)}) custom-call(s32[3]{0:T(128)S(1)} %pad_add_fusion.place_ref, bf16[2,3,192,384]{3,2,1,0:T(8,128)(2,1)S(1)} %get-tuple-element.57.shifted_ref.refs_0_, bf16[2,192,512]{2,1,0:T(8,128)(2,1)S(1)} %get-tuple-element.58.values_ref, ...), custom_call_target="tpu_custom_call" | custom-call | flops 1528823808 | bytes 1990656 | tf_op jit(solution)/shard_map/conv_1/pallas_call | solution.py:290
  42.3 2.7 %conv_2.3 = (bf16[2,192,128]{2,1,0:T(8,128)(2,1)S(1)}, bf16[2,192,128]{2,1,0:T(8,128)(2,1)S(1)}) custom-call(s32[3]{0:T(128)S(1)} %pad_add_fusion.place_ref, bf16[2,3,192,384]{3,2,1,0:T(8,128)(2,1)S(1)} %get-tuple-element.70.shifted_ref, bf16[2,192,384]{2,1,0:T(8,128)(2,1)S(1)} %get-tuple-element.71.values_ref, bf16[576,1728]{1,0:T(8,128)(2,1)S(1)} %weights.3.w_ref, ...), custom_call_target="tpu_custom_call" | custom-call | flops 1528823808 | bytes 1990656 | tf_op jit(solution)/shard_map/conv_2/pallas_call | solution.py:290
  45.0 0.1 collective-permute-start.8
  45.1 0.4 collective-permute-done.6.refs_0_
  45.5 2.9 %conv_2.2 = (bf16[2,192,128]{2,1,0:T(8,128)(2,1)S(1)}, bf16[2,192,128]{2,1,0:T(8,128)(2,1)S(1)}) custom-call(s32[3]{0:T(128)S(1)} %pad_add_fusion.place_ref, bf16[2,3,192,384]{3,2,1,0:T(8,128)(2,1)S(1)} %get-tuple-element.63.shifted_ref.refs_0_, bf16[2,192,384]{2,1,0:T(8,128)(2,1)S(1)} %get-tuple-element.64.values_ref, bf16[576,1728]{1,0:T(8,128)(2,1)S(1)} %weights.3.w_ref, ...), custom_call_target="tpu_custom_call" | custom-call | flops 1528823808 | bytes 1990656 | tf_op jit(solution)/shard_map/conv_2/pallas_call | solution.py:290
  48.4 0.1 collective-permute-start.7
  48.5 0.0 collective-permute-done.8.refs_3_
  48.5 1.2 %collective-permute-done.7.refs_2_ = bf16[2,192,128]{2,1,0:T(8,128)(2,1)S(1)} collective-permute-done((bf16[2,192,128]{2,1,0:T(8,128)(2,1)S(1)}, bf16[2,192,128]{2,1,0:T(8,128)(2,1)S(1)}, u32[]{:S(2)}, u32[]{:S(2)}) %collective-permute-start.7) | collective-permute-done | bytes 98336 | tf_op jit(solution)/shard_map/ppermute | solution.py:346
  49.8 1.5 %join.1 = bf16[4,2,192,128]{3,2,1,0:T(8,128)(2,1)} custom-call(s32[3]{0:T(128)S(1)} %pad_add_fusion.place_ref, bf16[2,192,128]{2,1,0:T(8,128)(2,1)S(1)} %get-tuple-element.69.refs_0_, bf16[2,192,128]{2,1,0:T(8,128)(2,1)S(1)} %get-tuple-element.72.refs_1_, bf16[2,192,128]{2,1,0:T(8,128)(2,1)S(1)} %collective-permute-done.7.refs_2_, ...), custom_call_target="tpu_custom_call" | custom-call | tf_op jit(solution)/shard_map/join/pallas_call | solution.py:326
  (1 shorter events, 0.0 us)
Async XLA Ops:
  0.0 3.7 %collective-permute-start.1 = (bf16[4,2,192,128]{3,2,1,0:T(8,128)(2,1)}, bf16[4,2,192,128]{3,2,1,0:T(8,128)(2,1)S(1)}, u32[]{:S(2)}, u32[]{:S(2)}) collective-permute-start(bf16[4,2,192,128]{3,2,1,0:T(8,128)(2,1)} %own_ref.1), channel_id=1, source_target_pairs={{0,1},{1,0},{2,3},{3,2},{4,5},{5,4},{6,7},{7,6},{8,9},{9,8},{10,11... | collective-permute-start | bytes 1179656 | tf_op jit(solution)/shard_map/ppermute | solution.py:346
  0.5 12.5 %collective-permute-start = (bf16[4,2,192,128]{3,2,1,0:T(8,128)(2,1)}, bf16[4,2,192,128]{3,2,1,0:T(8,128)(2,1)S(1)}, u32[]{:S(2)}, u32[]{:S(2)}) collective-permute-start(bf16[4,2,192,128]{3,2,1,0:T(8,128)(2,1)} %own_ref.1), channel_id=1, source_target_pairs={{0,2},{1,3},{2,0},{3,1},{4,6},{5,7},{6,4},{7,5},{8,10},{9,11},{10,... | collective-permute-start | bytes 1179656 | tf_op jit(solution)/shard_map/ppermute | solution.py:351
  3.7 1.0 %copy-start = (bf16[4,2,192,128]{3,2,1,0:T(8,128)(2,1)S(1)}, bf16[4,2,192,128]{3,2,1,0:T(8,128)(2,1)}, u32[]{:S(2)}) copy-start(bf16[4,2,192,128]{3,2,1,0:T(8,128)(2,1)} %own_ref.1) | copy-start | bytes 1179652
  5.9 8.0 %collective-permute-start.2 = (bf16[2,192,256]{2,1,0:T(8,128)(2,1)S(1)}, bf16[2,192,256]{2,1,0:T(8,128)(2,1)S(1)}, u32[]{:S(2)}, u32[]{:S(2)}) collective-permute-start(bf16[2,192,256]{2,1,0:T(8,128)(2,1)S(1)} %get-tuple-element.51.refs_1_), channel_id=1, source_target_pairs={{0,4},{4,8},{8,12},{1,5},{5,9},{9,13},{2,6},{6,10},{10,14},{3,7},{... | collective-permute-start | bytes 589832 | tf_op jit(solution)/shard_map/ppermute | solution.py:349
  13.9 2.7 %collective-permute-start.3 = (bf16[4,2,192,128]{3,2,1,0:T(8,128)(2,1)S(1)}, bf16[4,2,192,128]{3,2,1,0:T(8,128)(2,1)S(1)}, u32[]{:S(2)}, u32[]{:S(2)}) collective-permute-start(bf16[4,2,192,128]{3,2,1,0:T(8,128)(2,1)S(1)} %collective-permute-done.far_ref), channel_id=1, source_target_pairs={{0,1},{1,0},{2,3},{3,2},{4,5},{5,4},{6,7},{7,6},{8,9},{9,8},{10,11... | collective-permute-start | bytes 1179656 | tf_op jit(solution)/shard_map/ppermute | solution.py:346
  18.2 11.2 %collective-permute-start.4 = (bf16[2,192,256]{2,1,0:T(8,128)(2,1)S(1)}, bf16[2,192,256]{2,1,0:T(8,128)(2,1)S(1)}, u32[]{:S(2)}, u32[]{:S(2)}) collective-permute-start(bf16[2,192,256]{2,1,0:T(8,128)(2,1)S(1)} %get-tuple-element.56), channel_id=1, source_target_pairs={{0,4},{4,8},{8,12},{1,5},{5,9},{9,13},{2,6},{6,10},{10,14},{3,7},{... | collective-permute-start | bytes 589832 | tf_op jit(solution)/shard_map/ppermute | solution.py:349
  25.9 13.4 %collective-permute-start.5 = (bf16[2,192,512]{2,1,0:T(8,128)(2,1)S(1)}, bf16[2,192,512]{2,1,0:T(8,128)(2,1)S(1)}, u32[]{:S(2)}, u32[]{:S(2)}) collective-permute-start(bf16[2,192,512]{2,1,0:T(8,128)(2,1)S(1)} %get-tuple-element.62), channel_id=1, source_target_pairs={{0,4},{4,8},{8,12},{1,5},{5,9},{9,13},{2,6},{6,10},{10,14},{3,7},{... | collective-permute-start | bytes 1179656 | tf_op jit(solution)/shard_map/ppermute | solution.py:349
  35.7 9.8 %collective-permute-start.6 = (bf16[2,192,384]{2,1,0:T(8,128)(2,1)S(1)}, bf16[2,192,384]{2,1,0:T(8,128)(2,1)S(1)}, u32[]{:S(2)}, u32[]{:S(2)}) collective-permute-start(bf16[2,192,384]{2,1,0:T(8,128)(2,1)S(1)} %get-tuple-element.68), channel_id=1, source_target_pairs={{0,4},{4,8},{8,12},{1,5},{5,9},{9,13},{2,6},{6,10},{10,14},{3,7},{... | collective-permute-start | bytes 884744 | tf_op jit(solution)/shard_map/ppermute | solution.py:349
  45.0 3.5 %collective-permute-start.8 = (bf16[2,192,128]{2,1,0:T(8,128)(2,1)S(1)}, bf16[2,192,128]{2,1,0:T(8,128)(2,1)S(1)}, u32[]{:S(2)}, u32[]{:S(2)}) collective-permute-start(bf16[2,192,128]{2,1,0:T(8,128)(2,1)S(1)} %get-tuple-element.74), channel_id=1, source_target_pairs={{0,1},{1,0},{2,3},{3,2},{4,5},{5,4},{6,7},{7,6},{8,9},{9,8},{10,11... | collective-permute-start | bytes 294920 | tf_op jit(solution)/shard_map/ppermute | solution.py:346
  48.4 1.4 %collective-permute-start.7 = (bf16[2,192,128]{2,1,0:T(8,128)(2,1)S(1)}, bf16[2,192,128]{2,1,0:T(8,128)(2,1)S(1)}, u32[]{:S(2)}, u32[]{:S(2)}) collective-permute-start(bf16[2,192,128]{2,1,0:T(8,128)(2,1)S(1)} %get-tuple-element.73), channel_id=1, source_target_pairs={{0,1},{1,0},{2,3},{3,2},{4,5},{5,4},{6,7},{7,6},{8,9},{9,8},{10,11... | collective-permute-start | bytes 294920 | tf_op jit(solution)/shard_map/ppermute | solution.py:346

commit v2 on v1

--- a/solution.py
+++ b/solution.py
@@ -15,7 +15,7 @@
 SMEM = pl.BlockSpec(memory_space=pltpu.SMEM)
 ANY = pl.BlockSpec(memory_space=pl.ANY)
 LIMIT = 24 * 1024 * 1024
-LARGE = 48 * 1024 * 1024
+LARGE = 44 * 1024 * 1024
 
 
 def rounded(lanes):
@@ -227,28 +227,25 @@
     places = [(t, b) for t in range(PAIR) for b in range(chunks)]
     side = TILE // LANES
     tiles = []
-    for n in range(0, len(places), side):
-        rhs = jnp.concatenate([window(t, b) for t, b in places[n : n + side]], axis=1)
-        tiles.append(jnp.dot(w_ref[...], rhs, preferred_element_type=jnp.float32))
     bias = columns_ref[layer, 1]
     if not last:
         mask = filled(lanes, pitch)
         gain = columns_ref[layer + 1, 0]
-    for t in range(PAIR):
-
-        def sums(tap, b):
-            tile, at = divmod((t * chunks + b) * LANES, TILE)
-            return tiles[tile][tap * channels : (tap + 1) * channels, at : at + LANES]
-
+
+    def sums(t, tap, b):
+        tile, at = divmod((t * chunks + b) * LANES, TILE)
+        return tiles[tile][tap * channels : (tap + 1) * channels, at : at + LANES]
+
+    def finish(t):
         totals, acts = [], []
         from_left = 0.0
-        from_right = pltpu.roll(sums(2, 0), LANES - 1, 1)
+        from_right = pltpu.roll(sums(t, 2, 0), LANES - 1, 1)
         for b in range(chunks):
             at = slice(b * LANES, (b + 1) * LANES)
-            left = pltpu.roll(sums(0, b), 1, 1)
-            right = pltpu.roll(sums(2, b + 1), LANES - 1, 1) if b + 1 < chunks else 0.0
+            left = pltpu.roll(sums(t, 0, b), 1, 1)
+            right = pltpu.roll(sums(t, 2, b + 1), LANES - 1, 1) if b + 1 < chunks else 0.0
             summed = (
-                jnp.where(lane == 0, from_left, left) + sums(1, b) + jnp.where(lane == LANES - 1, right, from_right)
+                jnp.where(lane == 0, from_left, left) + sums(t, 1, b) + jnp.where(lane == LANES - 1, right, from_right)
             )
             from_left, from_right = left, right
             total = (values_ref[t, :, at].astype(jnp.float32) + summed + bias).astype(jnp.bfloat16)
@@ -260,21 +257,29 @@
                     outs[2][t, :, at] = acts[-1]
         if not last:
             spread(outs[1], t, jnp.concatenate(acts, axis=1), pitch)
-        else:
-            whole = jnp.concatenate(totals, axis=1)
-            halo = pitch - 1 - half
-            whole = jnp.where(place_ref[0] == 1, pltpu.roll(whole, lanes - halo, 1), whole)
-            left_half = lane < half
-
-            def rows_of(row):
-                one = whole if row == 0 else pltpu.roll(whole, lanes - row * pitch, 1)
-                two = pltpu.roll(whole, lanes - (row + 1) * pitch + half, 1)
-                return jnp.where(left_half, one[:, :LANES], two[:, :LANES])
-
-            outermost, inner = rows_of(0), rows_of(2)
-            outer = place_ref[2] == 1
-            outs[0][t] = jnp.where(outer, outermost, inner).astype(jnp.bfloat16)
-            outs[1][t] = jnp.where(outer, inner, outermost).astype(jnp.bfloat16)
+            return
+        whole = jnp.concatenate(totals, axis=1)
+        halo = pitch - 1 - half
+        whole = jnp.where(place_ref[0] == 1, pltpu.roll(whole, lanes - halo, 1), whole)
+        left_half = lane < half
+
+        def rows_of(row):
+            one = whole if row == 0 else pltpu.roll(whole, lanes - row * pitch, 1)
+            two = pltpu.roll(whole, lanes - (row + 1) * pitch + half, 1)
+            return jnp.where(left_half, one[:, :LANES], two[:, :LANES])
+
+        outermost, inner = rows_of(0), rows_of(2)
+        outer = place_ref[2] == 1
+        outs[0][t] = jnp.where(outer, outermost, inner).astype(jnp.bfloat16)
+        outs[1][t] = jnp.where(outer, inner, outermost).astype(jnp.bfloat16)
+
+    finished = 0
+    for n in range(0, len(places), side):
+        rhs = jnp.concatenate([window(t, b) for t, b in places[n : n + side]], axis=1)
+        tiles.append(jnp.dot(w_ref[...], rhs, preferred_element_type=jnp.float32))
+        while finished < PAIR and (finished + 1) * chunks <= n + side:
+            finish(finished)
+            finished += 1
 
 
 def conv(layer, last, sends, received, pitch, rows_left, half, place, earlier, shifted, values, weight, columns):
@@ -303,34 +308,37 @@
     )(place, shifted, values, weight, columns, *earlier)
 
 
-def join_kernel(place_ref, *refs):
-    out_ref = refs[-1]
-    kept, got = refs[: len(refs) // 2], refs[len(refs) // 2 : -1]
-    _, rows, _, width = out_ref.shape
+def join_kernel(pair, place_ref, kept_ref, got_ref, *refs):
+    out_ref, lines_ref, sem = refs[-3:]
+    _, rows, _, width = lines_ref.shape
     half = width // 2
     first, group = place_ref[0] == 0, place_ref[1]
     left_half = lane_of(width) < half
-    for p in range(len(kept)):
-        for t in range(PAIR):
-            mine, theirs = kept[p][t].astype(jnp.float32), got[p][t].astype(jnp.float32)
-            left, right = jnp.where(first, mine, theirs), jnp.where(first, theirs, mine)
-            lines = (
-                jnp.where(left_half, left, pltpu.roll(right, half, 1)),
-                jnp.where(left_half, pltpu.roll(left, half, 1), right),
-            )
-            for j in range(rows):
-                out_ref[PAIR * p + t, j + group * (rows - 1 - 2 * j)] = lines[j].astype(jnp.bfloat16)
-
-
-def join(place, kept, got, shape):
+    for t in range(PAIR):
+        mine, theirs = kept_ref[t].astype(jnp.float32), got_ref[t].astype(jnp.float32)
+        left, right = jnp.where(first, mine, theirs), jnp.where(first, theirs, mine)
+        lines = (
+            jnp.where(left_half, left, pltpu.roll(right, half, 1)),
+            jnp.where(left_half, pltpu.roll(left, half, 1), right),
+        )
+        for j in range(rows):
+            lines_ref[t, j + group * (rows - 1 - 2 * j)] = lines[j].astype(jnp.bfloat16)
+    copy = pltpu.make_async_copy(lines_ref, out_ref.at[pl.ds(PAIR * pair, PAIR)], sem)
+    copy.start()
+    copy.wait()
+
+
+def join(place, pair, kept, got, shape, *so_far):
     return pl.pallas_call(
-        join_kernel,
+        functools.partial(join_kernel, pair),
         out_shape=jax.ShapeDtypeStruct(shape, jnp.bfloat16),
-        in_specs=[SMEM] + [VMEM] * (2 * len(kept)),
-        out_specs=VMEM,
+        in_specs=[SMEM, VMEM, VMEM] + [ANY] * len(so_far),
+        out_specs=ANY,
+        scratch_shapes=[pltpu.VMEM((PAIR,) + shape[1:], jnp.bfloat16), pltpu.SemaphoreType.DMA],
+        input_output_aliases={3: 0} if so_far else {},
         compiler_params=pltpu.CompilerParams(vmem_limit_bytes=LIMIT),
         name="join",
-    )(place, *kept, *got)
+    )(place, kept, got, *so_far)
 
 
 def on_device(latents, conv_weight, norm_gains, biases):
@@ -351,16 +359,13 @@
     far = lax.ppermute(latents, "rows", [(i, i ^ 2) for i in range(strips)])
     mate = mate_of(latents)
     row_values = jnp.concatenate([norm_gains, biases], axis=0)
-    weight, (columns,) = weights(0, layers - 1, place, conv_weight, row_values)
+    weight, (columns,) = weights(0, layers, place, conv_weight, row_values)
     near_values, near_act = near(layers, place, latents, mate, row_values)
     halo_near = earlier_of(near_act[-1])
     far, weight, columns, near_values, near_act, halo_near = lax.optimization_barrier(
         (far, weight, columns, near_values, near_act, halo_near)
     )
-    last_weight, _ = weights(layers - 1, 1, place, conv_weight)
-    far_mate, last_weight = lax.optimization_barrier((mate_of(far), last_weight))
-    weight = weight + last_weight
-    values, shifted, send = beyond(layers, place, far, far_mate, near_values, near_act, columns)
+    values, shifted, send = beyond(layers, place, far, mate_of(far), near_values, near_act, columns)
     halo = (halo_near, earlier_of(send))
     pitch = width // 2 + layers + 1
     pairs = frames // PAIR
@@ -388,8 +393,10 @@
         values, shifted = [r[0] for r in results], [r[1] for r in results]
         if not last:
             halo = (earlier_of(results[-1][2]),)
-    got = [mate_of(send) for send in shifted]
-    return join(place, values, got, latents.shape)
+    result = ()
+    for p in reversed(range(pairs)):
+        result = (join(place, p, values[p], mate_of(shifted[p]), latents.shape, *result),)
+    return result[0]
 
 
 def solution(mesh):

time: 51.5 us -> 50.7 us (0.984)
  waiting for transfers between devices: 2.68 us -> 1.99 us
  Pallas kernels: 28.4 us -> 27.8 us
    pallas_call x2 -> x1, Pallas kernels: 6.19 us -> 4.3 us  [weights(): pl.pallas_call(functools.partial(weights_kernel, first, columns), out_sha...]
    pallas_call x1 -> x2, Pallas kernels: 1.48 us -> 2.71 us  [join(): pl.pallas_call(functools.partial(join_kernel, pair), out_shape=jax.ShapeD...]
    ppermute x4, waiting for transfers between devices: 1.44 us -> 0.26 us  [earlier_of(): return lax.ppermute(block, 'tm', [(i, i + 1) for i in range(blocks - 1)])]
  transfers between devices with their start and end apart: 9 -> 9, of which waited for: 3 -> 2; matrix products, arithmetic and copies ran while one was open for 2% -> 2% of each run, Pallas kernels for 50% -> 49%
where the time goes in v2:
time: 50.7 us; the launch traced here: 50.5 us
  Pallas kernels  27.8 us (55%)
  starting transfers between devices  18.6 us (37%)
  waiting for transfers between devices  1.99 us (4%)
  local copies, waits for them, and re-layouts  0.99 us (2%)
  other arithmetic  0.79 us (2%)
    pallas_call x6, Pallas kernels, conv(): pl.pallas_call(functools.partial(conv_kernel, layer, last, sends, receive...  18.1 us
    ppermute x4, starting transfers between devices, earlier_of(): return lax.ppermute(block, 'tm', [(i, i + 1) for i in range(blocks - 1)])  15 us
    pallas_call x1, Pallas kernels, weights(): pl.pallas_call(functools.partial(weights_kernel, first, columns), out_sha...  4.3 us
    pallas_call x2, Pallas kernels, join(): pl.pallas_call(functools.partial(join_kernel, pair), out_shape=jax.ShapeD...  2.71 us
    ppermute x1, starting transfers between devices, on_device(): far = lax.ppermute(latents, 'rows', [(i, i ^ 2) for i in range(strips)])  2.49 us
    ppermute x4, waiting for transfers between devices, mate_of(): return lax.ppermute(block, 'rows', [(i, i ^ 1) for i in range(strips)])  1.73 us
    pallas_call x1, Pallas kernels, beyond(): pl.pallas_call(functools.partial(far_kernel, halo, pairs), out_shape=(out...  1.55 us
    pallas_call x1, Pallas kernels, near(): pl.pallas_call(functools.partial(near_kernel, halo), out_shape=(jax.Shape...  1.18 us
  transfers between devices with their start and end apart: 9, of which 2 were waited for; matrix products, arithmetic and copies ran while one was open for 2% of the time, Pallas kernels for 49%

profile of v2, /device:TPU:0, one launch (start us, length us, event | category | flops | bytes accessed | tf_op | source)
XLA Modules:
  0.0 50.5 jit_solution(8078277494786571247)
XLA Ops:
  0.0 0.5 collective-permute-start.1
  0.5 2.5 %collective-permute-start = (bf16[4,2,192,128]{3,2,1,0:T(8,128)(2,1)}, bf16[4,2,192,128]{3,2,1,0:T(8,128)(2,1)S(1)}, u32[]{:S(2)}, u32[]{:S(2)}) collective-permute-start(bf16[4,2,192,128]{3,2,1,0:T(8,128)(2,1)} %own_ref.1), channel_id=1, source_target_pairs={{0,2},{1,3},{2,0},{3,1},{4,6},{5,7},{6,4},{7,5},{8,10},{9,11},{10,... | collective-permute-start | bytes 1179656 | tf_op jit(solution)/shard_map/ppermute | solution.py:359
  2.9 0.1 pad_add_fusion.place_ref
  3.0 0.7 %pad_maximum_fusion.refs_0_.gains_ref = f32[6,192]{1,0:T(8,128)S(1)} fusion(f32[3,192]{1,0:T(4,128)} %param.7, f32[3,192]{1,0:T(4,128)} %param.6), kind=kLoop, calls=%fused_computation | loop fusion | flops 1152 | bytes 9216 | tf_op jit(solution)/shard_map/concatenate | solution.py:361
  3.7 0.0 collective-permute-done.1.mate_ref
  3.7 0.0 copy-start
  3.7 1.0 %copy-done = bf16[4,2,192,128]{3,2,1,0:T(8,128)(2,1)S(1)} copy-done((bf16[4,2,192,128]{3,2,1,0:T(8,128)(2,1)S(1)}, bf16[4,2,192,128]{3,2,1,0:T(8,128)(2,1)}, u32[]{:S(2)}) %copy-start) | copy-done | bytes 393240
  4.7 1.2 %near.1 = (bf16[4,192,384]{2,1,0:T(8,128)(2,1)S(1)}, bf16[2,192,256]{2,1,0:T(8,128)(2,1)S(1)}, bf16[2,192,256]{2,1,0:T(8,128)(2,1)S(1)}) custom-call(s32[3]{0:T(128)S(1)} %pad_add_fusion.place_ref, bf16[4,2,192,128]{3,2,1,0:T(8,128)(2,1)S(1)} %copy-done, bf16[4,2,192,128]{3,2,1,0:T(8,128)(2,1)S(1)} %collective-permute-done.1.mate_ref, ...), custom_call_target="tpu_custom_call" | custom-call | flops 7864320 | bytes 1572864 | tf_op jit(solution)/shard_map/near/pallas_call | solution.py:145
  5.9 3.5 %collective-permute-start.2 = (bf16[2,192,256]{2,1,0:T(8,128)(2,1)S(1)}, bf16[2,192,256]{2,1,0:T(8,128)(2,1)S(1)}, u32[]{:S(2)}, u32[]{:S(2)}) collective-permute-start(bf16[2,192,256]{2,1,0:T(8,128)(2,1)S(1)} %get-tuple-element.51.refs_1_), channel_id=1, source_target_pairs={{0,4},{4,8},{8,12},{1,5},{5,9},{9,13},{2,6},{6,10},{10,14},{3,7},{... | collective-permute-start | bytes 589832 | tf_op jit(solution)/shard_map/ppermute | solution.py:357
  9.4 4.3 %weights.1 = (bf16[576,1728]{1,0:T(8,128)(2,1)S(1)}, bf16[576,1728]{1,0:T(8,128)(2,1)S(1)}, bf16[576,1728]{1,0:T(8,128)(2,1)S(1)}, f32[3,2,192,128]{3,2,1,0:T(8,128)S(1)}) custom-call(s32[3]{0:T(128)S(1)} %pad_add_fusion.place_ref, bf16[3,27,192,192]{3,2,1,0:T(8,128)(2,1)} %w_ref.1, f32[6,192]{1,0:T(8,128)S(1)} %pad_maximum_fusion.refs_0_.gains_ref), custom_call_target="tpu_custom_call" | custom-call | bytes 11943936 | tf_op jit(solution)/shard_map/weights/pallas_call | solution.py:78
  13.7 0.0 collective-permute-done.far_ref
  13.7 0.2 collective-permute-done.2.refs_0_
  13.9 0.0 collective-permute-start.3
  14.0 1.7 %collective-permute-done.3.mate_ref = bf16[4,2,192,128]{3,2,1,0:T(8,128)(2,1)S(1)} collective-permute-done((bf16[4,2,192,128]{3,2,1,0:T(8,128)(2,1)S(1)}, bf16[4,2,192,128]{3,2,1,0:T(8,128)(2,1)S(1)}, u32[]{:S(2)}, u32[]{:S(2)}) %collective-permute-start.3) | collective-permute-done | bytes 393248 | tf_op jit(solution)/shard_map/ppermute | solution.py:354
  15.7 1.6 %beyond.1 = (bf16[2,192,512]{2,1,0:T(8,128)(2,1)S(1)}, bf16[2,192,512]{2,1,0:T(8,128)(2,1)S(1)}, bf16[2,3,192,512]{3,2,1,0:T(8,128)(2,1)S(1)}, bf16[2,3,192,512]...) custom-call(s32[3]{0:T(128)S(1)} %pad_add_fusion.place_ref, bf16[4,2,192,128]{3,2,1,0:T(8,128)(2,1)S(1)} %collective-permute-done.far_ref, ...), custom_call_target="tpu_custom_call" | custom-call | flops 7864320 | bytes 1572864 | tf_op jit(solution)/shard_map/beyond/pallas_call | solution.py:194
  17.2 4.4 %collective-permute-start.4 = (bf16[2,192,256]{2,1,0:T(8,128)(2,1)S(1)}, bf16[2,192,256]{2,1,0:T(8,128)(2,1)S(1)}, u32[]{:S(2)}, u32[]{:S(2)}) collective-permute-start(bf16[2,192,256]{2,1,0:T(8,128)(2,1)S(1)} %get-tuple-element.56), channel_id=1, source_target_pairs={{0,4},{4,8},{8,12},{1,5},{5,9},{9,13},{2,6},{6,10},{10,14},{3,7},{... | collective-permute-start | bytes 589832 | tf_op jit(solution)/shard_map/ppermute | solution.py:357
  21.6 3.3 %conv_0.3 = (bf16[2,192,512]{2,1,0:T(8,128)(2,1)S(1)}, bf16[2,3,192,384]{3,2,1,0:T(8,128)(2,1)S(1)}, bf16[2,192,512]{2,1,0:T(8,128)(2,1)S(1)}) custom-call(s32[3]{0:T(128)S(1)} %pad_add_fusion.place_ref, bf16[2,3,192,512]{3,2,1,0:T(8,128)(2,1)S(1)} %get-tuple-element.60.shifted_ref, bf16[2,192,512]{2,1,0:T(8,128)(2,1)S(1)} %get-tuple-element.61.values_ref, ...), custom_call_target="tpu_custom_call" | custom-call | flops 2038431744 | bytes 1990656 | tf_op jit(solution)/shard_map/conv_0/pallas_call | solution.py:295
  24.9 3.5 %collective-permute-start.5 = (bf16[2,192,512]{2,1,0:T(8,128)(2,1)S(1)}, bf16[2,192,512]{2,1,0:T(8,128)(2,1)S(1)}, u32[]{:S(2)}, u32[]{:S(2)}) collective-permute-start(bf16[2,192,512]{2,1,0:T(8,128)(2,1)S(1)} %get-tuple-element.62), channel_id=1, source_target_pairs={{0,4},{4,8},{8,12},{1,5},{5,9},{9,13},{2,6},{6,10},{10,14},{3,7},{... | collective-permute-start | bytes 1179656 | tf_op jit(solution)/shard_map/ppermute | solution.py:357
  28.4 0.0 collective-permute-done.4.refs_1_
  28.5 3.4 %conv_0.2 = (bf16[2,192,512]{2,1,0:T(8,128)(2,1)S(1)}, bf16[2,3,192,384]{3,2,1,0:T(8,128)(2,1)S(1)}) custom-call(s32[3]{0:T(128)S(1)} %pad_add_fusion.place_ref, bf16[2,3,192,512]{3,2,1,0:T(8,128)(2,1)S(1)} %get-tuple-element.52.shifted_ref.refs_0_, bf16[2,192,512]{2,1,0:T(8,128)(2,1)S(1)} %get-tuple-element.53.values_ref, ...), custom_call_target="tpu_custom_call" | custom-call | flops 2038431744 | bytes 1990656 | tf_op jit(solution)/shard_map/conv_0/pallas_call | solution.py:295
  31.9 2.8 %conv_1.3 = (bf16[2,192,384]{2,1,0:T(8,128)(2,1)S(1)}, bf16[2,3,192,384]{3,2,1,0:T(8,128)(2,1)S(1)}, bf16[2,192,384]{2,1,0:T(8,128)(2,1)S(1)}) custom-call(s32[3]{0:T(128)S(1)} %pad_add_fusion.place_ref, bf16[2,3,192,384]{3,2,1,0:T(8,128)(2,1)S(1)} %get-tuple-element.66.shifted_ref, bf16[2,192,512]{2,1,0:T(8,128)(2,1)S(1)} %get-tuple-element.67.values_ref, ...), custom_call_target="tpu_custom_call" | custom-call | flops 1528823808 | bytes 1990656 | tf_op jit(solution)/shard_map/conv_1/pallas_call | solution.py:295
  34.7 3.7 %collective-permute-start.6 = (bf16[2,192,384]{2,1,0:T(8,128)(2,1)S(1)}, bf16[2,192,384]{2,1,0:T(8,128)(2,1)S(1)}, u32[]{:S(2)}, u32[]{:S(2)}) collective-permute-start(bf16[2,192,384]{2,1,0:T(8,128)(2,1)S(1)} %get-tuple-element.68), channel_id=1, source_target_pairs={{0,4},{4,8},{8,12},{1,5},{5,9},{9,13},{2,6},{6,10},{10,14},{3,7},{... | collective-permute-start | bytes 884744 | tf_op jit(solution)/shard_map/ppermute | solution.py:357
  38.4 0.0 collective-permute-done.5.refs_0_
  38.4 2.9 %conv_1.2 = (bf16[2,192,384]{2,1,0:T(8,128)(2,1)S(1)}, bf16[2,3,192,384]{3,2,1,0:T(8,128)(2,1)S(1)}) custom-call(s32[3]{0:T(128)S(1)} %pad_add_fusion.place_ref, bf16[2,3,192,384]{3,2,1,0:T(8,128)(2,1)S(1)} %get-tuple-element.57.shifted_ref.refs_0_, bf16[2,192,512]{2,1,0:T(8,128)(2,1)S(1)} %get-tuple-element.58.values_ref, ...), custom_call_target="tpu_custom_call" | custom-call | flops 1528823808 | bytes 1990656 | tf_op jit(solution)/shard_map/conv_1/pallas_call | solution.py:295
  41.3 2.7 %conv_2.3 = (bf16[2,192,128]{2,1,0:T(8,128)(2,1)S(1)}, bf16[2,192,128]{2,1,0:T(8,128)(2,1)S(1)}) custom-call(s32[3]{0:T(128)S(1)} %pad_add_fusion.place_ref, bf16[2,3,192,384]{3,2,1,0:T(8,128)(2,1)S(1)} %get-tuple-element.71.shifted_ref, bf16[2,192,384]{2,1,0:T(8,128)(2,1)S(1)} %get-tuple-element.72.values_ref, ...), custom_call_target="tpu_custom_call" | custom-call | flops 1528823808 | bytes 1990656 | tf_op jit(solution)/shard_map/conv_2/pallas_call | solution.py:295
  44.0 0.1 collective-permute-start.8
  44.1 0.1 collective-permute-done.6.refs_0_
  44.2 2.9 %conv_2.2 = (bf16[2,192,128]{2,1,0:T(8,128)(2,1)S(1)}, bf16[2,192,128]{2,1,0:T(8,128)(2,1)S(1)}) custom-call(s32[3]{0:T(128)S(1)} %pad_add_fusion.place_ref, bf16[2,3,192,384]{3,2,1,0:T(8,128)(2,1)S(1)} %get-tuple-element.63.shifted_ref.refs_0_, bf16[2,192,384]{2,1,0:T(8,128)(2,1)S(1)} %get-tuple-element.64.values_ref, ...), custom_call_target="tpu_custom_call" | custom-call | flops 1528823808 | bytes 1990656 | tf_op jit(solution)/shard_map/conv_2/pallas_call | solution.py:295
  47.1 0.5 %collective-permute-start.7 = (bf16[2,192,128]{2,1,0:T(8,128)(2,1)S(1)}, bf16[2,192,128]{2,1,0:T(8,128)(2,1)S(1)}, u32[]{:S(2)}, u32[]{:S(2)}) collective-permute-start(bf16[2,192,128]{2,1,0:T(8,128)(2,1)S(1)} %get-tuple-element.70), channel_id=1, source_target_pairs={{0,1},{1,0},{2,3},{3,2},{4,5},{5,4},{6,7},{7,6},{8,9},{9,8},{10,11... | collective-permute-start | bytes 294920 | tf_op jit(solution)/shard_map/ppermute | solution.py:354
  47.6 1.4 %join.2.refs_0_ = bf16[4,2,192,128]{3,2,1,0:T(8,128)(2,1)} custom-call(s32[3]{0:T(128)S(1)} %pad_add_fusion.place_ref, bf16[2,192,128]{2,1,0:T(8,128)(2,1)S(1)} %get-tuple-element.73.kept_ref, bf16[2,192,128]{2,1,0:T(8,128)(2,1)S(1)} %collective-permute-done.8.got_ref), custom_call_target="tpu_custom_call" | custom-call | tf_op jit(solution)/shard_map/join/pallas_call | solution.py:332
  48.9 0.0 collective-permute-done.7.got_ref
  48.9 1.4 %join.3 = bf16[4,2,192,128]{3,2,1,0:T(8,128)(2,1)} custom-call(s32[3]{0:T(128)S(1)} %pad_add_fusion.place_ref, bf16[2,192,128]{2,1,0:T(8,128)(2,1)S(1)} %get-tuple-element.69.kept_ref, bf16[2,192,128]{2,1,0:T(8,128)(2,1)S(1)} %collective-permute-done.7.got_ref, bf16[4,2,192,128]{3,2,1,0:T(8,128)(2,1)} %join.2.refs_0_), custom_call_target="tpu_custom_call", output_to_operand_aliasing={{}: (3, {})} | custom-call | tf_op jit(solution)/shard_map/join/pallas_call | solution.py:332
  (1 shorter events, 0.0 us)
Async XLA Ops:
  0.0 3.7 %collective-permute-start.1 = (bf16[4,2,192,128]{3,2,1,0:T(8,128)(2,1)}, bf16[4,2,192,128]{3,2,1,0:T(8,128)(2,1)S(1)}, u32[]{:S(2)}, u32[]{:S(2)}) collective-permute-start(bf16[4,2,192,128]{3,2,1,0:T(8,128)(2,1)} %own_ref.1), channel_id=1, source_target_pairs={{0,1},{1,0},{2,3},{3,2},{4,5},{5,4},{6,7},{7,6},{8,9},{9,8},{10,11... | collective-permute-start | bytes 1179656 | tf_op jit(solution)/shard_map/ppermute | solution.py:354
  0.5 13.3 %collective-permute-start = (bf16[4,2,192,128]{3,2,1,0:T(8,128)(2,1)}, bf16[4,2,192,128]{3,2,1,0:T(8,128)(2,1)S(1)}, u32[]{:S(2)}, u32[]{:S(2)}) collective-permute-start(bf16[4,2,192,128]{3,2,1,0:T(8,128)(2,1)} %own_ref.1), channel_id=1, source_target_pairs={{0,2},{1,3},{2,0},{3,1},{4,6},{5,7},{6,4},{7,5},{8,10},{9,11},{10,... | collective-permute-start | bytes 1179656 | tf_op jit(solution)/shard_map/ppermute | solution.py:359
  3.7 1.0 %copy-start = (bf16[4,2,192,128]{3,2,1,0:T(8,128)(2,1)S(1)}, bf16[4,2,192,128]{3,2,1,0:T(8,128)(2,1)}, u32[]{:S(2)}) copy-start(bf16[4,2,192,128]{3,2,1,0:T(8,128)(2,1)} %own_ref.1) | copy-start | bytes 1179652
  5.9 8.0 %collective-permute-start.2 = (bf16[2,192,256]{2,1,0:T(8,128)(2,1)S(1)}, bf16[2,192,256]{2,1,0:T(8,128)(2,1)S(1)}, u32[]{:S(2)}, u32[]{:S(2)}) collective-permute-start(bf16[2,192,256]{2,1,0:T(8,128)(2,1)S(1)} %get-tuple-element.51.refs_1_), channel_id=1, source_target_pairs={{0,4},{4,8},{8,12},{1,5},{5,9},{9,13},{2,6},{6,10},{10,14},{3,7},{... | collective-permute-start | bytes 589832 | tf_op jit(solution)/shard_map/ppermute | solution.py:357
  13.9 1.7 %collective-permute-start.3 = (bf16[4,2,192,128]{3,2,1,0:T(8,128)(2,1)S(1)}, bf16[4,2,192,128]{3,2,1,0:T(8,128)(2,1)S(1)}, u32[]{:S(2)}, u32[]{:S(2)}) collective-permute-start(bf16[4,2,192,128]{3,2,1,0:T(8,128)(2,1)S(1)} %collective-permute-done.far_ref), channel_id=1, source_target_pairs={{0,1},{1,0},{2,3},{3,2},{4,5},{5,4},{6,7},{7,6},{8,9},{9,8},{10,11... | collective-permute-start | bytes 1179656 | tf_op jit(solution)/shard_map/ppermute | solution.py:354
  17.2 11.2 %collective-permute-start.4 = (bf16[2,192,256]{2,1,0:T(8,128)(2,1)S(1)}, bf16[2,192,256]{2,1,0:T(8,128)(2,1)S(1)}, u32[]{:S(2)}, u32[]{:S(2)}) collective-permute-start(bf16[2,192,256]{2,1,0:T(8,128)(2,1)S(1)} %get-tuple-element.56), channel_id=1, source_target_pairs={{0,4},{4,8},{8,12},{1,5},{5,9},{9,13},{2,6},{6,10},{10,14},{3,7},{... | collective-permute-start | bytes 589832 | tf_op jit(solution)/shard_map/ppermute | solution.py:357
  24.9 13.4 %collective-permute-start.5 = (bf16[2,192,512]{2,1,0:T(8,128)(2,1)S(1)}, bf16[2,192,512]{2,1,0:T(8,128)(2,1)S(1)}, u32[]{:S(2)}, u32[]{:S(2)}) collective-permute-start(bf16[2,192,512]{2,1,0:T(8,128)(2,1)S(1)} %get-tuple-element.62), channel_id=1, source_target_pairs={{0,4},{4,8},{8,12},{1,5},{5,9},{9,13},{2,6},{6,10},{10,14},{3,7},{... | collective-permute-start | bytes 1179656 | tf_op jit(solution)/shard_map/ppermute | solution.py:357
  34.7 9.5 %collective-permute-start.6 = (bf16[2,192,384]{2,1,0:T(8,128)(2,1)S(1)}, bf16[2,192,384]{2,1,0:T(8,128)(2,1)S(1)}, u32[]{:S(2)}, u32[]{:S(2)}) collective-permute-start(bf16[2,192,384]{2,1,0:T(8,128)(2,1)S(1)} %get-tuple-element.68), channel_id=1, source_target_pairs={{0,4},{4,8},{8,12},{1,5},{5,9},{9,13},{2,6},{6,10},{10,14},{3,7},{... | collective-permute-start | bytes 884744 | tf_op jit(solution)/shard_map/ppermute | solution.py:357
  44.0 3.5 %collective-permute-start.8 = (bf16[2,192,128]{2,1,0:T(8,128)(2,1)S(1)}, bf16[2,192,128]{2,1,0:T(8,128)(2,1)S(1)}, u32[]{:S(2)}, u32[]{:S(2)}) collective-permute-start(bf16[2,192,128]{2,1,0:T(8,128)(2,1)S(1)} %get-tuple-element.74), channel_id=1, source_target_pairs={{0,1},{1,0},{2,3},{3,2},{4,5},{5,4},{6,7},{7,6},{8,9},{9,8},{10,11... | collective-permute-start | bytes 294920 | tf_op jit(solution)/shard_map/ppermute | solution.py:354
  47.1 1.9 %collective-permute-start.7 = (bf16[2,192,128]{2,1,0:T(8,128)(2,1)S(1)}, bf16[2,192,128]{2,1,0:T(8,128)(2,1)S(1)}, u32[]{:S(2)}, u32[]{:S(2)}) collective-permute-start(bf16[2,192,128]{2,1,0:T(8,128)(2,1)S(1)} %get-tuple-element.70), channel_id=1, source_target_pairs={{0,1},{1,0},{2,3},{3,2},{4,5},{5,4},{6,7},{7,6},{8,9},{9,8},{10,11... | collective-permute-start | bytes 294920 | tf_op jit(solution)/shard_map/ppermute | solution.py:354

commit v3 on v2

--- a/solution.py
+++ b/solution.py
@@ -12,10 +12,15 @@
 LANES = 128
 TILE = 256
 VMEM = pl.BlockSpec(memory_space=pltpu.VMEM)
-SMEM = pl.BlockSpec(memory_space=pltpu.SMEM)
 ANY = pl.BlockSpec(memory_space=pl.ANY)
 LIMIT = 24 * 1024 * 1024
 LARGE = 44 * 1024 * 1024
+
+
+def place():
+    strip = lax.axis_index("rows").astype(jnp.int32)
+    core, group = strip & 1, strip >> 1
+    return core, group, core == group
 
 
 def rounded(lanes):
@@ -51,11 +56,11 @@
     return copies
 
 
-def weights_kernel(first, columns, place_ref, w_ref, *refs):
+def weights_kernel(first, columns, w_ref, *refs):
     outs, held_ref, sems = refs[columns:-2], refs[-2], refs[-1]
     count, _, channels_out, ins = held_ref.shape
     copies = fetched([(w_ref.at[first + i], held_ref.at[i]) for i in range(count)], sems)
-    flipped = place_ref[1]
+    _, flipped, _ = place()
     if columns:
         rows_ref = refs[0]
         layers = rows_ref.shape[0] // 2
@@ -71,14 +76,14 @@
                 outs[i][:, at : at + ins] = held_ref[i, pl.ds(source, 3)].reshape(3 * channels_out, ins)
 
 
-def weights(first, count, place, conv_weight, *rows):
+def weights(first, count, conv_weight, *rows):
     layers, taps, outs, ins = conv_weight.shape
     one = jax.ShapeDtypeStruct((3 * outs, 9 * ins), conv_weight.dtype)
     columns = len(rows)
     results = pl.pallas_call(
         functools.partial(weights_kernel, first, columns),
         out_shape=(one,) * count + (jax.ShapeDtypeStruct((layers, 2, outs, LANES), jnp.float32),) * columns,
-        in_specs=[SMEM, ANY] + [VMEM] * columns,
+        in_specs=[ANY] + [VMEM] * columns,
         out_specs=(VMEM,) * (count + columns),
         scratch_shapes=[
             pltpu.VMEM((count, taps, outs, ins), conv_weight.dtype),
@@ -89,7 +94,7 @@
             flops=0, bytes_accessed=4 * conv_weight.size * count // layers, transcendentals=0
         ),
         name="weights",
-    )(place, conv_weight, *rows)
+    )(conv_weight, *rows)
     return list(results[:count]), results[count:]
 
 
@@ -104,11 +109,11 @@
     out_ref[index, 2] = below[:, :lanes]
 
 
-def placed(blocks, place_ref, row, window, line):
+def placed(blocks, core, row, window, line):
     pitch, width = window + 1, line.shape[1]
     lane = lane_of(LANES)
     block, low = divmod(row * pitch, LANES)
-    shift = lax.rem(low + LANES - place_ref[0] * (width - window), LANES)
+    shift = lax.rem(low + LANES - core * (width - window), LANES)
     turned = pltpu.roll(line, shift, 1)
     here = (lane >= low) & (lane < low + window)
     blocks[block] = blocks.get(block, 0.0) + jnp.where(here, turned, 0.0)
@@ -116,10 +121,10 @@
         blocks[block + 1] = blocks.get(block + 1, 0.0) + jnp.where(lane < low + window - LANES, turned, 0.0)
 
 
-def near_kernel(halo, place_ref, own_ref, mate_ref, gains_ref, values_ref, *act_refs):
+def near_kernel(halo, own_ref, mate_ref, gains_ref, values_ref, *act_refs):
     frames, rows, _, width = own_ref.shape
     window = width // 2 + halo
-    group, outer = place_ref[1], place_ref[2] == 1
+    core, group, outer = place()
     gain = column(gains_ref[0:1, :])
     done = act_refs[0].shape[2]
     mask = filled(done, window + 1)
@@ -130,7 +135,7 @@
             index = at + group * (rows - 1 - 2 * at)
             one, two = (own_ref, mate_ref) if row < rows else (mate_ref, own_ref)
             line = jnp.where(outer, one[f, index], two[f, index]).astype(jnp.float32)
-            placed(blocks, place_ref, row, window, line)
+            placed(blocks, core, row, window, line)
         for b in blocks:
             part = slice(b * LANES, (b + 1) * LANES)
             values_ref[f, :, part] = blocks[b].astype(jnp.bfloat16)
@@ -138,7 +143,7 @@
                 act_refs[f // PAIR][f % PAIR, :, part] = activated(blocks[b], gain, mask[:, part])
 
 
-def near(halo, place, own, mate, gains):
+def near(halo, own, mate, gains):
     frames, rows, channels, width = own.shape
     lanes = 2 * rows * (width // 2 + halo + 1)
     pairs = frames // PAIR
@@ -146,20 +151,20 @@
         functools.partial(near_kernel, halo),
         out_shape=(jax.ShapeDtypeStruct((frames, channels, rounded(lanes)), jnp.bfloat16),)
         + (jax.ShapeDtypeStruct((PAIR, channels, lanes // LANES * LANES), jnp.bfloat16),) * pairs,
-        in_specs=[SMEM] + [VMEM] * 3,
+        in_specs=[VMEM] * 3,
         out_specs=(VMEM,) * (1 + pairs),
         compiler_params=pltpu.CompilerParams(vmem_limit_bytes=LIMIT),
         cost_estimate=pl.CostEstimate(flops=40 * own.size, bytes_accessed=8 * own.size, transcendentals=2 * own.size),
         name="near",
-    )(place, own, mate, gains)
+    )(own, mate, gains)
     return outs[0], outs[1:]
 
 
-def far_kernel(halo, pairs, place_ref, far_ref, mate_ref, near_ref, columns_ref, *refs):
+def far_kernel(halo, pairs, far_ref, mate_ref, near_ref, columns_ref, *refs):
     act_refs, value_refs, out_refs, send_ref = refs[:pairs], refs[pairs : 2 * pairs], refs[2 * pairs : -1], refs[-1]
     frames, rows, _, width = far_ref.shape
     window = width // 2 + halo
-    group, outer = place_ref[1], place_ref[2] == 1
+    core, group, outer = place()
     lanes, done = value_refs[0].shape[2], act_refs[0].shape[2]
     mask = filled(lanes, window + 1)
     for f in range(frames):
@@ -173,7 +178,7 @@
             index = at + (1 - group) * (rows - 1 - 2 * at)
             one, two = (mate_ref, far_ref) if local < rows else (far_ref, mate_ref)
             line = jnp.where(outer, one[f, index], two[f, index]).astype(jnp.float32)
-            placed(blocks, place_ref, row, window, line)
+            placed(blocks, core, row, window, line)
         for b in sorted(blocks):
             part = slice(b * LANES, (b + 1) * LANES)
             value_refs[p][t, :, part] = blocks[b].astype(jnp.bfloat16)
@@ -184,7 +189,7 @@
         spread(out_refs[p], t, jnp.concatenate(acts, axis=1), window + 1)
 
 
-def beyond(halo, place, far, mate, near_values, near_act, columns):
+def beyond(halo, far, mate, near_values, near_act, columns):
     frames, rows, channels, width = far.shape
     lanes = rounded((2 * rows + halo) * (width // 2 + halo + 1))
     out = jax.ShapeDtypeStruct((PAIR, channels, lanes), jnp.bfloat16)
@@ -194,17 +199,17 @@
     outs = pl.pallas_call(
         functools.partial(far_kernel, halo, pairs),
         out_shape=(out,) * pairs + (shifted,) * pairs + (send,),
-        in_specs=[SMEM] + [VMEM] * (4 + pairs),
+        in_specs=[VMEM] * (4 + pairs),
         out_specs=(VMEM,) * (2 * pairs + 1),
         compiler_params=pltpu.CompilerParams(vmem_limit_bytes=LIMIT),
         cost_estimate=pl.CostEstimate(flops=40 * far.size, bytes_accessed=8 * far.size, transcendentals=2 * far.size),
         name="beyond",
-    )(place, far, mate, near_values, columns, *near_act)
+    )(far, mate, near_values, columns, *near_act)
     return outs[:pairs], outs[pairs : 2 * pairs], outs[-1]
 
 
 def conv_kernel(
-    layer, last, sends, received, pitch, half, place_ref, shifted_ref, values_ref, w_ref, columns_ref, *refs
+    layer, last, sends, received, pitch, half, shifted_ref, values_ref, w_ref, columns_ref, *refs
 ):
     scratch = refs[-1:] if received else ()
     outs = refs[received or 1 : len(refs) - len(scratch)]
@@ -260,7 +265,8 @@
             return
         whole = jnp.concatenate(totals, axis=1)
         halo = pitch - 1 - half
-        whole = jnp.where(place_ref[0] == 1, pltpu.roll(whole, lanes - halo, 1), whole)
+        core, _, outer = place()
+        whole = jnp.where(core == 1, pltpu.roll(whole, lanes - halo, 1), whole)
         left_half = lane < half
 
         def rows_of(row):
@@ -269,7 +275,6 @@
             return jnp.where(left_half, one[:, :LANES], two[:, :LANES])
 
         outermost, inner = rows_of(0), rows_of(2)
-        outer = place_ref[2] == 1
         outs[0][t] = jnp.where(outer, outermost, inner).astype(jnp.bfloat16)
         outs[1][t] = jnp.where(outer, inner, outermost).astype(jnp.bfloat16)
 
@@ -282,7 +287,7 @@
             finished += 1
 
 
-def conv(layer, last, sends, received, pitch, rows_left, half, place, earlier, shifted, values, weight, columns):
+def conv(layer, last, sends, received, pitch, rows_left, half, earlier, shifted, values, weight, columns):
     _, _, channels, lanes = shifted.shape
     if last:
         out_shape = (jax.ShapeDtypeStruct((PAIR, channels, LANES), jnp.bfloat16),) * 2
@@ -295,7 +300,7 @@
     return pl.pallas_call(
         functools.partial(conv_kernel, layer, last, sends, received, pitch, half),
         out_shape=out_shape,
-        in_specs=[SMEM] + [VMEM] * (4 + len(earlier)),
+        in_specs=[VMEM] * (4 + len(earlier)),
         out_specs=(VMEM,) * len(out_shape),
         scratch_shapes=[pltpu.VMEM((PAIR, 3, channels, lanes), jnp.bfloat16)] * (received > 0),
         compiler_params=pltpu.CompilerParams(vmem_limit_bytes=LIMIT),
@@ -305,14 +310,15 @@
             transcendentals=PAIR * channels * lanes,
         ),
         name=f"conv_{layer}",
-    )(place, shifted, values, weight, columns, *earlier)
-
-
-def join_kernel(pair, place_ref, kept_ref, got_ref, *refs):
+    )(shifted, values, weight, columns, *earlier)
+
+
+def join_kernel(pair, kept_ref, got_ref, *refs):
     out_ref, lines_ref, sem = refs[-3:]
     _, rows, _, width = lines_ref.shape
     half = width // 2
-    first, group = place_ref[0] == 0, place_ref[1]
+    core, group, _ = place()
+    first = core == 0
     left_half = lane_of(width) < half
     for t in range(PAIR):
         mine, theirs = kept_ref[t].astype(jnp.float32), got_ref[t].astype(jnp.float32)
@@ -328,17 +334,17 @@
     copy.wait()
 
 
-def join(place, pair, kept, got, shape, *so_far):
+def join(pair, kept, got, shape, *so_far):
     return pl.pallas_call(
         functools.partial(join_kernel, pair),
         out_shape=jax.ShapeDtypeStruct(shape, jnp.bfloat16),
-        in_specs=[SMEM, VMEM, VMEM] + [ANY] * len(so_far),
+        in_specs=[VMEM, VMEM] + [ANY] * len(so_far),
         out_specs=ANY,
         scratch_shapes=[pltpu.VMEM((PAIR,) + shape[1:], jnp.bfloat16), pltpu.SemaphoreType.DMA],
-        input_output_aliases={3: 0} if so_far else {},
+        input_output_aliases={2: 0} if so_far else {},
         compiler_params=pltpu.CompilerParams(vmem_limit_bytes=LIMIT),
         name="join",
-    )(place, kept, got, *so_far)
+    )(kept, got, *so_far)
 
 
 def on_device(latents, conv_weight, norm_gains, biases):
@@ -346,9 +352,6 @@
     frames, rows, channels, width = latents.shape
     strips, blocks = lax.axis_size("rows"), lax.axis_size("tm")
     assert strips == 4 and rows == 2 and frames % PAIR == 0 and width == LANES
-    strip = lax.axis_index("rows").astype(jnp.int32)
-    core, group = strip & 1, strip >> 1
-    place = jnp.stack([core, group, (core == group).astype(jnp.int32)])
 
     def mate_of(block):
         return lax.ppermute(block, "rows", [(i, i ^ 1) for i in range(strips)])
@@ -359,13 +362,13 @@
     far = lax.ppermute(latents, "rows", [(i, i ^ 2) for i in range(strips)])
     mate = mate_of(latents)
     row_values = jnp.concatenate([norm_gains, biases], axis=0)
-    weight, (columns,) = weights(0, layers, place, conv_weight, row_values)
-    near_values, near_act = near(layers, place, latents, mate, row_values)
+    weight, (columns,) = weights(0, layers, conv_weight, row_values)
+    near_values, near_act = near(layers, latents, mate, row_values)
     halo_near = earlier_of(near_act[-1])
     far, weight, columns, near_values, near_act, halo_near = lax.optimization_barrier(
         (far, weight, columns, near_values, near_act, halo_near)
     )
-    values, shifted, send = beyond(layers, place, far, mate_of(far), near_values, near_act, columns)
+    values, shifted, send = beyond(layers, far, mate_of(far), near_values, near_act, columns)
     halo = (halo_near, earlier_of(send))
     pitch = width // 2 + layers + 1
     pairs = frames // PAIR
@@ -383,7 +386,6 @@
                 pitch,
                 rows_left,
                 width // 2,
-                place,
                 earlier,
                 shifted[p],
                 values[p],
@@ -395,7 +397,7 @@
             halo = (earlier_of(results[-1][2]),)
     result = ()
     for p in reversed(range(pairs)):
-        result = (join(place, p, values[p], mate_of(shifted[p]), latents.shape, *result),)
+        result = (join(p, values[p], mate_of(shifted[p]), latents.shape, *result),)
     return result[0]
 
 

time: 50.7 us -> 46.3 us (0.913)
  Pallas kernels: 27.8 us -> 21.7 us
  waiting for transfers between devices: 1.99 us -> 4.15 us
    pallas_call x6, Pallas kernels: 18.1 us -> 14.7 us  [conv(): pl.pallas_call(functools.partial(conv_kernel, layer, last, sends, receive...]
    ppermute x4, waiting for transfers between devices: 0.26 us -> 1.61 us  [earlier_of(): return lax.ppermute(block, 'tm', [(i, i + 1) for i in range(blocks - 1)])]
    pallas_call x2, Pallas kernels: 2.71 us -> 1.63 us  [join(): pl.pallas_call(functools.partial(join_kernel, pair), out_shape=jax.ShapeD...]
    pallas_call x1, Pallas kernels: 1.18 us -> 0.63 us  [near(): pl.pallas_call(functools.partial(near_kernel, halo), out_shape=(jax.Shape...]
    pallas_call x1, Pallas kernels: 1.55 us -> 1 us  [beyond(): pl.pallas_call(functools.partial(far_kernel, halo, pairs), out_shape=(out...]
    pallas_call x1, Pallas kernels: 4.3 us -> 3.77 us  [weights(): pl.pallas_call(functools.partial(weights_kernel, first, columns), out_sha...]
  transfers between devices with their start and end apart: 9 -> 9, of which waited for: 2 -> 5; matrix products, arithmetic and copies ran while one was open for 2% -> 2% of each run, Pallas kernels for 49% -> 43%
where the time goes in v3:
time: 46.3 us; the launch traced here: 46 us
  Pallas kernels  21.7 us (47%)
  starting transfers between devices  18.1 us (39%)
  waiting for transfers between devices  4.15 us (9%)
  local copies, waits for them, and re-layouts  0.99 us (2%)
  other arithmetic  0.71 us (2%)
    ppermute x4, starting transfers between devices, earlier_of(): return lax.ppermute(block, 'tm', [(i, i + 1) for i in range(blocks - 1)])  15 us
    pallas_call x6, Pallas kernels, conv(): pl.pallas_call(functools.partial(conv_kernel, layer, last, sends, receive...  14.7 us
    pallas_call x1, Pallas kernels, weights(): pl.pallas_call(functools.partial(weights_kernel, first, columns), out_sha...  3.77 us
    ppermute x1, starting transfers between devices, on_device(): far = lax.ppermute(latents, 'rows', [(i, i ^ 2) for i in range(strips)])  2.49 us
    ppermute x4, waiting for transfers between devices, mate_of(): return lax.ppermute(block, 'rows', [(i, i ^ 1) for i in range(strips)])  2.18 us
    pallas_call x2, Pallas kernels, join(): pl.pallas_call(functools.partial(join_kernel, pair), out_shape=jax.ShapeD...  1.63 us
    ppermute x4, waiting for transfers between devices, earlier_of(): return lax.ppermute(block, 'tm', [(i, i + 1) for i in range(blocks - 1)])  1.61 us
    pallas_call x1, Pallas kernels, beyond(): pl.pallas_call(functools.partial(far_kernel, halo, pairs), out_shape=(out...  1 us
  transfers between devices with their start and end apart: 9, of which 5 were waited for; matrix products, arithmetic and copies ran while one was open for 2% of the time, Pallas kernels for 43%

profile of v3, /device:TPU:0, one launch (start us, length us, event | category | flops | bytes accessed | tf_op | source)
XLA Modules:
  0.0 46.0 jit_solution(8258060417855618457)
XLA Ops:
  0.0 0.5 collective-permute-start.1
  0.5 2.5 %collective-permute-start = (bf16[4,2,192,128]{3,2,1,0:T(8,128)(2,1)}, bf16[4,2,192,128]{3,2,1,0:T(8,128)(2,1)S(1)}, u32[]{:S(2)}, u32[]{:S(2)}) collective-permute-start(bf16[4,2,192,128]{3,2,1,0:T(8,128)(2,1)} %own_ref.1), channel_id=1, source_target_pairs={{0,2},{1,3},{2,0},{3,1},{4,6},{5,7},{6,4},{7,5},{8,10},{9,11},{10,... | collective-permute-start | bytes 1179656 | tf_op jit(solution)/shard_map/ppermute | solution.py:362
  2.9 0.7 %pad_maximum_fusion.refs_0_.gains_ref = f32[6,192]{1,0:T(8,128)S(1)} fusion(f32[3,192]{1,0:T(4,128)} %param.7, f32[3,192]{1,0:T(4,128)} %param.6), kind=kLoop, calls=%fused_computation | loop fusion | flops 1152 | bytes 9216 | tf_op jit(solution)/shard_map/concatenate | solution.py:364
  3.7 0.0 collective-permute-done.1.mate_ref
  3.7 0.0 copy-start
  3.7 1.0 %copy-done = bf16[4,2,192,128]{3,2,1,0:T(8,128)(2,1)S(1)} copy-done((bf16[4,2,192,128]{3,2,1,0:T(8,128)(2,1)S(1)}, bf16[4,2,192,128]{3,2,1,0:T(8,128)(2,1)}, u32[]{:S(2)}) %copy-start) | copy-done | bytes 393240
  4.7 0.6 %near.1 = (bf16[4,192,384]{2,1,0:T(8,128)(2,1)S(1)}, bf16[2,192,256]{2,1,0:T(8,128)(2,1)S(1)}, bf16[2,192,256]{2,1,0:T(8,128)(2,1)S(1)}) custom-call(bf16[4,2,192,128]{3,2,1,0:T(8,128)(2,1)S(1)} %copy-done, bf16[4,2,192,128]{3,2,1,0:T(8,128)(2,1)S(1)} %collective-permute-done.1.mate_ref, f32[6,192]{1,0:T(8,128)S(1)} %pad_maximum_fusion.refs_0_.gains_ref), custom_call_target="tpu_custom_call" | custom-call | flops 7864320 | bytes 1572864 | tf_op jit(solution)/shard_map/near/pallas_call | solution.py:150
  5.3 3.5 %collective-permute-start.2 = (bf16[2,192,256]{2,1,0:T(8,128)(2,1)S(1)}, bf16[2,192,256]{2,1,0:T(8,128)(2,1)S(1)}, u32[]{:S(2)}, u32[]{:S(2)}) collective-permute-start(bf16[2,192,256]{2,1,0:T(8,128)(2,1)S(1)} %get-tuple-element.51.refs_1_), channel_id=1, source_target_pairs={{0,4},{4,8},{8,12},{1,5},{5,9},{9,13},{2,6},{6,10},{10,14},{3,7},{... | collective-permute-start | bytes 589832 | tf_op jit(solution)/shard_map/ppermute | solution.py:360
  8.8 3.8 %weights.1 = (bf16[576,1728]{1,0:T(8,128)(2,1)S(1)}, bf16[576,1728]{1,0:T(8,128)(2,1)S(1)}, bf16[576,1728]{1,0:T(8,128)(2,1)S(1)}, f32[3,2,192,128]{3,2,1,0:T(8,128)S(1)}) custom-call(bf16[3,27,192,192]{3,2,1,0:T(8,128)(2,1)} %w_ref.1, f32[6,192]{1,0:T(8,128)S(1)} %pad_maximum_fusion.refs_0_.gains_ref), custom_call_target="tpu_custom_call" | custom-call | bytes 11943936 | tf_op jit(solution)/shard_map/weights/pallas_call | solution.py:83
  12.6 0.4 collective-permute-done.far_ref
  12.9 0.4 collective-permute-done.2.refs_0_
  13.3 0.0 collective-permute-start.3
  13.3 1.7 %collective-permute-done.3.mate_ref = bf16[4,2,192,128]{3,2,1,0:T(8,128)(2,1)S(1)} collective-permute-done((bf16[4,2,192,128]{3,2,1,0:T(8,128)(2,1)S(1)}, bf16[4,2,192,128]{3,2,1,0:T(8,128)(2,1)S(1)}, u32[]{:S(2)}, u32[]{:S(2)}) %collective-permute-start.3) | collective-permute-done | bytes 393248 | tf_op jit(solution)/shard_map/ppermute | solution.py:357
  15.0 1.0 %beyond.1 = (bf16[2,192,512]{2,1,0:T(8,128)(2,1)S(1)}, bf16[2,192,512]{2,1,0:T(8,128)(2,1)S(1)}, bf16[2,3,192,512]{3,2,1,0:T(8,128)(2,1)S(1)}, bf16[2,3,192,512]...) custom-call(bf16[4,2,192,128]{3,2,1,0:T(8,128)(2,1)S(1)} %collective-permute-done.far_ref, ...), custom_call_target="tpu_custom_call" | custom-call | flops 7864320 | bytes 1572864 | tf_op jit(solution)/shard_map/beyond/pallas_call | solution.py:199
  16.1 4.4 %collective-permute-start.4 = (bf16[2,192,256]{2,1,0:T(8,128)(2,1)S(1)}, bf16[2,192,256]{2,1,0:T(8,128)(2,1)S(1)}, u32[]{:S(2)}, u32[]{:S(2)}) collective-permute-start(bf16[2,192,256]{2,1,0:T(8,128)(2,1)S(1)} %get-tuple-element.56), channel_id=1, source_target_pairs={{0,4},{4,8},{8,12},{1,5},{5,9},{9,13},{2,6},{6,10},{10,14},{3,7},{... | collective-permute-start | bytes 589832 | tf_op jit(solution)/shard_map/ppermute | solution.py:360
  20.5 2.7 %conv_0.3 = (bf16[2,192,512]{2,1,0:T(8,128)(2,1)S(1)}, bf16[2,3,192,384]{3,2,1,0:T(8,128)(2,1)S(1)}, bf16[2,192,512]{2,1,0:T(8,128)(2,1)S(1)}) custom-call(bf16[2,3,192,512]{3,2,1,0:T(8,128)(2,1)S(1)} %get-tuple-element.60.shifted_ref, bf16[2,192,512]{2,1,0:T(8,128)(2,1)S(1)} %get-tuple-element.61.values_ref, bf16[576,1728]{1,0:T(8,128)(2,1)S(1)} %get-tuple-element.54.w_ref, ...), custom_call_target="tpu_custom_call" | custom-call | flops 2038431744 | bytes 1990656 | tf_op jit(solution)/shard_map/conv_0/pallas_call | solution.py:300
  23.2 3.5 %collective-permute-start.5 = (bf16[2,192,512]{2,1,0:T(8,128)(2,1)S(1)}, bf16[2,192,512]{2,1,0:T(8,128)(2,1)S(1)}, u32[]{:S(2)}, u32[]{:S(2)}) collective-permute-start(bf16[2,192,512]{2,1,0:T(8,128)(2,1)S(1)} %get-tuple-element.62), channel_id=1, source_target_pairs={{0,4},{4,8},{8,12},{1,5},{5,9},{9,13},{2,6},{6,10},{10,14},{3,7},{... | collective-permute-start | bytes 1179656 | tf_op jit(solution)/shard_map/ppermute | solution.py:360
  26.7 0.0 collective-permute-done.4.refs_1_
  26.7 2.9 %conv_0.2 = (bf16[2,192,512]{2,1,0:T(8,128)(2,1)S(1)}, bf16[2,3,192,384]{3,2,1,0:T(8,128)(2,1)S(1)}) custom-call(bf16[2,3,192,512]{3,2,1,0:T(8,128)(2,1)S(1)} %get-tuple-element.52.shifted_ref.refs_0_, bf16[2,192,512]{2,1,0:T(8,128)(2,1)S(1)} %get-tuple-element.53.values_ref, bf16[576,1728]{1,0:T(8,128)(2,1)S(1)} %get-tuple-element.54.w_ref, ...), custom_call_target="tpu_custom_call" | custom-call | flops 2038431744 | bytes 1990656 | tf_op jit(solution)/shard_map/conv_0/pallas_call | solution.py:300
  29.6 2.3 %conv_1.3 = (bf16[2,192,384]{2,1,0:T(8,128)(2,1)S(1)}, bf16[2,3,192,384]{3,2,1,0:T(8,128)(2,1)S(1)}, bf16[2,192,384]{2,1,0:T(8,128)(2,1)S(1)}) custom-call(bf16[2,3,192,384]{3,2,1,0:T(8,128)(2,1)S(1)} %get-tuple-element.66.shifted_ref, bf16[2,192,512]{2,1,0:T(8,128)(2,1)S(1)} %get-tuple-element.67.values_ref, bf16[576,1728]{1,0:T(8,128)(2,1)S(1)} %get-tuple-element.59.w_ref, ...), custom_call_target="tpu_custom_call" | custom-call | flops 1528823808 | bytes 1990656 | tf_op jit(solution)/shard_map/conv_1/pallas_call | solution.py:300
  31.8 3.6 %collective-permute-start.6 = (bf16[2,192,384]{2,1,0:T(8,128)(2,1)S(1)}, bf16[2,192,384]{2,1,0:T(8,128)(2,1)S(1)}, u32[]{:S(2)}, u32[]{:S(2)}) collective-permute-start(bf16[2,192,384]{2,1,0:T(8,128)(2,1)S(1)} %get-tuple-element.68), channel_id=1, source_target_pairs={{0,4},{4,8},{8,12},{1,5},{5,9},{9,13},{2,6},{6,10},{10,14},{3,7},{... | collective-permute-start | bytes 884744 | tf_op jit(solution)/shard_map/ppermute | solution.py:360
  35.5 0.0 collective-permute-done.5.refs_0_
  35.5 2.4 %conv_1.2 = (bf16[2,192,384]{2,1,0:T(8,128)(2,1)S(1)}, bf16[2,3,192,384]{3,2,1,0:T(8,128)(2,1)S(1)}) custom-call(bf16[2,3,192,384]{3,2,1,0:T(8,128)(2,1)S(1)} %get-tuple-element.57.shifted_ref.refs_0_, bf16[2,192,512]{2,1,0:T(8,128)(2,1)S(1)} %get-tuple-element.58.values_ref, bf16[576,1728]{1,0:T(8,128)(2,1)S(1)} %get-tuple-element.59.w_ref, ...), custom_call_target="tpu_custom_call" | custom-call | flops 1528823808 | bytes 1990656 | tf_op jit(solution)/shard_map/conv_1/pallas_call | solution.py:300
  37.9 2.2 %conv_2.3 = (bf16[2,192,128]{2,1,0:T(8,128)(2,1)S(1)}, bf16[2,192,128]{2,1,0:T(8,128)(2,1)S(1)}) custom-call(bf16[2,3,192,384]{3,2,1,0:T(8,128)(2,1)S(1)} %get-tuple-element.71.shifted_ref, bf16[2,192,384]{2,1,0:T(8,128)(2,1)S(1)} %get-tuple-element.72.values_ref, bf16[576,1728]{1,0:T(8,128)(2,1)S(1)} %get-tuple-element.65.w_ref, ...), custom_call_target="tpu_custom_call" | custom-call | flops 1528823808 | bytes 1990656 | tf_op jit(solution)/shard_map/conv_2/pallas_call | solution.py:300
  40.1 0.1 collective-permute-start.8
  40.1 1.2 %collective-permute-done.6.refs_0_ = bf16[2,192,384]{2,1,0:T(8,128)(2,1)S(1)} collective-permute-done((bf16[2,192,384]{2,1,0:T(8,128)(2,1)S(1)}, bf16[2,192,384]{2,1,0:T(8,128)(2,1)S(1)}, u32[]{:S(2)}, u32[]{:S(2)}) %collective-permute-start.6) | collective-permute-done | bytes 294944 | tf_op jit(solution)/shard_map/ppermute | solution.py:360
  41.4 2.3 %conv_2.2 = (bf16[2,192,128]{2,1,0:T(8,128)(2,1)S(1)}, bf16[2,192,128]{2,1,0:T(8,128)(2,1)S(1)}) custom-call(bf16[2,3,192,384]{3,2,1,0:T(8,128)(2,1)S(1)} %get-tuple-element.63.shifted_ref.refs_0_, bf16[2,192,384]{2,1,0:T(8,128)(2,1)S(1)} %get-tuple-element.64.values_ref, bf16[576,1728]{1,0:T(8,128)(2,1)S(1)} %get-tuple-element.65.w_ref, ...), custom_call_target="tpu_custom_call" | custom-call | flops 1528823808 | bytes 1990656 | tf_op jit(solution)/shard_map/conv_2/pallas_call | solution.py:300
  43.7 0.1 collective-permute-start.7
  43.8 0.0 collective-permute-done.8.got_ref
  43.8 0.8 %join.2.refs_0_ = bf16[4,2,192,128]{3,2,1,0:T(8,128)(2,1)} custom-call(bf16[2,192,128]{2,1,0:T(8,128)(2,1)S(1)} %get-tuple-element.73.kept_ref, bf16[2,192,128]{2,1,0:T(8,128)(2,1)S(1)} %collective-permute-done.8.got_ref), custom_call_target="tpu_custom_call" | custom-call | tf_op jit(solution)/shard_map/join/pallas_call | solution.py:338
  44.6 0.5 collective-permute-done.7.got_ref
  45.1 0.8 %join.3 = bf16[4,2,192,128]{3,2,1,0:T(8,128)(2,1)} custom-call(bf16[2,192,128]{2,1,0:T(8,128)(2,1)S(1)} %get-tuple-element.69.kept_ref, bf16[2,192,128]{2,1,0:T(8,128)(2,1)S(1)} %collective-permute-done.7.got_ref, bf16[4,2,192,128]{3,2,1,0:T(8,128)(2,1)} %join.2.refs_0_), custom_call_target="tpu_custom_call", output_to_operand_aliasing={{}: (2, {})} | custom-call | tf_op jit(solution)/shard_map/join/pallas_call | solution.py:338
Async XLA Ops:
  0.0 3.7 %collective-permute-start.1 = (bf16[4,2,192,128]{3,2,1,0:T(8,128)(2,1)}, bf16[4,2,192,128]{3,2,1,0:T(8,128)(2,1)S(1)}, u32[]{:S(2)}, u32[]{:S(2)}) collective-permute-start(bf16[4,2,192,128]{3,2,1,0:T(8,128)(2,1)} %own_ref.1), channel_id=1, source_target_pairs={{0,1},{1,0},{2,3},{3,2},{4,5},{5,4},{6,7},{7,6},{8,9},{9,8},{10,11... | collective-permute-start | bytes 1179656 | tf_op jit(solution)/shard_map/ppermute | solution.py:357
  0.5 12.5 %collective-permute-start = (bf16[4,2,192,128]{3,2,1,0:T(8,128)(2,1)}, bf16[4,2,192,128]{3,2,1,0:T(8,128)(2,1)S(1)}, u32[]{:S(2)}, u32[]{:S(2)}) collective-permute-start(bf16[4,2,192,128]{3,2,1,0:T(8,128)(2,1)} %own_ref.1), channel_id=1, source_target_pairs={{0,2},{1,3},{2,0},{3,1},{4,6},{5,7},{6,4},{7,5},{8,10},{9,11},{10,... | collective-permute-start | bytes 1179656 | tf_op jit(solution)/shard_map/ppermute | solution.py:362
  3.7 1.0 %copy-start = (bf16[4,2,192,128]{3,2,1,0:T(8,128)(2,1)S(1)}, bf16[4,2,192,128]{3,2,1,0:T(8,128)(2,1)}, u32[]{:S(2)}) copy-start(bf16[4,2,192,128]{3,2,1,0:T(8,128)(2,1)} %own_ref.1) | copy-start | bytes 1179652
  5.3 8.0 %collective-permute-start.2 = (bf16[2,192,256]{2,1,0:T(8,128)(2,1)S(1)}, bf16[2,192,256]{2,1,0:T(8,128)(2,1)S(1)}, u32[]{:S(2)}, u32[]{:S(2)}) collective-permute-start(bf16[2,192,256]{2,1,0:T(8,128)(2,1)S(1)} %get-tuple-element.51.refs_1_), channel_id=1, source_target_pairs={{0,4},{4,8},{8,12},{1,5},{5,9},{9,13},{2,6},{6,10},{10,14},{3,7},{... | collective-permute-start | bytes 589832 | tf_op jit(solution)/shard_map/ppermute | solution.py:360
  13.3 1.7 %collective-permute-start.3 = (bf16[4,2,192,128]{3,2,1,0:T(8,128)(2,1)S(1)}, bf16[4,2,192,128]{3,2,1,0:T(8,128)(2,1)S(1)}, u32[]{:S(2)}, u32[]{:S(2)}) collective-permute-start(bf16[4,2,192,128]{3,2,1,0:T(8,128)(2,1)S(1)} %collective-permute-done.far_ref), channel_id=1, source_target_pairs={{0,1},{1,0},{2,3},{3,2},{4,5},{5,4},{6,7},{7,6},{8,9},{9,8},{10,11... | collective-permute-start | bytes 1179656 | tf_op jit(solution)/shard_map/ppermute | solution.py:357
  16.1 10.6 %collective-permute-start.4 = (bf16[2,192,256]{2,1,0:T(8,128)(2,1)S(1)}, bf16[2,192,256]{2,1,0:T(8,128)(2,1)S(1)}, u32[]{:S(2)}, u32[]{:S(2)}) collective-permute-start(bf16[2,192,256]{2,1,0:T(8,128)(2,1)S(1)} %get-tuple-element.56), channel_id=1, source_target_pairs={{0,4},{4,8},{8,12},{1,5},{5,9},{9,13},{2,6},{6,10},{10,14},{3,7},{... | collective-permute-start | bytes 589832 | tf_op jit(solution)/shard_map/ppermute | solution.py:360
  23.2 12.3 %collective-permute-start.5 = (bf16[2,192,512]{2,1,0:T(8,128)(2,1)S(1)}, bf16[2,192,512]{2,1,0:T(8,128)(2,1)S(1)}, u32[]{:S(2)}, u32[]{:S(2)}) collective-permute-start(bf16[2,192,512]{2,1,0:T(8,128)(2,1)S(1)} %get-tuple-element.62), channel_id=1, source_target_pairs={{0,4},{4,8},{8,12},{1,5},{5,9},{9,13},{2,6},{6,10},{10,14},{3,7},{... | collective-permute-start | bytes 1179656 | tf_op jit(solution)/shard_map/ppermute | solution.py:360
  31.8 9.5 %collective-permute-start.6 = (bf16[2,192,384]{2,1,0:T(8,128)(2,1)S(1)}, bf16[2,192,384]{2,1,0:T(8,128)(2,1)S(1)}, u32[]{:S(2)}, u32[]{:S(2)}) collective-permute-start(bf16[2,192,384]{2,1,0:T(8,128)(2,1)S(1)} %get-tuple-element.68), channel_id=1, source_target_pairs={{0,4},{4,8},{8,12},{1,5},{5,9},{9,13},{2,6},{6,10},{10,14},{3,7},{... | collective-permute-start | bytes 884744 | tf_op jit(solution)/shard_map/ppermute | solution.py:360
  40.1 3.7 %collective-permute-start.8 = (bf16[2,192,128]{2,1,0:T(8,128)(2,1)S(1)}, bf16[2,192,128]{2,1,0:T(8,128)(2,1)S(1)}, u32[]{:S(2)}, u32[]{:S(2)}) collective-permute-start(bf16[2,192,128]{2,1,0:T(8,128)(2,1)S(1)} %get-tuple-element.74), channel_id=1, source_target_pairs={{0,1},{1,0},{2,3},{3,2},{4,5},{5,4},{6,7},{7,6},{8,9},{9,8},{10,11... | collective-permute-start | bytes 294920 | tf_op jit(solution)/shard_map/ppermute | solution.py:357
  43.7 1.4 %collective-permute-start.7 = (bf16[2,192,128]{2,1,0:T(8,128)(2,1)S(1)}, bf16[2,192,128]{2,1,0:T(8,128)(2,1)S(1)}, u32[]{:S(2)}, u32[]{:S(2)}) collective-permute-start(bf16[2,192,128]{2,1,0:T(8,128)(2,1)S(1)} %get-tuple-element.70), channel_id=1, source_target_pairs={{0,1},{1,0},{2,3},{3,2},{4,5},{5,4},{6,7},{7,6},{8,9},{9,8},{10,11... | collective-permute-start | bytes 294920 | tf_op jit(solution)/shard_map/ppermute | solution.py:357

commit v4 on v3

--- a/solution.py
+++ b/solution.py
@@ -11,6 +11,7 @@
 PAIR = 2
 LANES = 128
 TILE = 256
+IN_FLIGHT = 3
 VMEM = pl.BlockSpec(memory_space=pltpu.VMEM)
 ANY = pl.BlockSpec(memory_space=pl.ANY)
 LIMIT = 24 * 1024 * 1024
@@ -49,53 +50,53 @@
     return (halved + halved * jnp.tanh(halved)).astype(jnp.bfloat16)
 
 
-def fetched(pairs, sems):
-    copies = [pltpu.make_async_copy(source, to, sems.at[i]) for i, (source, to) in enumerate(pairs)]
-    for copy in copies:
+def weights_kernel(w_ref, rows_ref, *refs):
+    outs, columns_ref, held_ref, sems = refs[:-3], refs[-3], refs[-2], refs[-1]
+    layers, taps, channels_out, ins = w_ref.shape
+    step = taps // 3
+    places = [(layer, time_tap) for layer in range(layers) for time_tap in range(3)]
+    copies = []
+    for n, (layer, time_tap) in enumerate(places):
+        part = pl.ds(step * time_tap, step)
+        copies.append(pltpu.make_async_copy(w_ref.at[layer, part], held_ref.at[n], sems.at[n]))
+    for copy in copies[:IN_FLIGHT]:
         copy.start()
-    return copies
-
-
-def weights_kernel(first, columns, w_ref, *refs):
-    outs, held_ref, sems = refs[columns:-2], refs[-2], refs[-1]
-    count, _, channels_out, ins = held_ref.shape
-    copies = fetched([(w_ref.at[first + i], held_ref.at[i]) for i in range(count)], sems)
     _, flipped, _ = place()
-    if columns:
-        rows_ref = refs[0]
-        layers = rows_ref.shape[0] // 2
-        for layer in range(layers):
-            outs[-1][layer, 0] = column(rows_ref[layer : layer + 1, :])
-            outs[-1][layer, 1] = column(rows_ref[layers + layer : layers + layer + 1, :])
-    for i in range(count):
-        copies[i].wait()
-        for time_tap in range(3):
-            for row_tap in range(3):
-                source = 9 * time_tap + 3 * (row_tap + flipped * (2 - 2 * row_tap))
-                at = (3 * time_tap + row_tap) * ins
-                outs[i][:, at : at + ins] = held_ref[i, pl.ds(source, 3)].reshape(3 * channels_out, ins)
-
-
-def weights(first, count, conv_weight, *rows):
+    for layer in range(layers):
+        columns_ref[layer, 0] = column(rows_ref[layer : layer + 1, :])
+        columns_ref[layer, 1] = column(rows_ref[layers + layer : layers + layer + 1, :])
+    for n, (layer, time_tap) in enumerate(places):
+        copies[n].wait()
+        if n + IN_FLIGHT < len(copies):
+            copies[n + IN_FLIGHT].start()
+        for row_tap in range(3):
+            source = 3 * (row_tap + flipped * (2 - 2 * row_tap))
+            at = (3 * time_tap + row_tap) * ins
+            outs[layer][:, at : at + ins] = held_ref[n, pl.ds(source, 3)].reshape(3 * channels_out, ins)
+
+
+def weights(conv_weight, rows):
     layers, taps, outs, ins = conv_weight.shape
     one = jax.ShapeDtypeStruct((3 * outs, 9 * ins), conv_weight.dtype)
-    columns = len(rows)
     results = pl.pallas_call(
-        functools.partial(weights_kernel, first, columns),
-        out_shape=(one,) * count + (jax.ShapeDtypeStruct((layers, 2, outs, LANES), jnp.float32),) * columns,
-        in_specs=[ANY] + [VMEM] * columns,
-        out_specs=(VMEM,) * (count + columns),
+        weights_kernel,
+        out_shape=(one,) * layers + (jax.ShapeDtypeStruct((layers, 2, outs, LANES), jnp.float32),),
+        in_specs=[ANY, VMEM],
+        out_specs=(VMEM,) * (layers + 1),
         scratch_shapes=[
-            pltpu.VMEM((count, taps, outs, ins), conv_weight.dtype),
-            pltpu.SemaphoreType.DMA((count,)),
+            pltpu.VMEM((3 * layers, taps // 3, outs, ins), conv_weight.dtype),
+            pltpu.SemaphoreType.DMA((3 * layers,)),
         ],
         compiler_params=pltpu.CompilerParams(vmem_limit_bytes=LARGE),
-        cost_estimate=pl.CostEstimate(
-            flops=0, bytes_accessed=4 * conv_weight.size * count // layers, transcendentals=0
-        ),
+        cost_estimate=pl.CostEstimate(flops=0, bytes_accessed=4 * conv_weight.size, transcendentals=0),
         name="weights",
-    )(conv_weight, *rows)
-    return list(results[:count]), results[count:]
+    )(conv_weight, rows)
+    return results[:-1], results[-1]
+
+
+def joined(valid):
+    rest = valid % LANES
+    return rest if 0 < PAIR * rest <= LANES else 0
 
 
 def spread(out_ref, index, act, pitch):
@@ -209,15 +210,22 @@
 
 
 def conv_kernel(
-    layer, last, sends, received, pitch, half, shifted_ref, values_ref, w_ref, columns_ref, *refs
+    layer, last, sends, rest_sent, received, rest, pitch, half, shifted_ref, values_ref, w_ref, columns_ref, *refs
 ):
     scratch = refs[-1:] if received else ()
     outs = refs[received or 1 : len(refs) - len(scratch)]
     if received:
         earlier_ref = scratch[0]
         for t in range(PAIR):
-            parts = [ref[t] for ref in refs[:received]]
-            spread(earlier_ref, t, parts[0] if received == 1 else jnp.concatenate(parts, axis=1), pitch)
+            if rest:
+                whole = (refs[0].shape[1] - LANES) // PAIR
+                tail = refs[0][:, PAIR * whole :].astype(jnp.float32)
+                tail = tail if t == 0 else pltpu.roll(tail, LANES - t * (LANES // PAIR), 1)
+                tail = jnp.where(lane_of(LANES) < rest, tail, 0.0).astype(jnp.bfloat16)
+                parts = [refs[0][:, t * whole : (t + 1) * whole], tail]
+            else:
+                parts = [ref[t] for ref in refs[:received]]
+            spread(earlier_ref, t, parts[0] if len(parts) == 1 else jnp.concatenate(parts, axis=1), pitch)
     else:
         earlier_ref = refs[0]
     _, _, channels, lanes = shifted_ref.shape
@@ -239,7 +247,9 @@
 
     def sums(t, tap, b):
         tile, at = divmod((t * chunks + b) * LANES, TILE)
-        return tiles[tile][tap * channels : (tap + 1) * channels, at : at + LANES]
+        return tiles[tile][tap][:, at : at + LANES]
+
+    tails = []
 
     def finish(t):
         totals, acts = [], []
@@ -258,8 +268,15 @@
             if not last:
                 outs[0][t, :, at] = total
                 acts.append(activated(totals[-1], gain, mask[:, at]))
-                if sends:
+                if not sends:
+                    continue
+                if not rest_sent:
                     outs[2][t, :, at] = acts[-1]
+                elif b < chunks - 1:
+                    outs[2][:, (t * (chunks - 1) + b) * LANES : (t * (chunks - 1) + b + 1) * LANES] = acts[-1]
+                else:
+                    tail = jnp.where(lane < rest_sent, acts[-1].astype(jnp.float32), 0.0)
+                    tails.append(tail if t == 0 else pltpu.roll(tail, t * (LANES // PAIR), 1))
         if not last:
             spread(outs[1], t, jnp.concatenate(acts, axis=1), pitch)
             return
@@ -281,14 +298,22 @@
     finished = 0
     for n in range(0, len(places), side):
         rhs = jnp.concatenate([window(t, b) for t, b in places[n : n + side]], axis=1)
-        tiles.append(jnp.dot(w_ref[...], rhs, preferred_element_type=jnp.float32))
+        tiles.append(
+            [
+                jnp.dot(w_ref[tap * channels : (tap + 1) * channels], rhs, preferred_element_type=jnp.float32)
+                for tap in range(3)
+            ]
+        )
         while finished < PAIR and (finished + 1) * chunks <= n + side:
             finish(finished)
             finished += 1
-
-
-def conv(layer, last, sends, received, pitch, rows_left, half, earlier, shifted, values, weight, columns):
+    if sends and rest_sent:
+        outs[2][:, PAIR * (chunks - 1) * LANES :] = sum(tails).astype(jnp.bfloat16)
+
+
+def conv(layer, last, sends, received, rest, pitch, rows_left, half, earlier, shifted, values, weight, columns):
     _, _, channels, lanes = shifted.shape
+    rest_sent = joined(rows_left * pitch)
     if last:
         out_shape = (jax.ShapeDtypeStruct((PAIR, channels, LANES), jnp.bfloat16),) * 2
     else:
@@ -296,9 +321,13 @@
             jax.ShapeDtypeStruct((PAIR, channels, lanes), jnp.bfloat16),
             jax.ShapeDtypeStruct((PAIR, 3, channels, rounded((rows_left - 1) * pitch)), jnp.bfloat16),
         )
-        out_shape += out_shape[:1] * sends
+        if sends and rest_sent:
+            sent = PAIR * (lanes - LANES) + LANES
+            out_shape += (jax.ShapeDtypeStruct((channels, sent), jnp.bfloat16),)
+        elif sends:
+            out_shape += out_shape[:1]
     return pl.pallas_call(
-        functools.partial(conv_kernel, layer, last, sends, received, pitch, half),
+        functools.partial(conv_kernel, layer, last, sends and not last, rest_sent, received, rest, pitch, half),
         out_shape=out_shape,
         in_specs=[VMEM] * (4 + len(earlier)),
         out_specs=(VMEM,) * len(out_shape),
@@ -362,14 +391,14 @@
     far = lax.ppermute(latents, "rows", [(i, i ^ 2) for i in range(strips)])
     mate = mate_of(latents)
     row_values = jnp.concatenate([norm_gains, biases], axis=0)
-    weight, (columns,) = weights(0, layers, conv_weight, row_values)
+    weight, columns = weights(conv_weight, row_values)
     near_values, near_act = near(layers, latents, mate, row_values)
     halo_near = earlier_of(near_act[-1])
     far, weight, columns, near_values, near_act, halo_near = lax.optimization_barrier(
         (far, weight, columns, near_values, near_act, halo_near)
     )
     values, shifted, send = beyond(layers, far, mate_of(far), near_values, near_act, columns)
-    halo = (halo_near, earlier_of(send))
+    halo, rest = (halo_near, earlier_of(send)), 0
     pitch = width // 2 + layers + 1
     pairs = frames // PAIR
     for layer in range(layers):
@@ -383,6 +412,7 @@
                 last,
                 p == pairs - 1,
                 received,
+                rest if received else 0,
                 pitch,
                 rows_left,
                 width // 2,
@@ -394,7 +424,7 @@
             )
         values, shifted = [r[0] for r in results], [r[1] for r in results]
         if not last:
-            halo = (earlier_of(results[-1][2]),)
+            halo, rest = (earlier_of(results[-1][2]),), joined(rows_left * pitch)
     result = ()
     for p in reversed(range(pairs)):
         result = (join(p, values[p], mate_of(shifted[p]), latents.shape, *result),)

time: 46.3 us -> 46.2 us (level)
  waiting for transfers between devices: 4.15 us -> 3.35 us
  Pallas kernels: 21.7 us -> 22.3 us
    pallas_call x7, Pallas kernels: 18.5 us -> 19.1 us  [the longest x6 14.6 us: conv(): pl.pallas_call(functools.partial(conv_kernel, layer, last, sends and (not...]
  transfers between devices with their start and end apart: 9 -> 9, of which waited for: 5 -> 3; matrix products, arithmetic and copies ran while one was open for 2% -> 2% of each run, Pallas kernels for 43% -> 45%
where the time goes in v4:
time: 46.2 us; the launch traced here: 45.9 us
  Pallas kernels  22.3 us (48%)
  starting transfers between devices  18.1 us (39%)
  waiting for transfers between devices  3.35 us (7%)
  local copies, waits for them, and re-layouts  0.99 us (2%)
  other arithmetic  0.71 us (2%)
    ppermute x4, starting transfers between devices, earlier_of(): return lax.ppermute(block, 'tm', [(i, i + 1) for i in range(blocks - 1)])  15 us
    pallas_call x6, Pallas kernels, conv(): pl.pallas_call(functools.partial(conv_kernel, layer, last, sends and (not...  14.6 us
    pallas_call x1, Pallas kernels, weights(): pl.pallas_call(weights_kernel, out_shape=(one,) * layers + (jax.ShapeDtyp...  4.51 us
    ppermute x1, starting transfers between devices, on_device(): far = lax.ppermute(latents, 'rows', [(i, i ^ 2) for i in range(strips)])  2.49 us
    ppermute x4, waiting for transfers between devices, mate_of(): return lax.ppermute(block, 'rows', [(i, i ^ 1) for i in range(strips)])  2.17 us
    pallas_call x2, Pallas kernels, join(): pl.pallas_call(functools.partial(join_kernel, pair), out_shape=jax.ShapeD...  1.63 us
    ppermute x4, waiting for transfers between devices, earlier_of(): return lax.ppermute(block, 'tm', [(i, i + 1) for i in range(blocks - 1)])  1.18 us
    pallas_call x1, Pallas kernels, beyond(): pl.pallas_call(functools.partial(far_kernel, halo, pairs), out_shape=(out...  1 us
  transfers between devices with their start and end apart: 9, of which 3 were waited for; matrix products, arithmetic and copies ran while one was open for 2% of the time, Pallas kernels for 45%

profile of v4, /device:TPU:0, one launch (start us, length us, event | category | flops | bytes accessed | tf_op | source)
XLA Modules:
  0.0 45.9 jit_solution(4528934099713185958)
XLA Ops:
  0.0 0.5 collective-permute-start.1
  0.5 2.5 %collective-permute-start = (bf16[4,2,192,128]{3,2,1,0:T(8,128)(2,1)}, bf16[4,2,192,128]{3,2,1,0:T(8,128)(2,1)S(1)}, u32[]{:S(2)}, u32[]{:S(2)}) collective-permute-start(bf16[4,2,192,128]{3,2,1,0:T(8,128)(2,1)} %own_ref.1), channel_id=1, source_target_pairs={{0,2},{1,3},{2,0},{3,1},{4,6},{5,7},{6,4},{7,5},{8,10},{9,11},{10,... | collective-permute-start | bytes 1179656 | tf_op jit(solution)/shard_map/ppermute | solution.py:391
  2.9 0.7 %pad_maximum_fusion.rows_ref.gains_ref = f32[6,192]{1,0:T(8,128)S(1)} fusion(f32[3,192]{1,0:T(4,128)} %param.7, f32[3,192]{1,0:T(4,128)} %param.6), kind=kLoop, calls=%fused_computation | loop fusion | flops 1152 | bytes 9216 | tf_op jit(solution)/shard_map/concatenate | solution.py:393
  3.7 0.0 collective-permute-done.1.mate_ref
  3.7 0.0 copy-start
  3.7 1.0 %copy-done = bf16[4,2,192,128]{3,2,1,0:T(8,128)(2,1)S(1)} copy-done((bf16[4,2,192,128]{3,2,1,0:T(8,128)(2,1)S(1)}, bf16[4,2,192,128]{3,2,1,0:T(8,128)(2,1)}, u32[]{:S(2)}) %copy-start) | copy-done | bytes 393240
  4.7 0.6 %near.1 = (bf16[4,192,384]{2,1,0:T(8,128)(2,1)S(1)}, bf16[2,192,256]{2,1,0:T(8,128)(2,1)S(1)}, bf16[2,192,256]{2,1,0:T(8,128)(2,1)S(1)}) custom-call(bf16[4,2,192,128]{3,2,1,0:T(8,128)(2,1)S(1)} %copy-done, bf16[4,2,192,128]{3,2,1,0:T(8,128)(2,1)S(1)} %collective-permute-done.1.mate_ref, f32[6,192]{1,0:T(8,128)S(1)} %pad_maximum_fusion.rows_ref.gains_ref), custom_call_target="tpu_custom_call" | custom-call | flops 7864320 | bytes 1572864 | tf_op jit(solution)/shard_map/near/pallas_call | solution.py:151
  5.3 3.5 %collective-permute-start.2 = (bf16[2,192,256]{2,1,0:T(8,128)(2,1)S(1)}, bf16[2,192,256]{2,1,0:T(8,128)(2,1)S(1)}, u32[]{:S(2)}, u32[]{:S(2)}) collective-permute-start(bf16[2,192,256]{2,1,0:T(8,128)(2,1)S(1)} %get-tuple-element.51.refs_1_), channel_id=1, source_target_pairs={{0,4},{4,8},{8,12},{1,5},{5,9},{9,13},{2,6},{6,10},{10,14},{3,7},{... | collective-permute-start | bytes 589832 | tf_op jit(solution)/shard_map/ppermute | solution.py:389
  8.8 4.5 %weights.1 = (bf16[576,1728]{1,0:T(8,128)(2,1)S(1)}, bf16[576,1728]{1,0:T(8,128)(2,1)S(1)}, bf16[576,1728]{1,0:T(8,128)(2,1)S(1)}, f32[3,2,192,128]{3,2,1,0:T(8,128)S(1)}) custom-call(bf16[3,27,192,192]{3,2,1,0:T(8,128)(2,1)} %w_ref.1, f32[6,192]{1,0:T(8,128)S(1)} %pad_maximum_fusion.rows_ref.gains_ref), custom_call_target="tpu_custom_call" | custom-call | bytes 11943936 | tf_op jit(solution)/shard_map/weights/pallas_call | solution.py:81
  13.3 0.0 collective-permute-done.far_ref
  13.3 0.0 collective-permute-done.2.refs_0_
  13.3 0.1 collective-permute-start.3
  13.4 1.7 %collective-permute-done.3.mate_ref = bf16[4,2,192,128]{3,2,1,0:T(8,128)(2,1)S(1)} collective-permute-done((bf16[4,2,192,128]{3,2,1,0:T(8,128)(2,1)S(1)}, bf16[4,2,192,128]{3,2,1,0:T(8,128)(2,1)S(1)}, u32[]{:S(2)}, u32[]{:S(2)}) %collective-permute-start.3) | collective-permute-done | bytes 393248 | tf_op jit(solution)/shard_map/ppermute | solution.py:386
  15.1 1.0 %beyond.1 = (bf16[2,192,512]{2,1,0:T(8,128)(2,1)S(1)}, bf16[2,192,512]{2,1,0:T(8,128)(2,1)S(1)}, bf16[2,3,192,512]{3,2,1,0:T(8,128)(2,1)S(1)}, bf16[2,3,192,512]...) custom-call(bf16[4,2,192,128]{3,2,1,0:T(8,128)(2,1)S(1)} %collective-permute-done.far_ref, ...), custom_call_target="tpu_custom_call" | custom-call | flops 7864320 | bytes 1572864 | tf_op jit(solution)/shard_map/beyond/pallas_call | solution.py:200
  16.1 4.3 %collective-permute-start.4 = (bf16[2,192,256]{2,1,0:T(8,128)(2,1)S(1)}, bf16[2,192,256]{2,1,0:T(8,128)(2,1)S(1)}, u32[]{:S(2)}, u32[]{:S(2)}) collective-permute-start(bf16[2,192,256]{2,1,0:T(8,128)(2,1)S(1)} %get-tuple-element.56), channel_id=1, source_target_pairs={{0,4},{4,8},{8,12},{1,5},{5,9},{9,13},{2,6},{6,10},{10,14},{3,7},{... | collective-permute-start | bytes 589832 | tf_op jit(solution)/shard_map/ppermute | solution.py:389
  20.5 2.7 %conv_0.3 = (bf16[2,192,512]{2,1,0:T(8,128)(2,1)S(1)}, bf16[2,3,192,384]{3,2,1,0:T(8,128)(2,1)S(1)}, bf16[192,896]{1,0:T(8,128)(2,1)S(1)}) custom-call(bf16[2,3,192,512]{3,2,1,0:T(8,128)(2,1)S(1)} %get-tuple-element.60.shifted_ref, bf16[2,192,512]{2,1,0:T(8,128)(2,1)S(1)} %get-tuple-element.61.values_ref, bf16[576,1728]{1,0:T(8,128)(2,1)S(1)} %get-tuple-element.54.w_ref, ...), custom_call_target="tpu_custom_call" | custom-call | flops 2038431744 | bytes 1990656 | tf_op jit(solution)/shard_map/conv_0/pallas_call | solution.py:329
  23.2 3.5 %collective-permute-start.5 = (bf16[192,896]{1,0:T(8,128)(2,1)S(1)}, bf16[192,896]{1,0:T(8,128)(2,1)S(1)}, u32[]{:S(2)}, u32[]{:S(2)}) collective-permute-start(bf16[192,896]{1,0:T(8,128)(2,1)S(1)} %get-tuple-element.62), channel_id=1, source_target_pairs={{0,4},{4,8},{8,12},{1,5},{5,9},{9,13},{2,6},{6,10},{10,14},{3,7},{... | collective-permute-start | bytes 1032200 | tf_op jit(solution)/shard_map/ppermute | solution.py:389
  26.7 0.0 collective-permute-done.4.refs_1_
  26.7 2.8 %conv_0.2 = (bf16[2,192,512]{2,1,0:T(8,128)(2,1)S(1)}, bf16[2,3,192,384]{3,2,1,0:T(8,128)(2,1)S(1)}) custom-call(bf16[2,3,192,512]{3,2,1,0:T(8,128)(2,1)S(1)} %get-tuple-element.52.shifted_ref.refs_0_, bf16[2,192,512]{2,1,0:T(8,128)(2,1)S(1)} %get-tuple-element.53.values_ref, bf16[576,1728]{1,0:T(8,128)(2,1)S(1)} %get-tuple-element.54.w_ref, ...), custom_call_target="tpu_custom_call" | custom-call | flops 2038431744 | bytes 1990656 | tf_op jit(solution)/shard_map/conv_0/pallas_call | solution.py:329
  29.5 2.2 %conv_1.3 = (bf16[2,192,384]{2,1,0:T(8,128)(2,1)S(1)}, bf16[2,3,192,384]{3,2,1,0:T(8,128)(2,1)S(1)}, bf16[2,192,384]{2,1,0:T(8,128)(2,1)S(1)}) custom-call(bf16[2,3,192,384]{3,2,1,0:T(8,128)(2,1)S(1)} %get-tuple-element.66.shifted_ref, bf16[2,192,512]{2,1,0:T(8,128)(2,1)S(1)} %get-tuple-element.67.values_ref, bf16[576,1728]{1,0:T(8,128)(2,1)S(1)} %get-tuple-element.59.w_ref, ...), custom_call_target="tpu_custom_call" | custom-call | flops 1528823808 | bytes 1990656 | tf_op jit(solution)/shard_map/conv_1/pallas_call | solution.py:329
  31.7 3.7 %collective-permute-start.6 = (bf16[2,192,384]{2,1,0:T(8,128)(2,1)S(1)}, bf16[2,192,384]{2,1,0:T(8,128)(2,1)S(1)}, u32[]{:S(2)}, u32[]{:S(2)}) collective-permute-start(bf16[2,192,384]{2,1,0:T(8,128)(2,1)S(1)} %get-tuple-element.68), channel_id=1, source_target_pairs={{0,4},{4,8},{8,12},{1,5},{5,9},{9,13},{2,6},{6,10},{10,14},{3,7},{... | collective-permute-start | bytes 884744 | tf_op jit(solution)/shard_map/ppermute | solution.py:389
  35.4 0.0 collective-permute-done.5.refs_0_
  35.4 2.4 %conv_1.2 = (bf16[2,192,384]{2,1,0:T(8,128)(2,1)S(1)}, bf16[2,3,192,384]{3,2,1,0:T(8,128)(2,1)S(1)}) custom-call(bf16[2,3,192,384]{3,2,1,0:T(8,128)(2,1)S(1)} %get-tuple-element.57.shifted_ref.refs_0_, bf16[2,192,512]{2,1,0:T(8,128)(2,1)S(1)} %get-tuple-element.58.values_ref, bf16[576,1728]{1,0:T(8,128)(2,1)S(1)} %get-tuple-element.59.w_ref, ...), custom_call_target="tpu_custom_call" | custom-call | flops 1528823808 | bytes 1990656 | tf_op jit(solution)/shard_map/conv_1/pallas_call | solution.py:329
  37.8 2.2 %conv_2.3 = (bf16[2,192,128]{2,1,0:T(8,128)(2,1)S(1)}, bf16[2,192,128]{2,1,0:T(8,128)(2,1)S(1)}) custom-call(bf16[2,3,192,384]{3,2,1,0:T(8,128)(2,1)S(1)} %get-tuple-element.71.shifted_ref, bf16[2,192,384]{2,1,0:T(8,128)(2,1)S(1)} %get-tuple-element.72.values_ref, bf16[576,1728]{1,0:T(8,128)(2,1)S(1)} %get-tuple-element.65.w_ref, ...), custom_call_target="tpu_custom_call" | custom-call | flops 1528823808 | bytes 1990656 | tf_op jit(solution)/shard_map/conv_2/pallas_call | solution.py:329
  39.9 0.1 collective-permute-start.8
  40.0 1.2 %collective-permute-done.6.refs_0_ = bf16[2,192,384]{2,1,0:T(8,128)(2,1)S(1)} collective-permute-done((bf16[2,192,384]{2,1,0:T(8,128)(2,1)S(1)}, bf16[2,192,384]{2,1,0:T(8,128)(2,1)S(1)}, u32[]{:S(2)}, u32[]{:S(2)}) %collective-permute-start.6) | collective-permute-done | bytes 294944 | tf_op jit(solution)/shard_map/ppermute | solution.py:389
  41.2 2.3 %conv_2.2 = (bf16[2,192,128]{2,1,0:T(8,128)(2,1)S(1)}, bf16[2,192,128]{2,1,0:T(8,128)(2,1)S(1)}) custom-call(bf16[2,3,192,384]{3,2,1,0:T(8,128)(2,1)S(1)} %get-tuple-element.63.shifted_ref.refs_0_, bf16[2,192,384]{2,1,0:T(8,128)(2,1)S(1)} %get-tuple-element.64.values_ref, bf16[576,1728]{1,0:T(8,128)(2,1)S(1)} %get-tuple-element.65.w_ref, ...), custom_call_target="tpu_custom_call" | custom-call | flops 1528823808 | bytes 1990656 | tf_op jit(solution)/shard_map/conv_2/pallas_call | solution.py:329
  43.5 0.1 collective-permute-start.7
  43.6 0.0 collective-permute-done.8.got_ref
  43.6 0.8 %join.2.refs_0_ = bf16[4,2,192,128]{3,2,1,0:T(8,128)(2,1)} custom-call(bf16[2,192,128]{2,1,0:T(8,128)(2,1)S(1)} %get-tuple-element.73.kept_ref, bf16[2,192,128]{2,1,0:T(8,128)(2,1)S(1)} %collective-permute-done.8.got_ref), custom_call_target="tpu_custom_call" | custom-call | tf_op jit(solution)/shard_map/join/pallas_call | solution.py:367
  44.4 0.5 collective-permute-done.7.got_ref
  44.9 0.8 %join.3 = bf16[4,2,192,128]{3,2,1,0:T(8,128)(2,1)} custom-call(bf16[2,192,128]{2,1,0:T(8,128)(2,1)S(1)} %get-tuple-element.69.kept_ref, bf16[2,192,128]{2,1,0:T(8,128)(2,1)S(1)} %collective-permute-done.7.got_ref, bf16[4,2,192,128]{3,2,1,0:T(8,128)(2,1)} %join.2.refs_0_), custom_call_target="tpu_custom_call", output_to_operand_aliasing={{}: (2, {})} | custom-call | tf_op jit(solution)/shard_map/join/pallas_call | solution.py:367
Async XLA Ops:
  0.0 3.7 %collective-permute-start.1 = (bf16[4,2,192,128]{3,2,1,0:T(8,128)(2,1)}, bf16[4,2,192,128]{3,2,1,0:T(8,128)(2,1)S(1)}, u32[]{:S(2)}, u32[]{:S(2)}) collective-permute-start(bf16[4,2,192,128]{3,2,1,0:T(8,128)(2,1)} %own_ref.1), channel_id=1, source_target_pairs={{0,1},{1,0},{2,3},{3,2},{4,5},{5,4},{6,7},{7,6},{8,9},{9,8},{10,11... | collective-permute-start | bytes 1179656 | tf_op jit(solution)/shard_map/ppermute | solution.py:386
  0.5 12.9 %collective-permute-start = (bf16[4,2,192,128]{3,2,1,0:T(8,128)(2,1)}, bf16[4,2,192,128]{3,2,1,0:T(8,128)(2,1)S(1)}, u32[]{:S(2)}, u32[]{:S(2)}) collective-permute-start(bf16[4,2,192,128]{3,2,1,0:T(8,128)(2,1)} %own_ref.1), channel_id=1, source_target_pairs={{0,2},{1,3},{2,0},{3,1},{4,6},{5,7},{6,4},{7,5},{8,10},{9,11},{10,... | collective-permute-start | bytes 1179656 | tf_op jit(solution)/shard_map/ppermute | solution.py:391
  3.7 1.0 %copy-start = (bf16[4,2,192,128]{3,2,1,0:T(8,128)(2,1)S(1)}, bf16[4,2,192,128]{3,2,1,0:T(8,128)(2,1)}, u32[]{:S(2)}) copy-start(bf16[4,2,192,128]{3,2,1,0:T(8,128)(2,1)} %own_ref.1) | copy-start | bytes 1179652
  5.3 8.0 %collective-permute-start.2 = (bf16[2,192,256]{2,1,0:T(8,128)(2,1)S(1)}, bf16[2,192,256]{2,1,0:T(8,128)(2,1)S(1)}, u32[]{:S(2)}, u32[]{:S(2)}) collective-permute-start(bf16[2,192,256]{2,1,0:T(8,128)(2,1)S(1)} %get-tuple-element.51.refs_1_), channel_id=1, source_target_pairs={{0,4},{4,8},{8,12},{1,5},{5,9},{9,13},{2,6},{6,10},{10,14},{3,7},{... | collective-permute-start | bytes 589832 | tf_op jit(solution)/shard_map/ppermute | solution.py:389
  13.3 1.8 %collective-permute-start.3 = (bf16[4,2,192,128]{3,2,1,0:T(8,128)(2,1)S(1)}, bf16[4,2,192,128]{3,2,1,0:T(8,128)(2,1)S(1)}, u32[]{:S(2)}, u32[]{:S(2)}) collective-permute-start(bf16[4,2,192,128]{3,2,1,0:T(8,128)(2,1)S(1)} %collective-permute-done.far_ref), channel_id=1, source_target_pairs={{0,1},{1,0},{2,3},{3,2},{4,5},{5,4},{6,7},{7,6},{8,9},{9,8},{10,11... | collective-permute-start | bytes 1179656 | tf_op jit(solution)/shard_map/ppermute | solution.py:386
  16.1 10.5 %collective-permute-start.4 = (bf16[2,192,256]{2,1,0:T(8,128)(2,1)S(1)}, bf16[2,192,256]{2,1,0:T(8,128)(2,1)S(1)}, u32[]{:S(2)}, u32[]{:S(2)}) collective-permute-start(bf16[2,192,256]{2,1,0:T(8,128)(2,1)S(1)} %get-tuple-element.56), channel_id=1, source_target_pairs={{0,4},{4,8},{8,12},{1,5},{5,9},{9,13},{2,6},{6,10},{10,14},{3,7},{... | collective-permute-start | bytes 589832 | tf_op jit(solution)/shard_map/ppermute | solution.py:389
  23.2 12.2 %collective-permute-start.5 = (bf16[192,896]{1,0:T(8,128)(2,1)S(1)}, bf16[192,896]{1,0:T(8,128)(2,1)S(1)}, u32[]{:S(2)}, u32[]{:S(2)}) collective-permute-start(bf16[192,896]{1,0:T(8,128)(2,1)S(1)} %get-tuple-element.62), channel_id=1, source_target_pairs={{0,4},{4,8},{8,12},{1,5},{5,9},{9,13},{2,6},{6,10},{10,14},{3,7},{... | collective-permute-start | bytes 1032200 | tf_op jit(solution)/shard_map/ppermute | solution.py:389
  31.7 9.5 %collective-permute-start.6 = (bf16[2,192,384]{2,1,0:T(8,128)(2,1)S(1)}, bf16[2,192,384]{2,1,0:T(8,128)(2,1)S(1)}, u32[]{:S(2)}, u32[]{:S(2)}) collective-permute-start(bf16[2,192,384]{2,1,0:T(8,128)(2,1)S(1)} %get-tuple-element.68), channel_id=1, source_target_pairs={{0,4},{4,8},{8,12},{1,5},{5,9},{9,13},{2,6},{6,10},{10,14},{3,7},{... | collective-permute-start | bytes 884744 | tf_op jit(solution)/shard_map/ppermute | solution.py:389
  39.9 3.7 %collective-permute-start.8 = (bf16[2,192,128]{2,1,0:T(8,128)(2,1)S(1)}, bf16[2,192,128]{2,1,0:T(8,128)(2,1)S(1)}, u32[]{:S(2)}, u32[]{:S(2)}) collective-permute-start(bf16[2,192,128]{2,1,0:T(8,128)(2,1)S(1)} %get-tuple-element.74), channel_id=1, source_target_pairs={{0,1},{1,0},{2,3},{3,2},{4,5},{5,4},{6,7},{7,6},{8,9},{9,8},{10,11... | collective-permute-start | bytes 294920 | tf_op jit(solution)/shard_map/ppermute | solution.py:386
  43.5 1.4 %collective-permute-start.7 = (bf16[2,192,128]{2,1,0:T(8,128)(2,1)S(1)}, bf16[2,192,128]{2,1,0:T(8,128)(2,1)S(1)}, u32[]{:S(2)}, u32[]{:S(2)}) collective-permute-start(bf16[2,192,128]{2,1,0:T(8,128)(2,1)S(1)} %get-tuple-element.70), channel_id=1, source_target_pairs={{0,1},{1,0},{2,3},{3,2},{4,5},{5,4},{6,7},{7,6},{8,9},{9,8},{10,11... | collective-permute-start | bytes 294920 | tf_op jit(solution)/shard_map/ppermute | solution.py:386

commit v5 on v4

v5 whole, which is shorter than its diff:
```python
import functools

import jax
import jax.numpy as jnp
from jax import lax
from jax.experimental import pallas as pl
from jax.experimental.pallas import tpu as pltpu
from jax.sharding import PartitionSpec as P

EPSILON = 1e-06
PAIR = 2
LANES = 128
TILE = 256
VMEM = pl.BlockSpec(memory_space=pltpu.VMEM)
ANY = pl.BlockSpec(memory_space=pl.ANY)
LIMIT = 44 * 1024 * 1024


def place():
    strip = lax.axis_index("rows").astype(jnp.int32)
    core, group = strip & 1, strip >> 1
    return core, group, core == group


def rounded(lanes):
    return -(-lanes // LANES) * LANES


def column(row):
    return jnp.transpose(jnp.broadcast_to(row, (LANES, row.shape[1])))


def lane_of(lanes):
    return lax.broadcasted_iota(jnp.int32, (1, lanes), 1)


def filled(lanes, pitch):
    lane = lane_of(lanes)
    gaps = lane < 0
    for end in range(pitch - 1, lanes, pitch):
        gaps = gaps | (lane == end)
    return jnp.where(gaps, 0.0, 1.0)


def activated(values, gain, mask):
    squares = jnp.mean(values * values, axis=0, keepdims=True)
    halved = values * (lax.rsqrt(squares + EPSILON) * (0.5 * mask)) * gain
    return (halved + halved * jnp.tanh(halved)).astype(jnp.bfloat16)


def fetches(layer, w_ref, held_ref, sems):
    step = w_ref.shape[1] // 3
    return [
        pltpu.make_async_copy(w_ref.at[layer, pl.ds(step * tap, step)], held_ref.at[tap], sems.at[tap]) for tap in range(3)
    ]


def laid_out(copies, held_ref, out_ref):
    _, _, outs, ins = held_ref.shape
    _, flipped, _ = place()
    for time_tap in range(3):
        copies[time_tap].wait()
        for row_tap in range(3):
            source = 3 * (row_tap + flipped * (2 - 2 * row_tap))
            at = (3 * time_tap + row_tap) * ins
            out_ref[:, at : at + ins] = held_ref[time_tap, pl.ds(source, 3)].reshape(3 * outs, ins)


def held(conv_weight):
    _, taps, outs, ins = conv_weight.shape
    return [pltpu.VMEM((3, taps // 3, outs, ins), conv_weight.dtype), pltpu.SemaphoreType.DMA((3,))]


def laid_shape(conv_weight):
    _, _, outs, ins = conv_weight.shape
    return jax.ShapeDtypeStruct((3 * outs, 9 * ins), conv_weight.dtype)


def weights_kernel(w_ref, rows_ref, out_ref, columns_ref, held_ref, sems):
    copies = fetches(0, w_ref, held_ref, sems)
    for copy in copies:
        copy.start()
    layers = w_ref.shape[0]
    for layer in range(layers):
        columns_ref[layer, 0] = column(rows_ref[layer : layer + 1, :])
        columns_ref[layer, 1] = column(rows_ref[layers + layer : layers + layer + 1, :])
    laid_out(copies, held_ref, out_ref)


def weights(conv_weight, rows):
    layers, _, outs, _ = conv_weight.shape
    return pl.pallas_call(
        weights_kernel,
        out_shape=(laid_shape(conv_weight), jax.ShapeDtypeStruct((layers, 2, outs, LANES), jnp.float32)),
        in_specs=[ANY, VMEM],
        out_specs=(VMEM, VMEM),
        scratch_shapes=held(conv_weight),
        compiler_params=pltpu.CompilerParams(vmem_limit_bytes=LIMIT),
        cost_estimate=pl.CostEstimate(flops=0, bytes_accessed=4 * conv_weight.size // layers, transcendentals=0),
        name="weights",
    )(conv_weight, rows)


def split_kernel(in_ref, *out_refs):
    for p, out_ref in enumerate(out_refs):
        out_ref[...] = in_ref[PAIR * p : PAIR * (p + 1)]


def split(latents):
    pairs = latents.shape[0] // PAIR
    return pl.pallas_call(
        split_kernel,
        out_shape=(jax.ShapeDtypeStruct((PAIR,) + latents.shape[1:], latents.dtype),) * pairs,
        in_specs=[VMEM],
        out_specs=(VMEM,) * pairs,
        compiler_params=pltpu.CompilerParams(vmem_limit_bytes=LIMIT),
        name="split",
    )(latents)


def joined(valid):
    rest = valid % LANES
    return rest if 0 < PAIR * rest <= LANES else 0


def spread(out_ref, index, act, pitch):
    lanes = out_ref.shape[3]
    above = pltpu.roll(act, pitch, 1)
    below = pltpu.roll(act, act.shape[1] - pitch, 1)
    edge = jnp.where(lane_of(LANES) < pitch, 0.0, above[:, :LANES].astype(jnp.float32))
    out_ref[index, 0, :, :LANES] = edge.astype(jnp.bfloat16)
    out_ref[index, 0, :, LANES:] = above[:, LANES:lanes]
    out_ref[index, 1] = act[:, :lanes]
    out_ref[index, 2] = below[:, :lanes]


def placed(blocks, core, row, window, line):
    pitch, width = window + 1, line.shape[1]
    lane = lane_of(LANES)
    block, low = divmod(row * pitch, LANES)
    shift = lax.rem(low + LANES - core * (width - window), LANES)
    turned = pltpu.roll(line, shift, 1)
    here = (lane >= low) & (lane < low + window)
    blocks[block] = blocks.get(block, 0.0) + jnp.where(here, turned, 0.0)
    if low + window > LANES:
        blocks[block + 1] = blocks.get(block + 1, 0.0) + jnp.where(lane < low + window - LANES, turned, 0.0)


def near_kernel(halo, pairs, mate_ref, gains_ref, *refs):
    own_refs, value_refs, act_refs = refs[:pairs], refs[pairs : 2 * pairs], refs[2 * pairs :]
    frames, rows, _, width = mate_ref.shape
    window = width // 2 + halo
    core, group, outer = place()
    gain = column(gains_ref[0:1, :])
    done = act_refs[0].shape[2]
    mask = filled(done, window + 1)
    for f in range(frames):
        p, t = divmod(f, PAIR)
        blocks = {}
        for row in range(2 * rows):
            at = row % rows
            index = at + group * (rows - 1 - 2 * at)
            own, mate = own_refs[p][t, index], mate_ref[f, index]
            one, two = (own, mate) if row < rows else (mate, own)
            placed(blocks, core, row, window, jnp.where(outer, one, two).astype(jnp.float32))
        for b in blocks:
            part = slice(b * LANES, (b + 1) * LANES)
            value_refs[p][t, :, part] = blocks[b].astype(jnp.bfloat16)
            if part.stop <= done:
                act_refs[p][t, :, part] = activated(blocks[b], gain, mask[:, part])


def near(halo, mate, gains, own):
    frames, rows, channels, width = mate.shape
    lanes = 2 * rows * (width // 2 + halo + 1)
    pairs = len(own)
    outs = pl.pallas_call(
        functools.partial(near_kernel, halo, pairs),
        out_shape=(jax.ShapeDtypeStruct((PAIR, channels, rounded(lanes)), jnp.bfloat16),) * pairs
        + (jax.ShapeDtypeStruct((PAIR, channels, lanes // LANES * LANES), jnp.bfloat16),) * pairs,
        in_specs=[VMEM] * (2 + pairs),
        out_specs=(VMEM,) * (2 * pairs),
        compiler_params=pltpu.CompilerParams(vmem_limit_bytes=LIMIT),
        cost_estimate=pl.CostEstimate(flops=40 * mate.size, bytes_accessed=8 * mate.size, transcendentals=2 * mate.size),
        name="near",
    )(mate, gains, *own)
    return outs[:pairs], outs[pairs:]


def add_far(halo, far_ref, mate_ref, near_ref, act_ref, columns_ref, values_ref, shifted_ref, send_ref=None):
    pair, rows, _, width = far_ref.shape
    window = width // 2 + halo
    core, group, outer = place()
    lanes, done = values_ref.shape[2], act_ref.shape[2]
    mask = filled(lanes, window + 1)
    for t in range(pair):
        values_ref[t, :, :done] = near_ref[t, :, :done]
        acts = [act_ref[t]]
        blocks = {done // LANES: near_ref[t, :, done:].astype(jnp.float32)}
        for row in range(2 * rows, 2 * rows + halo):
            local = 4 * rows - 1 - row
            at = local % rows
            index = at + (1 - group) * (rows - 1 - 2 * at)
            one, two = (mate_ref, far_ref) if local < rows else (far_ref, mate_ref)
            line = jnp.where(outer, one[t, index], two[t, index]).astype(jnp.float32)
            placed(blocks, core, row, window, line)
        for b in sorted(blocks):
            part = slice(b * LANES, (b + 1) * LANES)
            values_ref[t, :, part] = blocks[b].astype(jnp.bfloat16)
            acts.append(activated(blocks[b], columns_ref[0, 0], mask[:, part]))
        act = jnp.concatenate(acts, axis=1)
        spread(shifted_ref, t, act, window + 1)
        if send_ref is not None:
            send_ref[t] = act


def far_shapes(rows, halo, channels, half):
    pitch = half + halo + 1
    return (
        jax.ShapeDtypeStruct((PAIR, channels, rounded((2 * rows + halo) * pitch)), jnp.bfloat16),
        jax.ShapeDtypeStruct((PAIR, 3, channels, rounded((2 * rows + halo - 1) * pitch)), jnp.bfloat16),
    )


def beyond(halo, columns, *parts):
    far = parts[0]
    _, rows, channels, width = far.shape
    values, shifted = far_shapes(rows, halo, channels, width // 2)

    def kernel(columns_ref, far_ref, mate_ref, near_ref, act_ref, *outs):
        add_far(halo, far_ref, mate_ref, near_ref, act_ref, columns_ref, *outs)

    return pl.pallas_call(
        kernel,
        out_shape=(values, shifted, values),
        in_specs=[VMEM] * 5,
        out_specs=(VMEM,) * 3,
        compiler_params=pltpu.CompilerParams(vmem_limit_bytes=LIMIT),
        cost_estimate=pl.CostEstimate(flops=40 * far.size, bytes_accessed=8 * far.size, transcendentals=2 * far.size),
        name="beyond",
    )(columns, *parts)


def conv_kernel(plan, shifted_ref, values_ref, w_ref, columns_ref, *refs):
    layer, pitch, half, received = plan["layer"], plan["pitch"], plan["half"], plan["received"]
    last, sends, rest, rest_sent = plan["last"], plan["sends"], plan["rest"], plan["rest_sent"]
    refs = list(refs)
    earlier_refs = [refs.pop(0) for _ in range(plan["inputs"])]
    if plan["fetches"]:
        next_ref, sems, held_ref = refs.pop(0), refs.pop(), refs.pop()
        copies = fetches(layer + 1, next_ref, held_ref, sems)
        for copy in copies:
            copy.start()
    earlier_ref = refs.pop() if received else earlier_refs[0]
    if received:
        for t in range(PAIR):
            if rest:
                whole = (earlier_refs[0].shape[1] - LANES) // PAIR
                tail = earlier_refs[0][:, PAIR * whole :].astype(jnp.float32)
                tail = tail if t == 0 else pltpu.roll(tail, LANES - t * (LANES // PAIR), 1)
                tail = jnp.where(lane_of(LANES) < rest, tail, 0.0).astype(jnp.bfloat16)
                act = jnp.concatenate([earlier_refs[0][:, t * whole : (t + 1) * whole], tail], axis=1)
            else:
                act = earlier_refs[0][t]
            spread(earlier_ref, t, act, pitch)
    outs = refs
    if plan["fetches"]:
        laid_ref = outs.pop()
    if plan["builds"]:
        earlier_ref = outs.pop()
        add_far(pitch - 1 - half, *earlier_refs, columns_ref, outs.pop(), earlier_ref)
    _, _, channels, lanes = shifted_ref.shape
    chunks = lanes // LANES
    lane = lane_of(LANES)

    def window(t, b):
        taken = [(earlier_ref, t + a) if t + a < PAIR else (shifted_ref, t + a - PAIR) for a in range(3)]
        at = slice(b * LANES, (b + 1) * LANES)
        return jnp.concatenate([ref[j, :, :, at].reshape(3 * channels, LANES) for ref, j in taken], axis=0)

    places = [(t, b) for t in range(PAIR) for b in range(chunks)]
    side = TILE // LANES
    tiles = []
    bias = columns_ref[layer, 1]
    if not last:
        mask = filled(lanes, pitch)
        gain = columns_ref[layer + 1, 0]

    def sums(t, tap, b):
        tile, at = divmod((t * chunks + b) * LANES, TILE)
        return tiles[tile][tap * channels : (tap + 1) * channels, at : at + LANES]

    tails = []

    def finish(t):
        totals, acts = [], []
        from_left = 0.0
        from_right = pltpu.roll(sums(t, 2, 0), LANES - 1, 1)
        for b in range(chunks):
            at = slice(b * LANES, (b + 1) * LANES)
            left = pltpu.roll(sums(t, 0, b), 1, 1)
            right = pltpu.roll(sums(t, 2, b + 1), LANES - 1, 1) if b + 1 < chunks else 0.0
            summed = (
                jnp.where(lane == 0, from_left, left) + sums(t, 1, b) + jnp.where(lane == LANES - 1, right, from_right)
            )
            from_left, from_right = left, right
            total = (values_ref[t, :, at].astype(jnp.float32) + summed + bias).astype(jnp.bfloat16)
            totals.append(total.astype(jnp.float32))
            if not last:
                outs[0][t, :, at] = total
                acts.append(activated(totals[-1], gain, mask[:, at]))
                if not sends:
                    continue
                if not rest_sent:
                    outs[2][t, :, at] = acts[-1]
                elif b < chunks - 1:
                    outs[2][:, (t * (chunks - 1) + b) * LANES : (t * (chunks - 1) + b + 1) * LANES] = acts[-1]
                else:
                    tail = jnp.where(lane < rest_sent, acts[-1].astype(jnp.float32), 0.0)
                    tails.append(tail if t == 0 else pltpu.roll(tail, t * (LANES // PAIR), 1))
        if not last:
            spread(outs[1], t, jnp.concatenate(acts, axis=1), pitch)
            return
        whole = jnp.concatenate(totals, axis=1)
        halo = pitch - 1 - half
        core, _, outer = place()
        whole = jnp.where(core == 1, pltpu.roll(whole, lanes - halo, 1), whole)
        left_half = lane < half

        def rows_of(row):
            one = whole if row == 0 else pltpu.roll(whole, lanes - row * pitch, 1)
            two = pltpu.roll(whole, lanes - (row + 1) * pitch + half, 1)
            return jnp.where(left_half, one[:, :LANES], two[:, :LANES])

        outermost, inner = rows_of(0), rows_of(2)
        outs[0][t] = jnp.where(outer, outermost, inner).astype(jnp.bfloat16)
        outs[1][t] = jnp.where(outer, inner, outermost).astype(jnp.bfloat16)

    finished = 0
    for n in range(0, len(places), side):
        rhs = jnp.concatenate([window(t, b) for t, b in places[n : n + side]], axis=1)
        tiles.append(jnp.dot(w_ref[...], rhs, preferred_element_type=jnp.float32))
        while finished < PAIR and (finished + 1) * chunks <= n + side:
            finish(finished)
            finished += 1
    if plan["fetches"]:
        laid_out(copies, held_ref, laid_ref)
    if sends and rest_sent:
        outs[2][:, PAIR * (chunks - 1) * LANES :] = sum(tails).astype(jnp.bfloat16)


def conv(plan, earlier, shifted, values, weight, columns, conv_weight):
    _, _, channels, lanes = shifted.shape
    pitch, half, received = plan["pitch"], plan["half"], plan["received"]
    if plan["last"]:
        out_shape = (jax.ShapeDtypeStruct((PAIR, channels, LANES), jnp.bfloat16),) * 2
    else:
        out_shape = (
            jax.ShapeDtypeStruct((PAIR, channels, lanes), jnp.bfloat16),
            jax.ShapeDtypeStruct((PAIR, 3, channels, rounded((plan["rows"] - 1) * pitch)), jnp.bfloat16),
        )
        if plan["sends"] and plan["rest_sent"]:
            out_shape += (jax.ShapeDtypeStruct((channels, PAIR * (lanes - LANES) + LANES), jnp.bfloat16),)
        elif plan["sends"]:
            out_shape += out_shape[:1]
    scratch = [pltpu.VMEM((PAIR, 3, channels, lanes), jnp.bfloat16)] * received
    extra = ()
    if plan["builds"]:
        out_shape += far_shapes(earlier[0].shape[1], pitch - 1 - half, channels, half)
    if plan["fetches"]:
        extra = (conv_weight,)
        out_shape += (laid_shape(conv_weight),)
        scratch += held(conv_weight)
    return pl.pallas_call(
        functools.partial(conv_kernel, plan),
        out_shape=out_shape,
        in_specs=[VMEM] * (4 + len(earlier)) + [ANY] * len(extra),
        out_specs=(VMEM,) * len(out_shape),
        scratch_shapes=scratch,
        compiler_params=pltpu.CompilerParams(vmem_limit_bytes=LIMIT),
        cost_estimate=pl.CostEstimate(
            flops=54 * channels * channels * PAIR * lanes,
            bytes_accessed=2 * weight.size,
            transcendentals=PAIR * channels * lanes,
        ),
        name=f"conv_{plan['layer']}",
    )(shifted, values, weight, columns, *earlier, *extra)


def join_kernel(pair, kept_ref, got_ref, *refs):
    out_ref, lines_ref, sem = refs[-3:]
    _, rows, _, width = lines_ref.shape
    half = width // 2
    core, group, _ = place()
    first = core == 0
    left_half = lane_of(width) < half
    for t in range(PAIR):
        mine, theirs = kept_ref[t].astype(jnp.float32), got_ref[t].astype(jnp.float32)
        left, right = jnp.where(first, mine, theirs), jnp.where(first, theirs, mine)
        lines = (
            jnp.where(left_half, left, pltpu.roll(right, half, 1)),
            jnp.where(left_half, pltpu.roll(left, half, 1), right),
        )
        for j in range(rows):
            lines_ref[t, j + group * (rows - 1 - 2 * j)] = lines[j].astype(jnp.bfloat16)
    copy = pltpu.make_async_copy(lines_ref, out_ref.at[pl.ds(PAIR * pair, PAIR)], sem)
    copy.start()
    copy.wait()


def join(pair, kept, got, shape, *so_far):
    return pl.pallas_call(
        functools.partial(join_kernel, pair),
        out_shape=jax.ShapeDtypeStruct(shape, jnp.bfloat16),
        in_specs=[VMEM, VMEM] + [ANY] * len(so_far),
        out_specs=ANY,
        scratch_shapes=[pltpu.VMEM((PAIR,) + shape[1:], jnp.bfloat16), pltpu.SemaphoreType.DMA],
        input_output_aliases={2: 0} if so_far else {},
        compiler_params=pltpu.CompilerParams(vmem_limit_bytes=LIMIT),
        name="join",
    )(kept, got, *so_far)


def on_device(latents, conv_weight, norm_gains, biases):
    layers = conv_weight.shape[0]
    frames, rows, channels, width = latents.shape
    strips, blocks = lax.axis_size("rows"), lax.axis_size("tm")
    assert strips == 4 and rows == 2 and frames % PAIR == 0 and width == LANES

    def mate_of(block):
        return lax.ppermute(block, "rows", [(i, i ^ 1) for i in range(strips)])

    def earlier_of(block):
        return lax.ppermute(block, "tm", [(i, i + 1) for i in range(blocks - 1)])

    def beyond_of(block):
        return lax.ppermute(block, "rows", [(i, i ^ 2) for i in range(strips)])

    mate = mate_of(latents)
    pairs = frames // PAIR
    own = split(latents)
    far = [beyond_of(own[p]) for p in reversed(range(pairs))][::-1]
    row_values = jnp.concatenate([norm_gains, biases], axis=0)
    weight, columns = weights(conv_weight, row_values)
    near_values, near_act = near(layers, mate, row_values, own)
    far[-1], weight, columns, near_values, near_act = lax.optimization_barrier(
        (far[-1], weight, columns, near_values, near_act)
    )
    parts = [(far[p], mate_of(far[p]), near_values[p], near_act[p]) for p in reversed(range(pairs))][::-1]
    values, shifted = [None] * pairs, [None] * pairs
    values[-1], shifted[-1], send = beyond(layers, columns, *parts[-1])
    halo, rest = earlier_of(send), 0
    half = width // 2
    pitch = half + layers + 1
    for layer in range(layers):
        last = layer == layers - 1
        rows_left = 2 * rows + layers - 1 - layer
        results = [None] * pairs
        for p in reversed(range(pairs)):
            builds = layer == 0 and p > 0
            earlier = (halo,) if p == 0 else parts[p - 1] if builds else (shifted[p - 1],)
            plan = {
                "layer": layer,
                "last": last,
                "sends": p == pairs - 1 and not last,
                "rest_sent": joined(rows_left * pitch),
                "received": p == 0,
                "rest": 0 if p else rest,
                "builds": builds,
                "fetches": p == 0 and not last,
                "inputs": len(earlier),
                "pitch": pitch,
                "half": half,
                "rows": rows_left,
            }
            outs = list(conv(plan, earlier, shifted[p], values[p], weight, columns, conv_weight))
            if plan["fetches"]:
                next_weight = outs.pop()
            if builds:
                shifted[p - 1], values[p - 1] = outs.pop(), outs.pop()
            results[p] = outs
            if plan["sends"]:
                arriving = earlier_of(outs[2])
        values, shifted = [r[0] for r in results], [r[1] for r in results]
        if not last:
            halo, rest, weight = arriving, joined(rows_left * pitch), next_weight
    result = ()
    for p in reversed(range(pairs)):
        result = (join(p, values[p], mate_of(shifted[p]), latents.shape, *result),)
    return result[0]


def solution(mesh):
    in_specs = (P(("clips", "tm"), "rows", None, None), P(), P(), P())
    out_specs = P(("clips", "tm"), "rows", None, None)
    return jax.shard_map(on_device, mesh=mesh, in_specs=in_specs, out_specs=out_specs, check_vma=False)
```

time: 46.2 us -> 46.6 us (level)
  waiting for transfers between devices: 3.35 us -> 6.03 us
  starting transfers between devices: 18.1 us -> 15.9 us
    ppermute x4 -> x3, starting transfers between devices: 15 us -> 10.9 us  [earlier_of(): return lax.ppermute(block, 'tm', [(i, i + 1) for i in range(blocks - 1)])]
    ppermute x1 -> x2, waiting for transfers between devices: 0.01 us -> 3.83 us  [beyond_of(): return lax.ppermute(block, 'rows', [(i, i ^ 2) for i in range(strips)])]
    ppermute x1 -> x2, starting transfers between devices: 2.49 us -> 4.29 us  [beyond_of(): return lax.ppermute(block, 'rows', [(i, i ^ 2) for i in range(strips)])]
    ppermute x4 -> x3, waiting for transfers between devices: 1.18 us -> 0.39 us  [earlier_of(): return lax.ppermute(block, 'tm', [(i, i + 1) for i in range(blocks - 1)])]
    ppermute x4 -> x5, waiting for transfers between devices: 2.17 us -> 1.81 us  [mate_of(): return lax.ppermute(block, 'rows', [(i, i ^ 1) for i in range(strips)])]
    pallas_call x9 -> x10, Pallas kernels: 20.7 us -> 20.7 us  [the longest x6 17.6 us: conv(): pl.pallas_call(functools.partial(conv_kernel, plan), out_shape=out_shape,...]
  transfers between devices with their start and end apart: 9 -> 10, of which waited for: 3 -> 5; matrix products, arithmetic and copies ran while one was open for 2% -> 2% of each run, Pallas kernels for 45% -> 46%
where the time goes in v5:
time: 46.6 us; the launch traced here: 46.2 us
  Pallas kernels  22.3 us (48%)
  starting transfers between devices  15.9 us (34%)
  waiting for transfers between devices  6.03 us (13%)
  local copies, waits for them, and re-layouts  1 us (2%)
  other arithmetic  0.71 us (2%)
    pallas_call x6, Pallas kernels, conv(): pl.pallas_call(functools.partial(conv_kernel, plan), out_shape=out_shape,...  17.6 us
    ppermute x3, starting transfers between devices, earlier_of(): return lax.ppermute(block, 'tm', [(i, i + 1) for i in range(blocks - 1)])  10.9 us
    ppermute x2, starting transfers between devices, beyond_of(): return lax.ppermute(block, 'rows', [(i, i ^ 2) for i in range(strips)])  4.29 us
    ppermute x2, waiting for transfers between devices, beyond_of(): return lax.ppermute(block, 'rows', [(i, i ^ 2) for i in range(strips)])  3.83 us
    pallas_call x1, Pallas kernels, weights(): pl.pallas_call(weights_kernel, out_shape=(laid_shape(conv_weight), jax.Sh...  1.89 us
    ppermute x5, waiting for transfers between devices, mate_of(): return lax.ppermute(block, 'rows', [(i, i ^ 1) for i in range(strips)])  1.81 us
    pallas_call x2, Pallas kernels, join(): pl.pallas_call(functools.partial(join_kernel, pair), out_shape=jax.ShapeD...  1.62 us
    unnamed x2, local copies, waits for them, and re-layouts  1 us
  transfers between devices with their start and end apart: 10, of which 5 were waited for; matrix products, arithmetic and copies ran while one was open for 2% of the time, Pallas kernels for 46%

profile of v5, /device:TPU:0, one launch (start us, length us, event | category | flops | bytes accessed | tf_op | source)
XLA Modules:
  0.0 46.2 jit_solution(17806236231028391704)
XLA Ops:
  0.0 0.5 collective-permute-start.1
  0.5 1.0 %copy-done = bf16[4,2,192,128]{3,2,1,0:T(8,128)(2,1)S(1)} copy-done((bf16[4,2,192,128]{3,2,1,0:T(8,128)(2,1)S(1)}, bf16[4,2,192,128]{3,2,1,0:T(8,128)(2,1)}, u32[]{:S(2)}) %copy-start) | copy-done | bytes 393240
  1.5 2.6 %collective-permute-start = (bf16[2,2,192,128]{3,2,1,0:T(8,128)(2,1)S(1)}, bf16[2,2,192,128]{3,2,1,0:T(8,128)(2,1)S(1)}, u32[]{:S(2)}, u32[]{:S(2)}) collective-permute-start(bf16[2,2,192,128]{3,2,1,0:T(8,128)(2,1)S(1)} %get-tuple-element.41.refs_1_), channel_id=1, source_target_pairs={{0,2},{1,3},{2,0},{3,1},{4,6},{5,7},{6,4},{7,5},{8,10},{9,11},{10,... | collective-permute-start | bytes 589832 | tf_op jit(solution)/shard_map/ppermute | solution.py:437
  4.0 0.7 %pad_maximum_fusion.rows_ref.gains_ref = f32[6,192]{1,0:T(8,128)S(1)} fusion(f32[3,192]{1,0:T(4,128)} %param.7, f32[3,192]{1,0:T(4,128)} %param.6), kind=kLoop, calls=%fused_computation | loop fusion | flops 1152 | bytes 9216 | tf_op jit(solution)/shard_map/concatenate | solution.py:443
  4.7 1.9 %weights.1 = (bf16[576,1728]{1,0:T(8,128)(2,1)S(1)}, f32[3,2,192,128]{3,2,1,0:T(8,128)S(1)}) custom-call(bf16[3,27,192,192]{3,2,1,0:T(8,128)(2,1)} %refs_1_.3, f32[6,192]{1,0:T(8,128)S(1)} %pad_maximum_fusion.rows_ref.gains_ref), custom_call_target="tpu_custom_call" | custom-call | bytes 3981312 | tf_op jit(solution)/shard_map/weights/pallas_call | solution.py:92
  6.6 0.0 collective-permute-done.1.mate_ref
  6.7 0.6 %near.1 = (bf16[2,192,384]{2,1,0:T(8,128)(2,1)S(1)}, bf16[2,192,384]{2,1,0:T(8,128)(2,1)S(1)}, bf16[2,192,256]{2,1,0:T(8,128)(2,1)S(1)}, bf16[2,192,256]{2,1,0:T(8,128)(2,1)S(1)}) custom-call(bf16[4,2,192,128]{3,2,1,0:T(8,128)(2,1)S(1)} %collective-permute-done.1.mate_ref, f32[6,192]{1,0:T(8,128)S(1)} %pad_maximum_fusion.rows_ref.gains_ref, ...), custom_call_target="tpu_custom_call" | custom-call | flops 7864320 | bytes 1572864 | tf_op jit(solution)/shard_map/near/pallas_call | solution.py:177
  7.3 2.3 %collective-permute-done.far_ref = bf16[2,2,192,128]{3,2,1,0:T(8,128)(2,1)S(1)} collective-permute-done((bf16[2,2,192,128]{3,2,1,0:T(8,128)(2,1)S(1)}, bf16[2,2,192,128]{3,2,1,0:T(8,128)(2,1)S(1)}, u32[]{:S(2)}, u32[]{:S(2)}) %collective-permute-start) | collective-permute-done | bytes 196640 | tf_op jit(solution)/shard_map/ppermute | solution.py:437
  9.6 0.0 collective-permute-start.2
  9.6 1.7 %collective-permute-start.3 = (bf16[2,2,192,128]{3,2,1,0:T(8,128)(2,1)S(1)}, bf16[2,2,192,128]{3,2,1,0:T(8,128)(2,1)S(1)}, u32[]{:S(2)}, u32[]{:S(2)}) collective-permute-start(bf16[2,2,192,128]{3,2,1,0:T(8,128)(2,1)S(1)} %get-tuple-element.44.refs_0_), channel_id=1, source_target_pairs={{0,2},{1,3},{2,0},{3,1},{4,6},{5,7},{6,4},{7,5},{8,10},{9,11},{10,... | collective-permute-start | bytes 589832 | tf_op jit(solution)/shard_map/ppermute | solution.py:437
  11.4 0.0 collective-permute-done.2.mate_ref
  11.4 0.5 %beyond.1 = (bf16[2,192,512]{2,1,0:T(8,128)(2,1)S(1)}, bf16[2,3,192,512]{3,2,1,0:T(8,128)(2,1)S(1)}, bf16[2,192,512]{2,1,0:T(8,128)(2,1)S(1)}) custom-call(f32[3,2,192,128]{3,2,1,0:T(8,128)S(1)} %get-tuple-element.49.columns_ref, bf16[2,2,192,128]{3,2,1,0:T(8,128)(2,1)S(1)} %collective-permute-done.far_ref, ...), custom_call_target="tpu_custom_call" | custom-call | flops 3932160 | bytes 786432 | tf_op jit(solution)/shard_map/beyond/pallas_call | solution.py:233
  11.9 3.5 %collective-permute-start.5 = (bf16[2,192,512]{2,1,0:T(8,128)(2,1)S(1)}, bf16[2,192,512]{2,1,0:T(8,128)(2,1)S(1)}, u32[]{:S(2)}, u32[]{:S(2)}) collective-permute-start(bf16[2,192,512]{2,1,0:T(8,128)(2,1)S(1)} %get-tuple-element.60), channel_id=1, source_target_pairs={{0,4},{4,8},{8,12},{1,5},{5,9},{9,13},{2,6},{6,10},{10,14},{3,7},{... | collective-permute-start | bytes 1179656 | tf_op jit(solution)/shard_map/ppermute | solution.py:434
  15.4 1.5 %collective-permute-done.3.refs_0_ = bf16[2,2,192,128]{3,2,1,0:T(8,128)(2,1)S(1)} collective-permute-done((bf16[2,2,192,128]{3,2,1,0:T(8,128)(2,1)S(1)}, bf16[2,2,192,128]{3,2,1,0:T(8,128)(2,1)S(1)}, u32[]{:S(2)}, u32[]{:S(2)}) %collective-permute-start.3) | collective-permute-done | bytes 196640 | tf_op jit(solution)/shard_map/ppermute | solution.py:437
  16.9 0.0 collective-permute-start.4
  16.9 1.4 %collective-permute-done.4.refs_1_ = bf16[2,2,192,128]{3,2,1,0:T(8,128)(2,1)S(1)} collective-permute-done((bf16[2,2,192,128]{3,2,1,0:T(8,128)(2,1)S(1)}, bf16[2,2,192,128]{3,2,1,0:T(8,128)(2,1)S(1)}, u32[]{:S(2)}, u32[]{:S(2)}) %collective-permute-start.4) | collective-permute-done | bytes 196640 | tf_op jit(solution)/shard_map/ppermute | solution.py:431
  18.4 3.0 %conv_0.2 = (bf16[2,192,512]{2,1,0:T(8,128)(2,1)S(1)}, bf16[2,3,192,384]{3,2,1,0:T(8,128)(2,1)S(1)}, bf16[192,896]{1,0:T(8,128)(2,1)S(1)}, bf16[2,192,512]{2,1,0:T(8,128)(2,1)S(1)}, bf16[2,3,192,512]{3,2,1,0:T(8,128)(2,1)S(1)}) custom-call(bf16[2,3,192,512]{3,2,1,0:T(8,128)(2,1)S(1)} %get-tuple-element.53.shifted_ref, ...), custom_call_target="tpu_custom_call" | custom-call | flops 2038431744 | bytes 1990656 | tf_op jit(solution)/shard_map/conv_0/pallas_call | solution.py:374
  21.4 3.8 %collective-permute-start.6 = (bf16[192,896]{1,0:T(8,128)(2,1)S(1)}, bf16[192,896]{1,0:T(8,128)(2,1)S(1)}, u32[]{:S(2)}, u32[]{:S(2)}) collective-permute-start(bf16[192,896]{1,0:T(8,128)(2,1)S(1)} %get-tuple-element.64), channel_id=1, source_target_pairs={{0,4},{4,8},{8,12},{1,5},{5,9},{9,13},{2,6},{6,10},{10,14},{3,7},{... | collective-permute-start | bytes 1032200 | tf_op jit(solution)/shard_map/ppermute | solution.py:434
  25.1 0.0 collective-permute-done.5.refs_0_
  25.1 4.5 %conv_0.3 = (bf16[2,192,512]{2,1,0:T(8,128)(2,1)S(1)}, bf16[2,3,192,384]{3,2,1,0:T(8,128)(2,1)S(1)}, bf16[576,1728]{1,0:T(8,128)(2,1)S(1)}) custom-call(bf16[2,3,192,512]{3,2,1,0:T(8,128)(2,1)S(1)} %get-tuple-element.58.shifted_ref, bf16[2,192,512]{2,1,0:T(8,128)(2,1)S(1)} %get-tuple-element.59.values_ref, bf16[576,1728]{1,0:T(8,128)(2,1)S(1)} %get-tuple-element.55.w_ref, ...), custom_call_target="tpu_custom_call" | custom-call | flops 2038431744 | bytes 1990656 | tf_op jit(solution)/shard_map/conv_0/pallas_call | solution.py:374
  29.7 2.2 %conv_1.3 = (bf16[2,192,384]{2,1,0:T(8,128)(2,1)S(1)}, bf16[2,3,192,384]{3,2,1,0:T(8,128)(2,1)S(1)}, bf16[2,192,384]{2,1,0:T(8,128)(2,1)S(1)}) custom-call(bf16[2,3,192,384]{3,2,1,0:T(8,128)(2,1)S(1)} %get-tuple-element.68.shifted_ref, bf16[2,192,512]{2,1,0:T(8,128)(2,1)S(1)} %get-tuple-element.69.values_ref, bf16[576,1728]{1,0:T(8,128)(2,1)S(1)} %get-tuple-element.63.w_ref, ...), custom_call_target="tpu_custom_call" | custom-call | flops 1528823808 | bytes 1990656 | tf_op jit(solution)/shard_map/conv_1/pallas_call | solution.py:374
  31.9 3.7 %collective-permute-start.7 = (bf16[2,192,384]{2,1,0:T(8,128)(2,1)S(1)}, bf16[2,192,384]{2,1,0:T(8,128)(2,1)S(1)}, u32[]{:S(2)}, u32[]{:S(2)}) collective-permute-start(bf16[2,192,384]{2,1,0:T(8,128)(2,1)S(1)} %get-tuple-element.70), channel_id=1, source_target_pairs={{0,4},{4,8},{8,12},{1,5},{5,9},{9,13},{2,6},{6,10},{10,14},{3,7},{... | collective-permute-start | bytes 884744 | tf_op jit(solution)/shard_map/ppermute | solution.py:434
  35.5 0.0 collective-permute-done.6.refs_0_
  35.5 3.5 %conv_1.2 = (bf16[2,192,384]{2,1,0:T(8,128)(2,1)S(1)}, bf16[2,3,192,384]{3,2,1,0:T(8,128)(2,1)S(1)}, bf16[576,1728]{1,0:T(8,128)(2,1)S(1)}) custom-call(bf16[2,3,192,384]{3,2,1,0:T(8,128)(2,1)S(1)} %get-tuple-element.61.shifted_ref.refs_0_, bf16[2,192,512]{2,1,0:T(8,128)(2,1)S(1)} %get-tuple-element.62.values_ref, ...), custom_call_target="tpu_custom_call" | custom-call | flops 1528823808 | bytes 1990656 | tf_op jit(solution)/shard_map/conv_1/pallas_call | solution.py:374
  39.0 2.1 %conv_2.3 = (bf16[2,192,128]{2,1,0:T(8,128)(2,1)S(1)}, bf16[2,192,128]{2,1,0:T(8,128)(2,1)S(1)}) custom-call(bf16[2,3,192,384]{3,2,1,0:T(8,128)(2,1)S(1)} %get-tuple-element.73.shifted_ref, bf16[2,192,384]{2,1,0:T(8,128)(2,1)S(1)} %get-tuple-element.74.values_ref, bf16[576,1728]{1,0:T(8,128)(2,1)S(1)} %get-tuple-element.67.w_ref, ...), custom_call_target="tpu_custom_call" | custom-call | flops 1528823808 | bytes 1990656 | tf_op jit(solution)/shard_map/conv_2/pallas_call | solution.py:374
  41.2 0.1 collective-permute-start.9
  41.2 0.4 collective-permute-done.7.refs_0_
  41.6 2.3 %conv_2.2 = (bf16[2,192,128]{2,1,0:T(8,128)(2,1)S(1)}, bf16[2,192,128]{2,1,0:T(8,128)(2,1)S(1)}) custom-call(bf16[2,3,192,384]{3,2,1,0:T(8,128)(2,1)S(1)} %get-tuple-element.65.shifted_ref.refs_0_, bf16[2,192,384]{2,1,0:T(8,128)(2,1)S(1)} %get-tuple-element.66.values_ref, bf16[576,1728]{1,0:T(8,128)(2,1)S(1)} %get-tuple-element.67.w_ref, ...), custom_call_target="tpu_custom_call" | custom-call | flops 1528823808 | bytes 1990656 | tf_op jit(solution)/shard_map/conv_2/pallas_call | solution.py:374
  43.9 0.2 collective-permute-start.8
  44.1 0.8 %join.2.refs_0_ = bf16[4,2,192,128]{3,2,1,0:T(8,128)(2,1)} custom-call(bf16[2,192,128]{2,1,0:T(8,128)(2,1)S(1)} %get-tuple-element.75.kept_ref, bf16[2,192,128]{2,1,0:T(8,128)(2,1)S(1)} %collective-permute-done.9.got_ref), custom_call_target="tpu_custom_call" | custom-call | tf_op jit(solution)/shard_map/join/pallas_call | solution.py:412
  44.9 0.4 collective-permute-done.8.got_ref
  45.3 0.8 %join.3 = bf16[4,2,192,128]{3,2,1,0:T(8,128)(2,1)} custom-call(bf16[2,192,128]{2,1,0:T(8,128)(2,1)S(1)} %get-tuple-element.71.kept_ref, bf16[2,192,128]{2,1,0:T(8,128)(2,1)S(1)} %collective-permute-done.8.got_ref, bf16[4,2,192,128]{3,2,1,0:T(8,128)(2,1)} %join.2.refs_0_), custom_call_target="tpu_custom_call", output_to_operand_aliasing={{}: (2, {})} | custom-call | tf_op jit(solution)/shard_map/join/pallas_call | solution.py:412
  (3 shorter events, 0.0 us)
Async XLA Ops:
  0.0 6.6 %collective-permute-start.1 = (bf16[4,2,192,128]{3,2,1,0:T(8,128)(2,1)}, bf16[4,2,192,128]{3,2,1,0:T(8,128)(2,1)S(1)}, u32[]{:S(2)}, u32[]{:S(2)}) collective-permute-start(bf16[4,2,192,128]{3,2,1,0:T(8,128)(2,1)} %in_ref.1), channel_id=1, source_target_pairs={{0,1},{1,0},{2,3},{3,2},{4,5},{5,4},{6,7},{7,6},{8,9},{9,8},{10,11... | collective-permute-start | bytes 1179656 | tf_op jit(solution)/shard_map/ppermute | solution.py:431
  0.5 1.0 %copy-start = (bf16[4,2,192,128]{3,2,1,0:T(8,128)(2,1)S(1)}, bf16[4,2,192,128]{3,2,1,0:T(8,128)(2,1)}, u32[]{:S(2)}) copy-start(bf16[4,2,192,128]{3,2,1,0:T(8,128)(2,1)} %in_ref.1) | copy-start | bytes 1179652
  1.5 8.1 %collective-permute-start = (bf16[2,2,192,128]{3,2,1,0:T(8,128)(2,1)S(1)}, bf16[2,2,192,128]{3,2,1,0:T(8,128)(2,1)S(1)}, u32[]{:S(2)}, u32[]{:S(2)}) collective-permute-start(bf16[2,2,192,128]{3,2,1,0:T(8,128)(2,1)S(1)} %get-tuple-element.41.refs_1_), channel_id=1, source_target_pairs={{0,2},{1,3},{2,0},{3,1},{4,6},{5,7},{6,4},{7,5},{8,10},{9,11},{10,... | collective-permute-start | bytes 589832 | tf_op jit(solution)/shard_map/ppermute | solution.py:437
  9.6 1.7 %collective-permute-start.2 = (bf16[2,2,192,128]{3,2,1,0:T(8,128)(2,1)S(1)}, bf16[2,2,192,128]{3,2,1,0:T(8,128)(2,1)S(1)}, u32[]{:S(2)}, u32[]{:S(2)}) collective-permute-start(bf16[2,2,192,128]{3,2,1,0:T(8,128)(2,1)S(1)} %collective-permute-done.far_ref), channel_id=1, source_target_pairs={{0,1},{1,0},{2,3},{3,2},{4,5},{5,4},{6,7},{7,6},{8,9},{9,8},{10,11... | collective-permute-start | bytes 589832 | tf_op jit(solution)/shard_map/ppermute | solution.py:431
  9.6 7.3 %collective-permute-start.3 = (bf16[2,2,192,128]{3,2,1,0:T(8,128)(2,1)S(1)}, bf16[2,2,192,128]{3,2,1,0:T(8,128)(2,1)S(1)}, u32[]{:S(2)}, u32[]{:S(2)}) collective-permute-start(bf16[2,2,192,128]{3,2,1,0:T(8,128)(2,1)S(1)} %get-tuple-element.44.refs_0_), channel_id=1, source_target_pairs={{0,2},{1,3},{2,0},{3,1},{4,6},{5,7},{6,4},{7,5},{8,10},{9,11},{10,... | collective-permute-start | bytes 589832 | tf_op jit(solution)/shard_map/ppermute | solution.py:437
  11.9 13.3 %collective-permute-start.5 = (bf16[2,192,512]{2,1,0:T(8,128)(2,1)S(1)}, bf16[2,192,512]{2,1,0:T(8,128)(2,1)S(1)}, u32[]{:S(2)}, u32[]{:S(2)}) collective-permute-start(bf16[2,192,512]{2,1,0:T(8,128)(2,1)S(1)} %get-tuple-element.60), channel_id=1, source_target_pairs={{0,4},{4,8},{8,12},{1,5},{5,9},{9,13},{2,6},{6,10},{10,14},{3,7},{... | collective-permute-start | bytes 1179656 | tf_op jit(solution)/shard_map/ppermute | solution.py:434
  16.9 1.4 %collective-permute-start.4 = (bf16[2,2,192,128]{3,2,1,0:T(8,128)(2,1)S(1)}, bf16[2,2,192,128]{3,2,1,0:T(8,128)(2,1)S(1)}, u32[]{:S(2)}, u32[]{:S(2)}) collective-permute-start(bf16[2,2,192,128]{3,2,1,0:T(8,128)(2,1)S(1)} %collective-permute-done.3.refs_0_), channel_id=1, source_target_pairs={{0,1},{1,0},{2,3},{3,2},{4,5},{5,4},{6,7},{7,6},{8,9},{9,8},{10,11... | collective-permute-start | bytes 589832 | tf_op jit(solution)/shard_map/ppermute | solution.py:431
  21.4 14.2 %collective-permute-start.6 = (bf16[192,896]{1,0:T(8,128)(2,1)S(1)}, bf16[192,896]{1,0:T(8,128)(2,1)S(1)}, u32[]{:S(2)}, u32[]{:S(2)}) collective-permute-start(bf16[192,896]{1,0:T(8,128)(2,1)S(1)} %get-tuple-element.64), channel_id=1, source_target_pairs={{0,4},{4,8},{8,12},{1,5},{5,9},{9,13},{2,6},{6,10},{10,14},{3,7},{... | collective-permute-start | bytes 1032200 | tf_op jit(solution)/shard_map/ppermute | solution.py:434
  31.9 9.7 %collective-permute-start.7 = (bf16[2,192,384]{2,1,0:T(8,128)(2,1)S(1)}, bf16[2,192,384]{2,1,0:T(8,128)(2,1)S(1)}, u32[]{:S(2)}, u32[]{:S(2)}) collective-permute-start(bf16[2,192,384]{2,1,0:T(8,128)(2,1)S(1)} %get-tuple-element.70), channel_id=1, source_target_pairs={{0,4},{4,8},{8,12},{1,5},{5,9},{9,13},{2,6},{6,10},{10,14},{3,7},{... | collective-permute-start | bytes 884744 | tf_op jit(solution)/shard_map/ppermute | solution.py:434
  41.2 2.9 %collective-permute-start.9 = (bf16[2,192,128]{2,1,0:T(8,128)(2,1)S(1)}, bf16[2,192,128]{2,1,0:T(8,128)(2,1)S(1)}, u32[]{:S(2)}, u32[]{:S(2)}) collective-permute-start(bf16[2,192,128]{2,1,0:T(8,128)(2,1)S(1)} %get-tuple-element.76), channel_id=1, source_target_pairs={{0,1},{1,0},{2,3},{3,2},{4,5},{5,4},{6,7},{7,6},{8,9},{9,8},{10,11... | collective-permute-start | bytes 294920 | tf_op jit(solution)/shard_map/ppermute | solution.py:431
  43.9 1.4 %collective-permute-start.8 = (bf16[2,192,128]{2,1,0:T(8,128)(2,1)S(1)}, bf16[2,192,128]{2,1,0:T(8,128)(2,1)S(1)}, u32[]{:S(2)}, u32[]{:S(2)}) collective-permute-start(bf16[2,192,128]{2,1,0:T(8,128)(2,1)S(1)} %get-tuple-element.72), channel_id=1, source_target_pairs={{0,1},{1,0},{2,3},{3,2},{4,5},{5,4},{6,7},{7,6},{8,9},{9,8},{10,11... | collective-permute-start | bytes 294920 | tf_op jit(solution)/shard_map/ppermute | solution.py:431

commit v6 on v5

--- a/solution.py
+++ b/solution.py
@@ -13,7 +13,8 @@
 TILE = 256
 VMEM = pl.BlockSpec(memory_space=pltpu.VMEM)
 ANY = pl.BlockSpec(memory_space=pl.ANY)
-LIMIT = 44 * 1024 * 1024
+LIMIT = 24 * 1024 * 1024
+LARGE = 44 * 1024 * 1024
 
 
 def place():
@@ -48,57 +49,45 @@
     return (halved + halved * jnp.tanh(halved)).astype(jnp.bfloat16)
 
 
-def fetches(layer, w_ref, held_ref, sems):
-    step = w_ref.shape[1] // 3
-    return [
-        pltpu.make_async_copy(w_ref.at[layer, pl.ds(step * tap, step)], held_ref.at[tap], sems.at[tap]) for tap in range(3)
-    ]
-
-
-def laid_out(copies, held_ref, out_ref):
-    _, _, outs, ins = held_ref.shape
+def weights_kernel(w_ref, rows_ref, *refs):
+    outs, columns_ref, held_ref, sems = refs[:-3], refs[-3], refs[-2], refs[-1]
+    layers, taps, channels_out, ins = w_ref.shape
+    step = taps // 3
+    places = [(layer, time_tap) for layer in range(layers) for time_tap in range(3)]
+    copies = []
+    for n, (layer, time_tap) in enumerate(places):
+        part = pl.ds(step * time_tap, step)
+        copies.append(pltpu.make_async_copy(w_ref.at[layer, part], held_ref.at[n], sems.at[n]))
+        copies[-1].start()
     _, flipped, _ = place()
-    for time_tap in range(3):
-        copies[time_tap].wait()
+    for layer in range(layers):
+        columns_ref[layer, 0] = column(rows_ref[layer : layer + 1, :])
+        columns_ref[layer, 1] = column(rows_ref[layers + layer : layers + layer + 1, :])
+    for n, (layer, time_tap) in enumerate(places):
+        copies[n].wait()
         for row_tap in range(3):
             source = 3 * (row_tap + flipped * (2 - 2 * row_tap))
             at = (3 * time_tap + row_tap) * ins
-            out_ref[:, at : at + ins] = held_ref[time_tap, pl.ds(source, 3)].reshape(3 * outs, ins)
-
-
-def held(conv_weight):
-    _, taps, outs, ins = conv_weight.shape
-    return [pltpu.VMEM((3, taps // 3, outs, ins), conv_weight.dtype), pltpu.SemaphoreType.DMA((3,))]
-
-
-def laid_shape(conv_weight):
-    _, _, outs, ins = conv_weight.shape
-    return jax.ShapeDtypeStruct((3 * outs, 9 * ins), conv_weight.dtype)
-
-
-def weights_kernel(w_ref, rows_ref, out_ref, columns_ref, held_ref, sems):
-    copies = fetches(0, w_ref, held_ref, sems)
-    for copy in copies:
-        copy.start()
-    layers = w_ref.shape[0]
-    for layer in range(layers):
-        columns_ref[layer, 0] = column(rows_ref[layer : layer + 1, :])
-        columns_ref[layer, 1] = column(rows_ref[layers + layer : layers + layer + 1, :])
-    laid_out(copies, held_ref, out_ref)
+            outs[layer][:, at : at + ins] = held_ref[n, pl.ds(source, 3)].reshape(3 * channels_out, ins)
 
 
 def weights(conv_weight, rows):
-    layers, _, outs, _ = conv_weight.shape
-    return pl.pallas_call(
+    layers, taps, outs, ins = conv_weight.shape
+    one = jax.ShapeDtypeStruct((3 * outs, 9 * ins), conv_weight.dtype)
+    results = pl.pallas_call(
         weights_kernel,
-        out_shape=(laid_shape(conv_weight), jax.ShapeDtypeStruct((layers, 2, outs, LANES), jnp.float32)),
+        out_shape=(one,) * layers + (jax.ShapeDtypeStruct((layers, 2, outs, LANES), jnp.float32),),
         in_specs=[ANY, VMEM],
-        out_specs=(VMEM, VMEM),
-        scratch_shapes=held(conv_weight),
-        compiler_params=pltpu.CompilerParams(vmem_limit_bytes=LIMIT),
-        cost_estimate=pl.CostEstimate(flops=0, bytes_accessed=4 * conv_weight.size // layers, transcendentals=0),
+        out_specs=(VMEM,) * (layers + 1),
+        scratch_shapes=[
+            pltpu.VMEM((3 * layers, taps // 3, outs, ins), conv_weight.dtype),
+            pltpu.SemaphoreType.DMA((3 * layers,)),
+        ],
+        compiler_params=pltpu.CompilerParams(vmem_limit_bytes=LARGE),
+        cost_estimate=pl.CostEstimate(flops=0, bytes_accessed=4 * conv_weight.size, transcendentals=0),
         name="weights",
     )(conv_weight, rows)
+    return results[:-1], results[-1]
 
 
 def split_kernel(in_ref, *out_refs):
@@ -246,11 +235,6 @@
     last, sends, rest, rest_sent = plan["last"], plan["sends"], plan["rest"], plan["rest_sent"]
     refs = list(refs)
     earlier_refs = [refs.pop(0) for _ in range(plan["inputs"])]
-    if plan["fetches"]:
-        next_ref, sems, held_ref = refs.pop(0), refs.pop(), refs.pop()
-        copies = fetches(layer + 1, next_ref, held_ref, sems)
-        for copy in copies:
-            copy.start()
     earlier_ref = refs.pop() if received else earlier_refs[0]
     if received:
         for t in range(PAIR):
@@ -264,8 +248,6 @@
                 act = earlier_refs[0][t]
             spread(earlier_ref, t, act, pitch)
     outs = refs
-    if plan["fetches"]:
-        laid_ref = outs.pop()
     if plan["builds"]:
         earlier_ref = outs.pop()
         add_far(pitch - 1 - half, *earlier_refs, columns_ref, outs.pop(), earlier_ref)
@@ -343,13 +325,11 @@
         while finished < PAIR and (finished + 1) * chunks <= n + side:
             finish(finished)
             finished += 1
-    if plan["fetches"]:
-        laid_out(copies, held_ref, laid_ref)
     if sends and rest_sent:
         outs[2][:, PAIR * (chunks - 1) * LANES :] = sum(tails).astype(jnp.bfloat16)
 
 
-def conv(plan, earlier, shifted, values, weight, columns, conv_weight):
+def conv(plan, earlier, shifted, values, weight, columns):
     _, _, channels, lanes = shifted.shape
     pitch, half, received = plan["pitch"], plan["half"], plan["received"]
     if plan["last"]:
@@ -364,17 +344,12 @@
         elif plan["sends"]:
             out_shape += out_shape[:1]
     scratch = [pltpu.VMEM((PAIR, 3, channels, lanes), jnp.bfloat16)] * received
-    extra = ()
     if plan["builds"]:
         out_shape += far_shapes(earlier[0].shape[1], pitch - 1 - half, channels, half)
-    if plan["fetches"]:
-        extra = (conv_weight,)
-        out_shape += (laid_shape(conv_weight),)
-        scratch += held(conv_weight)
     return pl.pallas_call(
         functools.partial(conv_kernel, plan),
         out_shape=out_shape,
-        in_specs=[VMEM] * (4 + len(earlier)) + [ANY] * len(extra),
+        in_specs=[VMEM] * (4 + len(earlier)),
         out_specs=(VMEM,) * len(out_shape),
         scratch_shapes=scratch,
         compiler_params=pltpu.CompilerParams(vmem_limit_bytes=LIMIT),
@@ -384,7 +359,7 @@
             transcendentals=PAIR * channels * lanes,
         ),
         name=f"conv_{plan['layer']}",
-    )(shifted, values, weight, columns, *earlier, *extra)
+    )(shifted, values, weight, columns, *earlier)
 
 
 def join_kernel(pair, kept_ref, got_ref, *refs):
@@ -467,15 +442,12 @@
                 "received": p == 0,
                 "rest": 0 if p else rest,
                 "builds": builds,
-                "fetches": p == 0 and not last,
                 "inputs": len(earlier),
                 "pitch": pitch,
                 "half": half,
                 "rows": rows_left,
             }
-            outs = list(conv(plan, earlier, shifted[p], values[p], weight, columns, conv_weight))
-            if plan["fetches"]:
-                next_weight = outs.pop()
+            outs = list(conv(plan, earlier, shifted[p], values[p], weight[layer], columns))
             if builds:
                 shifted[p - 1], values[p - 1] = outs.pop(), outs.pop()
             results[p] = outs
@@ -483,7 +455,7 @@
                 arriving = earlier_of(outs[2])
         values, shifted = [r[0] for r in results], [r[1] for r in results]
         if not last:
-            halo, rest, weight = arriving, joined(rows_left * pitch), next_weight
+            halo, rest = arriving, joined(rows_left * pitch)
     result = ()
     for p in reversed(range(pairs)):
         result = (join(p, values[p], mate_of(shifted[p]), latents.shape, *result),)

time: 46.6 us -> 45 us (0.966)
  Pallas kernels: 22.3 us -> 21.4 us
  waiting for transfers between devices: 6.03 us -> 5.49 us
    pallas_call x6, Pallas kernels: 17.6 us -> 15.1 us  [conv(): pl.pallas_call(functools.partial(conv_kernel, plan), out_shape=out_shape,...]
    pallas_call x1, Pallas kernels: 1.89 us -> 3.54 us  [weights(): pl.pallas_call(weights_kernel, out_shape=(one,) * layers + (jax.ShapeDtyp...]
    ppermute x2, waiting for transfers between devices: 3.83 us -> 2.19 us  [beyond_of(): return lax.ppermute(block, 'rows', [(i, i ^ 2) for i in range(strips)])]
    ppermute x3, waiting for transfers between devices: 0.39 us -> 1.4 us  [earlier_of(): return lax.ppermute(block, 'tm', [(i, i + 1) for i in range(blocks - 1)])]
where the time goes in v6:
time: 45 us; the launch traced here: 44.8 us
  Pallas kernels  21.4 us (48%)
  starting transfers between devices  15.8 us (35%)
  waiting for transfers between devices  5.49 us (12%)
  local copies, waits for them, and re-layouts  1 us (2%)
  other arithmetic  0.71 us (2%)
    pallas_call x6, Pallas kernels, conv(): pl.pallas_call(functools.partial(conv_kernel, plan), out_shape=out_shape,...  15.1 us
    ppermute x3, starting transfers between devices, earlier_of(): return lax.ppermute(block, 'tm', [(i, i + 1) for i in range(blocks - 1)])  10.9 us
    ppermute x2, starting transfers between devices, beyond_of(): return lax.ppermute(block, 'rows', [(i, i ^ 2) for i in range(strips)])  4.29 us
    pallas_call x1, Pallas kernels, weights(): pl.pallas_call(weights_kernel, out_shape=(one,) * layers + (jax.ShapeDtyp...  3.54 us
    ppermute x2, waiting for transfers between devices, beyond_of(): return lax.ppermute(block, 'rows', [(i, i ^ 2) for i in range(strips)])  2.19 us
    ppermute x5, waiting for transfers between devices, mate_of(): return lax.ppermute(block, 'rows', [(i, i ^ 1) for i in range(strips)])  1.9 us
    pallas_call x2, Pallas kernels, join(): pl.pallas_call(functools.partial(join_kernel, pair), out_shape=jax.ShapeD...  1.63 us
    ppermute x3, waiting for transfers between devices, earlier_of(): return lax.ppermute(block, 'tm', [(i, i + 1) for i in range(blocks - 1)])  1.4 us
  transfers between devices with their start and end apart: 10, of which 5 were waited for; matrix products, arithmetic and copies ran while one was open for 2% of the time, Pallas kernels for 46%

profile of v6, /device:TPU:0, one launch (start us, length us, event | category | flops | bytes accessed | tf_op | source)
XLA Modules:
  0.0 44.8 jit_solution(2632777106186271967)
XLA Ops:
  0.0 0.5 %collective-permute-start.1 = (bf16[4,2,192,128]{3,2,1,0:T(8,128)(2,1)}, bf16[4,2,192,128]{3,2,1,0:T(8,128)(2,1)S(1)}, u32[]{:S(2)}, u32[]{:S(2)}) collective-permute-start(bf16[4,2,192,128]{3,2,1,0:T(8,128)(2,1)} %in_ref.1), channel_id=1, source_target_pairs={{0,1},{1,0},{2,3},{3,2},{4,5},{5,4},{6,7},{7,6},{8,9},{9,8},{10,11... | collective-permute-start | bytes 1179656 | tf_op jit(solution)/shard_map/ppermute | solution.py:406
  0.5 1.0 %copy-done = bf16[4,2,192,128]{3,2,1,0:T(8,128)(2,1)S(1)} copy-done((bf16[4,2,192,128]{3,2,1,0:T(8,128)(2,1)S(1)}, bf16[4,2,192,128]{3,2,1,0:T(8,128)(2,1)}, u32[]{:S(2)}) %copy-start) | copy-done | bytes 393240
  1.5 2.6 %collective-permute-start = (bf16[2,2,192,128]{3,2,1,0:T(8,128)(2,1)S(1)}, bf16[2,2,192,128]{3,2,1,0:T(8,128)(2,1)S(1)}, u32[]{:S(2)}, u32[]{:S(2)}) collective-permute-start(bf16[2,2,192,128]{3,2,1,0:T(8,128)(2,1)S(1)} %get-tuple-element.43.refs_1_), channel_id=1, source_target_pairs={{0,2},{1,3},{2,0},{3,1},{4,6},{5,7},{6,4},{7,5},{8,10},{9,11},{10,... | collective-permute-start | bytes 589832 | tf_op jit(solution)/shard_map/ppermute | solution.py:412
  4.0 0.7 %pad_maximum_fusion.rows_ref.gains_ref = f32[6,192]{1,0:T(8,128)S(1)} fusion(f32[3,192]{1,0:T(4,128)} %param.7, f32[3,192]{1,0:T(4,128)} %param.6), kind=kLoop, calls=%fused_computation | loop fusion | flops 1152 | bytes 9216 | tf_op jit(solution)/shard_map/concatenate | solution.py:418
  4.7 3.5 %weights.1 = (bf16[576,1728]{1,0:T(8,128)(2,1)S(1)}, bf16[576,1728]{1,0:T(8,128)(2,1)S(1)}, bf16[576,1728]{1,0:T(8,128)(2,1)S(1)}, f32[3,2,192,128]{3,2,1,0:T(8,128)S(1)}) custom-call(bf16[3,27,192,192]{3,2,1,0:T(8,128)(2,1)} %w_ref.1, f32[6,192]{1,0:T(8,128)S(1)} %pad_maximum_fusion.rows_ref.gains_ref), custom_call_target="tpu_custom_call" | custom-call | bytes 11943936 | tf_op jit(solution)/shard_map/weights/pallas_call | solution.py:77
  8.3 0.0 collective-permute-done.1.mate_ref
  8.3 0.6 %near.1 = (bf16[2,192,384]{2,1,0:T(8,128)(2,1)S(1)}, bf16[2,192,384]{2,1,0:T(8,128)(2,1)S(1)}, bf16[2,192,256]{2,1,0:T(8,128)(2,1)S(1)}, bf16[2,192,256]{2,1,0:T(8,128)(2,1)S(1)}) custom-call(bf16[4,2,192,128]{3,2,1,0:T(8,128)(2,1)S(1)} %collective-permute-done.1.mate_ref, f32[6,192]{1,0:T(8,128)S(1)} %pad_maximum_fusion.rows_ref.gains_ref, ...), custom_call_target="tpu_custom_call" | custom-call | flops 7864320 | bytes 1572864 | tf_op jit(solution)/shard_map/near/pallas_call | solution.py:166
  8.9 0.7 %collective-permute-done.far_ref = bf16[2,2,192,128]{3,2,1,0:T(8,128)(2,1)S(1)} collective-permute-done((bf16[2,2,192,128]{3,2,1,0:T(8,128)(2,1)S(1)}, bf16[2,2,192,128]{3,2,1,0:T(8,128)(2,1)S(1)}, u32[]{:S(2)}, u32[]{:S(2)}) %collective-permute-start) | collective-permute-done | bytes 196640 | tf_op jit(solution)/shard_map/ppermute | solution.py:412
  9.6 0.0 collective-permute-start.2
  9.6 1.7 %collective-permute-start.3 = (bf16[2,2,192,128]{3,2,1,0:T(8,128)(2,1)S(1)}, bf16[2,2,192,128]{3,2,1,0:T(8,128)(2,1)S(1)}, u32[]{:S(2)}, u32[]{:S(2)}) collective-permute-start(bf16[2,2,192,128]{3,2,1,0:T(8,128)(2,1)S(1)} %get-tuple-element.48.refs_0_), channel_id=1, source_target_pairs={{0,2},{1,3},{2,0},{3,1},{4,6},{5,7},{6,4},{7,5},{8,10},{9,11},{10,... | collective-permute-start | bytes 589832 | tf_op jit(solution)/shard_map/ppermute | solution.py:412
  11.4 0.0 collective-permute-done.2.mate_ref
  11.4 0.5 %beyond.1 = (bf16[2,192,512]{2,1,0:T(8,128)(2,1)S(1)}, bf16[2,3,192,512]{3,2,1,0:T(8,128)(2,1)S(1)}, bf16[2,192,512]{2,1,0:T(8,128)(2,1)S(1)}) custom-call(f32[3,2,192,128]{3,2,1,0:T(8,128)S(1)} %get-tuple-element.53.columns_ref, bf16[2,2,192,128]{3,2,1,0:T(8,128)(2,1)S(1)} %collective-permute-done.far_ref, ...), custom_call_target="tpu_custom_call" | custom-call | flops 3932160 | bytes 786432 | tf_op jit(solution)/shard_map/beyond/pallas_call | solution.py:222
  11.9 3.5 %collective-permute-start.5 = (bf16[2,192,512]{2,1,0:T(8,128)(2,1)S(1)}, bf16[2,192,512]{2,1,0:T(8,128)(2,1)S(1)}, u32[]{:S(2)}, u32[]{:S(2)}) collective-permute-start(bf16[2,192,512]{2,1,0:T(8,128)(2,1)S(1)} %get-tuple-element.64), channel_id=1, source_target_pairs={{0,4},{4,8},{8,12},{1,5},{5,9},{9,13},{2,6},{6,10},{10,14},{3,7},{... | collective-permute-start | bytes 1179656 | tf_op jit(solution)/shard_map/ppermute | solution.py:409
  15.4 1.5 %collective-permute-done.3.refs_0_ = bf16[2,2,192,128]{3,2,1,0:T(8,128)(2,1)S(1)} collective-permute-done((bf16[2,2,192,128]{3,2,1,0:T(8,128)(2,1)S(1)}, bf16[2,2,192,128]{3,2,1,0:T(8,128)(2,1)S(1)}, u32[]{:S(2)}, u32[]{:S(2)}) %collective-permute-start.3) | collective-permute-done | bytes 196640 | tf_op jit(solution)/shard_map/ppermute | solution.py:412
  16.9 0.0 collective-permute-start.4
  16.9 1.4 %collective-permute-done.4.refs_1_ = bf16[2,2,192,128]{3,2,1,0:T(8,128)(2,1)S(1)} collective-permute-done((bf16[2,2,192,128]{3,2,1,0:T(8,128)(2,1)S(1)}, bf16[2,2,192,128]{3,2,1,0:T(8,128)(2,1)S(1)}, u32[]{:S(2)}, u32[]{:S(2)}) %collective-permute-start.4) | collective-permute-done | bytes 196640 | tf_op jit(solution)/shard_map/ppermute | solution.py:406
  18.4 3.0 %conv_0.2 = (bf16[2,192,512]{2,1,0:T(8,128)(2,1)S(1)}, bf16[2,3,192,384]{3,2,1,0:T(8,128)(2,1)S(1)}, bf16[192,896]{1,0:T(8,128)(2,1)S(1)}, bf16[2,192,512]{2,1,0:T(8,128)(2,1)S(1)}, bf16[2,3,192,512]{3,2,1,0:T(8,128)(2,1)S(1)}) custom-call(bf16[2,3,192,512]{3,2,1,0:T(8,128)(2,1)S(1)} %get-tuple-element.57.shifted_ref, ...), custom_call_target="tpu_custom_call" | custom-call | flops 2038431744 | bytes 1990656 | tf_op jit(solution)/shard_map/conv_0/pallas_call | solution.py:349
  21.4 3.8 %collective-permute-start.6 = (bf16[192,896]{1,0:T(8,128)(2,1)S(1)}, bf16[192,896]{1,0:T(8,128)(2,1)S(1)}, u32[]{:S(2)}, u32[]{:S(2)}) collective-permute-start(bf16[192,896]{1,0:T(8,128)(2,1)S(1)} %get-tuple-element.68), channel_id=1, source_target_pairs={{0,4},{4,8},{8,12},{1,5},{5,9},{9,13},{2,6},{6,10},{10,14},{3,7},{... | collective-permute-start | bytes 1032200 | tf_op jit(solution)/shard_map/ppermute | solution.py:409
  25.2 0.0 collective-permute-done.5.refs_0_
  25.2 2.9 %conv_0.3 = (bf16[2,192,512]{2,1,0:T(8,128)(2,1)S(1)}, bf16[2,3,192,384]{3,2,1,0:T(8,128)(2,1)S(1)}) custom-call(bf16[2,3,192,512]{3,2,1,0:T(8,128)(2,1)S(1)} %get-tuple-element.62.shifted_ref, bf16[2,192,512]{2,1,0:T(8,128)(2,1)S(1)} %get-tuple-element.63.values_ref, bf16[576,1728]{1,0:T(8,128)(2,1)S(1)} %get-tuple-element.59.w_ref, ...), custom_call_target="tpu_custom_call" | custom-call | flops 2038431744 | bytes 1990656 | tf_op jit(solution)/shard_map/conv_0/pallas_call | solution.py:349
  28.1 2.3 %conv_1.3 = (bf16[2,192,384]{2,1,0:T(8,128)(2,1)S(1)}, bf16[2,3,192,384]{3,2,1,0:T(8,128)(2,1)S(1)}, bf16[2,192,384]{2,1,0:T(8,128)(2,1)S(1)}) custom-call(bf16[2,3,192,384]{3,2,1,0:T(8,128)(2,1)S(1)} %get-tuple-element.72.shifted_ref, bf16[2,192,512]{2,1,0:T(8,128)(2,1)S(1)} %get-tuple-element.73.values_ref, bf16[576,1728]{1,0:T(8,128)(2,1)S(1)} %get-tuple-element.67.w_ref, ...), custom_call_target="tpu_custom_call" | custom-call | flops 1528823808 | bytes 1990656 | tf_op jit(solution)/shard_map/conv_1/pallas_call | solution.py:349
  30.3 3.7 %collective-permute-start.7 = (bf16[2,192,384]{2,1,0:T(8,128)(2,1)S(1)}, bf16[2,192,384]{2,1,0:T(8,128)(2,1)S(1)}, u32[]{:S(2)}, u32[]{:S(2)}) collective-permute-start(bf16[2,192,384]{2,1,0:T(8,128)(2,1)S(1)} %get-tuple-element.74), channel_id=1, source_target_pairs={{0,4},{4,8},{8,12},{1,5},{5,9},{9,13},{2,6},{6,10},{10,14},{3,7},{... | collective-permute-start | bytes 884744 | tf_op jit(solution)/shard_map/ppermute | solution.py:409
  34.0 2.4 %conv_1.2 = (bf16[2,192,384]{2,1,0:T(8,128)(2,1)S(1)}, bf16[2,3,192,384]{3,2,1,0:T(8,128)(2,1)S(1)}) custom-call(bf16[2,3,192,384]{3,2,1,0:T(8,128)(2,1)S(1)} %get-tuple-element.65.shifted_ref.refs_0_, bf16[2,192,512]{2,1,0:T(8,128)(2,1)S(1)} %get-tuple-element.66.values_ref, bf16[576,1728]{1,0:T(8,128)(2,1)S(1)} %get-tuple-element.67.w_ref, ...), custom_call_target="tpu_custom_call" | custom-call | flops 1528823808 | bytes 1990656 | tf_op jit(solution)/shard_map/conv_1/pallas_call | solution.py:349
  36.4 2.2 %conv_2.3 = (bf16[2,192,128]{2,1,0:T(8,128)(2,1)S(1)}, bf16[2,192,128]{2,1,0:T(8,128)(2,1)S(1)}) custom-call(bf16[2,3,192,384]{3,2,1,0:T(8,128)(2,1)S(1)} %get-tuple-element.77.shifted_ref, bf16[2,192,384]{2,1,0:T(8,128)(2,1)S(1)} %get-tuple-element.78.values_ref, bf16[576,1728]{1,0:T(8,128)(2,1)S(1)} %get-tuple-element.71.w_ref, ...), custom_call_target="tpu_custom_call" | custom-call | flops 1528823808 | bytes 1990656 | tf_op jit(solution)/shard_map/conv_2/pallas_call | solution.py:349
  38.6 0.1 collective-permute-start.9
  38.7 1.4 %collective-permute-done.7.refs_0_ = bf16[2,192,384]{2,1,0:T(8,128)(2,1)S(1)} collective-permute-done((bf16[2,192,384]{2,1,0:T(8,128)(2,1)S(1)}, bf16[2,192,384]{2,1,0:T(8,128)(2,1)S(1)}, u32[]{:S(2)}, u32[]{:S(2)}) %collective-permute-start.7) | collective-permute-done | bytes 294944 | tf_op jit(solution)/shard_map/ppermute | solution.py:409
  40.1 2.3 %conv_2.2 = (bf16[2,192,128]{2,1,0:T(8,128)(2,1)S(1)}, bf16[2,192,128]{2,1,0:T(8,128)(2,1)S(1)}) custom-call(bf16[2,3,192,384]{3,2,1,0:T(8,128)(2,1)S(1)} %get-tuple-element.69.shifted_ref.refs_0_, bf16[2,192,384]{2,1,0:T(8,128)(2,1)S(1)} %get-tuple-element.70.values_ref, bf16[576,1728]{1,0:T(8,128)(2,1)S(1)} %get-tuple-element.71.w_ref, ...), custom_call_target="tpu_custom_call" | custom-call | flops 1528823808 | bytes 1990656 | tf_op jit(solution)/shard_map/conv_2/pallas_call | solution.py:349
  42.4 0.1 collective-permute-start.8
  42.5 0.0 collective-permute-done.9.got_ref
  42.5 0.8 %join.2.refs_0_ = bf16[4,2,192,128]{3,2,1,0:T(8,128)(2,1)} custom-call(bf16[2,192,128]{2,1,0:T(8,128)(2,1)S(1)} %get-tuple-element.79.kept_ref, bf16[2,192,128]{2,1,0:T(8,128)(2,1)S(1)} %collective-permute-done.9.got_ref), custom_call_target="tpu_custom_call" | custom-call | tf_op jit(solution)/shard_map/join/pallas_call | solution.py:387
  43.3 0.5 %collective-permute-done.8.got_ref = bf16[2,192,128]{2,1,0:T(8,128)(2,1)S(1)} collective-permute-done((bf16[2,192,128]{2,1,0:T(8,128)(2,1)S(1)}, bf16[2,192,128]{2,1,0:T(8,128)(2,1)S(1)}, u32[]{:S(2)}, u32[]{:S(2)}) %collective-permute-start.8) | collective-permute-done | bytes 98336 | tf_op jit(solution)/shard_map/ppermute | solution.py:406
  43.8 0.8 %join.3 = bf16[4,2,192,128]{3,2,1,0:T(8,128)(2,1)} custom-call(bf16[2,192,128]{2,1,0:T(8,128)(2,1)S(1)} %get-tuple-element.75.kept_ref, bf16[2,192,128]{2,1,0:T(8,128)(2,1)S(1)} %collective-permute-done.8.got_ref, bf16[4,2,192,128]{3,2,1,0:T(8,128)(2,1)} %join.2.refs_0_), custom_call_target="tpu_custom_call", output_to_operand_aliasing={{}: (2, {})} | custom-call | tf_op jit(solution)/shard_map/join/pallas_call | solution.py:387
  (3 shorter events, 0.0 us)
Async XLA Ops:
  0.0 8.3 %collective-permute-start.1 = (bf16[4,2,192,128]{3,2,1,0:T(8,128)(2,1)}, bf16[4,2,192,128]{3,2,1,0:T(8,128)(2,1)S(1)}, u32[]{:S(2)}, u32[]{:S(2)}) collective-permute-start(bf16[4,2,192,128]{3,2,1,0:T(8,128)(2,1)} %in_ref.1), channel_id=1, source_target_pairs={{0,1},{1,0},{2,3},{3,2},{4,5},{5,4},{6,7},{7,6},{8,9},{9,8},{10,11... | collective-permute-start | bytes 1179656 | tf_op jit(solution)/shard_map/ppermute | solution.py:406
  0.5 1.0 %copy-start = (bf16[4,2,192,128]{3,2,1,0:T(8,128)(2,1)S(1)}, bf16[4,2,192,128]{3,2,1,0:T(8,128)(2,1)}, u32[]{:S(2)}) copy-start(bf16[4,2,192,128]{3,2,1,0:T(8,128)(2,1)} %in_ref.1) | copy-start | bytes 1179652
  1.5 8.1 %collective-permute-start = (bf16[2,2,192,128]{3,2,1,0:T(8,128)(2,1)S(1)}, bf16[2,2,192,128]{3,2,1,0:T(8,128)(2,1)S(1)}, u32[]{:S(2)}, u32[]{:S(2)}) collective-permute-start(bf16[2,2,192,128]{3,2,1,0:T(8,128)(2,1)S(1)} %get-tuple-element.43.refs_1_), channel_id=1, source_target_pairs={{0,2},{1,3},{2,0},{3,1},{4,6},{5,7},{6,4},{7,5},{8,10},{9,11},{10,... | collective-permute-start | bytes 589832 | tf_op jit(solution)/shard_map/ppermute | solution.py:412
  9.6 1.7 %collective-permute-start.2 = (bf16[2,2,192,128]{3,2,1,0:T(8,128)(2,1)S(1)}, bf16[2,2,192,128]{3,2,1,0:T(8,128)(2,1)S(1)}, u32[]{:S(2)}, u32[]{:S(2)}) collective-permute-start(bf16[2,2,192,128]{3,2,1,0:T(8,128)(2,1)S(1)} %collective-permute-done.far_ref), channel_id=1, source_target_pairs={{0,1},{1,0},{2,3},{3,2},{4,5},{5,4},{6,7},{7,6},{8,9},{9,8},{10,11... | collective-permute-start | bytes 589832 | tf_op jit(solution)/shard_map/ppermute | solution.py:406
  9.6 7.3 %collective-permute-start.3 = (bf16[2,2,192,128]{3,2,1,0:T(8,128)(2,1)S(1)}, bf16[2,2,192,128]{3,2,1,0:T(8,128)(2,1)S(1)}, u32[]{:S(2)}, u32[]{:S(2)}) collective-permute-start(bf16[2,2,192,128]{3,2,1,0:T(8,128)(2,1)S(1)} %get-tuple-element.48.refs_0_), channel_id=1, source_target_pairs={{0,2},{1,3},{2,0},{3,1},{4,6},{5,7},{6,4},{7,5},{8,10},{9,11},{10,... | collective-permute-start | bytes 589832 | tf_op jit(solution)/shard_map/ppermute | solution.py:412
  11.9 13.3 %collective-permute-start.5 = (bf16[2,192,512]{2,1,0:T(8,128)(2,1)S(1)}, bf16[2,192,512]{2,1,0:T(8,128)(2,1)S(1)}, u32[]{:S(2)}, u32[]{:S(2)}) collective-permute-start(bf16[2,192,512]{2,1,0:T(8,128)(2,1)S(1)} %get-tuple-element.64), channel_id=1, source_target_pairs={{0,4},{4,8},{8,12},{1,5},{5,9},{9,13},{2,6},{6,10},{10,14},{3,7},{... | collective-permute-start | bytes 1179656 | tf_op jit(solution)/shard_map/ppermute | solution.py:409
  16.9 1.4 %collective-permute-start.4 = (bf16[2,2,192,128]{3,2,1,0:T(8,128)(2,1)S(1)}, bf16[2,2,192,128]{3,2,1,0:T(8,128)(2,1)S(1)}, u32[]{:S(2)}, u32[]{:S(2)}) collective-permute-start(bf16[2,2,192,128]{3,2,1,0:T(8,128)(2,1)S(1)} %collective-permute-done.3.refs_0_), channel_id=1, source_target_pairs={{0,1},{1,0},{2,3},{3,2},{4,5},{5,4},{6,7},{7,6},{8,9},{9,8},{10,11... | collective-permute-start | bytes 589832 | tf_op jit(solution)/shard_map/ppermute | solution.py:406
  21.4 12.6 %collective-permute-start.6 = (bf16[192,896]{1,0:T(8,128)(2,1)S(1)}, bf16[192,896]{1,0:T(8,128)(2,1)S(1)}, u32[]{:S(2)}, u32[]{:S(2)}) collective-permute-start(bf16[192,896]{1,0:T(8,128)(2,1)S(1)} %get-tuple-element.68), channel_id=1, source_target_pairs={{0,4},{4,8},{8,12},{1,5},{5,9},{9,13},{2,6},{6,10},{10,14},{3,7},{... | collective-permute-start | bytes 1032200 | tf_op jit(solution)/shard_map/ppermute | solution.py:409
  30.3 9.7 %collective-permute-start.7 = (bf16[2,192,384]{2,1,0:T(8,128)(2,1)S(1)}, bf16[2,192,384]{2,1,0:T(8,128)(2,1)S(1)}, u32[]{:S(2)}, u32[]{:S(2)}) collective-permute-start(bf16[2,192,384]{2,1,0:T(8,128)(2,1)S(1)} %get-tuple-element.74), channel_id=1, source_target_pairs={{0,4},{4,8},{8,12},{1,5},{5,9},{9,13},{2,6},{6,10},{10,14},{3,7},{... | collective-permute-start | bytes 884744 | tf_op jit(solution)/shard_map/ppermute | solution.py:409
  38.6 3.9 %collective-permute-start.9 = (bf16[2,192,128]{2,1,0:T(8,128)(2,1)S(1)}, bf16[2,192,128]{2,1,0:T(8,128)(2,1)S(1)}, u32[]{:S(2)}, u32[]{:S(2)}) collective-permute-start(bf16[2,192,128]{2,1,0:T(8,128)(2,1)S(1)} %get-tuple-element.80), channel_id=1, source_target_pairs={{0,1},{1,0},{2,3},{3,2},{4,5},{5,4},{6,7},{7,6},{8,9},{9,8},{10,11... | collective-permute-start | bytes 294920 | tf_op jit(solution)/shard_map/ppermute | solution.py:406
  42.4 1.4 %collective-permute-start.8 = (bf16[2,192,128]{2,1,0:T(8,128)(2,1)S(1)}, bf16[2,192,128]{2,1,0:T(8,128)(2,1)S(1)}, u32[]{:S(2)}, u32[]{:S(2)}) collective-permute-start(bf16[2,192,128]{2,1,0:T(8,128)(2,1)S(1)} %get-tuple-element.76), channel_id=1, source_target_pairs={{0,1},{1,0},{2,3},{3,2},{4,5},{5,4},{6,7},{7,6},{8,9},{9,8},{10,11... | collective-permute-start | bytes 294920 | tf_op jit(solution)/shard_map/ppermute | solution.py:406

commit v7 on v6

--- a/solution.py
+++ b/solution.py
@@ -67,7 +67,7 @@
         copies[n].wait()
         for row_tap in range(3):
             source = 3 * (row_tap + flipped * (2 - 2 * row_tap))
-            at = (3 * time_tap + row_tap) * ins
+            at = (3 * (2 - time_tap) + row_tap) * ins
             outs[layer][:, at : at + ins] = held_ref[n, pl.ds(source, 3)].reshape(3 * channels_out, ins)
 
 
@@ -230,10 +230,58 @@
     )(columns, *parts)
 
 
+def lines_of(ref, frame):
+    return ref[frame].reshape(3 * ref.shape[2], ref.shape[3])
+
+
+def by_taps(sums):
+    channels, lanes = sums.shape[0] // 3, sums.shape[1]
+    return [
+        [sums[tap * channels : (tap + 1) * channels, at : at + LANES] for at in range(0, lanes, LANES)]
+        for tap in range(3)
+    ]
+
+
+def column_sums(taps):
+    lane = lane_of(LANES)
+    left, middle, right = taps
+    lefts = [pltpu.roll(block, 1, 1) for block in left]
+    rights = [pltpu.roll(block, LANES - 1, 1) for block in right] + [0.0]
+    return [
+        jnp.where(lane == 0, lefts[b - 1] if b else 0.0, lefts[b])
+        + middle[b]
+        + jnp.where(lane == LANES - 1, rights[b + 1], rights[b])
+        for b in range(len(middle))
+    ]
+
+
+def begin_kernel(shifted_ref, w_ref, out_ref):
+    depth = 3 * shifted_ref.shape[2]
+    for t in range(PAIR):
+        rhs = jnp.concatenate([lines_of(shifted_ref, j) for j in range(t, -1, -1)], axis=0)
+        sums = jnp.dot(w_ref[:, : (t + 1) * depth], rhs, preferred_element_type=jnp.float32)
+        for b, block in enumerate(column_sums(by_taps(sums))):
+            out_ref[t, :, b * LANES : (b + 1) * LANES] = block
+
+
+def begin(shifted, weight):
+    _, _, channels, lanes = shifted.shape
+    return pl.pallas_call(
+        begin_kernel,
+        out_shape=jax.ShapeDtypeStruct((PAIR, channels, lanes), jnp.float32),
+        in_specs=[VMEM] * 2,
+        out_specs=VMEM,
+        compiler_params=pltpu.CompilerParams(vmem_limit_bytes=LIMIT),
+        cost_estimate=pl.CostEstimate(flops=0, bytes_accessed=0, transcendentals=0),
+        name="begin",
+    )(shifted, weight)
+
+
 def conv_kernel(plan, shifted_ref, values_ref, w_ref, columns_ref, *refs):
     layer, pitch, half, received = plan["layer"], plan["pitch"], plan["half"], plan["received"]
     last, sends, rest, rest_sent = plan["last"], plan["sends"], plan["rest"], plan["rest_sent"]
     refs = list(refs)
+    begun_ref = refs.pop(0) if plan["begun"] else None
     earlier_refs = [refs.pop(0) for _ in range(plan["inputs"])]
     earlier_ref = refs.pop() if received else earlier_refs[0]
     if received:
@@ -256,50 +304,37 @@
     lane = lane_of(LANES)
 
     def window(t, b):
-        taken = [(earlier_ref, t + a) if t + a < PAIR else (shifted_ref, t + a - PAIR) for a in range(3)]
+        taken = [(earlier_ref, t + a) if t + a < PAIR else (shifted_ref, t + a - PAIR) for a in (2, 1, 0)]
         at = slice(b * LANES, (b + 1) * LANES)
         return jnp.concatenate([ref[j, :, :, at].reshape(3 * channels, LANES) for ref, j in taken], axis=0)
 
-    places = [(t, b) for t in range(PAIR) for b in range(chunks)]
-    side = TILE // LANES
-    tiles = []
     bias = columns_ref[layer, 1]
+    tails = []
     if not last:
         mask = filled(lanes, pitch)
         gain = columns_ref[layer + 1, 0]
 
-    def sums(t, tap, b):
-        tile, at = divmod((t * chunks + b) * LANES, TILE)
-        return tiles[tile][tap * channels : (tap + 1) * channels, at : at + LANES]
-
-    tails = []
-
-    def finish(t):
+    def finish(t, taps):
         totals, acts = [], []
-        from_left = 0.0
-        from_right = pltpu.roll(sums(t, 2, 0), LANES - 1, 1)
-        for b in range(chunks):
+        for b, conv in enumerate(column_sums(taps)):
             at = slice(b * LANES, (b + 1) * LANES)
-            left = pltpu.roll(sums(t, 0, b), 1, 1)
-            right = pltpu.roll(sums(t, 2, b + 1), LANES - 1, 1) if b + 1 < chunks else 0.0
-            summed = (
-                jnp.where(lane == 0, from_left, left) + sums(t, 1, b) + jnp.where(lane == LANES - 1, right, from_right)
-            )
-            from_left, from_right = left, right
-            total = (values_ref[t, :, at].astype(jnp.float32) + summed + bias).astype(jnp.bfloat16)
+            if begun_ref is not None:
+                conv = conv + begun_ref[t, :, at]
+            total = (values_ref[t, :, at].astype(jnp.float32) + conv + bias).astype(jnp.bfloat16)
             totals.append(total.astype(jnp.float32))
-            if not last:
-                outs[0][t, :, at] = total
-                acts.append(activated(totals[-1], gain, mask[:, at]))
-                if not sends:
-                    continue
-                if not rest_sent:
-                    outs[2][t, :, at] = acts[-1]
-                elif b < chunks - 1:
-                    outs[2][:, (t * (chunks - 1) + b) * LANES : (t * (chunks - 1) + b + 1) * LANES] = acts[-1]
-                else:
-                    tail = jnp.where(lane < rest_sent, acts[-1].astype(jnp.float32), 0.0)
-                    tails.append(tail if t == 0 else pltpu.roll(tail, t * (LANES // PAIR), 1))
+            if last:
+                continue
+            outs[0][t, :, at] = total
+            acts.append(activated(totals[-1], gain, mask[:, at]))
+            if not sends:
+                continue
+            if not rest_sent:
+                outs[2][t, :, at] = acts[-1]
+            elif b < chunks - 1:
+                outs[2][:, (t * (chunks - 1) + b) * LANES : (t * (chunks - 1) + b + 1) * LANES] = acts[-1]
+            else:
+                tail = jnp.where(lane < rest_sent, acts[-1].astype(jnp.float32), 0.0)
+                tails.append(tail if t == 0 else pltpu.roll(tail, t * (LANES // PAIR), 1))
         if not last:
             spread(outs[1], t, jnp.concatenate(acts, axis=1), pitch)
             return
@@ -318,18 +353,35 @@
         outs[0][t] = jnp.where(outer, outermost, inner).astype(jnp.bfloat16)
         outs[1][t] = jnp.where(outer, inner, outermost).astype(jnp.bfloat16)
 
-    finished = 0
-    for n in range(0, len(places), side):
-        rhs = jnp.concatenate([window(t, b) for t, b in places[n : n + side]], axis=1)
-        tiles.append(jnp.dot(w_ref[...], rhs, preferred_element_type=jnp.float32))
-        while finished < PAIR and (finished + 1) * chunks <= n + side:
-            finish(finished)
-            finished += 1
+    if plan["begun"]:
+        depth = 3 * channels
+        for t in range(PAIR):
+            at = (t + 1) * depth
+            lead = at % LANES
+            lines = [lines_of(earlier_ref, j) for j in range(PAIR - 1, t - 1, -1)]
+            if lead:
+                lines.insert(0, jnp.zeros((lead, lanes), jnp.bfloat16))
+            sums = jnp.dot(w_ref[:, at - lead :], jnp.concatenate(lines, axis=0), preferred_element_type=jnp.float32)
+            finish(t, by_taps(sums))
+    else:
+        places = [(t, b) for t in range(PAIR) for b in range(chunks)]
+        side = TILE // LANES
+        taps = {t: [[], [], []] for t in range(PAIR)}
+        finished = 0
+        for n in range(0, len(places), side):
+            rhs = jnp.concatenate([window(t, b) for t, b in places[n : n + side]], axis=1)
+            sums = by_taps(jnp.dot(w_ref[...], rhs, preferred_element_type=jnp.float32))
+            for i, (t, _) in enumerate(places[n : n + side]):
+                for tap in range(3):
+                    taps[t][tap].append(sums[tap][i])
+            while finished < PAIR and (finished + 1) * chunks <= n + side:
+                finish(finished, taps[finished])
+                finished += 1
     if sends and rest_sent:
         outs[2][:, PAIR * (chunks - 1) * LANES :] = sum(tails).astype(jnp.bfloat16)
 
 
-def conv(plan, earlier, shifted, values, weight, columns):
+def conv(plan, begun, earlier, shifted, values, weight, columns):
     _, _, channels, lanes = shifted.shape
     pitch, half, received = plan["pitch"], plan["half"], plan["received"]
     if plan["last"]:
@@ -349,7 +401,7 @@
     return pl.pallas_call(
         functools.partial(conv_kernel, plan),
         out_shape=out_shape,
-        in_specs=[VMEM] * (4 + len(earlier)),
+        in_specs=[VMEM] * (4 + len(begun) + len(earlier)),
         out_specs=(VMEM,) * len(out_shape),
         scratch_shapes=scratch,
         compiler_params=pltpu.CompilerParams(vmem_limit_bytes=LIMIT),
@@ -359,7 +411,7 @@
             transcendentals=PAIR * channels * lanes,
         ),
         name=f"conv_{plan['layer']}",
-    )(shifted, values, weight, columns, *earlier)
+    )(shifted, values, weight, columns, *begun, *earlier)
 
 
 def join_kernel(pair, kept_ref, got_ref, *refs):
@@ -421,10 +473,14 @@
     far[-1], weight, columns, near_values, near_act = lax.optimization_barrier(
         (far[-1], weight, columns, near_values, near_act)
     )
-    parts = [(far[p], mate_of(far[p]), near_values[p], near_act[p]) for p in reversed(range(pairs))][::-1]
     values, shifted = [None] * pairs, [None] * pairs
-    values[-1], shifted[-1], send = beyond(layers, columns, *parts[-1])
+    values[-1], shifted[-1], send = beyond(
+        layers, columns, far[-1], mate_of(far[-1]), near_values[-1], near_act[-1]
+    )
     halo, rest = earlier_of(send), 0
+    first_begun = begin(shifted[-1], weight[0])
+    *far[:-1], first_begun = lax.optimization_barrier((*far[:-1], first_begun))
+    parts = [(far[p], mate_of(far[p]), near_values[p], near_act[p]) for p in reversed(range(pairs - 1))][::-1]
     half = width // 2
     pitch = half + layers + 1
     for layer in range(layers):
@@ -434,8 +490,14 @@
         for p in reversed(range(pairs)):
             builds = layer == 0 and p > 0
             earlier = (halo,) if p == 0 else parts[p - 1] if builds else (shifted[p - 1],)
+            waits = builds or (last and p == 0)
+            if builds and p == pairs - 1:
+                begun = (first_begun,)
+            else:
+                begun = (begin(shifted[p], weight[layer]),) if waits else ()
             plan = {
                 "layer": layer,
+                "begun": waits,
                 "last": last,
                 "sends": p == pairs - 1 and not last,
                 "rest_sent": joined(rows_left * pitch),
@@ -447,7 +509,7 @@
                 "half": half,
                 "rows": rows_left,
             }
-            outs = list(conv(plan, earlier, shifted[p], values[p], weight[layer], columns))
+            outs = list(conv(plan, begun, earlier, shifted[p], values[p], weight[layer], columns))
             if builds:
                 shifted[p - 1], values[p - 1] = outs.pop(), outs.pop()
             results[p] = outs

time: 45 us -> 44.3 us (0.984)
  waiting for transfers between devices: 5.49 us -> 2.23 us
  Pallas kernels: 21.4 us -> 22.8 us
  starting transfers between devices: 15.8 us -> 17 us
    pallas_call x0 -> x2, Pallas kernels: none -> 2.95 us  [begin(): pl.pallas_call(begin_kernel, out_shape=jax.ShapeDtypeStruct((PAIR, channe...]
    pallas_call x6, Pallas kernels: 15.1 us -> 13.5 us  [conv(): pl.pallas_call(functools.partial(conv_kernel, plan), out_shape=out_shape,...]
    ppermute x2, waiting for transfers between devices: 2.19 us -> 0.67 us  [beyond_of(): return lax.ppermute(block, 'rows', [(i, i ^ 2) for i in range(strips)])]
    ppermute x3, waiting for transfers between devices: 1.4 us -> 0.01 us  [earlier_of(): return lax.ppermute(block, 'tm', [(i, i + 1) for i in range(blocks - 1)])]
    ppermute x3, starting transfers between devices: 10.9 us -> 11.6 us  [earlier_of(): return lax.ppermute(block, 'tm', [(i, i + 1) for i in range(blocks - 1)])]
    ppermute x5, starting transfers between devices: 0.6 us -> 1.16 us  [mate_of(): return lax.ppermute(block, 'rows', [(i, i ^ 1) for i in range(strips)])]
  transfers between devices with their start and end apart: 10 -> 10, of which waited for: 5 -> 3; matrix products, arithmetic and copies ran while one was open for 2% -> 2% of each run, Pallas kernels for 46% -> 50%
where the time goes in v7:
time: 44.3 us; the launch traced here: 44.1 us
  Pallas kernels  22.8 us (51%)
  starting transfers between devices  17 us (38%)
  waiting for transfers between devices  2.23 us (5%)
  local copies, waits for them, and re-layouts  1 us (2%)
  other arithmetic  0.71 us (2%)
    pallas_call x6, Pallas kernels, conv(): pl.pallas_call(functools.partial(conv_kernel, plan), out_shape=out_shape,...  13.5 us
    ppermute x3, starting transfers between devices, earlier_of(): return lax.ppermute(block, 'tm', [(i, i + 1) for i in range(blocks - 1)])  11.6 us
    ppermute x2, starting transfers between devices, beyond_of(): return lax.ppermute(block, 'rows', [(i, i ^ 2) for i in range(strips)])  4.29 us
    pallas_call x1, Pallas kernels, weights(): pl.pallas_call(weights_kernel, out_shape=(one,) * layers + (jax.ShapeDtyp...  3.54 us
    pallas_call x2, Pallas kernels, begin(): pl.pallas_call(begin_kernel, out_shape=jax.ShapeDtypeStruct((PAIR, channe...  2.95 us
    pallas_call x2, Pallas kernels, join(): pl.pallas_call(functools.partial(join_kernel, pair), out_shape=jax.ShapeD...  1.62 us
    ppermute x5, waiting for transfers between devices, mate_of(): return lax.ppermute(block, 'rows', [(i, i ^ 1) for i in range(strips)])  1.56 us
    ppermute x5, starting transfers between devices, mate_of(): return lax.ppermute(block, 'rows', [(i, i ^ 1) for i in range(strips)])  1.16 us
  transfers between devices with their start and end apart: 10, of which 3 were waited for; matrix products, arithmetic and copies ran while one was open for 2% of the time, Pallas kernels for 50%

profile of v7, /device:TPU:0, one launch (start us, length us, event | category | flops | bytes accessed | tf_op | source)
XLA Modules:
  0.0 44.1 jit_solution(13356250053109977994)
XLA Ops:
  0.0 0.5 %collective-permute-start.1 = (bf16[4,2,192,128]{3,2,1,0:T(8,128)(2,1)}, bf16[4,2,192,128]{3,2,1,0:T(8,128)(2,1)S(1)}, u32[]{:S(2)}, u32[]{:S(2)}) collective-permute-start(bf16[4,2,192,128]{3,2,1,0:T(8,128)(2,1)} %in_ref.1), channel_id=1, source_target_pairs={{0,1},{1,0},{2,3},{3,2},{4,5},{5,4},{6,7},{7,6},{8,9},{9,8},{10,11... | collective-permute-start | bytes 1179656 | tf_op jit(solution)/shard_map/ppermute | solution.py:458
  0.5 1.0 %copy-done = bf16[4,2,192,128]{3,2,1,0:T(8,128)(2,1)S(1)} copy-done((bf16[4,2,192,128]{3,2,1,0:T(8,128)(2,1)S(1)}, bf16[4,2,192,128]{3,2,1,0:T(8,128)(2,1)}, u32[]{:S(2)}) %copy-start) | copy-done | bytes 393240
  1.5 2.6 %collective-permute-start = (bf16[2,2,192,128]{3,2,1,0:T(8,128)(2,1)S(1)}, bf16[2,2,192,128]{3,2,1,0:T(8,128)(2,1)S(1)}, u32[]{:S(2)}, u32[]{:S(2)}) collective-permute-start(bf16[2,2,192,128]{3,2,1,0:T(8,128)(2,1)S(1)} %get-tuple-element.45.refs_1_), channel_id=1, source_target_pairs={{0,2},{1,3},{2,0},{3,1},{4,6},{5,7},{6,4},{7,5},{8,10},{9,11},{10,... | collective-permute-start | bytes 589832 | tf_op jit(solution)/shard_map/ppermute | solution.py:464
  4.0 0.7 %pad_maximum_fusion.rows_ref.gains_ref = f32[6,192]{1,0:T(8,128)S(1)} fusion(f32[3,192]{1,0:T(4,128)} %param.7, f32[3,192]{1,0:T(4,128)} %param.6), kind=kLoop, calls=%fused_computation | loop fusion | flops 1152 | bytes 9216 | tf_op jit(solution)/shard_map/concatenate | solution.py:470
  4.7 3.5 %weights.1 = (bf16[576,1728]{1,0:T(8,128)(2,1)S(1)}, bf16[576,1728]{1,0:T(8,128)(2,1)S(1)}, bf16[576,1728]{1,0:T(8,128)(2,1)S(1)}, f32[3,2,192,128]{3,2,1,0:T(8,128)S(1)}) custom-call(bf16[3,27,192,192]{3,2,1,0:T(8,128)(2,1)} %w_ref.1, f32[6,192]{1,0:T(8,128)S(1)} %pad_maximum_fusion.rows_ref.gains_ref), custom_call_target="tpu_custom_call" | custom-call | bytes 11943936 | tf_op jit(solution)/shard_map/weights/pallas_call | solution.py:77
  8.3 0.6 %near.1 = (bf16[2,192,384]{2,1,0:T(8,128)(2,1)S(1)}, bf16[2,192,384]{2,1,0:T(8,128)(2,1)S(1)}, bf16[2,192,256]{2,1,0:T(8,128)(2,1)S(1)}, bf16[2,192,256]{2,1,0:T(8,128)(2,1)S(1)}) custom-call(bf16[4,2,192,128]{3,2,1,0:T(8,128)(2,1)S(1)} %collective-permute-done.1.mate_ref, f32[6,192]{1,0:T(8,128)S(1)} %pad_maximum_fusion.rows_ref.gains_ref, ...), custom_call_target="tpu_custom_call" | custom-call | flops 7864320 | bytes 1572864 | tf_op jit(solution)/shard_map/near/pallas_call | solution.py:166
  8.9 0.7 %collective-permute-done.far_ref = bf16[2,2,192,128]{3,2,1,0:T(8,128)(2,1)S(1)} collective-permute-done((bf16[2,2,192,128]{3,2,1,0:T(8,128)(2,1)S(1)}, bf16[2,2,192,128]{3,2,1,0:T(8,128)(2,1)S(1)}, u32[]{:S(2)}, u32[]{:S(2)}) %collective-permute-start) | collective-permute-done | bytes 196640 | tf_op jit(solution)/shard_map/ppermute | solution.py:464
  9.6 1.7 %collective-permute-start.3 = (bf16[2,2,192,128]{3,2,1,0:T(8,128)(2,1)S(1)}, bf16[2,2,192,128]{3,2,1,0:T(8,128)(2,1)S(1)}, u32[]{:S(2)}, u32[]{:S(2)}) collective-permute-start(bf16[2,2,192,128]{3,2,1,0:T(8,128)(2,1)S(1)} %get-tuple-element.50.refs_0_), channel_id=1, source_target_pairs={{0,2},{1,3},{2,0},{3,1},{4,6},{5,7},{6,4},{7,5},{8,10},{9,11},{10,... | collective-permute-start | bytes 589832 | tf_op jit(solution)/shard_map/ppermute | solution.py:464
  11.4 0.0 collective-permute-done.2.mate_ref
  11.4 0.5 %beyond.1 = (bf16[2,192,512]{2,1,0:T(8,128)(2,1)S(1)}, bf16[2,3,192,512]{3,2,1,0:T(8,128)(2,1)S(1)}, bf16[2,192,512]{2,1,0:T(8,128)(2,1)S(1)}) custom-call(f32[3,2,192,128]{3,2,1,0:T(8,128)S(1)} %get-tuple-element.55.columns_ref, bf16[2,2,192,128]{3,2,1,0:T(8,128)(2,1)S(1)} %collective-permute-done.far_ref, ...), custom_call_target="tpu_custom_call" | custom-call | flops 3932160 | bytes 786432 | tf_op jit(solution)/shard_map/beyond/pallas_call | solution.py:222
  11.9 3.5 %collective-permute-start.5 = (bf16[2,192,512]{2,1,0:T(8,128)(2,1)S(1)}, bf16[2,192,512]{2,1,0:T(8,128)(2,1)S(1)}, u32[]{:S(2)}, u32[]{:S(2)}) collective-permute-start(bf16[2,192,512]{2,1,0:T(8,128)(2,1)S(1)} %get-tuple-element.68), channel_id=1, source_target_pairs={{0,4},{4,8},{8,12},{1,5},{5,9},{9,13},{2,6},{6,10},{10,14},{3,7},{... | collective-permute-start | bytes 1179656 | tf_op jit(solution)/shard_map/ppermute | solution.py:461
  15.4 1.5 %begin.2.refs_0_ = f32[2,192,512]{2,1,0:T(8,128)S(1)} custom-call(bf16[2,3,192,512]{3,2,1,0:T(8,128)(2,1)S(1)} %get-tuple-element.59.shifted_ref, bf16[576,1728]{1,0:T(8,128)(2,1)S(1)} %get-tuple-element.61.w_ref), custom_call_target="tpu_custom_call" | custom-call | tf_op jit(solution)/shard_map/begin/pallas_call | solution.py:269
  16.9 0.1 collective-permute-start.4
  17.0 1.4 %collective-permute-done.4.refs_2_ = bf16[2,2,192,128]{3,2,1,0:T(8,128)(2,1)S(1)} collective-permute-done((bf16[2,2,192,128]{3,2,1,0:T(8,128)(2,1)S(1)}, bf16[2,2,192,128]{3,2,1,0:T(8,128)(2,1)S(1)}, u32[]{:S(2)}, u32[]{:S(2)}) %collective-permute-start.4) | collective-permute-done | bytes 196640 | tf_op jit(solution)/shard_map/ppermute | solution.py:458
  18.4 2.2 %conv_0.2 = (bf16[2,192,512]{2,1,0:T(8,128)(2,1)S(1)}, bf16[2,3,192,384]{3,2,1,0:T(8,128)(2,1)S(1)}, bf16[192,896]{1,0:T(8,128)(2,1)S(1)}, bf16[2,192,512]{2,1,0:T(8,128)(2,1)S(1)}, bf16[2,3,192,512]{3,2,1,0:T(8,128)(2,1)S(1)}) custom-call(bf16[2,3,192,512]{3,2,1,0:T(8,128)(2,1)S(1)} %get-tuple-element.59.shifted_ref, ...), custom_call_target="tpu_custom_call" | custom-call | flops 2038431744 | bytes 1990656 | tf_op jit(solution)/shard_map/conv_0/pallas_call | solution.py:401
  20.6 3.7 %collective-permute-start.6 = (bf16[192,896]{1,0:T(8,128)(2,1)S(1)}, bf16[192,896]{1,0:T(8,128)(2,1)S(1)}, u32[]{:S(2)}, u32[]{:S(2)}) collective-permute-start(bf16[192,896]{1,0:T(8,128)(2,1)S(1)} %get-tuple-element.72), channel_id=1, source_target_pairs={{0,4},{4,8},{8,12},{1,5},{5,9},{9,13},{2,6},{6,10},{10,14},{3,7},{... | collective-permute-start | bytes 1032200 | tf_op jit(solution)/shard_map/ppermute | solution.py:461
  24.3 0.0 collective-permute-done.5.refs_0_
  24.3 2.8 %conv_0.3 = (bf16[2,192,512]{2,1,0:T(8,128)(2,1)S(1)}, bf16[2,3,192,384]{3,2,1,0:T(8,128)(2,1)S(1)}) custom-call(bf16[2,3,192,512]{3,2,1,0:T(8,128)(2,1)S(1)} %get-tuple-element.66.shifted_ref, bf16[2,192,512]{2,1,0:T(8,128)(2,1)S(1)} %get-tuple-element.67.values_ref, bf16[576,1728]{1,0:T(8,128)(2,1)S(1)} %get-tuple-element.61.w_ref, ...), custom_call_target="tpu_custom_call" | custom-call | flops 2038431744 | bytes 1990656 | tf_op jit(solution)/shard_map/conv_0/pallas_call | solution.py:401
  27.1 2.2 %conv_1.3 = (bf16[2,192,384]{2,1,0:T(8,128)(2,1)S(1)}, bf16[2,3,192,384]{3,2,1,0:T(8,128)(2,1)S(1)}, bf16[2,192,384]{2,1,0:T(8,128)(2,1)S(1)}) custom-call(bf16[2,3,192,384]{3,2,1,0:T(8,128)(2,1)S(1)} %get-tuple-element.76.shifted_ref, bf16[2,192,512]{2,1,0:T(8,128)(2,1)S(1)} %get-tuple-element.77.values_ref, bf16[576,1728]{1,0:T(8,128)(2,1)S(1)} %get-tuple-element.71.w_ref, ...), custom_call_target="tpu_custom_call" | custom-call | flops 1528823808 | bytes 1990656 | tf_op jit(solution)/shard_map/conv_1/pallas_call | solution.py:401
  29.4 4.4 %collective-permute-start.7 = (bf16[2,192,384]{2,1,0:T(8,128)(2,1)S(1)}, bf16[2,192,384]{2,1,0:T(8,128)(2,1)S(1)}, u32[]{:S(2)}, u32[]{:S(2)}) collective-permute-start(bf16[2,192,384]{2,1,0:T(8,128)(2,1)S(1)} %get-tuple-element.78), channel_id=1, source_target_pairs={{0,4},{4,8},{8,12},{1,5},{5,9},{9,13},{2,6},{6,10},{10,14},{3,7},{... | collective-permute-start | bytes 884744 | tf_op jit(solution)/shard_map/ppermute | solution.py:461
  33.8 0.0 collective-permute-done.6.refs_0_
  33.8 2.3 %conv_1.2 = (bf16[2,192,384]{2,1,0:T(8,128)(2,1)S(1)}, bf16[2,3,192,384]{3,2,1,0:T(8,128)(2,1)S(1)}) custom-call(bf16[2,3,192,384]{3,2,1,0:T(8,128)(2,1)S(1)} %get-tuple-element.69.shifted_ref.refs_0_, bf16[2,192,512]{2,1,0:T(8,128)(2,1)S(1)} %get-tuple-element.70.values_ref, bf16[576,1728]{1,0:T(8,128)(2,1)S(1)} %get-tuple-element.71.w_ref, ...), custom_call_target="tpu_custom_call" | custom-call | flops 1528823808 | bytes 1990656 | tf_op jit(solution)/shard_map/conv_1/pallas_call | solution.py:401
  36.1 1.4 %begin.3.refs_0_ = f32[2,192,384]{2,1,0:T(8,128)S(1)} custom-call(bf16[2,3,192,384]{3,2,1,0:T(8,128)(2,1)S(1)} %get-tuple-element.73.shifted_ref.refs_0_, bf16[576,1728]{1,0:T(8,128)(2,1)S(1)} %get-tuple-element.75.w_ref), custom_call_target="tpu_custom_call" | custom-call | tf_op jit(solution)/shard_map/begin/pallas_call | solution.py:269
  37.5 2.2 %conv_2.3 = (bf16[2,192,128]{2,1,0:T(8,128)(2,1)S(1)}, bf16[2,192,128]{2,1,0:T(8,128)(2,1)S(1)}) custom-call(bf16[2,3,192,384]{3,2,1,0:T(8,128)(2,1)S(1)} %get-tuple-element.81.shifted_ref, bf16[2,192,384]{2,1,0:T(8,128)(2,1)S(1)} %get-tuple-element.82.values_ref, bf16[576,1728]{1,0:T(8,128)(2,1)S(1)} %get-tuple-element.75.w_ref, ...), custom_call_target="tpu_custom_call" | custom-call | flops 1528823808 | bytes 1990656 | tf_op jit(solution)/shard_map/conv_2/pallas_call | solution.py:401
  39.7 0.1 collective-permute-start.9
  39.7 0.0 collective-permute-done.7.refs_1_
  39.8 1.8 %conv_2.2 = (bf16[2,192,128]{2,1,0:T(8,128)(2,1)S(1)}, bf16[2,192,128]{2,1,0:T(8,128)(2,1)S(1)}) custom-call(bf16[2,3,192,384]{3,2,1,0:T(8,128)(2,1)S(1)} %get-tuple-element.73.shifted_ref.refs_0_, bf16[2,192,384]{2,1,0:T(8,128)(2,1)S(1)} %get-tuple-element.74.values_ref, bf16[576,1728]{1,0:T(8,128)(2,1)S(1)} %get-tuple-element.75.w_ref, ...), custom_call_target="tpu_custom_call" | custom-call | flops 1528823808 | bytes 1990656 | tf_op jit(solution)/shard_map/conv_2/pallas_call | solution.py:401
  41.6 0.6 %collective-permute-start.8 = (bf16[2,192,128]{2,1,0:T(8,128)(2,1)S(1)}, bf16[2,192,128]{2,1,0:T(8,128)(2,1)S(1)}, u32[]{:S(2)}, u32[]{:S(2)}) collective-permute-start(bf16[2,192,128]{2,1,0:T(8,128)(2,1)S(1)} %get-tuple-element.80), channel_id=1, source_target_pairs={{0,1},{1,0},{2,3},{3,2},{4,5},{5,4},{6,7},{7,6},{8,9},{9,8},{10,11... | collective-permute-start | bytes 294920 | tf_op jit(solution)/shard_map/ppermute | solution.py:458
  42.2 0.0 collective-permute-done.9.got_ref
  42.2 0.8 %join.2.refs_0_ = bf16[4,2,192,128]{3,2,1,0:T(8,128)(2,1)} custom-call(bf16[2,192,128]{2,1,0:T(8,128)(2,1)S(1)} %get-tuple-element.83.kept_ref, bf16[2,192,128]{2,1,0:T(8,128)(2,1)S(1)} %collective-permute-done.9.got_ref), custom_call_target="tpu_custom_call" | custom-call | tf_op jit(solution)/shard_map/join/pallas_call | solution.py:439
  43.0 0.1 collective-permute-done.8.got_ref
  43.1 0.8 %join.3 = bf16[4,2,192,128]{3,2,1,0:T(8,128)(2,1)} custom-call(bf16[2,192,128]{2,1,0:T(8,128)(2,1)S(1)} %get-tuple-element.79.kept_ref, bf16[2,192,128]{2,1,0:T(8,128)(2,1)S(1)} %collective-permute-done.8.got_ref, bf16[4,2,192,128]{3,2,1,0:T(8,128)(2,1)} %join.2.refs_0_), custom_call_target="tpu_custom_call", output_to_operand_aliasing={{}: (2, {})} | custom-call | tf_op jit(solution)/shard_map/join/pallas_call | solution.py:439
  (5 shorter events, 0.0 us)
Async XLA Ops:
  0.0 8.3 %collective-permute-start.1 = (bf16[4,2,192,128]{3,2,1,0:T(8,128)(2,1)}, bf16[4,2,192,128]{3,2,1,0:T(8,128)(2,1)S(1)}, u32[]{:S(2)}, u32[]{:S(2)}) collective-permute-start(bf16[4,2,192,128]{3,2,1,0:T(8,128)(2,1)} %in_ref.1), channel_id=1, source_target_pairs={{0,1},{1,0},{2,3},{3,2},{4,5},{5,4},{6,7},{7,6},{8,9},{9,8},{10,11... | collective-permute-start | bytes 1179656 | tf_op jit(solution)/shard_map/ppermute | solution.py:458
  0.5 1.0 %copy-start = (bf16[4,2,192,128]{3,2,1,0:T(8,128)(2,1)S(1)}, bf16[4,2,192,128]{3,2,1,0:T(8,128)(2,1)}, u32[]{:S(2)}) copy-start(bf16[4,2,192,128]{3,2,1,0:T(8,128)(2,1)} %in_ref.1) | copy-start | bytes 1179652
  1.5 8.1 %collective-permute-start = (bf16[2,2,192,128]{3,2,1,0:T(8,128)(2,1)S(1)}, bf16[2,2,192,128]{3,2,1,0:T(8,128)(2,1)S(1)}, u32[]{:S(2)}, u32[]{:S(2)}) collective-permute-start(bf16[2,2,192,128]{3,2,1,0:T(8,128)(2,1)S(1)} %get-tuple-element.45.refs_1_), channel_id=1, source_target_pairs={{0,2},{1,3},{2,0},{3,1},{4,6},{5,7},{6,4},{7,5},{8,10},{9,11},{10,... | collective-permute-start | bytes 589832 | tf_op jit(solution)/shard_map/ppermute | solution.py:464
  9.6 1.7 %collective-permute-start.2 = (bf16[2,2,192,128]{3,2,1,0:T(8,128)(2,1)S(1)}, bf16[2,2,192,128]{3,2,1,0:T(8,128)(2,1)S(1)}, u32[]{:S(2)}, u32[]{:S(2)}) collective-permute-start(bf16[2,2,192,128]{3,2,1,0:T(8,128)(2,1)S(1)} %collective-permute-done.far_ref), channel_id=1, source_target_pairs={{0,1},{1,0},{2,3},{3,2},{4,5},{5,4},{6,7},{7,6},{8,9},{9,8},{10,11... | collective-permute-start | bytes 589832 | tf_op jit(solution)/shard_map/ppermute | solution.py:458
  9.6 7.3 %collective-permute-start.3 = (bf16[2,2,192,128]{3,2,1,0:T(8,128)(2,1)S(1)}, bf16[2,2,192,128]{3,2,1,0:T(8,128)(2,1)S(1)}, u32[]{:S(2)}, u32[]{:S(2)}) collective-permute-start(bf16[2,2,192,128]{3,2,1,0:T(8,128)(2,1)S(1)} %get-tuple-element.50.refs_0_), channel_id=1, source_target_pairs={{0,2},{1,3},{2,0},{3,1},{4,6},{5,7},{6,4},{7,5},{8,10},{9,11},{10,... | collective-permute-start | bytes 589832 | tf_op jit(solution)/shard_map/ppermute | solution.py:464
  11.9 12.4 %collective-permute-start.5 = (bf16[2,192,512]{2,1,0:T(8,128)(2,1)S(1)}, bf16[2,192,512]{2,1,0:T(8,128)(2,1)S(1)}, u32[]{:S(2)}, u32[]{:S(2)}) collective-permute-start(bf16[2,192,512]{2,1,0:T(8,128)(2,1)S(1)} %get-tuple-element.68), channel_id=1, source_target_pairs={{0,4},{4,8},{8,12},{1,5},{5,9},{9,13},{2,6},{6,10},{10,14},{3,7},{... | collective-permute-start | bytes 1179656 | tf_op jit(solution)/shard_map/ppermute | solution.py:461
  16.9 1.5 %collective-permute-start.4 = (bf16[2,2,192,128]{3,2,1,0:T(8,128)(2,1)S(1)}, bf16[2,2,192,128]{3,2,1,0:T(8,128)(2,1)S(1)}, u32[]{:S(2)}, u32[]{:S(2)}) collective-permute-start(bf16[2,2,192,128]{3,2,1,0:T(8,128)(2,1)S(1)} %collective-permute-done.3.refs_1_), channel_id=1, source_target_pairs={{0,1},{1,0},{2,3},{3,2},{4,5},{5,4},{6,7},{7,6},{8,9},{9,8},{10,11... | collective-permute-start | bytes 589832 | tf_op jit(solution)/shard_map/ppermute | solution.py:458
  20.6 13.2 %collective-permute-start.6 = (bf16[192,896]{1,0:T(8,128)(2,1)S(1)}, bf16[192,896]{1,0:T(8,128)(2,1)S(1)}, u32[]{:S(2)}, u32[]{:S(2)}) collective-permute-start(bf16[192,896]{1,0:T(8,128)(2,1)S(1)} %get-tuple-element.72), channel_id=1, source_target_pairs={{0,4},{4,8},{8,12},{1,5},{5,9},{9,13},{2,6},{6,10},{10,14},{3,7},{... | collective-permute-start | bytes 1032200 | tf_op jit(solution)/shard_map/ppermute | solution.py:461
  29.4 10.4 %collective-permute-start.7 = (bf16[2,192,384]{2,1,0:T(8,128)(2,1)S(1)}, bf16[2,192,384]{2,1,0:T(8,128)(2,1)S(1)}, u32[]{:S(2)}, u32[]{:S(2)}) collective-permute-start(bf16[2,192,384]{2,1,0:T(8,128)(2,1)S(1)} %get-tuple-element.78), channel_id=1, source_target_pairs={{0,4},{4,8},{8,12},{1,5},{5,9},{9,13},{2,6},{6,10},{10,14},{3,7},{... | collective-permute-start | bytes 884744 | tf_op jit(solution)/shard_map/ppermute | solution.py:461
  39.7 2.5 %collective-permute-start.9 = (bf16[2,192,128]{2,1,0:T(8,128)(2,1)S(1)}, bf16[2,192,128]{2,1,0:T(8,128)(2,1)S(1)}, u32[]{:S(2)}, u32[]{:S(2)}) collective-permute-start(bf16[2,192,128]{2,1,0:T(8,128)(2,1)S(1)} %get-tuple-element.84), channel_id=1, source_target_pairs={{0,1},{1,0},{2,3},{3,2},{4,5},{5,4},{6,7},{7,6},{8,9},{9,8},{10,11... | collective-permute-start | bytes 294920 | tf_op jit(solution)/shard_map/ppermute | solution.py:458
  41.6 1.5 %collective-permute-start.8 = (bf16[2,192,128]{2,1,0:T(8,128)(2,1)S(1)}, bf16[2,192,128]{2,1,0:T(8,128)(2,1)S(1)}, u32[]{:S(2)}, u32[]{:S(2)}) collective-permute-start(bf16[2,192,128]{2,1,0:T(8,128)(2,1)S(1)} %get-tuple-element.80), channel_id=1, source_target_pairs={{0,1},{1,0},{2,3},{3,2},{4,5},{5,4},{6,7},{7,6},{8,9},{9,8},{10,11... | collective-permute-start | bytes 294920 | tf_op jit(solution)/shard_map/ppermute | solution.py:458

commit v8 on v7

--- a/solution.py
+++ b/solution.py
@@ -303,42 +303,51 @@
     chunks = lanes // LANES
     lane = lane_of(LANES)
 
-    def window(t, b):
-        taken = [(earlier_ref, t + a) if t + a < PAIR else (shifted_ref, t + a - PAIR) for a in (2, 1, 0)]
-        at = slice(b * LANES, (b + 1) * LANES)
-        return jnp.concatenate([ref[j, :, :, at].reshape(3 * channels, LANES) for ref, j in taken], axis=0)
+    def frame_of(j):
+        return (earlier_ref, j) if j < PAIR else (shifted_ref, j - PAIR)
+
+    def rows_of_frames(frames, blocks):
+        at = slice(blocks[0] * LANES, (blocks[-1] + 1) * LANES)
+        taken = [frame_of(j) for j in frames]
+        return [ref[j, :, :, at].reshape(3 * channels, len(blocks) * LANES) for ref, j in taken]
 
     bias = columns_ref[layer, 1]
     tails = []
     if not last:
         mask = filled(lanes, pitch)
         gain = columns_ref[layer + 1, 0]
-
-    def finish(t, taps):
-        totals, acts = [], []
-        for b, conv in enumerate(column_sums(taps)):
-            at = slice(b * LANES, (b + 1) * LANES)
-            if begun_ref is not None:
-                conv = conv + begun_ref[t, :, at]
-            total = (values_ref[t, :, at].astype(jnp.float32) + conv + bias).astype(jnp.bfloat16)
-            totals.append(total.astype(jnp.float32))
-            if last:
-                continue
-            outs[0][t, :, at] = total
-            acts.append(activated(totals[-1], gain, mask[:, at]))
-            if not sends:
-                continue
-            if not rest_sent:
-                outs[2][t, :, at] = acts[-1]
-            elif b < chunks - 1:
-                outs[2][:, (t * (chunks - 1) + b) * LANES : (t * (chunks - 1) + b + 1) * LANES] = acts[-1]
-            else:
-                tail = jnp.where(lane < rest_sent, acts[-1].astype(jnp.float32), 0.0)
-                tails.append(tail if t == 0 else pltpu.roll(tail, t * (LANES // PAIR), 1))
+    sums = {}
+    done = {t: [] for t in range(PAIR)}
+
+    def finish(t, b):
+        left = jnp.where(lane == 0, sums["left", t, b - 1] if b else 0.0, sums["left", t, b])
+        follows = sums["right", t, b + 1] if b < chunks - 1 else 0.0
+        conv = left + sums["middle", t, b] + jnp.where(lane == LANES - 1, follows, sums["right", t, b])
+        at = slice(b * LANES, (b + 1) * LANES)
+        if begun_ref is not None:
+            conv = conv + begun_ref[t, :, at]
+        total = (values_ref[t, :, at].astype(jnp.float32) + conv + bias).astype(jnp.bfloat16)
+        if last:
+            done[t].append(total.astype(jnp.float32))
+            return
+        outs[0][t, :, at] = total
+        act = activated(total.astype(jnp.float32), gain, mask[:, at])
+        done[t].append(act)
+        if not sends:
+            return
+        if not rest_sent:
+            outs[2][t, :, at] = act
+        elif b < chunks - 1:
+            outs[2][:, (t * (chunks - 1) + b) * LANES : (t * (chunks - 1) + b + 1) * LANES] = act
+        else:
+            tail = jnp.where(lane < rest_sent, act.astype(jnp.float32), 0.0)
+            tails.append(tail if t == 0 else pltpu.roll(tail, t * (LANES // PAIR), 1))
+
+    def finish_frame(t):
+        whole = jnp.concatenate(done[t], axis=1)
         if not last:
-            spread(outs[1], t, jnp.concatenate(acts, axis=1), pitch)
+            spread(outs[1], t, whole, pitch)
             return
-        whole = jnp.concatenate(totals, axis=1)
         halo = pitch - 1 - half
         core, _, outer = place()
         whole = jnp.where(core == 1, pltpu.roll(whole, lanes - halo, 1), whole)
@@ -353,30 +362,46 @@
         outs[0][t] = jnp.where(outer, outermost, inner).astype(jnp.bfloat16)
         outs[1][t] = jnp.where(outer, inner, outermost).astype(jnp.bfloat16)
 
+    side = TILE // LANES
+    tiles = []
     if plan["begun"]:
-        depth = 3 * channels
         for t in range(PAIR):
-            at = (t + 1) * depth
-            lead = at % LANES
-            lines = [lines_of(earlier_ref, j) for j in range(PAIR - 1, t - 1, -1)]
-            if lead:
-                lines.insert(0, jnp.zeros((lead, lanes), jnp.bfloat16))
-            sums = jnp.dot(w_ref[:, at - lead :], jnp.concatenate(lines, axis=0), preferred_element_type=jnp.float32)
-            finish(t, by_taps(sums))
+            for b in range(0, chunks, side):
+                places = [(t, c) for c in range(b, min(b + side, chunks))]
+                tiles.append((places, list(range(PAIR - 1, t - 1, -1)), (t + 1) * 3 * channels))
     else:
         places = [(t, b) for t in range(PAIR) for b in range(chunks)]
-        side = TILE // LANES
-        taps = {t: [[], [], []] for t in range(PAIR)}
-        finished = 0
-        for n in range(0, len(places), side):
-            rhs = jnp.concatenate([window(t, b) for t, b in places[n : n + side]], axis=1)
-            sums = by_taps(jnp.dot(w_ref[...], rhs, preferred_element_type=jnp.float32))
-            for i, (t, _) in enumerate(places[n : n + side]):
-                for tap in range(3):
-                    taps[t][tap].append(sums[tap][i])
-            while finished < PAIR and (finished + 1) * chunks <= n + side:
-                finish(finished, taps[finished])
-                finished += 1
+        tiles = [(places[n : n + side], None, 0) for n in range(0, len(places), side)]
+    waiting = []
+    for places, frames, start in tiles:
+        if frames is None:
+            columns = [jnp.concatenate(rows_of_frames((t + 2, t + 1, t), [b]), axis=0) for t, b in places]
+            rhs = jnp.concatenate(columns, axis=1)
+            lead = 0
+        else:
+            lead = start % LANES
+            lines = rows_of_frames(frames, [b for _, b in places])
+            zeros = [jnp.zeros((lead, len(places) * LANES), jnp.bfloat16)] if lead else []
+            rhs = jnp.concatenate(zeros + lines, axis=0)
+        share = -(-len(waiting) // 3)
+        for tap, name in enumerate(("left", "middle", "right")):
+            rows = slice(tap * channels, (tap + 1) * channels)
+            product = jnp.dot(w_ref[rows, start - lead :], rhs, preferred_element_type=jnp.float32)
+            for i, (t, b) in enumerate(places):
+                part = product[:, i * LANES : (i + 1) * LANES]
+                turn = {"left": 1, "right": LANES - 1}.get(name)
+                sums[name, t, b] = part if turn is None else pltpu.roll(part, turn, 1)
+            for work in waiting[tap * share : (tap + 1) * share]:
+                work()
+        waiting = []
+        for t, b in places:
+            if b:
+                waiting.append(functools.partial(finish, t, b - 1))
+            if b == chunks - 1:
+                waiting.append(functools.partial(finish, t, b))
+                waiting.append(functools.partial(finish_frame, t))
+    for work in waiting:
+        work()
     if sends and rest_sent:
         outs[2][:, PAIR * (chunks - 1) * LANES :] = sum(tails).astype(jnp.bfloat16)
 

time: 44.3 us -> 44.4 us (level)
  no operation moved by 1% of the time
where the time goes in v8:
time: 44.4 us; the launch traced here: 44.1 us
  Pallas kernels  23 us (52%)
  starting transfers between devices  16.9 us (38%)
  waiting for transfers between devices  2.23 us (5%)
  local copies, waits for them, and re-layouts  1 us (2%)
  other arithmetic  0.71 us (2%)
    pallas_call x6, Pallas kernels, conv(): pl.pallas_call(functools.partial(conv_kernel, plan), out_shape=out_shape,...  13.7 us
    ppermute x3, starting transfers between devices, earlier_of(): return lax.ppermute(block, 'tm', [(i, i + 1) for i in range(blocks - 1)])  11.4 us
    ppermute x2, starting transfers between devices, beyond_of(): return lax.ppermute(block, 'rows', [(i, i ^ 2) for i in range(strips)])  4.29 us
    pallas_call x1, Pallas kernels, weights(): pl.pallas_call(weights_kernel, out_shape=(one,) * layers + (jax.ShapeDtyp...  3.54 us
    pallas_call x2, Pallas kernels, begin(): pl.pallas_call(begin_kernel, out_shape=jax.ShapeDtypeStruct((PAIR, channe...  2.94 us
    pallas_call x2, Pallas kernels, join(): pl.pallas_call(functools.partial(join_kernel, pair), out_shape=jax.ShapeD...  1.62 us
    ppermute x5, waiting for transfers between devices, mate_of(): return lax.ppermute(block, 'rows', [(i, i ^ 1) for i in range(strips)])  1.56 us
    ppermute x5, starting transfers between devices, mate_of(): return lax.ppermute(block, 'rows', [(i, i ^ 1) for i in range(strips)])  1.15 us
  transfers between devices with their start and end apart: 10, of which 3 were waited for; matrix products, arithmetic and copies ran while one was open for 2% of the time, Pallas kernels for 50%

profile of v8, /device:TPU:0, one launch (start us, length us, event | category | flops | bytes accessed | tf_op | source)
XLA Modules:
  0.0 44.1 jit_solution(15109994435872457084)
XLA Ops:
  0.0 0.5 %collective-permute-start.1 = (bf16[4,2,192,128]{3,2,1,0:T(8,128)(2,1)}, bf16[4,2,192,128]{3,2,1,0:T(8,128)(2,1)S(1)}, u32[]{:S(2)}, u32[]{:S(2)}) collective-permute-start(bf16[4,2,192,128]{3,2,1,0:T(8,128)(2,1)} %in_ref.1), channel_id=1, source_target_pairs={{0,1},{1,0},{2,3},{3,2},{4,5},{5,4},{6,7},{7,6},{8,9},{9,8},{10,11... | collective-permute-start | bytes 1179656 | tf_op jit(solution)/shard_map/ppermute | solution.py:483
  0.5 1.0 %copy-done = bf16[4,2,192,128]{3,2,1,0:T(8,128)(2,1)S(1)} copy-done((bf16[4,2,192,128]{3,2,1,0:T(8,128)(2,1)S(1)}, bf16[4,2,192,128]{3,2,1,0:T(8,128)(2,1)}, u32[]{:S(2)}) %copy-start) | copy-done | bytes 393240
  1.5 2.6 %collective-permute-start = (bf16[2,2,192,128]{3,2,1,0:T(8,128)(2,1)S(1)}, bf16[2,2,192,128]{3,2,1,0:T(8,128)(2,1)S(1)}, u32[]{:S(2)}, u32[]{:S(2)}) collective-permute-start(bf16[2,2,192,128]{3,2,1,0:T(8,128)(2,1)S(1)} %get-tuple-element.45.refs_1_), channel_id=1, source_target_pairs={{0,2},{1,3},{2,0},{3,1},{4,6},{5,7},{6,4},{7,5},{8,10},{9,11},{10,... | collective-permute-start | bytes 589832 | tf_op jit(solution)/shard_map/ppermute | solution.py:489
  4.0 0.7 %pad_maximum_fusion.rows_ref.gains_ref = f32[6,192]{1,0:T(8,128)S(1)} fusion(f32[3,192]{1,0:T(4,128)} %param.7, f32[3,192]{1,0:T(4,128)} %param.6), kind=kLoop, calls=%fused_computation | loop fusion | flops 1152 | bytes 9216 | tf_op jit(solution)/shard_map/concatenate | solution.py:495
  4.7 3.5 %weights.1 = (bf16[576,1728]{1,0:T(8,128)(2,1)S(1)}, bf16[576,1728]{1,0:T(8,128)(2,1)S(1)}, bf16[576,1728]{1,0:T(8,128)(2,1)S(1)}, f32[3,2,192,128]{3,2,1,0:T(8,128)S(1)}) custom-call(bf16[3,27,192,192]{3,2,1,0:T(8,128)(2,1)} %w_ref.1, f32[6,192]{1,0:T(8,128)S(1)} %pad_maximum_fusion.rows_ref.gains_ref), custom_call_target="tpu_custom_call" | custom-call | bytes 11943936 | tf_op jit(solution)/shard_map/weights/pallas_call | solution.py:77
  8.3 0.0 collective-permute-done.1.mate_ref
  8.3 0.6 %near.1 = (bf16[2,192,384]{2,1,0:T(8,128)(2,1)S(1)}, bf16[2,192,384]{2,1,0:T(8,128)(2,1)S(1)}, bf16[2,192,256]{2,1,0:T(8,128)(2,1)S(1)}, bf16[2,192,256]{2,1,0:T(8,128)(2,1)S(1)}) custom-call(bf16[4,2,192,128]{3,2,1,0:T(8,128)(2,1)S(1)} %collective-permute-done.1.mate_ref, f32[6,192]{1,0:T(8,128)S(1)} %pad_maximum_fusion.rows_ref.gains_ref, ...), custom_call_target="tpu_custom_call" | custom-call | flops 7864320 | bytes 1572864 | tf_op jit(solution)/shard_map/near/pallas_call | solution.py:166
  8.9 0.7 %collective-permute-done.far_ref = bf16[2,2,192,128]{3,2,1,0:T(8,128)(2,1)S(1)} collective-permute-done((bf16[2,2,192,128]{3,2,1,0:T(8,128)(2,1)S(1)}, bf16[2,2,192,128]{3,2,1,0:T(8,128)(2,1)S(1)}, u32[]{:S(2)}, u32[]{:S(2)}) %collective-permute-start) | collective-permute-done | bytes 196640 | tf_op jit(solution)/shard_map/ppermute | solution.py:489
  9.6 0.0 collective-permute-start.2
  9.6 1.7 %collective-permute-start.3 = (bf16[2,2,192,128]{3,2,1,0:T(8,128)(2,1)S(1)}, bf16[2,2,192,128]{3,2,1,0:T(8,128)(2,1)S(1)}, u32[]{:S(2)}, u32[]{:S(2)}) collective-permute-start(bf16[2,2,192,128]{3,2,1,0:T(8,128)(2,1)S(1)} %get-tuple-element.50.refs_0_), channel_id=1, source_target_pairs={{0,2},{1,3},{2,0},{3,1},{4,6},{5,7},{6,4},{7,5},{8,10},{9,11},{10,... | collective-permute-start | bytes 589832 | tf_op jit(solution)/shard_map/ppermute | solution.py:489
  11.4 0.0 collective-permute-done.2.mate_ref
  11.4 0.5 %beyond.1 = (bf16[2,192,512]{2,1,0:T(8,128)(2,1)S(1)}, bf16[2,3,192,512]{3,2,1,0:T(8,128)(2,1)S(1)}, bf16[2,192,512]{2,1,0:T(8,128)(2,1)S(1)}) custom-call(f32[3,2,192,128]{3,2,1,0:T(8,128)S(1)} %get-tuple-element.55.columns_ref, bf16[2,2,192,128]{3,2,1,0:T(8,128)(2,1)S(1)} %collective-permute-done.far_ref, ...), custom_call_target="tpu_custom_call" | custom-call | flops 3932160 | bytes 786432 | tf_op jit(solution)/shard_map/beyond/pallas_call | solution.py:222
  11.9 3.5 %collective-permute-start.5 = (bf16[2,192,512]{2,1,0:T(8,128)(2,1)S(1)}, bf16[2,192,512]{2,1,0:T(8,128)(2,1)S(1)}, u32[]{:S(2)}, u32[]{:S(2)}) collective-permute-start(bf16[2,192,512]{2,1,0:T(8,128)(2,1)S(1)} %get-tuple-element.68), channel_id=1, source_target_pairs={{0,4},{4,8},{8,12},{1,5},{5,9},{9,13},{2,6},{6,10},{10,14},{3,7},{... | collective-permute-start | bytes 1179656 | tf_op jit(solution)/shard_map/ppermute | solution.py:486
  15.4 1.5 %begin.2.refs_0_ = f32[2,192,512]{2,1,0:T(8,128)S(1)} custom-call(bf16[2,3,192,512]{3,2,1,0:T(8,128)(2,1)S(1)} %get-tuple-element.59.shifted_ref, bf16[576,1728]{1,0:T(8,128)(2,1)S(1)} %get-tuple-element.61.w_ref), custom_call_target="tpu_custom_call" | custom-call | tf_op jit(solution)/shard_map/begin/pallas_call | solution.py:269
  16.9 0.0 collective-permute-done.3.refs_1_
  16.9 0.1 collective-permute-start.4
  17.0 1.4 %collective-permute-done.4.refs_2_ = bf16[2,2,192,128]{3,2,1,0:T(8,128)(2,1)S(1)} collective-permute-done((bf16[2,2,192,128]{3,2,1,0:T(8,128)(2,1)S(1)}, bf16[2,2,192,128]{3,2,1,0:T(8,128)(2,1)S(1)}, u32[]{:S(2)}, u32[]{:S(2)}) %collective-permute-start.4) | collective-permute-done | bytes 196640 | tf_op jit(solution)/shard_map/ppermute | solution.py:483
  18.4 2.3 %conv_0.2 = (bf16[2,192,512]{2,1,0:T(8,128)(2,1)S(1)}, bf16[2,3,192,384]{3,2,1,0:T(8,128)(2,1)S(1)}, bf16[192,896]{1,0:T(8,128)(2,1)S(1)}, bf16[2,192,512]{2,1,0:T(8,128)(2,1)S(1)}, bf16[2,3,192,512]{3,2,1,0:T(8,128)(2,1)S(1)}) custom-call(bf16[2,3,192,512]{3,2,1,0:T(8,128)(2,1)S(1)} %get-tuple-element.59.shifted_ref, ...), custom_call_target="tpu_custom_call" | custom-call | flops 2038431744 | bytes 1990656 | tf_op jit(solution)/shard_map/conv_0/pallas_call | solution.py:426
  20.8 3.7 %collective-permute-start.6 = (bf16[192,896]{1,0:T(8,128)(2,1)S(1)}, bf16[192,896]{1,0:T(8,128)(2,1)S(1)}, u32[]{:S(2)}, u32[]{:S(2)}) collective-permute-start(bf16[192,896]{1,0:T(8,128)(2,1)S(1)} %get-tuple-element.72), channel_id=1, source_target_pairs={{0,4},{4,8},{8,12},{1,5},{5,9},{9,13},{2,6},{6,10},{10,14},{3,7},{... | collective-permute-start | bytes 1032200 | tf_op jit(solution)/shard_map/ppermute | solution.py:486
  24.5 0.0 collective-permute-done.5.refs_0_
  24.5 2.7 %conv_0.3 = (bf16[2,192,512]{2,1,0:T(8,128)(2,1)S(1)}, bf16[2,3,192,384]{3,2,1,0:T(8,128)(2,1)S(1)}) custom-call(bf16[2,3,192,512]{3,2,1,0:T(8,128)(2,1)S(1)} %get-tuple-element.66.shifted_ref, bf16[2,192,512]{2,1,0:T(8,128)(2,1)S(1)} %get-tuple-element.67.values_ref, bf16[576,1728]{1,0:T(8,128)(2,1)S(1)} %get-tuple-element.61.w_ref, ...), custom_call_target="tpu_custom_call" | custom-call | flops 2038431744 | bytes 1990656 | tf_op jit(solution)/shard_map/conv_0/pallas_call | solution.py:426
  27.2 2.3 %conv_1.3 = (bf16[2,192,384]{2,1,0:T(8,128)(2,1)S(1)}, bf16[2,3,192,384]{3,2,1,0:T(8,128)(2,1)S(1)}, bf16[2,192,384]{2,1,0:T(8,128)(2,1)S(1)}) custom-call(bf16[2,3,192,384]{3,2,1,0:T(8,128)(2,1)S(1)} %get-tuple-element.76.shifted_ref, bf16[2,192,512]{2,1,0:T(8,128)(2,1)S(1)} %get-tuple-element.77.values_ref, bf16[576,1728]{1,0:T(8,128)(2,1)S(1)} %get-tuple-element.71.w_ref, ...), custom_call_target="tpu_custom_call" | custom-call | flops 1528823808 | bytes 1990656 | tf_op jit(solution)/shard_map/conv_1/pallas_call | solution.py:426
  29.5 4.2 %collective-permute-start.7 = (bf16[2,192,384]{2,1,0:T(8,128)(2,1)S(1)}, bf16[2,192,384]{2,1,0:T(8,128)(2,1)S(1)}, u32[]{:S(2)}, u32[]{:S(2)}) collective-permute-start(bf16[2,192,384]{2,1,0:T(8,128)(2,1)S(1)} %get-tuple-element.78), channel_id=1, source_target_pairs={{0,4},{4,8},{8,12},{1,5},{5,9},{9,13},{2,6},{6,10},{10,14},{3,7},{... | collective-permute-start | bytes 884744 | tf_op jit(solution)/shard_map/ppermute | solution.py:486
  33.7 2.4 %conv_1.2 = (bf16[2,192,384]{2,1,0:T(8,128)(2,1)S(1)}, bf16[2,3,192,384]{3,2,1,0:T(8,128)(2,1)S(1)}) custom-call(bf16[2,3,192,384]{3,2,1,0:T(8,128)(2,1)S(1)} %get-tuple-element.69.shifted_ref.refs_0_, bf16[2,192,512]{2,1,0:T(8,128)(2,1)S(1)} %get-tuple-element.70.values_ref, bf16[576,1728]{1,0:T(8,128)(2,1)S(1)} %get-tuple-element.71.w_ref, ...), custom_call_target="tpu_custom_call" | custom-call | flops 1528823808 | bytes 1990656 | tf_op jit(solution)/shard_map/conv_1/pallas_call | solution.py:426
  36.1 1.4 %begin.3.refs_0_ = f32[2,192,384]{2,1,0:T(8,128)S(1)} custom-call(bf16[2,3,192,384]{3,2,1,0:T(8,128)(2,1)S(1)} %get-tuple-element.73.shifted_ref.refs_0_, bf16[576,1728]{1,0:T(8,128)(2,1)S(1)} %get-tuple-element.75.w_ref), custom_call_target="tpu_custom_call" | custom-call | tf_op jit(solution)/shard_map/begin/pallas_call | solution.py:269
  37.5 2.1 %conv_2.3 = (bf16[2,192,128]{2,1,0:T(8,128)(2,1)S(1)}, bf16[2,192,128]{2,1,0:T(8,128)(2,1)S(1)}) custom-call(bf16[2,3,192,384]{3,2,1,0:T(8,128)(2,1)S(1)} %get-tuple-element.81.shifted_ref, bf16[2,192,384]{2,1,0:T(8,128)(2,1)S(1)} %get-tuple-element.82.values_ref, bf16[576,1728]{1,0:T(8,128)(2,1)S(1)} %get-tuple-element.75.w_ref, ...), custom_call_target="tpu_custom_call" | custom-call | flops 1528823808 | bytes 1990656 | tf_op jit(solution)/shard_map/conv_2/pallas_call | solution.py:426
  39.7 0.1 collective-permute-start.9
  39.8 1.9 %conv_2.2 = (bf16[2,192,128]{2,1,0:T(8,128)(2,1)S(1)}, bf16[2,192,128]{2,1,0:T(8,128)(2,1)S(1)}) custom-call(bf16[2,3,192,384]{3,2,1,0:T(8,128)(2,1)S(1)} %get-tuple-element.73.shifted_ref.refs_0_, bf16[2,192,384]{2,1,0:T(8,128)(2,1)S(1)} %get-tuple-element.74.values_ref, bf16[576,1728]{1,0:T(8,128)(2,1)S(1)} %get-tuple-element.75.w_ref, ...), custom_call_target="tpu_custom_call" | custom-call | flops 1528823808 | bytes 1990656 | tf_op jit(solution)/shard_map/conv_2/pallas_call | solution.py:426
  41.7 0.6 %collective-permute-start.8 = (bf16[2,192,128]{2,1,0:T(8,128)(2,1)S(1)}, bf16[2,192,128]{2,1,0:T(8,128)(2,1)S(1)}, u32[]{:S(2)}, u32[]{:S(2)}) collective-permute-start(bf16[2,192,128]{2,1,0:T(8,128)(2,1)S(1)} %get-tuple-element.80), channel_id=1, source_target_pairs={{0,1},{1,0},{2,3},{3,2},{4,5},{5,4},{6,7},{7,6},{8,9},{9,8},{10,11... | collective-permute-start | bytes 294920 | tf_op jit(solution)/shard_map/ppermute | solution.py:483
  42.2 0.8 %join.2.refs_0_ = bf16[4,2,192,128]{3,2,1,0:T(8,128)(2,1)} custom-call(bf16[2,192,128]{2,1,0:T(8,128)(2,1)S(1)} %get-tuple-element.83.kept_ref, bf16[2,192,128]{2,1,0:T(8,128)(2,1)S(1)} %collective-permute-done.9.got_ref), custom_call_target="tpu_custom_call" | custom-call | tf_op jit(solution)/shard_map/join/pallas_call | solution.py:464
  43.0 0.1 collective-permute-done.8.got_ref
  43.2 0.8 %join.3 = bf16[4,2,192,128]{3,2,1,0:T(8,128)(2,1)} custom-call(bf16[2,192,128]{2,1,0:T(8,128)(2,1)S(1)} %get-tuple-element.79.kept_ref, bf16[2,192,128]{2,1,0:T(8,128)(2,1)S(1)} %collective-permute-done.8.got_ref, bf16[4,2,192,128]{3,2,1,0:T(8,128)(2,1)} %join.2.refs_0_), custom_call_target="tpu_custom_call", output_to_operand_aliasing={{}: (2, {})} | custom-call | tf_op jit(solution)/shard_map/join/pallas_call | solution.py:464
  (5 shorter events, 0.0 us)
Async XLA Ops:
  0.0 8.3 %collective-permute-start.1 = (bf16[4,2,192,128]{3,2,1,0:T(8,128)(2,1)}, bf16[4,2,192,128]{3,2,1,0:T(8,128)(2,1)S(1)}, u32[]{:S(2)}, u32[]{:S(2)}) collective-permute-start(bf16[4,2,192,128]{3,2,1,0:T(8,128)(2,1)} %in_ref.1), channel_id=1, source_target_pairs={{0,1},{1,0},{2,3},{3,2},{4,5},{5,4},{6,7},{7,6},{8,9},{9,8},{10,11... | collective-permute-start | bytes 1179656 | tf_op jit(solution)/shard_map/ppermute | solution.py:483
  0.5 1.0 %copy-start = (bf16[4,2,192,128]{3,2,1,0:T(8,128)(2,1)S(1)}, bf16[4,2,192,128]{3,2,1,0:T(8,128)(2,1)}, u32[]{:S(2)}) copy-start(bf16[4,2,192,128]{3,2,1,0:T(8,128)(2,1)} %in_ref.1) | copy-start | bytes 1179652
  1.5 8.1 %collective-permute-start = (bf16[2,2,192,128]{3,2,1,0:T(8,128)(2,1)S(1)}, bf16[2,2,192,128]{3,2,1,0:T(8,128)(2,1)S(1)}, u32[]{:S(2)}, u32[]{:S(2)}) collective-permute-start(bf16[2,2,192,128]{3,2,1,0:T(8,128)(2,1)S(1)} %get-tuple-element.45.refs_1_), channel_id=1, source_target_pairs={{0,2},{1,3},{2,0},{3,1},{4,6},{5,7},{6,4},{7,5},{8,10},{9,11},{10,... | collective-permute-start | bytes 589832 | tf_op jit(solution)/shard_map/ppermute | solution.py:489
  9.6 1.7 %collective-permute-start.2 = (bf16[2,2,192,128]{3,2,1,0:T(8,128)(2,1)S(1)}, bf16[2,2,192,128]{3,2,1,0:T(8,128)(2,1)S(1)}, u32[]{:S(2)}, u32[]{:S(2)}) collective-permute-start(bf16[2,2,192,128]{3,2,1,0:T(8,128)(2,1)S(1)} %collective-permute-done.far_ref), channel_id=1, source_target_pairs={{0,1},{1,0},{2,3},{3,2},{4,5},{5,4},{6,7},{7,6},{8,9},{9,8},{10,11... | collective-permute-start | bytes 589832 | tf_op jit(solution)/shard_map/ppermute | solution.py:483
  9.6 7.3 %collective-permute-start.3 = (bf16[2,2,192,128]{3,2,1,0:T(8,128)(2,1)S(1)}, bf16[2,2,192,128]{3,2,1,0:T(8,128)(2,1)S(1)}, u32[]{:S(2)}, u32[]{:S(2)}) collective-permute-start(bf16[2,2,192,128]{3,2,1,0:T(8,128)(2,1)S(1)} %get-tuple-element.50.refs_0_), channel_id=1, source_target_pairs={{0,2},{1,3},{2,0},{3,1},{4,6},{5,7},{6,4},{7,5},{8,10},{9,11},{10,... | collective-permute-start | bytes 589832 | tf_op jit(solution)/shard_map/ppermute | solution.py:489
  11.9 12.6 %collective-permute-start.5 = (bf16[2,192,512]{2,1,0:T(8,128)(2,1)S(1)}, bf16[2,192,512]{2,1,0:T(8,128)(2,1)S(1)}, u32[]{:S(2)}, u32[]{:S(2)}) collective-permute-start(bf16[2,192,512]{2,1,0:T(8,128)(2,1)S(1)} %get-tuple-element.68), channel_id=1, source_target_pairs={{0,4},{4,8},{8,12},{1,5},{5,9},{9,13},{2,6},{6,10},{10,14},{3,7},{... | collective-permute-start | bytes 1179656 | tf_op jit(solution)/shard_map/ppermute | solution.py:486
  16.9 1.5 %collective-permute-start.4 = (bf16[2,2,192,128]{3,2,1,0:T(8,128)(2,1)S(1)}, bf16[2,2,192,128]{3,2,1,0:T(8,128)(2,1)S(1)}, u32[]{:S(2)}, u32[]{:S(2)}) collective-permute-start(bf16[2,2,192,128]{3,2,1,0:T(8,128)(2,1)S(1)} %collective-permute-done.3.refs_1_), channel_id=1, source_target_pairs={{0,1},{1,0},{2,3},{3,2},{4,5},{5,4},{6,7},{7,6},{8,9},{9,8},{10,11... | collective-permute-start | bytes 589832 | tf_op jit(solution)/shard_map/ppermute | solution.py:483
  20.8 12.9 %collective-permute-start.6 = (bf16[192,896]{1,0:T(8,128)(2,1)S(1)}, bf16[192,896]{1,0:T(8,128)(2,1)S(1)}, u32[]{:S(2)}, u32[]{:S(2)}) collective-permute-start(bf16[192,896]{1,0:T(8,128)(2,1)S(1)} %get-tuple-element.72), channel_id=1, source_target_pairs={{0,4},{4,8},{8,12},{1,5},{5,9},{9,13},{2,6},{6,10},{10,14},{3,7},{... | collective-permute-start | bytes 1032200 | tf_op jit(solution)/shard_map/ppermute | solution.py:486
  29.5 10.3 %collective-permute-start.7 = (bf16[2,192,384]{2,1,0:T(8,128)(2,1)S(1)}, bf16[2,192,384]{2,1,0:T(8,128)(2,1)S(1)}, u32[]{:S(2)}, u32[]{:S(2)}) collective-permute-start(bf16[2,192,384]{2,1,0:T(8,128)(2,1)S(1)} %get-tuple-element.78), channel_id=1, source_target_pairs={{0,4},{4,8},{8,12},{1,5},{5,9},{9,13},{2,6},{6,10},{10,14},{3,7},{... | collective-permute-start | bytes 884744 | tf_op jit(solution)/shard_map/ppermute | solution.py:486
  39.7 2.5 %collective-permute-start.9 = (bf16[2,192,128]{2,1,0:T(8,128)(2,1)S(1)}, bf16[2,192,128]{2,1,0:T(8,128)(2,1)S(1)}, u32[]{:S(2)}, u32[]{:S(2)}) collective-permute-start(bf16[2,192,128]{2,1,0:T(8,128)(2,1)S(1)} %get-tuple-element.84), channel_id=1, source_target_pairs={{0,1},{1,0},{2,3},{3,2},{4,5},{5,4},{6,7},{7,6},{8,9},{9,8},{10,11... | collective-permute-start | bytes 294920 | tf_op jit(solution)/shard_map/ppermute | solution.py:483
  41.7 1.5 %collective-permute-start.8 = (bf16[2,192,128]{2,1,0:T(8,128)(2,1)S(1)}, bf16[2,192,128]{2,1,0:T(8,128)(2,1)S(1)}, u32[]{:S(2)}, u32[]{:S(2)}) collective-permute-start(bf16[2,192,128]{2,1,0:T(8,128)(2,1)S(1)} %get-tuple-element.80), channel_id=1, source_target_pairs={{0,1},{1,0},{2,3},{3,2},{4,5},{5,4},{6,7},{7,6},{8,9},{9,8},{10,11... | collective-permute-start | bytes 294920 | tf_op jit(solution)/shard_map/ppermute | solution.py:483

commit v9 on v7

--- a/solution.py
+++ b/solution.py
@@ -136,7 +136,8 @@
 
 
 def near_kernel(halo, pairs, mate_ref, gains_ref, *refs):
-    own_refs, value_refs, act_refs = refs[:pairs], refs[pairs : 2 * pairs], refs[2 * pairs :]
+    own_refs, value_refs, act_refs = refs[:pairs], refs[pairs : 2 * pairs], refs[2 * pairs : 3 * pairs]
+    send_refs = refs[3 * pairs :]
     frames, rows, _, width = mate_ref.shape
     window = width // 2 + halo
     core, group, outer = place()
@@ -145,13 +146,19 @@
     mask = filled(done, window + 1)
     for f in range(frames):
         p, t = divmod(f, PAIR)
-        blocks = {}
+        blocks, sent = {}, {}
         for row in range(2 * rows):
             at = row % rows
             index = at + group * (rows - 1 - 2 * at)
             own, mate = own_refs[p][t, index], mate_ref[f, index]
             one, two = (own, mate) if row < rows else (mate, own)
-            placed(blocks, core, row, window, jnp.where(outer, one, two).astype(jnp.float32))
+            line = jnp.where(outer, one, two).astype(jnp.float32)
+            placed(blocks, core, row, window, line)
+            there = 4 * rows - 1 - row
+            if p < pairs - 1 and there < 2 * rows + halo:
+                placed(sent, core, there, window, line)
+        for b in sent:
+            send_refs[p][t, :, b * LANES - done : (b + 1) * LANES - done] = sent[b].astype(jnp.bfloat16)
         for b in blocks:
             part = slice(b * LANES, (b + 1) * LANES)
             value_refs[p][t, :, part] = blocks[b].astype(jnp.bfloat16)
@@ -161,44 +168,51 @@
 
 def near(halo, mate, gains, own):
     frames, rows, channels, width = mate.shape
-    lanes = 2 * rows * (width // 2 + halo + 1)
+    pitch = width // 2 + halo + 1
+    lanes = 2 * rows * pitch
+    done = lanes // LANES * LANES
     pairs = len(own)
+    sent = jax.ShapeDtypeStruct((PAIR, channels, rounded(lanes + halo * pitch) - done), jnp.bfloat16)
     outs = pl.pallas_call(
         functools.partial(near_kernel, halo, pairs),
         out_shape=(jax.ShapeDtypeStruct((PAIR, channels, rounded(lanes)), jnp.bfloat16),) * pairs
-        + (jax.ShapeDtypeStruct((PAIR, channels, lanes // LANES * LANES), jnp.bfloat16),) * pairs,
+        + (jax.ShapeDtypeStruct((PAIR, channels, done), jnp.bfloat16),) * pairs
+        + (sent,) * (pairs - 1),
         in_specs=[VMEM] * (2 + pairs),
-        out_specs=(VMEM,) * (2 * pairs),
+        out_specs=(VMEM,) * (3 * pairs - 1),
         compiler_params=pltpu.CompilerParams(vmem_limit_bytes=LIMIT),
         cost_estimate=pl.CostEstimate(flops=40 * mate.size, bytes_accessed=8 * mate.size, transcendentals=2 * mate.size),
         name="near",
     )(mate, gains, *own)
-    return outs[:pairs], outs[pairs:]
-
-
-def add_far(halo, far_ref, mate_ref, near_ref, act_ref, columns_ref, values_ref, shifted_ref, send_ref=None):
-    pair, rows, _, width = far_ref.shape
-    window = width // 2 + halo
+    return outs[:pairs], outs[pairs : 2 * pairs], outs[2 * pairs :]
+
+
+def far_blocks(halo, far_ref, mate_ref, t, blocks):
+    _, rows, _, width = far_ref.shape
     core, group, outer = place()
+    for row in range(2 * rows, 2 * rows + halo):
+        local = 4 * rows - 1 - row
+        at = local % rows
+        index = at + (1 - group) * (rows - 1 - 2 * at)
+        one, two = (mate_ref, far_ref) if local < rows else (far_ref, mate_ref)
+        line = jnp.where(outer, one[t, index], two[t, index]).astype(jnp.float32)
+        placed(blocks, core, row, width // 2 + halo, line)
+
+
+def add_far(pitch, add, near_ref, act_ref, columns_ref, values_ref, shifted_ref, send_ref=None):
     lanes, done = values_ref.shape[2], act_ref.shape[2]
-    mask = filled(lanes, window + 1)
-    for t in range(pair):
+    mask = filled(lanes, pitch)
+    for t in range(PAIR):
         values_ref[t, :, :done] = near_ref[t, :, :done]
         acts = [act_ref[t]]
         blocks = {done // LANES: near_ref[t, :, done:].astype(jnp.float32)}
-        for row in range(2 * rows, 2 * rows + halo):
-            local = 4 * rows - 1 - row
-            at = local % rows
-            index = at + (1 - group) * (rows - 1 - 2 * at)
-            one, two = (mate_ref, far_ref) if local < rows else (far_ref, mate_ref)
-            line = jnp.where(outer, one[t, index], two[t, index]).astype(jnp.float32)
-            placed(blocks, core, row, window, line)
+        add(t, blocks)
         for b in sorted(blocks):
             part = slice(b * LANES, (b + 1) * LANES)
             values_ref[t, :, part] = blocks[b].astype(jnp.bfloat16)
             acts.append(activated(blocks[b], columns_ref[0, 0], mask[:, part]))
         act = jnp.concatenate(acts, axis=1)
-        spread(shifted_ref, t, act, window + 1)
+        spread(shifted_ref, t, act, pitch)
         if send_ref is not None:
             send_ref[t] = act
 
@@ -217,7 +231,8 @@
     values, shifted = far_shapes(rows, halo, channels, width // 2)
 
     def kernel(columns_ref, far_ref, mate_ref, near_ref, act_ref, *outs):
-        add_far(halo, far_ref, mate_ref, near_ref, act_ref, columns_ref, *outs)
+        add = functools.partial(far_blocks, halo, far_ref, mate_ref)
+        add_far(width // 2 + halo + 1, add, near_ref, act_ref, columns_ref, *outs)
 
     return pl.pallas_call(
         kernel,
@@ -298,7 +313,15 @@
     outs = refs
     if plan["builds"]:
         earlier_ref = outs.pop()
-        add_far(pitch - 1 - half, *earlier_refs, columns_ref, outs.pop(), earlier_ref)
+        came_ref, near_ref, act_ref = earlier_refs
+        done = act_ref.shape[2]
+
+        def add(t, blocks):
+            for at in range(0, came_ref.shape[2], LANES):
+                b = (done + at) // LANES
+                blocks[b] = blocks.get(b, 0.0) + came_ref[t, :, at : at + LANES].astype(jnp.float32)
+
+        add_far(pitch, add, near_ref, act_ref, columns_ref, outs.pop(), earlier_ref)
     _, _, channels, lanes = shifted_ref.shape
     chunks = lanes // LANES
     lane = lane_of(LANES)
@@ -338,16 +361,19 @@
         if not last:
             spread(outs[1], t, jnp.concatenate(acts, axis=1), pitch)
             return
-        whole = jnp.concatenate(totals, axis=1)
-        halo = pitch - 1 - half
         core, _, outer = place()
-        whole = jnp.where(core == 1, pltpu.roll(whole, lanes - halo, 1), whole)
-        left_half = lane < half
+        skipped = core * (pitch - 1 - half)
+
+        def columns_of(row, to):
+            b, low = divmod(row * pitch, LANES)
+            shift = lax.rem(to + 2 * LANES - low - skipped, LANES)
+            turned = pltpu.roll(totals[b], shift, 1)
+            if low + pitch - 1 <= LANES:
+                return turned
+            return jnp.where(lane < to + LANES - low - skipped, turned, pltpu.roll(totals[b + 1], shift, 1))
 
         def rows_of(row):
-            one = whole if row == 0 else pltpu.roll(whole, lanes - row * pitch, 1)
-            two = pltpu.roll(whole, lanes - (row + 1) * pitch + half, 1)
-            return jnp.where(left_half, one[:, :LANES], two[:, :LANES])
+            return jnp.where(lane < half, columns_of(row, 0), columns_of(row + 1, half))
 
         outermost, inner = rows_of(0), rows_of(2)
         outs[0][t] = jnp.where(outer, outermost, inner).astype(jnp.bfloat16)
@@ -397,7 +423,7 @@
             out_shape += out_shape[:1]
     scratch = [pltpu.VMEM((PAIR, 3, channels, lanes), jnp.bfloat16)] * received
     if plan["builds"]:
-        out_shape += far_shapes(earlier[0].shape[1], pitch - 1 - half, channels, half)
+        out_shape += far_shapes(plan["rows_near"] // 2, pitch - 1 - half, channels, half)
     return pl.pallas_call(
         functools.partial(conv_kernel, plan),
         out_shape=out_shape,
@@ -406,7 +432,7 @@
         scratch_shapes=scratch,
         compiler_params=pltpu.CompilerParams(vmem_limit_bytes=LIMIT),
         cost_estimate=pl.CostEstimate(
-            flops=54 * channels * channels * PAIR * lanes,
+            flops=54 * channels * channels * PAIR * lanes * (1 + plan["builds"]),
             bytes_accessed=2 * weight.size,
             transcendentals=PAIR * channels * lanes,
         ),
@@ -466,21 +492,20 @@
     mate = mate_of(latents)
     pairs = frames // PAIR
     own = split(latents)
-    far = [beyond_of(own[p]) for p in reversed(range(pairs))][::-1]
+    far = beyond_of(own[-1])
     row_values = jnp.concatenate([norm_gains, biases], axis=0)
     weight, columns = weights(conv_weight, row_values)
-    near_values, near_act = near(layers, mate, row_values, own)
-    far[-1], weight, columns, near_values, near_act = lax.optimization_barrier(
-        (far[-1], weight, columns, near_values, near_act)
+    near_values, near_act, near_sent = near(layers, mate, row_values, own)
+    came = [beyond_of(block) for block in near_sent]
+    far, weight, columns, near_values, near_act = lax.optimization_barrier(
+        (far, weight, columns, near_values, near_act)
     )
     values, shifted = [None] * pairs, [None] * pairs
-    values[-1], shifted[-1], send = beyond(
-        layers, columns, far[-1], mate_of(far[-1]), near_values[-1], near_act[-1]
-    )
+    values[-1], shifted[-1], send = beyond(layers, columns, far, mate_of(far), near_values[-1], near_act[-1])
     halo, rest = earlier_of(send), 0
     first_begun = begin(shifted[-1], weight[0])
-    *far[:-1], first_begun = lax.optimization_barrier((*far[:-1], first_begun))
-    parts = [(far[p], mate_of(far[p]), near_values[p], near_act[p]) for p in reversed(range(pairs - 1))][::-1]
+    *came, first_begun = lax.optimization_barrier((*came, first_begun))
+    parts = [(came[p], near_values[p], near_act[p]) for p in range(pairs - 1)]
     half = width // 2
     pitch = half + layers + 1
     for layer in range(layers):
@@ -498,6 +523,7 @@
             plan = {
                 "layer": layer,
                 "begun": waits,
+                "rows_near": 2 * rows,
                 "last": last,
                 "sends": p == pairs - 1 and not last,
                 "rest_sent": joined(rows_left * pitch),

time: 44.3 us -> 44.8 us (1.011)
  waiting for transfers between devices: 2.23 us -> 2.78 us
    ppermute x3, waiting for transfers between devices: 0.01 us -> 2.09 us  [earlier_of(): return lax.ppermute(block, 'tm', [(i, i + 1) for i in range(blocks - 1)])]
    ppermute x5 -> x4, waiting for transfers between devices: 1.56 us -> 0.13 us  [mate_of(): return lax.ppermute(block, 'rows', [(i, i ^ 1) for i in range(strips)])]
    ppermute x5 -> x4, starting transfers between devices: 1.16 us -> 1.08 us  [mate_of(): return lax.ppermute(block, 'rows', [(i, i ^ 1) for i in range(strips)])]
  transfers between devices with their start and end apart: 10 -> 9, of which waited for: 3 -> 3; matrix products, arithmetic and copies ran while one was open for 2% -> 2% of each run, Pallas kernels for 50% -> 49%
where the time goes in v9:
time: 44.8 us; the launch traced here: 44.6 us
  Pallas kernels  22.5 us (50%)
  starting transfers between devices  17.2 us (38%)
  waiting for transfers between devices  2.78 us (6%)
  local copies, waits for them, and re-layouts  1 us (2%)
  other arithmetic  0.71 us (2%)
    pallas_call x6, Pallas kernels, conv(): pl.pallas_call(functools.partial(conv_kernel, plan), out_shape=out_shape,...  13.2 us
    ppermute x3, starting transfers between devices, earlier_of(): return lax.ppermute(block, 'tm', [(i, i + 1) for i in range(blocks - 1)])  11.8 us
    ppermute x2, starting transfers between devices, beyond_of(): return lax.ppermute(block, 'rows', [(i, i ^ 2) for i in range(strips)])  4.29 us
    pallas_call x1, Pallas kernels, weights(): pl.pallas_call(weights_kernel, out_shape=(one,) * layers + (jax.ShapeDtyp...  3.54 us
    pallas_call x2, Pallas kernels, begin(): pl.pallas_call(begin_kernel, out_shape=jax.ShapeDtypeStruct((PAIR, channe...  2.94 us
    ppermute x3, waiting for transfers between devices, earlier_of(): return lax.ppermute(block, 'tm', [(i, i + 1) for i in range(blocks - 1)])  2.09 us
    pallas_call x2, Pallas kernels, join(): pl.pallas_call(functools.partial(join_kernel, pair), out_shape=jax.ShapeD...  1.62 us
    ppermute x4, starting transfers between devices, mate_of(): return lax.ppermute(block, 'rows', [(i, i ^ 1) for i in range(strips)])  1.08 us
  transfers between devices with their start and end apart: 9, of which 3 were waited for; matrix products, arithmetic and copies ran while one was open for 2% of the time, Pallas kernels for 49%

profile of v9, /device:TPU:0, one launch (start us, length us, event | category | flops | bytes accessed | tf_op | source)
XLA Modules:
  0.0 44.6 jit_solution(6937823520426345132)
XLA Ops:
  0.0 0.5 %collective-permute-start.1 = (bf16[4,2,192,128]{3,2,1,0:T(8,128)(2,1)}, bf16[4,2,192,128]{3,2,1,0:T(8,128)(2,1)S(1)}, u32[]{:S(2)}, u32[]{:S(2)}) collective-permute-start(bf16[4,2,192,128]{3,2,1,0:T(8,128)(2,1)} %in_ref.1), channel_id=1, source_target_pairs={{0,1},{1,0},{2,3},{3,2},{4,5},{5,4},{6,7},{7,6},{8,9},{9,8},{10,11... | collective-permute-start | bytes 1179656 | tf_op jit(solution)/shard_map/ppermute | solution.py:484
  0.5 1.0 %copy-done = bf16[4,2,192,128]{3,2,1,0:T(8,128)(2,1)S(1)} copy-done((bf16[4,2,192,128]{3,2,1,0:T(8,128)(2,1)S(1)}, bf16[4,2,192,128]{3,2,1,0:T(8,128)(2,1)}, u32[]{:S(2)}) %copy-start) | copy-done | bytes 393240
  1.5 2.6 %collective-permute-start = (bf16[2,2,192,128]{3,2,1,0:T(8,128)(2,1)S(1)}, bf16[2,2,192,128]{3,2,1,0:T(8,128)(2,1)S(1)}, u32[]{:S(2)}, u32[]{:S(2)}) collective-permute-start(bf16[2,2,192,128]{3,2,1,0:T(8,128)(2,1)S(1)} %get-tuple-element.46.refs_1_), channel_id=1, source_target_pairs={{0,2},{1,3},{2,0},{3,1},{4,6},{5,7},{6,4},{7,5},{8,10},{9,11},{10,... | collective-permute-start | bytes 589832 | tf_op jit(solution)/shard_map/ppermute | solution.py:490
  4.0 0.7 %pad_maximum_fusion.rows_ref.gains_ref = f32[6,192]{1,0:T(8,128)S(1)} fusion(f32[3,192]{1,0:T(4,128)} %param.7, f32[3,192]{1,0:T(4,128)} %param.6), kind=kLoop, calls=%fused_computation | loop fusion | flops 1152 | bytes 9216 | tf_op jit(solution)/shard_map/concatenate | solution.py:496
  4.7 3.5 %weights.1 = (bf16[576,1728]{1,0:T(8,128)(2,1)S(1)}, bf16[576,1728]{1,0:T(8,128)(2,1)S(1)}, bf16[576,1728]{1,0:T(8,128)(2,1)S(1)}, f32[3,2,192,128]{3,2,1,0:T(8,128)S(1)}) custom-call(bf16[3,27,192,192]{3,2,1,0:T(8,128)(2,1)} %w_ref.1, f32[6,192]{1,0:T(8,128)S(1)} %pad_maximum_fusion.rows_ref.gains_ref), custom_call_target="tpu_custom_call" | custom-call | bytes 11943936 | tf_op jit(solution)/shard_map/weights/pallas_call | solution.py:77
  8.3 0.0 collective-permute-done.1.mate_ref
  8.3 0.7 %near.1 = (bf16[2,192,384]{2,1,0:T(8,128)(2,1)S(1)}, bf16[2,192,384]{2,1,0:T(8,128)(2,1)S(1)}, bf16[2,192,256]{2,1,0:T(8,128)(2,1)S(1)}, bf16[2,192,256]{2,1,0:T(8,128)(2,1)S(1)}, bf16[2,192,256]{2,1,0:T(8,128)(2,1)S(1)}) custom-call(bf16[4,2,192,128]{3,2,1,0:T(8,128)(2,1)S(1)} %collective-permute-done.1.mate_ref, ...), custom_call_target="tpu_custom_call" | custom-call | flops 7864320 | bytes 1572864 | tf_op jit(solution)/shard_map/near/pallas_call | solution.py:176
  9.0 0.6 %collective-permute-done.far_ref = bf16[2,2,192,128]{3,2,1,0:T(8,128)(2,1)S(1)} collective-permute-done((bf16[2,2,192,128]{3,2,1,0:T(8,128)(2,1)S(1)}, bf16[2,2,192,128]{3,2,1,0:T(8,128)(2,1)S(1)}, u32[]{:S(2)}, u32[]{:S(2)}) %collective-permute-start) | collective-permute-done | bytes 196640 | tf_op jit(solution)/shard_map/ppermute | solution.py:490
  9.6 0.0 collective-permute-start.2
  9.6 1.7 %collective-permute-start.3 = (bf16[2,192,256]{2,1,0:T(8,128)(2,1)S(1)}, bf16[2,192,256]{2,1,0:T(8,128)(2,1)S(1)}, u32[]{:S(2)}, u32[]{:S(2)}) collective-permute-start(bf16[2,192,256]{2,1,0:T(8,128)(2,1)S(1)} %get-tuple-element.63), channel_id=1, source_target_pairs={{0,2},{1,3},{2,0},{3,1},{4,6},{5,7},{6,4},{7,5},{8,10},{9,11},{10,... | collective-permute-start | bytes 589832 | tf_op jit(solution)/shard_map/ppermute | solution.py:490
  11.4 0.0 collective-permute-done.2.mate_ref
  11.4 0.5 %beyond.1 = (bf16[2,192,512]{2,1,0:T(8,128)(2,1)S(1)}, bf16[2,3,192,512]{3,2,1,0:T(8,128)(2,1)S(1)}, bf16[2,192,512]{2,1,0:T(8,128)(2,1)S(1)}) custom-call(f32[3,2,192,128]{3,2,1,0:T(8,128)S(1)} %get-tuple-element.56.columns_ref, bf16[2,2,192,128]{3,2,1,0:T(8,128)(2,1)S(1)} %collective-permute-done.far_ref, ...), custom_call_target="tpu_custom_call" | custom-call | flops 3932160 | bytes 786432 | tf_op jit(solution)/shard_map/beyond/pallas_call | solution.py:237
  11.9 3.5 %collective-permute-start.4 = (bf16[2,192,512]{2,1,0:T(8,128)(2,1)S(1)}, bf16[2,192,512]{2,1,0:T(8,128)(2,1)S(1)}, u32[]{:S(2)}, u32[]{:S(2)}) collective-permute-start(bf16[2,192,512]{2,1,0:T(8,128)(2,1)S(1)} %get-tuple-element.70), channel_id=1, source_target_pairs={{0,4},{4,8},{8,12},{1,5},{5,9},{9,13},{2,6},{6,10},{10,14},{3,7},{... | collective-permute-start | bytes 1179656 | tf_op jit(solution)/shard_map/ppermute | solution.py:487
  15.4 1.5 %begin.2.refs_0_ = f32[2,192,512]{2,1,0:T(8,128)S(1)} custom-call(bf16[2,3,192,512]{3,2,1,0:T(8,128)(2,1)S(1)} %get-tuple-element.60.shifted_ref, bf16[576,1728]{1,0:T(8,128)(2,1)S(1)} %get-tuple-element.62.w_ref), custom_call_target="tpu_custom_call" | custom-call | tf_op jit(solution)/shard_map/begin/pallas_call | solution.py:284
  16.9 0.0 collective-permute-done.3.refs_1_
  16.9 2.1 %conv_0.2 = (bf16[2,192,512]{2,1,0:T(8,128)(2,1)S(1)}, bf16[2,3,192,384]{3,2,1,0:T(8,128)(2,1)S(1)}, bf16[192,896]{1,0:T(8,128)(2,1)S(1)}, bf16[2,192,512]{2,1,0:T(8,128)(2,1)S(1)}, bf16[2,3,192,512]{3,2,1,0:T(8,128)(2,1)S(1)}) custom-call(bf16[2,3,192,512]{3,2,1,0:T(8,128)(2,1)S(1)} %get-tuple-element.60.shifted_ref, ...), custom_call_target="tpu_custom_call" | custom-call | flops 4076863488 | bytes 1990656 | tf_op jit(solution)/shard_map/conv_0/pallas_call | solution.py:427
  19.0 3.7 %collective-permute-start.5 = (bf16[192,896]{1,0:T(8,128)(2,1)S(1)}, bf16[192,896]{1,0:T(8,128)(2,1)S(1)}, u32[]{:S(2)}, u32[]{:S(2)}) collective-permute-start(bf16[192,896]{1,0:T(8,128)(2,1)S(1)} %get-tuple-element.74), channel_id=1, source_target_pairs={{0,4},{4,8},{8,12},{1,5},{5,9},{9,13},{2,6},{6,10},{10,14},{3,7},{... | collective-permute-start | bytes 1032200 | tf_op jit(solution)/shard_map/ppermute | solution.py:487
  22.7 2.1 %collective-permute-done.4.refs_0_ = bf16[2,192,512]{2,1,0:T(8,128)(2,1)S(1)} collective-permute-done((bf16[2,192,512]{2,1,0:T(8,128)(2,1)S(1)}, bf16[2,192,512]{2,1,0:T(8,128)(2,1)S(1)}, u32[]{:S(2)}, u32[]{:S(2)}) %collective-permute-start.4) | collective-permute-done | bytes 393248 | tf_op jit(solution)/shard_map/ppermute | solution.py:487
  24.8 2.8 %conv_0.3 = (bf16[2,192,512]{2,1,0:T(8,128)(2,1)S(1)}, bf16[2,3,192,384]{3,2,1,0:T(8,128)(2,1)S(1)}) custom-call(bf16[2,3,192,512]{3,2,1,0:T(8,128)(2,1)S(1)} %get-tuple-element.68.shifted_ref, bf16[2,192,512]{2,1,0:T(8,128)(2,1)S(1)} %get-tuple-element.69.values_ref, bf16[576,1728]{1,0:T(8,128)(2,1)S(1)} %get-tuple-element.62.w_ref, ...), custom_call_target="tpu_custom_call" | custom-call | flops 2038431744 | bytes 1990656 | tf_op jit(solution)/shard_map/conv_0/pallas_call | solution.py:427
  27.6 2.2 %conv_1.3 = (bf16[2,192,384]{2,1,0:T(8,128)(2,1)S(1)}, bf16[2,3,192,384]{3,2,1,0:T(8,128)(2,1)S(1)}, bf16[2,192,384]{2,1,0:T(8,128)(2,1)S(1)}) custom-call(bf16[2,3,192,384]{3,2,1,0:T(8,128)(2,1)S(1)} %get-tuple-element.78.shifted_ref, bf16[2,192,512]{2,1,0:T(8,128)(2,1)S(1)} %get-tuple-element.79.values_ref, bf16[576,1728]{1,0:T(8,128)(2,1)S(1)} %get-tuple-element.73.w_ref, ...), custom_call_target="tpu_custom_call" | custom-call | flops 1528823808 | bytes 1990656 | tf_op jit(solution)/shard_map/conv_1/pallas_call | solution.py:427
  29.9 4.6 %collective-permute-start.6 = (bf16[2,192,384]{2,1,0:T(8,128)(2,1)S(1)}, bf16[2,192,384]{2,1,0:T(8,128)(2,1)S(1)}, u32[]{:S(2)}, u32[]{:S(2)}) collective-permute-start(bf16[2,192,384]{2,1,0:T(8,128)(2,1)S(1)} %get-tuple-element.80), channel_id=1, source_target_pairs={{0,4},{4,8},{8,12},{1,5},{5,9},{9,13},{2,6},{6,10},{10,14},{3,7},{... | collective-permute-start | bytes 884744 | tf_op jit(solution)/shard_map/ppermute | solution.py:487
  34.4 0.0 collective-permute-done.5.refs_0_
  34.5 2.3 %conv_1.2 = (bf16[2,192,384]{2,1,0:T(8,128)(2,1)S(1)}, bf16[2,3,192,384]{3,2,1,0:T(8,128)(2,1)S(1)}) custom-call(bf16[2,3,192,384]{3,2,1,0:T(8,128)(2,1)S(1)} %get-tuple-element.71.shifted_ref.refs_0_, bf16[2,192,512]{2,1,0:T(8,128)(2,1)S(1)} %get-tuple-element.72.values_ref, bf16[576,1728]{1,0:T(8,128)(2,1)S(1)} %get-tuple-element.73.w_ref, ...), custom_call_target="tpu_custom_call" | custom-call | flops 1528823808 | bytes 1990656 | tf_op jit(solution)/shard_map/conv_1/pallas_call | solution.py:427
  36.7 1.4 %begin.3.refs_0_ = f32[2,192,384]{2,1,0:T(8,128)S(1)} custom-call(bf16[2,3,192,384]{3,2,1,0:T(8,128)(2,1)S(1)} %get-tuple-element.75.shifted_ref.refs_0_, bf16[576,1728]{1,0:T(8,128)(2,1)S(1)} %get-tuple-element.77.w_ref), custom_call_target="tpu_custom_call" | custom-call | tf_op jit(solution)/shard_map/begin/pallas_call | solution.py:284
  38.2 2.1 %conv_2.3 = (bf16[2,192,128]{2,1,0:T(8,128)(2,1)S(1)}, bf16[2,192,128]{2,1,0:T(8,128)(2,1)S(1)}) custom-call(bf16[2,3,192,384]{3,2,1,0:T(8,128)(2,1)S(1)} %get-tuple-element.83.shifted_ref, bf16[2,192,384]{2,1,0:T(8,128)(2,1)S(1)} %get-tuple-element.84.values_ref, bf16[576,1728]{1,0:T(8,128)(2,1)S(1)} %get-tuple-element.77.w_ref, ...), custom_call_target="tpu_custom_call" | custom-call | flops 1528823808 | bytes 1990656 | tf_op jit(solution)/shard_map/conv_2/pallas_call | solution.py:427
  40.2 0.1 collective-permute-start.8
  40.3 1.8 %conv_2.2 = (bf16[2,192,128]{2,1,0:T(8,128)(2,1)S(1)}, bf16[2,192,128]{2,1,0:T(8,128)(2,1)S(1)}) custom-call(bf16[2,3,192,384]{3,2,1,0:T(8,128)(2,1)S(1)} %get-tuple-element.75.shifted_ref.refs_0_, bf16[2,192,384]{2,1,0:T(8,128)(2,1)S(1)} %get-tuple-element.76.values_ref, bf16[576,1728]{1,0:T(8,128)(2,1)S(1)} %get-tuple-element.77.w_ref, ...), custom_call_target="tpu_custom_call" | custom-call | flops 1528823808 | bytes 1990656 | tf_op jit(solution)/shard_map/conv_2/pallas_call | solution.py:427
  42.1 0.6 %collective-permute-start.7 = (bf16[2,192,128]{2,1,0:T(8,128)(2,1)S(1)}, bf16[2,192,128]{2,1,0:T(8,128)(2,1)S(1)}, u32[]{:S(2)}, u32[]{:S(2)}) collective-permute-start(bf16[2,192,128]{2,1,0:T(8,128)(2,1)S(1)} %get-tuple-element.82), channel_id=1, source_target_pairs={{0,1},{1,0},{2,3},{3,2},{4,5},{5,4},{6,7},{7,6},{8,9},{9,8},{10,11... | collective-permute-start | bytes 294920 | tf_op jit(solution)/shard_map/ppermute | solution.py:484
  42.6 0.0 collective-permute-done.8.got_ref
  42.6 0.8 %join.2.refs_0_ = bf16[4,2,192,128]{3,2,1,0:T(8,128)(2,1)} custom-call(bf16[2,192,128]{2,1,0:T(8,128)(2,1)S(1)} %get-tuple-element.85.kept_ref, bf16[2,192,128]{2,1,0:T(8,128)(2,1)S(1)} %collective-permute-done.8.got_ref), custom_call_target="tpu_custom_call" | custom-call | tf_op jit(solution)/shard_map/join/pallas_call | solution.py:465
  43.5 0.1 collective-permute-done.7.got_ref
  43.6 0.8 %join.3 = bf16[4,2,192,128]{3,2,1,0:T(8,128)(2,1)} custom-call(bf16[2,192,128]{2,1,0:T(8,128)(2,1)S(1)} %get-tuple-element.81.kept_ref, bf16[2,192,128]{2,1,0:T(8,128)(2,1)S(1)} %collective-permute-done.7.got_ref, bf16[4,2,192,128]{3,2,1,0:T(8,128)(2,1)} %join.2.refs_0_), custom_call_target="tpu_custom_call", output_to_operand_aliasing={{}: (2, {})} | custom-call | tf_op jit(solution)/shard_map/join/pallas_call | solution.py:465
  (3 shorter events, 0.0 us)
Async XLA Ops:
  0.0 8.3 %collective-permute-start.1 = (bf16[4,2,192,128]{3,2,1,0:T(8,128)(2,1)}, bf16[4,2,192,128]{3,2,1,0:T(8,128)(2,1)S(1)}, u32[]{:S(2)}, u32[]{:S(2)}) collective-permute-start(bf16[4,2,192,128]{3,2,1,0:T(8,128)(2,1)} %in_ref.1), channel_id=1, source_target_pairs={{0,1},{1,0},{2,3},{3,2},{4,5},{5,4},{6,7},{7,6},{8,9},{9,8},{10,11... | collective-permute-start | bytes 1179656 | tf_op jit(solution)/shard_map/ppermute | solution.py:484
  0.5 1.0 %copy-start = (bf16[4,2,192,128]{3,2,1,0:T(8,128)(2,1)S(1)}, bf16[4,2,192,128]{3,2,1,0:T(8,128)(2,1)}, u32[]{:S(2)}) copy-start(bf16[4,2,192,128]{3,2,1,0:T(8,128)(2,1)} %in_ref.1) | copy-start | bytes 1179652
  1.5 8.1 %collective-permute-start = (bf16[2,2,192,128]{3,2,1,0:T(8,128)(2,1)S(1)}, bf16[2,2,192,128]{3,2,1,0:T(8,128)(2,1)S(1)}, u32[]{:S(2)}, u32[]{:S(2)}) collective-permute-start(bf16[2,2,192,128]{3,2,1,0:T(8,128)(2,1)S(1)} %get-tuple-element.46.refs_1_), channel_id=1, source_target_pairs={{0,2},{1,3},{2,0},{3,1},{4,6},{5,7},{6,4},{7,5},{8,10},{9,11},{10,... | collective-permute-start | bytes 589832 | tf_op jit(solution)/shard_map/ppermute | solution.py:490
  9.6 1.7 %collective-permute-start.2 = (bf16[2,2,192,128]{3,2,1,0:T(8,128)(2,1)S(1)}, bf16[2,2,192,128]{3,2,1,0:T(8,128)(2,1)S(1)}, u32[]{:S(2)}, u32[]{:S(2)}) collective-permute-start(bf16[2,2,192,128]{3,2,1,0:T(8,128)(2,1)S(1)} %collective-permute-done.far_ref), channel_id=1, source_target_pairs={{0,1},{1,0},{2,3},{3,2},{4,5},{5,4},{6,7},{7,6},{8,9},{9,8},{10,11... | collective-permute-start | bytes 589832 | tf_op jit(solution)/shard_map/ppermute | solution.py:484
  9.6 7.3 %collective-permute-start.3 = (bf16[2,192,256]{2,1,0:T(8,128)(2,1)S(1)}, bf16[2,192,256]{2,1,0:T(8,128)(2,1)S(1)}, u32[]{:S(2)}, u32[]{:S(2)}) collective-permute-start(bf16[2,192,256]{2,1,0:T(8,128)(2,1)S(1)} %get-tuple-element.63), channel_id=1, source_target_pairs={{0,2},{1,3},{2,0},{3,1},{4,6},{5,7},{6,4},{7,5},{8,10},{9,11},{10,... | collective-permute-start | bytes 589832 | tf_op jit(solution)/shard_map/ppermute | solution.py:490
  11.9 12.9 %collective-permute-start.4 = (bf16[2,192,512]{2,1,0:T(8,128)(2,1)S(1)}, bf16[2,192,512]{2,1,0:T(8,128)(2,1)S(1)}, u32[]{:S(2)}, u32[]{:S(2)}) collective-permute-start(bf16[2,192,512]{2,1,0:T(8,128)(2,1)S(1)} %get-tuple-element.70), channel_id=1, source_target_pairs={{0,4},{4,8},{8,12},{1,5},{5,9},{9,13},{2,6},{6,10},{10,14},{3,7},{... | collective-permute-start | bytes 1179656 | tf_op jit(solution)/shard_map/ppermute | solution.py:487
  19.0 15.4 %collective-permute-start.5 = (bf16[192,896]{1,0:T(8,128)(2,1)S(1)}, bf16[192,896]{1,0:T(8,128)(2,1)S(1)}, u32[]{:S(2)}, u32[]{:S(2)}) collective-permute-start(bf16[192,896]{1,0:T(8,128)(2,1)S(1)} %get-tuple-element.74), channel_id=1, source_target_pairs={{0,4},{4,8},{8,12},{1,5},{5,9},{9,13},{2,6},{6,10},{10,14},{3,7},{... | collective-permute-start | bytes 1032200 | tf_op jit(solution)/shard_map/ppermute | solution.py:487
  29.9 10.5 %collective-permute-start.6 = (bf16[2,192,384]{2,1,0:T(8,128)(2,1)S(1)}, bf16[2,192,384]{2,1,0:T(8,128)(2,1)S(1)}, u32[]{:S(2)}, u32[]{:S(2)}) collective-permute-start(bf16[2,192,384]{2,1,0:T(8,128)(2,1)S(1)} %get-tuple-element.80), channel_id=1, source_target_pairs={{0,4},{4,8},{8,12},{1,5},{5,9},{9,13},{2,6},{6,10},{10,14},{3,7},{... | collective-permute-start | bytes 884744 | tf_op jit(solution)/shard_map/ppermute | solution.py:487
  40.2 2.4 %collective-permute-start.8 = (bf16[2,192,128]{2,1,0:T(8,128)(2,1)S(1)}, bf16[2,192,128]{2,1,0:T(8,128)(2,1)S(1)}, u32[]{:S(2)}, u32[]{:S(2)}) collective-permute-start(bf16[2,192,128]{2,1,0:T(8,128)(2,1)S(1)} %get-tuple-element.86), channel_id=1, source_target_pairs={{0,1},{1,0},{2,3},{3,2},{4,5},{5,4},{6,7},{7,6},{8,9},{9,8},{10,11... | collective-permute-start | bytes 294920 | tf_op jit(solution)/shard_map/ppermute | solution.py:484
  42.1 1.5 %collective-permute-start.7 = (bf16[2,192,128]{2,1,0:T(8,128)(2,1)S(1)}, bf16[2,192,128]{2,1,0:T(8,128)(2,1)S(1)}, u32[]{:S(2)}, u32[]{:S(2)}) collective-permute-start(bf16[2,192,128]{2,1,0:T(8,128)(2,1)S(1)} %get-tuple-element.82), channel_id=1, source_target_pairs={{0,1},{1,0},{2,3},{3,2},{4,5},{5,4},{6,7},{7,6},{8,9},{9,8},{10,11... | collective-permute-start | bytes 294920 | tf_op jit(solution)/shard_map/ppermute | solution.py:484

commit v10 on v9

--- a/solution.py
+++ b/solution.py
@@ -503,6 +503,7 @@
     values, shifted = [None] * pairs, [None] * pairs
     values[-1], shifted[-1], send = beyond(layers, columns, far, mate_of(far), near_values[-1], near_act[-1])
     halo, rest = earlier_of(send), 0
+    next_begun = None
     first_begun = begin(shifted[-1], weight[0])
     *came, first_begun = lax.optimization_barrier((*came, first_begun))
     parts = [(came[p], near_values[p], near_act[p]) for p in range(pairs - 1)]
@@ -515,9 +516,11 @@
         for p in reversed(range(pairs)):
             builds = layer == 0 and p > 0
             earlier = (halo,) if p == 0 else parts[p - 1] if builds else (shifted[p - 1],)
-            waits = builds or (last and p == 0)
+            waits = builds or (p == 0 and (last or layer == 0))
             if builds and p == pairs - 1:
                 begun = (first_begun,)
+            elif layer == 0 and p == 0 and next_begun is not None:
+                begun = (next_begun,)
             else:
                 begun = (begin(shifted[p], weight[layer]),) if waits else ()
             plan = {
@@ -540,7 +543,11 @@
                 shifted[p - 1], values[p - 1] = outs.pop(), outs.pop()
             results[p] = outs
             if plan["sends"]:
-                arriving = earlier_of(outs[2])
+                message = outs[2]
+                if layer == 0 and p == 1:
+                    next_begun = begin(shifted[0], weight[0])
+                    message, next_begun = lax.optimization_barrier((message, next_begun))
+                arriving = earlier_of(message)
         values, shifted = [r[0] for r in results], [r[1] for r in results]
         if not last:
             halo, rest = arriving, joined(rows_left * pitch)

time: 44.8 us -> 43.3 us (0.967)
  waiting for transfers between devices: 2.78 us -> 0.71 us
  Pallas kernels: 22.5 us -> 23.3 us
    ppermute x3, waiting for transfers between devices: 2.09 us -> 0.01 us  [earlier_of(): return lax.ppermute(block, 'tm', [(i, i + 1) for i in range(blocks - 1)])]
    pallas_call x2 -> x3, Pallas kernels: 2.94 us -> 4.46 us  [begin(): pl.pallas_call(begin_kernel, out_shape=jax.ShapeDtypeStruct((PAIR, channe...]
    pallas_call x6, Pallas kernels: 13.2 us -> 12.4 us  [conv(): pl.pallas_call(functools.partial(conv_kernel, plan), out_shape=out_shape,...]
  transfers between devices with their start and end apart: 9 -> 9, of which waited for: 3 -> 2; matrix products, arithmetic and copies ran while one was open for 2% -> 2% of each run, Pallas kernels for 49% -> 52%
where the time goes in v10:
time: 43.3 us; the launch traced here: 43.1 us
  Pallas kernels  23.3 us (54%)
  starting transfers between devices  17.1 us (39%)
  local copies, waits for them, and re-layouts  1 us (2%)
  other arithmetic  0.71 us (2%)
  waiting for transfers between devices  0.71 us (2%)
    pallas_call x6, Pallas kernels, conv(): pl.pallas_call(functools.partial(conv_kernel, plan), out_shape=out_shape,...  12.4 us
    ppermute x3, starting transfers between devices, earlier_of(): return lax.ppermute(block, 'tm', [(i, i + 1) for i in range(blocks - 1)])  11.7 us
    pallas_call x3, Pallas kernels, begin(): pl.pallas_call(begin_kernel, out_shape=jax.ShapeDtypeStruct((PAIR, channe...  4.46 us
    ppermute x2, starting transfers between devices, beyond_of(): return lax.ppermute(block, 'rows', [(i, i ^ 2) for i in range(strips)])  4.29 us
    pallas_call x1, Pallas kernels, weights(): pl.pallas_call(weights_kernel, out_shape=(one,) * layers + (jax.ShapeDtyp...  3.54 us
    pallas_call x2, Pallas kernels, join(): pl.pallas_call(functools.partial(join_kernel, pair), out_shape=jax.ShapeD...  1.62 us
    ppermute x4, starting transfers between devices, mate_of(): return lax.ppermute(block, 'rows', [(i, i ^ 1) for i in range(strips)])  1.09 us
    unnamed x2, local copies, waits for them, and re-layouts  1 us
  transfers between devices with their start and end apart: 9, of which 2 were waited for; matrix products, arithmetic and copies ran while one was open for 2% of the time, Pallas kernels for 52%

profile of v10, /device:TPU:0, one launch (start us, length us, event | category | flops | bytes accessed | tf_op | source)
XLA Modules:
  0.0 43.1 jit_solution(7821364294326842149)
XLA Ops:
  0.0 0.5 %collective-permute-start.1 = (bf16[4,2,192,128]{3,2,1,0:T(8,128)(2,1)}, bf16[4,2,192,128]{3,2,1,0:T(8,128)(2,1)S(1)}, u32[]{:S(2)}, u32[]{:S(2)}) collective-permute-start(bf16[4,2,192,128]{3,2,1,0:T(8,128)(2,1)} %in_ref.1), channel_id=1, source_target_pairs={{0,1},{1,0},{2,3},{3,2},{4,5},{5,4},{6,7},{7,6},{8,9},{9,8},{10,11... | collective-permute-start | bytes 1179656 | tf_op jit(solution)/shard_map/ppermute | solution.py:484
  0.5 1.0 %copy-done = bf16[4,2,192,128]{3,2,1,0:T(8,128)(2,1)S(1)} copy-done((bf16[4,2,192,128]{3,2,1,0:T(8,128)(2,1)S(1)}, bf16[4,2,192,128]{3,2,1,0:T(8,128)(2,1)}, u32[]{:S(2)}) %copy-start) | copy-done | bytes 393240
  1.5 2.6 %collective-permute-start = (bf16[2,2,192,128]{3,2,1,0:T(8,128)(2,1)S(1)}, bf16[2,2,192,128]{3,2,1,0:T(8,128)(2,1)S(1)}, u32[]{:S(2)}, u32[]{:S(2)}) collective-permute-start(bf16[2,2,192,128]{3,2,1,0:T(8,128)(2,1)S(1)} %get-tuple-element.48.refs_1_), channel_id=1, source_target_pairs={{0,2},{1,3},{2,0},{3,1},{4,6},{5,7},{6,4},{7,5},{8,10},{9,11},{10,... | collective-permute-start | bytes 589832 | tf_op jit(solution)/shard_map/ppermute | solution.py:490
  4.0 0.7 %pad_maximum_fusion.rows_ref.gains_ref = f32[6,192]{1,0:T(8,128)S(1)} fusion(f32[3,192]{1,0:T(4,128)} %param.7, f32[3,192]{1,0:T(4,128)} %param.6), kind=kLoop, calls=%fused_computation | loop fusion | flops 1152 | bytes 9216 | tf_op jit(solution)/shard_map/concatenate | solution.py:496
  4.7 3.5 %weights.1 = (bf16[576,1728]{1,0:T(8,128)(2,1)S(1)}, bf16[576,1728]{1,0:T(8,128)(2,1)S(1)}, bf16[576,1728]{1,0:T(8,128)(2,1)S(1)}, f32[3,2,192,128]{3,2,1,0:T(8,128)S(1)}) custom-call(bf16[3,27,192,192]{3,2,1,0:T(8,128)(2,1)} %w_ref.1, f32[6,192]{1,0:T(8,128)S(1)} %pad_maximum_fusion.rows_ref.gains_ref), custom_call_target="tpu_custom_call" | custom-call | bytes 11943936 | tf_op jit(solution)/shard_map/weights/pallas_call | solution.py:77
  8.3 0.7 %near.1 = (bf16[2,192,384]{2,1,0:T(8,128)(2,1)S(1)}, bf16[2,192,384]{2,1,0:T(8,128)(2,1)S(1)}, bf16[2,192,256]{2,1,0:T(8,128)(2,1)S(1)}, bf16[2,192,256]{2,1,0:T(8,128)(2,1)S(1)}, bf16[2,192,256]{2,1,0:T(8,128)(2,1)S(1)}) custom-call(bf16[4,2,192,128]{3,2,1,0:T(8,128)(2,1)S(1)} %collective-permute-done.1.mate_ref, ...), custom_call_target="tpu_custom_call" | custom-call | flops 7864320 | bytes 1572864 | tf_op jit(solution)/shard_map/near/pallas_call | solution.py:176
  9.0 0.6 %collective-permute-done.far_ref = bf16[2,2,192,128]{3,2,1,0:T(8,128)(2,1)S(1)} collective-permute-done((bf16[2,2,192,128]{3,2,1,0:T(8,128)(2,1)S(1)}, bf16[2,2,192,128]{3,2,1,0:T(8,128)(2,1)S(1)}, u32[]{:S(2)}, u32[]{:S(2)}) %collective-permute-start) | collective-permute-done | bytes 196640 | tf_op jit(solution)/shard_map/ppermute | solution.py:490
  9.6 0.0 collective-permute-start.2
  9.6 1.7 %collective-permute-start.3 = (bf16[2,192,256]{2,1,0:T(8,128)(2,1)S(1)}, bf16[2,192,256]{2,1,0:T(8,128)(2,1)S(1)}, u32[]{:S(2)}, u32[]{:S(2)}) collective-permute-start(bf16[2,192,256]{2,1,0:T(8,128)(2,1)S(1)} %get-tuple-element.65), channel_id=1, source_target_pairs={{0,2},{1,3},{2,0},{3,1},{4,6},{5,7},{6,4},{7,5},{8,10},{9,11},{10,... | collective-permute-start | bytes 589832 | tf_op jit(solution)/shard_map/ppermute | solution.py:490
  11.4 0.0 collective-permute-done.2.mate_ref
  11.4 0.5 %beyond.1 = (bf16[2,192,512]{2,1,0:T(8,128)(2,1)S(1)}, bf16[2,3,192,512]{3,2,1,0:T(8,128)(2,1)S(1)}, bf16[2,192,512]{2,1,0:T(8,128)(2,1)S(1)}) custom-call(f32[3,2,192,128]{3,2,1,0:T(8,128)S(1)} %get-tuple-element.58.columns_ref, bf16[2,2,192,128]{3,2,1,0:T(8,128)(2,1)S(1)} %collective-permute-done.far_ref, ...), custom_call_target="tpu_custom_call" | custom-call | flops 3932160 | bytes 786432 | tf_op jit(solution)/shard_map/beyond/pallas_call | solution.py:237
  11.9 3.5 %collective-permute-start.4 = (bf16[2,192,512]{2,1,0:T(8,128)(2,1)S(1)}, bf16[2,192,512]{2,1,0:T(8,128)(2,1)S(1)}, u32[]{:S(2)}, u32[]{:S(2)}) collective-permute-start(bf16[2,192,512]{2,1,0:T(8,128)(2,1)S(1)} %get-tuple-element.74), channel_id=1, source_target_pairs={{0,4},{4,8},{8,12},{1,5},{5,9},{9,13},{2,6},{6,10},{10,14},{3,7},{... | collective-permute-start | bytes 1179656 | tf_op jit(solution)/shard_map/ppermute | solution.py:487
  15.4 1.5 %begin.3.refs_0_ = f32[2,192,512]{2,1,0:T(8,128)S(1)} custom-call(bf16[2,3,192,512]{3,2,1,0:T(8,128)(2,1)S(1)} %get-tuple-element.62.shifted_ref, bf16[576,1728]{1,0:T(8,128)(2,1)S(1)} %get-tuple-element.64.w_ref), custom_call_target="tpu_custom_call" | custom-call | tf_op jit(solution)/shard_map/begin/pallas_call | solution.py:284
  16.9 0.0 collective-permute-done.3.refs_1_
  16.9 2.1 %conv_0.2 = (bf16[2,192,512]{2,1,0:T(8,128)(2,1)S(1)}, bf16[2,3,192,384]{3,2,1,0:T(8,128)(2,1)S(1)}, bf16[192,896]{1,0:T(8,128)(2,1)S(1)}, bf16[2,192,512]{2,1,0:T(8,128)(2,1)S(1)}, bf16[2,3,192,512]{3,2,1,0:T(8,128)(2,1)S(1)}) custom-call(bf16[2,3,192,512]{3,2,1,0:T(8,128)(2,1)S(1)} %get-tuple-element.62.shifted_ref, ...), custom_call_target="tpu_custom_call" | custom-call | flops 4076863488 | bytes 1990656 | tf_op jit(solution)/shard_map/conv_0/pallas_call | solution.py:427
  19.0 1.5 %begin.4.refs_0_ = f32[2,192,512]{2,1,0:T(8,128)S(1)} custom-call(bf16[2,3,192,512]{3,2,1,0:T(8,128)(2,1)S(1)} %get-tuple-element.70.shifted_ref, bf16[576,1728]{1,0:T(8,128)(2,1)S(1)} %get-tuple-element.64.w_ref), custom_call_target="tpu_custom_call" | custom-call | tf_op jit(solution)/shard_map/begin/pallas_call | solution.py:284
  20.5 3.7 %collective-permute-start.5 = (bf16[192,896]{1,0:T(8,128)(2,1)S(1)}, bf16[192,896]{1,0:T(8,128)(2,1)S(1)}, u32[]{:S(2)}, u32[]{:S(2)}) collective-permute-start(bf16[192,896]{1,0:T(8,128)(2,1)S(1)} %get-tuple-element.78), channel_id=1, source_target_pairs={{0,4},{4,8},{8,12},{1,5},{5,9},{9,13},{2,6},{6,10},{10,14},{3,7},{... | collective-permute-start | bytes 1032200 | tf_op jit(solution)/shard_map/ppermute | solution.py:487
  24.3 0.0 collective-permute-done.4.refs_1_
  24.3 2.0 %conv_0.3 = (bf16[2,192,512]{2,1,0:T(8,128)(2,1)S(1)}, bf16[2,3,192,384]{3,2,1,0:T(8,128)(2,1)S(1)}) custom-call(bf16[2,3,192,512]{3,2,1,0:T(8,128)(2,1)S(1)} %get-tuple-element.70.shifted_ref, bf16[2,192,512]{2,1,0:T(8,128)(2,1)S(1)} %get-tuple-element.71.values_ref, bf16[576,1728]{1,0:T(8,128)(2,1)S(1)} %get-tuple-element.64.w_ref, ...), custom_call_target="tpu_custom_call" | custom-call | flops 2038431744 | bytes 1990656 | tf_op jit(solution)/shard_map/conv_0/pallas_call | solution.py:427
  26.2 2.3 %conv_1.3 = (bf16[2,192,384]{2,1,0:T(8,128)(2,1)S(1)}, bf16[2,3,192,384]{3,2,1,0:T(8,128)(2,1)S(1)}, bf16[2,192,384]{2,1,0:T(8,128)(2,1)S(1)}) custom-call(bf16[2,3,192,384]{3,2,1,0:T(8,128)(2,1)S(1)} %get-tuple-element.82.shifted_ref, bf16[2,192,512]{2,1,0:T(8,128)(2,1)S(1)} %get-tuple-element.83.values_ref, bf16[576,1728]{1,0:T(8,128)(2,1)S(1)} %get-tuple-element.77.w_ref, ...), custom_call_target="tpu_custom_call" | custom-call | flops 1528823808 | bytes 1990656 | tf_op jit(solution)/shard_map/conv_1/pallas_call | solution.py:427
  28.5 4.4 %collective-permute-start.6 = (bf16[2,192,384]{2,1,0:T(8,128)(2,1)S(1)}, bf16[2,192,384]{2,1,0:T(8,128)(2,1)S(1)}, u32[]{:S(2)}, u32[]{:S(2)}) collective-permute-start(bf16[2,192,384]{2,1,0:T(8,128)(2,1)S(1)} %get-tuple-element.84), channel_id=1, source_target_pairs={{0,4},{4,8},{8,12},{1,5},{5,9},{9,13},{2,6},{6,10},{10,14},{3,7},{... | collective-permute-start | bytes 884744 | tf_op jit(solution)/shard_map/ppermute | solution.py:487
  32.9 0.0 collective-permute-done.5.refs_0_
  33.0 2.3 %conv_1.2 = (bf16[2,192,384]{2,1,0:T(8,128)(2,1)S(1)}, bf16[2,3,192,384]{3,2,1,0:T(8,128)(2,1)S(1)}) custom-call(bf16[2,3,192,384]{3,2,1,0:T(8,128)(2,1)S(1)} %get-tuple-element.75.shifted_ref.refs_0_, bf16[2,192,512]{2,1,0:T(8,128)(2,1)S(1)} %get-tuple-element.76.values_ref, bf16[576,1728]{1,0:T(8,128)(2,1)S(1)} %get-tuple-element.77.w_ref, ...), custom_call_target="tpu_custom_call" | custom-call | flops 1528823808 | bytes 1990656 | tf_op jit(solution)/shard_map/conv_1/pallas_call | solution.py:427
  35.2 1.4 %begin.5.refs_0_ = f32[2,192,384]{2,1,0:T(8,128)S(1)} custom-call(bf16[2,3,192,384]{3,2,1,0:T(8,128)(2,1)S(1)} %get-tuple-element.79.shifted_ref.refs_0_, bf16[576,1728]{1,0:T(8,128)(2,1)S(1)} %get-tuple-element.81.w_ref), custom_call_target="tpu_custom_call" | custom-call | tf_op jit(solution)/shard_map/begin/pallas_call | solution.py:284
  36.7 2.1 %conv_2.3 = (bf16[2,192,128]{2,1,0:T(8,128)(2,1)S(1)}, bf16[2,192,128]{2,1,0:T(8,128)(2,1)S(1)}) custom-call(bf16[2,3,192,384]{3,2,1,0:T(8,128)(2,1)S(1)} %get-tuple-element.87.shifted_ref, bf16[2,192,384]{2,1,0:T(8,128)(2,1)S(1)} %get-tuple-element.88.values_ref, bf16[576,1728]{1,0:T(8,128)(2,1)S(1)} %get-tuple-element.81.w_ref, ...), custom_call_target="tpu_custom_call" | custom-call | flops 1528823808 | bytes 1990656 | tf_op jit(solution)/shard_map/conv_2/pallas_call | solution.py:427
  38.8 0.1 collective-permute-start.8
  38.8 0.0 collective-permute-done.6.refs_1_
  38.8 1.8 %conv_2.2 = (bf16[2,192,128]{2,1,0:T(8,128)(2,1)S(1)}, bf16[2,192,128]{2,1,0:T(8,128)(2,1)S(1)}) custom-call(bf16[2,3,192,384]{3,2,1,0:T(8,128)(2,1)S(1)} %get-tuple-element.79.shifted_ref.refs_0_, bf16[2,192,384]{2,1,0:T(8,128)(2,1)S(1)} %get-tuple-element.80.values_ref, bf16[576,1728]{1,0:T(8,128)(2,1)S(1)} %get-tuple-element.81.w_ref, ...), custom_call_target="tpu_custom_call" | custom-call | flops 1528823808 | bytes 1990656 | tf_op jit(solution)/shard_map/conv_2/pallas_call | solution.py:427
  40.6 0.6 %collective-permute-start.7 = (bf16[2,192,128]{2,1,0:T(8,128)(2,1)S(1)}, bf16[2,192,128]{2,1,0:T(8,128)(2,1)S(1)}, u32[]{:S(2)}, u32[]{:S(2)}) collective-permute-start(bf16[2,192,128]{2,1,0:T(8,128)(2,1)S(1)} %get-tuple-element.86), channel_id=1, source_target_pairs={{0,1},{1,0},{2,3},{3,2},{4,5},{5,4},{6,7},{7,6},{8,9},{9,8},{10,11... | collective-permute-start | bytes 294920 | tf_op jit(solution)/shard_map/ppermute | solution.py:484
  41.2 0.8 %join.2.refs_0_ = bf16[4,2,192,128]{3,2,1,0:T(8,128)(2,1)} custom-call(bf16[2,192,128]{2,1,0:T(8,128)(2,1)S(1)} %get-tuple-element.89.kept_ref, bf16[2,192,128]{2,1,0:T(8,128)(2,1)S(1)} %collective-permute-done.8.got_ref), custom_call_target="tpu_custom_call" | custom-call | tf_op jit(solution)/shard_map/join/pallas_call | solution.py:465
  42.0 0.1 collective-permute-done.7.got_ref
  42.1 0.8 %join.3 = bf16[4,2,192,128]{3,2,1,0:T(8,128)(2,1)} custom-call(bf16[2,192,128]{2,1,0:T(8,128)(2,1)S(1)} %get-tuple-element.85.kept_ref, bf16[2,192,128]{2,1,0:T(8,128)(2,1)S(1)} %collective-permute-done.7.got_ref, bf16[4,2,192,128]{3,2,1,0:T(8,128)(2,1)} %join.2.refs_0_), custom_call_target="tpu_custom_call", output_to_operand_aliasing={{}: (2, {})} | custom-call | tf_op jit(solution)/shard_map/join/pallas_call | solution.py:465
  (4 shorter events, 0.0 us)
Async XLA Ops:
  0.0 8.3 %collective-permute-start.1 = (bf16[4,2,192,128]{3,2,1,0:T(8,128)(2,1)}, bf16[4,2,192,128]{3,2,1,0:T(8,128)(2,1)S(1)}, u32[]{:S(2)}, u32[]{:S(2)}) collective-permute-start(bf16[4,2,192,128]{3,2,1,0:T(8,128)(2,1)} %in_ref.1), channel_id=1, source_target_pairs={{0,1},{1,0},{2,3},{3,2},{4,5},{5,4},{6,7},{7,6},{8,9},{9,8},{10,11... | collective-permute-start | bytes 1179656 | tf_op jit(solution)/shard_map/ppermute | solution.py:484
  0.5 1.0 %copy-start = (bf16[4,2,192,128]{3,2,1,0:T(8,128)(2,1)S(1)}, bf16[4,2,192,128]{3,2,1,0:T(8,128)(2,1)}, u32[]{:S(2)}) copy-start(bf16[4,2,192,128]{3,2,1,0:T(8,128)(2,1)} %in_ref.1) | copy-start | bytes 1179652
  1.5 8.1 %collective-permute-start = (bf16[2,2,192,128]{3,2,1,0:T(8,128)(2,1)S(1)}, bf16[2,2,192,128]{3,2,1,0:T(8,128)(2,1)S(1)}, u32[]{:S(2)}, u32[]{:S(2)}) collective-permute-start(bf16[2,2,192,128]{3,2,1,0:T(8,128)(2,1)S(1)} %get-tuple-element.48.refs_1_), channel_id=1, source_target_pairs={{0,2},{1,3},{2,0},{3,1},{4,6},{5,7},{6,4},{7,5},{8,10},{9,11},{10,... | collective-permute-start | bytes 589832 | tf_op jit(solution)/shard_map/ppermute | solution.py:490
  9.6 1.7 %collective-permute-start.2 = (bf16[2,2,192,128]{3,2,1,0:T(8,128)(2,1)S(1)}, bf16[2,2,192,128]{3,2,1,0:T(8,128)(2,1)S(1)}, u32[]{:S(2)}, u32[]{:S(2)}) collective-permute-start(bf16[2,2,192,128]{3,2,1,0:T(8,128)(2,1)S(1)} %collective-permute-done.far_ref), channel_id=1, source_target_pairs={{0,1},{1,0},{2,3},{3,2},{4,5},{5,4},{6,7},{7,6},{8,9},{9,8},{10,11... | collective-permute-start | bytes 589832 | tf_op jit(solution)/shard_map/ppermute | solution.py:484
  9.6 7.3 %collective-permute-start.3 = (bf16[2,192,256]{2,1,0:T(8,128)(2,1)S(1)}, bf16[2,192,256]{2,1,0:T(8,128)(2,1)S(1)}, u32[]{:S(2)}, u32[]{:S(2)}) collective-permute-start(bf16[2,192,256]{2,1,0:T(8,128)(2,1)S(1)} %get-tuple-element.65), channel_id=1, source_target_pairs={{0,2},{1,3},{2,0},{3,1},{4,6},{5,7},{6,4},{7,5},{8,10},{9,11},{10,... | collective-permute-start | bytes 589832 | tf_op jit(solution)/shard_map/ppermute | solution.py:490
  11.9 12.4 %collective-permute-start.4 = (bf16[2,192,512]{2,1,0:T(8,128)(2,1)S(1)}, bf16[2,192,512]{2,1,0:T(8,128)(2,1)S(1)}, u32[]{:S(2)}, u32[]{:S(2)}) collective-permute-start(bf16[2,192,512]{2,1,0:T(8,128)(2,1)S(1)} %get-tuple-element.74), channel_id=1, source_target_pairs={{0,4},{4,8},{8,12},{1,5},{5,9},{9,13},{2,6},{6,10},{10,14},{3,7},{... | collective-permute-start | bytes 1179656 | tf_op jit(solution)/shard_map/ppermute | solution.py:487
  20.5 12.4 %collective-permute-start.5 = (bf16[192,896]{1,0:T(8,128)(2,1)S(1)}, bf16[192,896]{1,0:T(8,128)(2,1)S(1)}, u32[]{:S(2)}, u32[]{:S(2)}) collective-permute-start(bf16[192,896]{1,0:T(8,128)(2,1)S(1)} %get-tuple-element.78), channel_id=1, source_target_pairs={{0,4},{4,8},{8,12},{1,5},{5,9},{9,13},{2,6},{6,10},{10,14},{3,7},{... | collective-permute-start | bytes 1032200 | tf_op jit(solution)/shard_map/ppermute | solution.py:487
  28.5 10.3 %collective-permute-start.6 = (bf16[2,192,384]{2,1,0:T(8,128)(2,1)S(1)}, bf16[2,192,384]{2,1,0:T(8,128)(2,1)S(1)}, u32[]{:S(2)}, u32[]{:S(2)}) collective-permute-start(bf16[2,192,384]{2,1,0:T(8,128)(2,1)S(1)} %get-tuple-element.84), channel_id=1, source_target_pairs={{0,4},{4,8},{8,12},{1,5},{5,9},{9,13},{2,6},{6,10},{10,14},{3,7},{... | collective-permute-start | bytes 884744 | tf_op jit(solution)/shard_map/ppermute | solution.py:487
  38.8 2.4 %collective-permute-start.8 = (bf16[2,192,128]{2,1,0:T(8,128)(2,1)S(1)}, bf16[2,192,128]{2,1,0:T(8,128)(2,1)S(1)}, u32[]{:S(2)}, u32[]{:S(2)}) collective-permute-start(bf16[2,192,128]{2,1,0:T(8,128)(2,1)S(1)} %get-tuple-element.90), channel_id=1, source_target_pairs={{0,1},{1,0},{2,3},{3,2},{4,5},{5,4},{6,7},{7,6},{8,9},{9,8},{10,11... | collective-permute-start | bytes 294920 | tf_op jit(solution)/shard_map/ppermute | solution.py:484
  40.6 1.5 %collective-permute-start.7 = (bf16[2,192,128]{2,1,0:T(8,128)(2,1)S(1)}, bf16[2,192,128]{2,1,0:T(8,128)(2,1)S(1)}, u32[]{:S(2)}, u32[]{:S(2)}) collective-permute-start(bf16[2,192,128]{2,1,0:T(8,128)(2,1)S(1)} %get-tuple-element.86), channel_id=1, source_target_pairs={{0,1},{1,0},{2,3},{3,2},{4,5},{5,4},{6,7},{7,6},{8,9},{9,8},{10,11... | collective-permute-start | bytes 294920 | tf_op jit(solution)/shard_map/ppermute | solution.py:484

commit v11 on v10

--- a/solution.py
+++ b/solution.py
@@ -270,11 +270,25 @@
     ]
 
 
+def begun_rows(t, channels):
+    return (t + 1) * 3 * channels // TILE * TILE
+
+
+def rows_between(lines, start, stop):
+    taken, at = [], 0
+    for part in lines:
+        low, high = max(start - at, 0), min(stop - at, part.shape[0])
+        if low < high:
+            taken.append(part[low:high])
+        at += part.shape[0]
+    return jnp.concatenate(taken, axis=0)
+
+
 def begin_kernel(shifted_ref, w_ref, out_ref):
-    depth = 3 * shifted_ref.shape[2]
     for t in range(PAIR):
-        rhs = jnp.concatenate([lines_of(shifted_ref, j) for j in range(t, -1, -1)], axis=0)
-        sums = jnp.dot(w_ref[:, : (t + 1) * depth], rhs, preferred_element_type=jnp.float32)
+        cut = begun_rows(t, shifted_ref.shape[2])
+        rhs = rows_between([lines_of(shifted_ref, j) for j in range(t, -1, -1)], 0, cut)
+        sums = jnp.dot(w_ref[:, :cut], rhs, preferred_element_type=jnp.float32)
         for b, block in enumerate(column_sums(by_taps(sums))):
             out_ref[t, :, b * LANES : (b + 1) * LANES] = block
 
@@ -380,14 +394,12 @@
         outs[1][t] = jnp.where(outer, inner, outermost).astype(jnp.bfloat16)
 
     if plan["begun"]:
-        depth = 3 * channels
         for t in range(PAIR):
-            at = (t + 1) * depth
-            lead = at % LANES
-            lines = [lines_of(earlier_ref, j) for j in range(PAIR - 1, t - 1, -1)]
-            if lead:
-                lines.insert(0, jnp.zeros((lead, lanes), jnp.bfloat16))
-            sums = jnp.dot(w_ref[:, at - lead :], jnp.concatenate(lines, axis=0), preferred_element_type=jnp.float32)
+            cut = begun_rows(t, channels)
+            lines = [lines_of(shifted_ref, j) for j in range(t, -1, -1)]
+            lines += [lines_of(earlier_ref, j) for j in range(PAIR - 1, t - 1, -1)]
+            rhs = rows_between(lines, cut, w_ref.shape[1])
+            sums = jnp.dot(w_ref[:, cut:], rhs, preferred_element_type=jnp.float32)
             finish(t, by_taps(sums))
     else:
         places = [(t, b) for t in range(PAIR) for b in range(chunks)]
@@ -503,7 +515,7 @@
     values, shifted = [None] * pairs, [None] * pairs
     values[-1], shifted[-1], send = beyond(layers, columns, far, mate_of(far), near_values[-1], near_act[-1])
     halo, rest = earlier_of(send), 0
-    next_begun = None
+    next_begun = layer_begun = None
     first_begun = begin(shifted[-1], weight[0])
     *came, first_begun = lax.optimization_barrier((*came, first_begun))
     parts = [(came[p], near_values[p], near_act[p]) for p in range(pairs - 1)]
@@ -516,11 +528,13 @@
         for p in reversed(range(pairs)):
             builds = layer == 0 and p > 0
             earlier = (halo,) if p == 0 else parts[p - 1] if builds else (shifted[p - 1],)
-            waits = builds or (p == 0 and (last or layer == 0))
+            waits = builds or (p == 0 and (last or layer == 0)) or (layer == 1 and layer_begun is not None and p == pairs - 1)
             if builds and p == pairs - 1:
                 begun = (first_begun,)
             elif layer == 0 and p == 0 and next_begun is not None:
                 begun = (next_begun,)
+            elif layer == 1 and p == pairs - 1 and layer_begun is not None:
+                begun = (layer_begun,)
             else:
                 begun = (begin(shifted[p], weight[layer]),) if waits else ()
             plan = {
@@ -548,6 +562,9 @@
                     next_begun = begin(shifted[0], weight[0])
                     message, next_begun = lax.optimization_barrier((message, next_begun))
                 arriving = earlier_of(message)
+                if layer == 0 and p == 1 and not last:
+                    layer_begun = begin(outs[1], weight[1])
+                    halo, layer_begun = lax.optimization_barrier((halo, layer_begun))
         values, shifted = [r[0] for r in results], [r[1] for r in results]
         if not last:
             halo, rest = arriving, joined(rows_left * pitch)

time: 43.3 us -> 42.9 us (level)
  starting transfers between devices: 17.1 us -> 16.5 us
    ppermute x3, starting transfers between devices: 11.7 us -> 11.1 us  [earlier_of(): return lax.ppermute(block, 'tm', [(i, i + 1) for i in range(blocks - 1)])]
    pallas_call x6, Pallas kernels: 12.4 us -> 11.8 us  [conv(): pl.pallas_call(functools.partial(conv_kernel, plan), out_shape=out_shape,...]
    pallas_call x3 -> x4, Pallas kernels: 4.46 us -> 4.82 us  [begin(): pl.pallas_call(begin_kernel, out_shape=jax.ShapeDtypeStruct((PAIR, channe...]
  transfers between devices with their start and end apart: 9 -> 9, of which waited for: 2 -> 3; matrix products, arithmetic and copies ran while one was open for 2% -> 2% of each run, Pallas kernels for 52% -> 52%
where the time goes in v11:
time: 42.9 us; the launch traced here: 42.6 us
  Pallas kernels  23.1 us (54%)
  starting transfers between devices  16.5 us (38%)
  waiting for transfers between devices  1.01 us (2%)
  local copies, waits for them, and re-layouts  1 us (2%)
  other arithmetic  0.71 us (2%)
    pallas_call x6, Pallas kernels, conv(): pl.pallas_call(functools.partial(conv_kernel, plan), out_shape=out_shape,...  11.8 us
    ppermute x3, starting transfers between devices, earlier_of(): return lax.ppermute(block, 'tm', [(i, i + 1) for i in range(blocks - 1)])  11.1 us
    pallas_call x4, Pallas kernels, begin(): pl.pallas_call(begin_kernel, out_shape=jax.ShapeDtypeStruct((PAIR, channe...  4.82 us
    ppermute x2, starting transfers between devices, beyond_of(): return lax.ppermute(block, 'rows', [(i, i ^ 2) for i in range(strips)])  4.29 us
    pallas_call x1, Pallas kernels, weights(): pl.pallas_call(weights_kernel, out_shape=(one,) * layers + (jax.ShapeDtyp...  3.54 us
    pallas_call x2, Pallas kernels, join(): pl.pallas_call(functools.partial(join_kernel, pair), out_shape=jax.ShapeD...  1.62 us
    ppermute x4, starting transfers between devices, mate_of(): return lax.ppermute(block, 'rows', [(i, i ^ 1) for i in range(strips)])  1.08 us
    unnamed x2, local copies, waits for them, and re-layouts  1 us
  transfers between devices with their start and end apart: 9, of which 3 were waited for; matrix products, arithmetic and copies ran while one was open for 2% of the time, Pallas kernels for 52%

profile of v11, /device:TPU:0, one launch (start us, length us, event | category | flops | bytes accessed | tf_op | source)
XLA Modules:
  0.0 42.6 jit_solution(9471584333510173927)
XLA Ops:
  0.0 0.5 %collective-permute-start.1 = (bf16[4,2,192,128]{3,2,1,0:T(8,128)(2,1)}, bf16[4,2,192,128]{3,2,1,0:T(8,128)(2,1)S(1)}, u32[]{:S(2)}, u32[]{:S(2)}) collective-permute-start(bf16[4,2,192,128]{3,2,1,0:T(8,128)(2,1)} %in_ref.1), channel_id=1, source_target_pairs={{0,1},{1,0},{2,3},{3,2},{4,5},{5,4},{6,7},{7,6},{8,9},{9,8},{10,11... | collective-permute-start | bytes 1179656 | tf_op jit(solution)/shard_map/ppermute | solution.py:496
  0.5 1.0 %copy-done = bf16[4,2,192,128]{3,2,1,0:T(8,128)(2,1)S(1)} copy-done((bf16[4,2,192,128]{3,2,1,0:T(8,128)(2,1)S(1)}, bf16[4,2,192,128]{3,2,1,0:T(8,128)(2,1)}, u32[]{:S(2)}) %copy-start) | copy-done | bytes 393240
  1.5 2.6 %collective-permute-start = (bf16[2,2,192,128]{3,2,1,0:T(8,128)(2,1)S(1)}, bf16[2,2,192,128]{3,2,1,0:T(8,128)(2,1)S(1)}, u32[]{:S(2)}, u32[]{:S(2)}) collective-permute-start(bf16[2,2,192,128]{3,2,1,0:T(8,128)(2,1)S(1)} %get-tuple-element.50.refs_1_), channel_id=1, source_target_pairs={{0,2},{1,3},{2,0},{3,1},{4,6},{5,7},{6,4},{7,5},{8,10},{9,11},{10,... | collective-permute-start | bytes 589832 | tf_op jit(solution)/shard_map/ppermute | solution.py:502
  4.0 0.7 %pad_maximum_fusion.rows_ref.gains_ref = f32[6,192]{1,0:T(8,128)S(1)} fusion(f32[3,192]{1,0:T(4,128)} %param.7, f32[3,192]{1,0:T(4,128)} %param.6), kind=kLoop, calls=%fused_computation | loop fusion | flops 1152 | bytes 9216 | tf_op jit(solution)/shard_map/concatenate | solution.py:508
  4.7 3.5 %weights.1 = (bf16[576,1728]{1,0:T(8,128)(2,1)S(1)}, bf16[576,1728]{1,0:T(8,128)(2,1)S(1)}, bf16[576,1728]{1,0:T(8,128)(2,1)S(1)}, f32[3,2,192,128]{3,2,1,0:T(8,128)S(1)}) custom-call(bf16[3,27,192,192]{3,2,1,0:T(8,128)(2,1)} %w_ref.1, f32[6,192]{1,0:T(8,128)S(1)} %pad_maximum_fusion.rows_ref.gains_ref), custom_call_target="tpu_custom_call" | custom-call | bytes 11943936 | tf_op jit(solution)/shard_map/weights/pallas_call | solution.py:77
  8.3 0.0 collective-permute-done.1.mate_ref
  8.3 0.7 %near.1 = (bf16[2,192,384]{2,1,0:T(8,128)(2,1)S(1)}, bf16[2,192,384]{2,1,0:T(8,128)(2,1)S(1)}, bf16[2,192,256]{2,1,0:T(8,128)(2,1)S(1)}, bf16[2,192,256]{2,1,0:T(8,128)(2,1)S(1)}, bf16[2,192,256]{2,1,0:T(8,128)(2,1)S(1)}) custom-call(bf16[4,2,192,128]{3,2,1,0:T(8,128)(2,1)S(1)} %collective-permute-done.1.mate_ref, ...), custom_call_target="tpu_custom_call" | custom-call | flops 7864320 | bytes 1572864 | tf_op jit(solution)/shard_map/near/pallas_call | solution.py:176
  9.0 0.6 %collective-permute-done.far_ref = bf16[2,2,192,128]{3,2,1,0:T(8,128)(2,1)S(1)} collective-permute-done((bf16[2,2,192,128]{3,2,1,0:T(8,128)(2,1)S(1)}, bf16[2,2,192,128]{3,2,1,0:T(8,128)(2,1)S(1)}, u32[]{:S(2)}, u32[]{:S(2)}) %collective-permute-start) | collective-permute-done | bytes 196640 | tf_op jit(solution)/shard_map/ppermute | solution.py:502
  9.6 0.0 collective-permute-start.2
  9.6 1.7 %collective-permute-start.3 = (bf16[2,192,256]{2,1,0:T(8,128)(2,1)S(1)}, bf16[2,192,256]{2,1,0:T(8,128)(2,1)S(1)}, u32[]{:S(2)}, u32[]{:S(2)}) collective-permute-start(bf16[2,192,256]{2,1,0:T(8,128)(2,1)S(1)} %get-tuple-element.67), channel_id=1, source_target_pairs={{0,2},{1,3},{2,0},{3,1},{4,6},{5,7},{6,4},{7,5},{8,10},{9,11},{10,... | collective-permute-start | bytes 589832 | tf_op jit(solution)/shard_map/ppermute | solution.py:502
  11.4 0.5 %beyond.1 = (bf16[2,192,512]{2,1,0:T(8,128)(2,1)S(1)}, bf16[2,3,192,512]{3,2,1,0:T(8,128)(2,1)S(1)}, bf16[2,192,512]{2,1,0:T(8,128)(2,1)S(1)}) custom-call(f32[3,2,192,128]{3,2,1,0:T(8,128)S(1)} %get-tuple-element.60.columns_ref, bf16[2,2,192,128]{3,2,1,0:T(8,128)(2,1)S(1)} %collective-permute-done.far_ref, ...), custom_call_target="tpu_custom_call" | custom-call | flops 3932160 | bytes 786432 | tf_op jit(solution)/shard_map/beyond/pallas_call | solution.py:237
  11.9 3.5 %collective-permute-start.4 = (bf16[2,192,512]{2,1,0:T(8,128)(2,1)S(1)}, bf16[2,192,512]{2,1,0:T(8,128)(2,1)S(1)}, u32[]{:S(2)}, u32[]{:S(2)}) collective-permute-start(bf16[2,192,512]{2,1,0:T(8,128)(2,1)S(1)} %get-tuple-element.76), channel_id=1, source_target_pairs={{0,4},{4,8},{8,12},{1,5},{5,9},{9,13},{2,6},{6,10},{10,14},{3,7},{... | collective-permute-start | bytes 1179656 | tf_op jit(solution)/shard_map/ppermute | solution.py:499
  15.4 1.2 %begin.4.refs_0_ = f32[2,192,512]{2,1,0:T(8,128)S(1)} custom-call(bf16[2,3,192,512]{3,2,1,0:T(8,128)(2,1)S(1)} %get-tuple-element.64.shifted_ref, bf16[576,1728]{1,0:T(8,128)(2,1)S(1)} %get-tuple-element.66.w_ref), custom_call_target="tpu_custom_call" | custom-call | tf_op jit(solution)/shard_map/begin/pallas_call | solution.py:298
  16.6 0.3 collective-permute-done.3.refs_1_
  16.9 2.0 %conv_0.2 = (bf16[2,192,512]{2,1,0:T(8,128)(2,1)S(1)}, bf16[2,3,192,384]{3,2,1,0:T(8,128)(2,1)S(1)}, bf16[192,896]{1,0:T(8,128)(2,1)S(1)}, bf16[2,192,512]{2,1,0:T(8,128)(2,1)S(1)}, bf16[2,3,192,512]{3,2,1,0:T(8,128)(2,1)S(1)}) custom-call(bf16[2,3,192,512]{3,2,1,0:T(8,128)(2,1)S(1)} %get-tuple-element.64.shifted_ref, ...), custom_call_target="tpu_custom_call" | custom-call | flops 4076863488 | bytes 1990656 | tf_op jit(solution)/shard_map/conv_0/pallas_call | solution.py:439
  19.0 1.2 %begin.5.refs_0_ = f32[2,192,512]{2,1,0:T(8,128)S(1)} custom-call(bf16[2,3,192,512]{3,2,1,0:T(8,128)(2,1)S(1)} %get-tuple-element.72.shifted_ref, bf16[576,1728]{1,0:T(8,128)(2,1)S(1)} %get-tuple-element.66.w_ref), custom_call_target="tpu_custom_call" | custom-call | tf_op jit(solution)/shard_map/begin/pallas_call | solution.py:298
  20.2 3.8 %collective-permute-start.5 = (bf16[192,896]{1,0:T(8,128)(2,1)S(1)}, bf16[192,896]{1,0:T(8,128)(2,1)S(1)}, u32[]{:S(2)}, u32[]{:S(2)}) collective-permute-start(bf16[192,896]{1,0:T(8,128)(2,1)S(1)} %get-tuple-element.82), channel_id=1, source_target_pairs={{0,4},{4,8},{8,12},{1,5},{5,9},{9,13},{2,6},{6,10},{10,14},{3,7},{... | collective-permute-start | bytes 1032200 | tf_op jit(solution)/shard_map/ppermute | solution.py:499
  24.0 1.2 %begin.6.refs_0_ = f32[2,192,384]{2,1,0:T(8,128)S(1)} custom-call(bf16[2,3,192,384]{3,2,1,0:T(8,128)(2,1)S(1)} %get-tuple-element.77.shifted_ref, bf16[576,1728]{1,0:T(8,128)(2,1)S(1)} %get-tuple-element.78.w_ref), custom_call_target="tpu_custom_call" | custom-call | tf_op jit(solution)/shard_map/begin/pallas_call | solution.py:298
  25.2 0.0 collective-permute-done.4.refs_1_
  25.2 2.0 %conv_0.3 = (bf16[2,192,512]{2,1,0:T(8,128)(2,1)S(1)}, bf16[2,3,192,384]{3,2,1,0:T(8,128)(2,1)S(1)}) custom-call(bf16[2,3,192,512]{3,2,1,0:T(8,128)(2,1)S(1)} %get-tuple-element.72.shifted_ref, bf16[2,192,512]{2,1,0:T(8,128)(2,1)S(1)} %get-tuple-element.73.values_ref, bf16[576,1728]{1,0:T(8,128)(2,1)S(1)} %get-tuple-element.66.w_ref, ...), custom_call_target="tpu_custom_call" | custom-call | flops 2038431744 | bytes 1990656 | tf_op jit(solution)/shard_map/conv_0/pallas_call | solution.py:439
  27.1 1.8 %conv_1.3 = (bf16[2,192,384]{2,1,0:T(8,128)(2,1)S(1)}, bf16[2,3,192,384]{3,2,1,0:T(8,128)(2,1)S(1)}, bf16[2,192,384]{2,1,0:T(8,128)(2,1)S(1)}) custom-call(bf16[2,3,192,384]{3,2,1,0:T(8,128)(2,1)S(1)} %get-tuple-element.77.shifted_ref, bf16[2,192,512]{2,1,0:T(8,128)(2,1)S(1)} %get-tuple-element.86.values_ref, bf16[576,1728]{1,0:T(8,128)(2,1)S(1)} %get-tuple-element.78.w_ref, ...), custom_call_target="tpu_custom_call" | custom-call | flops 1528823808 | bytes 1990656 | tf_op jit(solution)/shard_map/conv_1/pallas_call | solution.py:439
  28.9 3.8 %collective-permute-start.6 = (bf16[2,192,384]{2,1,0:T(8,128)(2,1)S(1)}, bf16[2,192,384]{2,1,0:T(8,128)(2,1)S(1)}, u32[]{:S(2)}, u32[]{:S(2)}) collective-permute-start(bf16[2,192,384]{2,1,0:T(8,128)(2,1)S(1)} %get-tuple-element.88), channel_id=1, source_target_pairs={{0,4},{4,8},{8,12},{1,5},{5,9},{9,13},{2,6},{6,10},{10,14},{3,7},{... | collective-permute-start | bytes 884744 | tf_op jit(solution)/shard_map/ppermute | solution.py:499
  32.8 2.3 %conv_1.2 = (bf16[2,192,384]{2,1,0:T(8,128)(2,1)S(1)}, bf16[2,3,192,384]{3,2,1,0:T(8,128)(2,1)S(1)}) custom-call(bf16[2,3,192,384]{3,2,1,0:T(8,128)(2,1)S(1)} %get-tuple-element.80.shifted_ref.refs_1_, bf16[2,192,512]{2,1,0:T(8,128)(2,1)S(1)} %get-tuple-element.81.values_ref, bf16[576,1728]{1,0:T(8,128)(2,1)S(1)} %get-tuple-element.78.w_ref, ...), custom_call_target="tpu_custom_call" | custom-call | flops 1528823808 | bytes 1990656 | tf_op jit(solution)/shard_map/conv_1/pallas_call | solution.py:439
  35.1 1.2 %begin.7.refs_0_ = f32[2,192,384]{2,1,0:T(8,128)S(1)} custom-call(bf16[2,3,192,384]{3,2,1,0:T(8,128)(2,1)S(1)} %get-tuple-element.83.shifted_ref.refs_0_, bf16[576,1728]{1,0:T(8,128)(2,1)S(1)} %get-tuple-element.85.w_ref), custom_call_target="tpu_custom_call" | custom-call | tf_op jit(solution)/shard_map/begin/pallas_call | solution.py:298
  36.3 2.1 %conv_2.3 = (bf16[2,192,128]{2,1,0:T(8,128)(2,1)S(1)}, bf16[2,192,128]{2,1,0:T(8,128)(2,1)S(1)}) custom-call(bf16[2,3,192,384]{3,2,1,0:T(8,128)(2,1)S(1)} %get-tuple-element.91.shifted_ref, bf16[2,192,384]{2,1,0:T(8,128)(2,1)S(1)} %get-tuple-element.92.values_ref, bf16[576,1728]{1,0:T(8,128)(2,1)S(1)} %get-tuple-element.85.w_ref, ...), custom_call_target="tpu_custom_call" | custom-call | flops 1528823808 | bytes 1990656 | tf_op jit(solution)/shard_map/conv_2/pallas_call | solution.py:439
  38.3 0.1 collective-permute-start.8
  38.4 1.7 %conv_2.2 = (bf16[2,192,128]{2,1,0:T(8,128)(2,1)S(1)}, bf16[2,192,128]{2,1,0:T(8,128)(2,1)S(1)}) custom-call(bf16[2,3,192,384]{3,2,1,0:T(8,128)(2,1)S(1)} %get-tuple-element.83.shifted_ref.refs_0_, bf16[2,192,384]{2,1,0:T(8,128)(2,1)S(1)} %get-tuple-element.84.values_ref, bf16[576,1728]{1,0:T(8,128)(2,1)S(1)} %get-tuple-element.85.w_ref, ...), custom_call_target="tpu_custom_call" | custom-call | flops 1528823808 | bytes 1990656 | tf_op jit(solution)/shard_map/conv_2/pallas_call | solution.py:439
  40.2 0.6 %collective-permute-start.7 = (bf16[2,192,128]{2,1,0:T(8,128)(2,1)S(1)}, bf16[2,192,128]{2,1,0:T(8,128)(2,1)S(1)}, u32[]{:S(2)}, u32[]{:S(2)}) collective-permute-start(bf16[2,192,128]{2,1,0:T(8,128)(2,1)S(1)} %get-tuple-element.90), channel_id=1, source_target_pairs={{0,1},{1,0},{2,3},{3,2},{4,5},{5,4},{6,7},{7,6},{8,9},{9,8},{10,11... | collective-permute-start | bytes 294920 | tf_op jit(solution)/shard_map/ppermute | solution.py:496
  40.7 0.0 collective-permute-done.8.got_ref
  40.7 0.8 %join.2.refs_0_ = bf16[4,2,192,128]{3,2,1,0:T(8,128)(2,1)} custom-call(bf16[2,192,128]{2,1,0:T(8,128)(2,1)S(1)} %get-tuple-element.93.kept_ref, bf16[2,192,128]{2,1,0:T(8,128)(2,1)S(1)} %collective-permute-done.8.got_ref), custom_call_target="tpu_custom_call" | custom-call | tf_op jit(solution)/shard_map/join/pallas_call | solution.py:477
  41.5 0.1 collective-permute-done.7.got_ref
  41.7 0.8 %join.3 = bf16[4,2,192,128]{3,2,1,0:T(8,128)(2,1)} custom-call(bf16[2,192,128]{2,1,0:T(8,128)(2,1)S(1)} %get-tuple-element.89.kept_ref, bf16[2,192,128]{2,1,0:T(8,128)(2,1)S(1)} %collective-permute-done.7.got_ref, bf16[4,2,192,128]{3,2,1,0:T(8,128)(2,1)} %join.2.refs_0_), custom_call_target="tpu_custom_call", output_to_operand_aliasing={{}: (2, {})} | custom-call | tf_op jit(solution)/shard_map/join/pallas_call | solution.py:477
  (5 shorter events, 0.0 us)
Async XLA Ops:
  0.0 8.3 %collective-permute-start.1 = (bf16[4,2,192,128]{3,2,1,0:T(8,128)(2,1)}, bf16[4,2,192,128]{3,2,1,0:T(8,128)(2,1)S(1)}, u32[]{:S(2)}, u32[]{:S(2)}) collective-permute-start(bf16[4,2,192,128]{3,2,1,0:T(8,128)(2,1)} %in_ref.1), channel_id=1, source_target_pairs={{0,1},{1,0},{2,3},{3,2},{4,5},{5,4},{6,7},{7,6},{8,9},{9,8},{10,11... | collective-permute-start | bytes 1179656 | tf_op jit(solution)/shard_map/ppermute | solution.py:496
  0.5 1.0 %copy-start = (bf16[4,2,192,128]{3,2,1,0:T(8,128)(2,1)S(1)}, bf16[4,2,192,128]{3,2,1,0:T(8,128)(2,1)}, u32[]{:S(2)}) copy-start(bf16[4,2,192,128]{3,2,1,0:T(8,128)(2,1)} %in_ref.1) | copy-start | bytes 1179652
  1.5 8.1 %collective-permute-start = (bf16[2,2,192,128]{3,2,1,0:T(8,128)(2,1)S(1)}, bf16[2,2,192,128]{3,2,1,0:T(8,128)(2,1)S(1)}, u32[]{:S(2)}, u32[]{:S(2)}) collective-permute-start(bf16[2,2,192,128]{3,2,1,0:T(8,128)(2,1)S(1)} %get-tuple-element.50.refs_1_), channel_id=1, source_target_pairs={{0,2},{1,3},{2,0},{3,1},{4,6},{5,7},{6,4},{7,5},{8,10},{9,11},{10,... | collective-permute-start | bytes 589832 | tf_op jit(solution)/shard_map/ppermute | solution.py:502
  9.6 1.7 %collective-permute-start.2 = (bf16[2,2,192,128]{3,2,1,0:T(8,128)(2,1)S(1)}, bf16[2,2,192,128]{3,2,1,0:T(8,128)(2,1)S(1)}, u32[]{:S(2)}, u32[]{:S(2)}) collective-permute-start(bf16[2,2,192,128]{3,2,1,0:T(8,128)(2,1)S(1)} %collective-permute-done.far_ref), channel_id=1, source_target_pairs={{0,1},{1,0},{2,3},{3,2},{4,5},{5,4},{6,7},{7,6},{8,9},{9,8},{10,11... | collective-permute-start | bytes 589832 | tf_op jit(solution)/shard_map/ppermute | solution.py:496
  9.6 7.3 %collective-permute-start.3 = (bf16[2,192,256]{2,1,0:T(8,128)(2,1)S(1)}, bf16[2,192,256]{2,1,0:T(8,128)(2,1)S(1)}, u32[]{:S(2)}, u32[]{:S(2)}) collective-permute-start(bf16[2,192,256]{2,1,0:T(8,128)(2,1)S(1)} %get-tuple-element.67), channel_id=1, source_target_pairs={{0,2},{1,3},{2,0},{3,1},{4,6},{5,7},{6,4},{7,5},{8,10},{9,11},{10,... | collective-permute-start | bytes 589832 | tf_op jit(solution)/shard_map/ppermute | solution.py:502
  11.9 13.3 %collective-permute-start.4 = (bf16[2,192,512]{2,1,0:T(8,128)(2,1)S(1)}, bf16[2,192,512]{2,1,0:T(8,128)(2,1)S(1)}, u32[]{:S(2)}, u32[]{:S(2)}) collective-permute-start(bf16[2,192,512]{2,1,0:T(8,128)(2,1)S(1)} %get-tuple-element.76), channel_id=1, source_target_pairs={{0,4},{4,8},{8,12},{1,5},{5,9},{9,13},{2,6},{6,10},{10,14},{3,7},{... | collective-permute-start | bytes 1179656 | tf_op jit(solution)/shard_map/ppermute | solution.py:499
  20.2 12.6 %collective-permute-start.5 = (bf16[192,896]{1,0:T(8,128)(2,1)S(1)}, bf16[192,896]{1,0:T(8,128)(2,1)S(1)}, u32[]{:S(2)}, u32[]{:S(2)}) collective-permute-start(bf16[192,896]{1,0:T(8,128)(2,1)S(1)} %get-tuple-element.82), channel_id=1, source_target_pairs={{0,4},{4,8},{8,12},{1,5},{5,9},{9,13},{2,6},{6,10},{10,14},{3,7},{... | collective-permute-start | bytes 1032200 | tf_op jit(solution)/shard_map/ppermute | solution.py:499
  28.9 9.5 %collective-permute-start.6 = (bf16[2,192,384]{2,1,0:T(8,128)(2,1)S(1)}, bf16[2,192,384]{2,1,0:T(8,128)(2,1)S(1)}, u32[]{:S(2)}, u32[]{:S(2)}) collective-permute-start(bf16[2,192,384]{2,1,0:T(8,128)(2,1)S(1)} %get-tuple-element.88), channel_id=1, source_target_pairs={{0,4},{4,8},{8,12},{1,5},{5,9},{9,13},{2,6},{6,10},{10,14},{3,7},{... | collective-permute-start | bytes 884744 | tf_op jit(solution)/shard_map/ppermute | solution.py:499
  38.3 2.4 %collective-permute-start.8 = (bf16[2,192,128]{2,1,0:T(8,128)(2,1)S(1)}, bf16[2,192,128]{2,1,0:T(8,128)(2,1)S(1)}, u32[]{:S(2)}, u32[]{:S(2)}) collective-permute-start(bf16[2,192,128]{2,1,0:T(8,128)(2,1)S(1)} %get-tuple-element.94), channel_id=1, source_target_pairs={{0,1},{1,0},{2,3},{3,2},{4,5},{5,4},{6,7},{7,6},{8,9},{9,8},{10,11... | collective-permute-start | bytes 294920 | tf_op jit(solution)/shard_map/ppermute | solution.py:496
  40.2 1.5 %collective-permute-start.7 = (bf16[2,192,128]{2,1,0:T(8,128)(2,1)S(1)}, bf16[2,192,128]{2,1,0:T(8,128)(2,1)S(1)}, u32[]{:S(2)}, u32[]{:S(2)}) collective-permute-start(bf16[2,192,128]{2,1,0:T(8,128)(2,1)S(1)} %get-tuple-element.90), channel_id=1, source_target_pairs={{0,1},{1,0},{2,3},{3,2},{4,5},{5,4},{6,7},{7,6},{8,9},{9,8},{10,11... | collective-permute-start | bytes 294920 | tf_op jit(solution)/shard_map/ppermute | solution.py:496

commit v12 on v11

--- a/solution.py
+++ b/solution.py
@@ -245,10 +245,6 @@
     )(columns, *parts)
 
 
-def lines_of(ref, frame):
-    return ref[frame].reshape(3 * ref.shape[2], ref.shape[3])
-
-
 def by_taps(sums):
     channels, lanes = sums.shape[0] // 3, sums.shape[1]
     return [
@@ -284,13 +280,59 @@
     return jnp.concatenate(taken, axis=0)
 
 
+def block_lines(ref, frame, b):
+    return ref[frame, :, :, b * LANES : (b + 1) * LANES].reshape(3 * ref.shape[2], LANES)
+
+
+def padded_rows(lines, start, stop, low, high):
+    parts = [rows_between(lines, start, stop)]
+    if low < start:
+        parts.insert(0, jnp.zeros((start - low, LANES), jnp.bfloat16))
+    if stop < high:
+        parts.append(jnp.zeros((high - stop, LANES), jnp.bfloat16))
+    return parts[0] if len(parts) == 1 else jnp.concatenate(parts, axis=0)
+
+
+def tiled(lanes):
+    places = [(t, b) for t in range(PAIR) for b in range(lanes // LANES)]
+    side = TILE // LANES
+    return [places[n : n + side] for n in range(0, len(places), side)]
+
+
+def by_frames(lanes, tile_sums, finish):
+    taps = {t: [[], [], []] for t in range(PAIR)}
+    for places in tiled(lanes):
+        sums = by_taps(tile_sums(places))
+        for i, (t, b) in enumerate(places):
+            for tap in range(3):
+                taps[t][tap].append(sums[tap][i])
+        for t, b in places:
+            if b == lanes // LANES - 1:
+                finish(t, taps[t])
+
+
 def begin_kernel(shifted_ref, w_ref, out_ref):
-    for t in range(PAIR):
-        cut = begun_rows(t, shifted_ref.shape[2])
-        rhs = rows_between([lines_of(shifted_ref, j) for j in range(t, -1, -1)], 0, cut)
-        sums = jnp.dot(w_ref[:, :cut], rhs, preferred_element_type=jnp.float32)
-        for b, block in enumerate(column_sums(by_taps(sums))):
+    _, _, channels, lanes = shifted_ref.shape
+
+    def tile_sums(places):
+        depth = max(begun_rows(t, channels) for t, _ in places)
+        rhs = [
+            padded_rows(
+                [block_lines(shifted_ref, j, b) for j in range(t, -1, -1)],
+                0,
+                begun_rows(t, channels),
+                0,
+                depth,
+            )
+            for t, b in places
+        ]
+        return jnp.dot(w_ref[:, :depth], jnp.concatenate(rhs, axis=1), preferred_element_type=jnp.float32)
+
+    def finish(t, taps):
+        for b, block in enumerate(column_sums(taps)):
             out_ref[t, :, b * LANES : (b + 1) * LANES] = block
+
+    by_frames(lanes, tile_sums, finish)
 
 
 def begin(shifted, weight):
@@ -339,11 +381,6 @@
     _, _, channels, lanes = shifted_ref.shape
     chunks = lanes // LANES
     lane = lane_of(LANES)
-
-    def window(t, b):
-        taken = [(earlier_ref, t + a) if t + a < PAIR else (shifted_ref, t + a - PAIR) for a in (2, 1, 0)]
-        at = slice(b * LANES, (b + 1) * LANES)
-        return jnp.concatenate([ref[j, :, :, at].reshape(3 * channels, LANES) for ref, j in taken], axis=0)
 
     bias = columns_ref[layer, 1]
     tails = []
@@ -393,28 +430,16 @@
         outs[0][t] = jnp.where(outer, outermost, inner).astype(jnp.bfloat16)
         outs[1][t] = jnp.where(outer, inner, outermost).astype(jnp.bfloat16)
 
-    if plan["begun"]:
-        for t in range(PAIR):
-            cut = begun_rows(t, channels)
-            lines = [lines_of(shifted_ref, j) for j in range(t, -1, -1)]
-            lines += [lines_of(earlier_ref, j) for j in range(PAIR - 1, t - 1, -1)]
-            rhs = rows_between(lines, cut, w_ref.shape[1])
-            sums = jnp.dot(w_ref[:, cut:], rhs, preferred_element_type=jnp.float32)
-            finish(t, by_taps(sums))
-    else:
-        places = [(t, b) for t in range(PAIR) for b in range(chunks)]
-        side = TILE // LANES
-        taps = {t: [[], [], []] for t in range(PAIR)}
-        finished = 0
-        for n in range(0, len(places), side):
-            rhs = jnp.concatenate([window(t, b) for t, b in places[n : n + side]], axis=1)
-            sums = by_taps(jnp.dot(w_ref[...], rhs, preferred_element_type=jnp.float32))
-            for i, (t, _) in enumerate(places[n : n + side]):
-                for tap in range(3):
-                    taps[t][tap].append(sums[tap][i])
-            while finished < PAIR and (finished + 1) * chunks <= n + side:
-                finish(finished, taps[finished])
-                finished += 1
+    def tile_sums(places):
+        cuts = {t: begun_rows(t, channels) if plan["begun"] else 0 for t, _ in places}
+        start, stop = min(cuts.values()), w_ref.shape[1]
+        rhs = []
+        for t, b in places:
+            frames = [(earlier_ref, t + a) if t + a < PAIR else (shifted_ref, t + a - PAIR) for a in (2, 1, 0)]
+            rhs.append(padded_rows([block_lines(ref, j, b) for ref, j in frames], cuts[t], stop, start, stop))
+        return jnp.dot(w_ref[:, start:], jnp.concatenate(rhs, axis=1), preferred_element_type=jnp.float32)
+
+    by_frames(lanes, tile_sums, finish)
     if sends and rest_sent:
         outs[2][:, PAIR * (chunks - 1) * LANES :] = sum(tails).astype(jnp.bfloat16)
 
@@ -453,12 +478,13 @@
 
 
 def join_kernel(pair, kept_ref, got_ref, *refs):
-    out_ref, lines_ref, sem = refs[-3:]
+    out_ref, lines_ref, sems = refs[-3:]
     _, rows, _, width = lines_ref.shape
     half = width // 2
     core, group, _ = place()
     first = core == 0
     left_half = lane_of(width) < half
+    copies = []
     for t in range(PAIR):
         mine, theirs = kept_ref[t].astype(jnp.float32), got_ref[t].astype(jnp.float32)
         left, right = jnp.where(first, mine, theirs), jnp.where(first, theirs, mine)
@@ -468,9 +494,10 @@
         )
         for j in range(rows):
             lines_ref[t, j + group * (rows - 1 - 2 * j)] = lines[j].astype(jnp.bfloat16)
-    copy = pltpu.make_async_copy(lines_ref, out_ref.at[pl.ds(PAIR * pair, PAIR)], sem)
-    copy.start()
-    copy.wait()
+        copies.append(pltpu.make_async_copy(lines_ref.at[t], out_ref.at[PAIR * pair + t], sems.at[t]))
+        copies[-1].start()
+    for copy in copies:
+        copy.wait()
 
 
 def join(pair, kept, got, shape, *so_far):
@@ -479,7 +506,7 @@
         out_shape=jax.ShapeDtypeStruct(shape, jnp.bfloat16),
         in_specs=[VMEM, VMEM] + [ANY] * len(so_far),
         out_specs=ANY,
-        scratch_shapes=[pltpu.VMEM((PAIR,) + shape[1:], jnp.bfloat16), pltpu.SemaphoreType.DMA],
+        scratch_shapes=[pltpu.VMEM((PAIR,) + shape[1:], jnp.bfloat16), pltpu.SemaphoreType.DMA((PAIR,))],
         input_output_aliases={2: 0} if so_far else {},
         compiler_params=pltpu.CompilerParams(vmem_limit_bytes=LIMIT),
         name="join",

time: 42.9 us -> 42.5 us (level)
  Pallas kernels: 23.1 us -> 22.6 us
where the time goes in v12:
time: 42.5 us; the launch traced here: 42.2 us
  Pallas kernels  22.6 us (53%)
  starting transfers between devices  16.6 us (39%)
  waiting for transfers between devices  1.02 us (2%)
  local copies, waits for them, and re-layouts  1 us (2%)
  other arithmetic  0.71 us (2%)
    pallas_call x6, Pallas kernels, conv(): pl.pallas_call(functools.partial(conv_kernel, plan), out_shape=out_shape,...  11.7 us
    ppermute x3, starting transfers between devices, earlier_of(): return lax.ppermute(block, 'tm', [(i, i + 1) for i in range(blocks - 1)])  11.2 us
    pallas_call x4, Pallas kernels, begin(): pl.pallas_call(begin_kernel, out_shape=jax.ShapeDtypeStruct((PAIR, channe...  4.54 us
    ppermute x2, starting transfers between devices, beyond_of(): return lax.ppermute(block, 'rows', [(i, i ^ 2) for i in range(strips)])  4.29 us
    pallas_call x1, Pallas kernels, weights(): pl.pallas_call(weights_kernel, out_shape=(one,) * layers + (jax.ShapeDtyp...  3.54 us
    pallas_call x2, Pallas kernels, join(): pl.pallas_call(functools.partial(join_kernel, pair), out_shape=jax.ShapeD...  1.58 us
    ppermute x4, starting transfers between devices, mate_of(): return lax.ppermute(block, 'rows', [(i, i ^ 1) for i in range(strips)])  1.08 us
    unnamed x2, local copies, waits for them, and re-layouts  1 us
  transfers between devices with their start and end apart: 9, of which 3 were waited for; matrix products, arithmetic and copies ran while one was open for 2% of the time, Pallas kernels for 52%

profile of v12, /device:TPU:0, one launch (start us, length us, event | category | flops | bytes accessed | tf_op | source)
XLA Modules:
  0.0 42.2 jit_solution(15437073615953703950)
XLA Ops:
  0.0 0.5 %collective-permute-start.1 = (bf16[4,2,192,128]{3,2,1,0:T(8,128)(2,1)}, bf16[4,2,192,128]{3,2,1,0:T(8,128)(2,1)S(1)}, u32[]{:S(2)}, u32[]{:S(2)}) collective-permute-start(bf16[4,2,192,128]{3,2,1,0:T(8,128)(2,1)} %in_ref.1), channel_id=1, source_target_pairs={{0,1},{1,0},{2,3},{3,2},{4,5},{5,4},{6,7},{7,6},{8,9},{9,8},{10,11... | collective-permute-start | bytes 1179656 | tf_op jit(solution)/shard_map/ppermute | solution.py:523
  0.5 1.0 %copy-done = bf16[4,2,192,128]{3,2,1,0:T(8,128)(2,1)S(1)} copy-done((bf16[4,2,192,128]{3,2,1,0:T(8,128)(2,1)S(1)}, bf16[4,2,192,128]{3,2,1,0:T(8,128)(2,1)}, u32[]{:S(2)}) %copy-start) | copy-done | bytes 393240
  1.5 2.6 %collective-permute-start = (bf16[2,2,192,128]{3,2,1,0:T(8,128)(2,1)S(1)}, bf16[2,2,192,128]{3,2,1,0:T(8,128)(2,1)S(1)}, u32[]{:S(2)}, u32[]{:S(2)}) collective-permute-start(bf16[2,2,192,128]{3,2,1,0:T(8,128)(2,1)S(1)} %get-tuple-element.50.refs_1_), channel_id=1, source_target_pairs={{0,2},{1,3},{2,0},{3,1},{4,6},{5,7},{6,4},{7,5},{8,10},{9,11},{10,... | collective-permute-start | bytes 589832 | tf_op jit(solution)/shard_map/ppermute | solution.py:529
  4.0 0.7 %pad_maximum_fusion.rows_ref.gains_ref = f32[6,192]{1,0:T(8,128)S(1)} fusion(f32[3,192]{1,0:T(4,128)} %param.7, f32[3,192]{1,0:T(4,128)} %param.6), kind=kLoop, calls=%fused_computation | loop fusion | flops 1152 | bytes 9216 | tf_op jit(solution)/shard_map/concatenate | solution.py:535
  4.7 3.5 %weights.1 = (bf16[576,1728]{1,0:T(8,128)(2,1)S(1)}, bf16[576,1728]{1,0:T(8,128)(2,1)S(1)}, bf16[576,1728]{1,0:T(8,128)(2,1)S(1)}, f32[3,2,192,128]{3,2,1,0:T(8,128)S(1)}) custom-call(bf16[3,27,192,192]{3,2,1,0:T(8,128)(2,1)} %w_ref.1, f32[6,192]{1,0:T(8,128)S(1)} %pad_maximum_fusion.rows_ref.gains_ref), custom_call_target="tpu_custom_call" | custom-call | bytes 11943936 | tf_op jit(solution)/shard_map/weights/pallas_call | solution.py:77
  8.3 0.0 collective-permute-done.1.mate_ref
  8.3 0.7 %near.1 = (bf16[2,192,384]{2,1,0:T(8,128)(2,1)S(1)}, bf16[2,192,384]{2,1,0:T(8,128)(2,1)S(1)}, bf16[2,192,256]{2,1,0:T(8,128)(2,1)S(1)}, bf16[2,192,256]{2,1,0:T(8,128)(2,1)S(1)}, bf16[2,192,256]{2,1,0:T(8,128)(2,1)S(1)}) custom-call(bf16[4,2,192,128]{3,2,1,0:T(8,128)(2,1)S(1)} %collective-permute-done.1.mate_ref, ...), custom_call_target="tpu_custom_call" | custom-call | flops 7864320 | bytes 1572864 | tf_op jit(solution)/shard_map/near/pallas_call | solution.py:176
  9.0 0.6 %collective-permute-done.far_ref = bf16[2,2,192,128]{3,2,1,0:T(8,128)(2,1)S(1)} collective-permute-done((bf16[2,2,192,128]{3,2,1,0:T(8,128)(2,1)S(1)}, bf16[2,2,192,128]{3,2,1,0:T(8,128)(2,1)S(1)}, u32[]{:S(2)}, u32[]{:S(2)}) %collective-permute-start) | collective-permute-done | bytes 196640 | tf_op jit(solution)/shard_map/ppermute | solution.py:529
  9.6 1.7 %collective-permute-start.3 = (bf16[2,192,256]{2,1,0:T(8,128)(2,1)S(1)}, bf16[2,192,256]{2,1,0:T(8,128)(2,1)S(1)}, u32[]{:S(2)}, u32[]{:S(2)}) collective-permute-start(bf16[2,192,256]{2,1,0:T(8,128)(2,1)S(1)} %get-tuple-element.67), channel_id=1, source_target_pairs={{0,2},{1,3},{2,0},{3,1},{4,6},{5,7},{6,4},{7,5},{8,10},{9,11},{10,... | collective-permute-start | bytes 589832 | tf_op jit(solution)/shard_map/ppermute | solution.py:529
  11.4 0.0 collective-permute-done.2.mate_ref
  11.4 0.5 %beyond.1 = (bf16[2,192,512]{2,1,0:T(8,128)(2,1)S(1)}, bf16[2,3,192,512]{3,2,1,0:T(8,128)(2,1)S(1)}, bf16[2,192,512]{2,1,0:T(8,128)(2,1)S(1)}) custom-call(f32[3,2,192,128]{3,2,1,0:T(8,128)S(1)} %get-tuple-element.60.columns_ref, bf16[2,2,192,128]{3,2,1,0:T(8,128)(2,1)S(1)} %collective-permute-done.far_ref, ...), custom_call_target="tpu_custom_call" | custom-call | flops 3932160 | bytes 786432 | tf_op jit(solution)/shard_map/beyond/pallas_call | solution.py:237
  11.9 3.5 %collective-permute-start.4 = (bf16[2,192,512]{2,1,0:T(8,128)(2,1)S(1)}, bf16[2,192,512]{2,1,0:T(8,128)(2,1)S(1)}, u32[]{:S(2)}, u32[]{:S(2)}) collective-permute-start(bf16[2,192,512]{2,1,0:T(8,128)(2,1)S(1)} %get-tuple-element.76), channel_id=1, source_target_pairs={{0,4},{4,8},{8,12},{1,5},{5,9},{9,13},{2,6},{6,10},{10,14},{3,7},{... | collective-permute-start | bytes 1179656 | tf_op jit(solution)/shard_map/ppermute | solution.py:526
  15.4 1.2 %begin.4.refs_0_ = f32[2,192,512]{2,1,0:T(8,128)S(1)} custom-call(bf16[2,3,192,512]{3,2,1,0:T(8,128)(2,1)S(1)} %get-tuple-element.64.shifted_ref, bf16[576,1728]{1,0:T(8,128)(2,1)S(1)} %get-tuple-element.66.w_ref), custom_call_target="tpu_custom_call" | custom-call | tf_op jit(solution)/shard_map/begin/pallas_call | solution.py:340
  16.6 0.3 collective-permute-done.3.refs_1_
  16.9 2.1 %conv_0.2 = (bf16[2,192,512]{2,1,0:T(8,128)(2,1)S(1)}, bf16[2,3,192,384]{3,2,1,0:T(8,128)(2,1)S(1)}, bf16[192,896]{1,0:T(8,128)(2,1)S(1)}, bf16[2,192,512]{2,1,0:T(8,128)(2,1)S(1)}, bf16[2,3,192,512]{3,2,1,0:T(8,128)(2,1)S(1)}) custom-call(bf16[2,3,192,512]{3,2,1,0:T(8,128)(2,1)S(1)} %get-tuple-element.64.shifted_ref, ...), custom_call_target="tpu_custom_call" | custom-call | flops 4076863488 | bytes 1990656 | tf_op jit(solution)/shard_map/conv_0/pallas_call | solution.py:464
  19.0 1.2 %begin.5.refs_0_ = f32[2,192,512]{2,1,0:T(8,128)S(1)} custom-call(bf16[2,3,192,512]{3,2,1,0:T(8,128)(2,1)S(1)} %get-tuple-element.72.shifted_ref, bf16[576,1728]{1,0:T(8,128)(2,1)S(1)} %get-tuple-element.66.w_ref), custom_call_target="tpu_custom_call" | custom-call | tf_op jit(solution)/shard_map/begin/pallas_call | solution.py:340
  20.2 3.8 %collective-permute-start.5 = (bf16[192,896]{1,0:T(8,128)(2,1)S(1)}, bf16[192,896]{1,0:T(8,128)(2,1)S(1)}, u32[]{:S(2)}, u32[]{:S(2)}) collective-permute-start(bf16[192,896]{1,0:T(8,128)(2,1)S(1)} %get-tuple-element.82), channel_id=1, source_target_pairs={{0,4},{4,8},{8,12},{1,5},{5,9},{9,13},{2,6},{6,10},{10,14},{3,7},{... | collective-permute-start | bytes 1032200 | tf_op jit(solution)/shard_map/ppermute | solution.py:526
  24.0 1.1 %begin.6.refs_0_ = f32[2,192,384]{2,1,0:T(8,128)S(1)} custom-call(bf16[2,3,192,384]{3,2,1,0:T(8,128)(2,1)S(1)} %get-tuple-element.77.shifted_ref, bf16[576,1728]{1,0:T(8,128)(2,1)S(1)} %get-tuple-element.78.w_ref), custom_call_target="tpu_custom_call" | custom-call | tf_op jit(solution)/shard_map/begin/pallas_call | solution.py:340
  25.1 2.0 %conv_0.3 = (bf16[2,192,512]{2,1,0:T(8,128)(2,1)S(1)}, bf16[2,3,192,384]{3,2,1,0:T(8,128)(2,1)S(1)}) custom-call(bf16[2,3,192,512]{3,2,1,0:T(8,128)(2,1)S(1)} %get-tuple-element.72.shifted_ref, bf16[2,192,512]{2,1,0:T(8,128)(2,1)S(1)} %get-tuple-element.73.values_ref, bf16[576,1728]{1,0:T(8,128)(2,1)S(1)} %get-tuple-element.66.w_ref, ...), custom_call_target="tpu_custom_call" | custom-call | flops 2038431744 | bytes 1990656 | tf_op jit(solution)/shard_map/conv_0/pallas_call | solution.py:464
  27.0 1.7 %conv_1.3 = (bf16[2,192,384]{2,1,0:T(8,128)(2,1)S(1)}, bf16[2,3,192,384]{3,2,1,0:T(8,128)(2,1)S(1)}, bf16[2,192,384]{2,1,0:T(8,128)(2,1)S(1)}) custom-call(bf16[2,3,192,384]{3,2,1,0:T(8,128)(2,1)S(1)} %get-tuple-element.77.shifted_ref, bf16[2,192,512]{2,1,0:T(8,128)(2,1)S(1)} %get-tuple-element.86.values_ref, bf16[576,1728]{1,0:T(8,128)(2,1)S(1)} %get-tuple-element.78.w_ref, ...), custom_call_target="tpu_custom_call" | custom-call | flops 1528823808 | bytes 1990656 | tf_op jit(solution)/shard_map/conv_1/pallas_call | solution.py:464
  28.7 3.9 %collective-permute-start.6 = (bf16[2,192,384]{2,1,0:T(8,128)(2,1)S(1)}, bf16[2,192,384]{2,1,0:T(8,128)(2,1)S(1)}, u32[]{:S(2)}, u32[]{:S(2)}) collective-permute-start(bf16[2,192,384]{2,1,0:T(8,128)(2,1)S(1)} %get-tuple-element.88), channel_id=1, source_target_pairs={{0,4},{4,8},{8,12},{1,5},{5,9},{9,13},{2,6},{6,10},{10,14},{3,7},{... | collective-permute-start | bytes 884744 | tf_op jit(solution)/shard_map/ppermute | solution.py:526
  32.6 0.0 collective-permute-done.5.refs_0_
  32.6 2.3 %conv_1.2 = (bf16[2,192,384]{2,1,0:T(8,128)(2,1)S(1)}, bf16[2,3,192,384]{3,2,1,0:T(8,128)(2,1)S(1)}) custom-call(bf16[2,3,192,384]{3,2,1,0:T(8,128)(2,1)S(1)} %get-tuple-element.80.shifted_ref.refs_1_, bf16[2,192,512]{2,1,0:T(8,128)(2,1)S(1)} %get-tuple-element.81.values_ref, bf16[576,1728]{1,0:T(8,128)(2,1)S(1)} %get-tuple-element.78.w_ref, ...), custom_call_target="tpu_custom_call" | custom-call | flops 1528823808 | bytes 1990656 | tf_op jit(solution)/shard_map/conv_1/pallas_call | solution.py:464
  34.9 1.1 %begin.7.refs_0_ = f32[2,192,384]{2,1,0:T(8,128)S(1)} custom-call(bf16[2,3,192,384]{3,2,1,0:T(8,128)(2,1)S(1)} %get-tuple-element.83.shifted_ref.refs_0_, bf16[576,1728]{1,0:T(8,128)(2,1)S(1)} %get-tuple-element.85.w_ref), custom_call_target="tpu_custom_call" | custom-call | tf_op jit(solution)/shard_map/begin/pallas_call | solution.py:340
  36.0 2.1 %conv_2.3 = (bf16[2,192,128]{2,1,0:T(8,128)(2,1)S(1)}, bf16[2,192,128]{2,1,0:T(8,128)(2,1)S(1)}) custom-call(bf16[2,3,192,384]{3,2,1,0:T(8,128)(2,1)S(1)} %get-tuple-element.91.shifted_ref, bf16[2,192,384]{2,1,0:T(8,128)(2,1)S(1)} %get-tuple-element.92.values_ref, bf16[576,1728]{1,0:T(8,128)(2,1)S(1)} %get-tuple-element.85.w_ref, ...), custom_call_target="tpu_custom_call" | custom-call | flops 1528823808 | bytes 1990656 | tf_op jit(solution)/shard_map/conv_2/pallas_call | solution.py:464
  38.1 0.1 collective-permute-start.8
  38.2 1.6 %conv_2.2 = (bf16[2,192,128]{2,1,0:T(8,128)(2,1)S(1)}, bf16[2,192,128]{2,1,0:T(8,128)(2,1)S(1)}) custom-call(bf16[2,3,192,384]{3,2,1,0:T(8,128)(2,1)S(1)} %get-tuple-element.83.shifted_ref.refs_0_, bf16[2,192,384]{2,1,0:T(8,128)(2,1)S(1)} %get-tuple-element.84.values_ref, bf16[576,1728]{1,0:T(8,128)(2,1)S(1)} %get-tuple-element.85.w_ref, ...), custom_call_target="tpu_custom_call" | custom-call | flops 1528823808 | bytes 1990656 | tf_op jit(solution)/shard_map/conv_2/pallas_call | solution.py:464
  39.8 0.6 %collective-permute-start.7 = (bf16[2,192,128]{2,1,0:T(8,128)(2,1)S(1)}, bf16[2,192,128]{2,1,0:T(8,128)(2,1)S(1)}, u32[]{:S(2)}, u32[]{:S(2)}) collective-permute-start(bf16[2,192,128]{2,1,0:T(8,128)(2,1)S(1)} %get-tuple-element.90), channel_id=1, source_target_pairs={{0,1},{1,0},{2,3},{3,2},{4,5},{5,4},{6,7},{7,6},{8,9},{9,8},{10,11... | collective-permute-start | bytes 294920 | tf_op jit(solution)/shard_map/ppermute | solution.py:523
  40.4 0.0 collective-permute-done.8.got_ref
  40.4 0.8 %join.2.refs_0_ = bf16[4,2,192,128]{3,2,1,0:T(8,128)(2,1)} custom-call(bf16[2,192,128]{2,1,0:T(8,128)(2,1)S(1)} %get-tuple-element.93.kept_ref, bf16[2,192,128]{2,1,0:T(8,128)(2,1)S(1)} %collective-permute-done.8.got_ref), custom_call_target="tpu_custom_call" | custom-call | tf_op jit(solution)/shard_map/join/pallas_call | solution.py:504
  41.2 0.1 collective-permute-done.7.got_ref
  41.3 0.8 %join.3 = bf16[4,2,192,128]{3,2,1,0:T(8,128)(2,1)} custom-call(bf16[2,192,128]{2,1,0:T(8,128)(2,1)S(1)} %get-tuple-element.89.kept_ref, bf16[2,192,128]{2,1,0:T(8,128)(2,1)S(1)} %collective-permute-done.7.got_ref, bf16[4,2,192,128]{3,2,1,0:T(8,128)(2,1)} %join.2.refs_0_), custom_call_target="tpu_custom_call", output_to_operand_aliasing={{}: (2, {})} | custom-call | tf_op jit(solution)/shard_map/join/pallas_call | solution.py:504
  (5 shorter events, 0.0 us)
Async XLA Ops:
  0.0 8.3 %collective-permute-start.1 = (bf16[4,2,192,128]{3,2,1,0:T(8,128)(2,1)}, bf16[4,2,192,128]{3,2,1,0:T(8,128)(2,1)S(1)}, u32[]{:S(2)}, u32[]{:S(2)}) collective-permute-start(bf16[4,2,192,128]{3,2,1,0:T(8,128)(2,1)} %in_ref.1), channel_id=1, source_target_pairs={{0,1},{1,0},{2,3},{3,2},{4,5},{5,4},{6,7},{7,6},{8,9},{9,8},{10,11... | collective-permute-start | bytes 1179656 | tf_op jit(solution)/shard_map/ppermute | solution.py:523
  0.5 1.0 %copy-start = (bf16[4,2,192,128]{3,2,1,0:T(8,128)(2,1)S(1)}, bf16[4,2,192,128]{3,2,1,0:T(8,128)(2,1)}, u32[]{:S(2)}) copy-start(bf16[4,2,192,128]{3,2,1,0:T(8,128)(2,1)} %in_ref.1) | copy-start | bytes 1179652
  1.5 8.1 %collective-permute-start = (bf16[2,2,192,128]{3,2,1,0:T(8,128)(2,1)S(1)}, bf16[2,2,192,128]{3,2,1,0:T(8,128)(2,1)S(1)}, u32[]{:S(2)}, u32[]{:S(2)}) collective-permute-start(bf16[2,2,192,128]{3,2,1,0:T(8,128)(2,1)S(1)} %get-tuple-element.50.refs_1_), channel_id=1, source_target_pairs={{0,2},{1,3},{2,0},{3,1},{4,6},{5,7},{6,4},{7,5},{8,10},{9,11},{10,... | collective-permute-start | bytes 589832 | tf_op jit(solution)/shard_map/ppermute | solution.py:529
  9.6 1.7 %collective-permute-start.2 = (bf16[2,2,192,128]{3,2,1,0:T(8,128)(2,1)S(1)}, bf16[2,2,192,128]{3,2,1,0:T(8,128)(2,1)S(1)}, u32[]{:S(2)}, u32[]{:S(2)}) collective-permute-start(bf16[2,2,192,128]{3,2,1,0:T(8,128)(2,1)S(1)} %collective-permute-done.far_ref), channel_id=1, source_target_pairs={{0,1},{1,0},{2,3},{3,2},{4,5},{5,4},{6,7},{7,6},{8,9},{9,8},{10,11... | collective-permute-start | bytes 589832 | tf_op jit(solution)/shard_map/ppermute | solution.py:523
  9.6 7.3 %collective-permute-start.3 = (bf16[2,192,256]{2,1,0:T(8,128)(2,1)S(1)}, bf16[2,192,256]{2,1,0:T(8,128)(2,1)S(1)}, u32[]{:S(2)}, u32[]{:S(2)}) collective-permute-start(bf16[2,192,256]{2,1,0:T(8,128)(2,1)S(1)} %get-tuple-element.67), channel_id=1, source_target_pairs={{0,2},{1,3},{2,0},{3,1},{4,6},{5,7},{6,4},{7,5},{8,10},{9,11},{10,... | collective-permute-start | bytes 589832 | tf_op jit(solution)/shard_map/ppermute | solution.py:529
  11.9 13.2 %collective-permute-start.4 = (bf16[2,192,512]{2,1,0:T(8,128)(2,1)S(1)}, bf16[2,192,512]{2,1,0:T(8,128)(2,1)S(1)}, u32[]{:S(2)}, u32[]{:S(2)}) collective-permute-start(bf16[2,192,512]{2,1,0:T(8,128)(2,1)S(1)} %get-tuple-element.76), channel_id=1, source_target_pairs={{0,4},{4,8},{8,12},{1,5},{5,9},{9,13},{2,6},{6,10},{10,14},{3,7},{... | collective-permute-start | bytes 1179656 | tf_op jit(solution)/shard_map/ppermute | solution.py:526
  20.2 12.4 %collective-permute-start.5 = (bf16[192,896]{1,0:T(8,128)(2,1)S(1)}, bf16[192,896]{1,0:T(8,128)(2,1)S(1)}, u32[]{:S(2)}, u32[]{:S(2)}) collective-permute-start(bf16[192,896]{1,0:T(8,128)(2,1)S(1)} %get-tuple-element.82), channel_id=1, source_target_pairs={{0,4},{4,8},{8,12},{1,5},{5,9},{9,13},{2,6},{6,10},{10,14},{3,7},{... | collective-permute-start | bytes 1032200 | tf_op jit(solution)/shard_map/ppermute | solution.py:526
  28.7 9.5 %collective-permute-start.6 = (bf16[2,192,384]{2,1,0:T(8,128)(2,1)S(1)}, bf16[2,192,384]{2,1,0:T(8,128)(2,1)S(1)}, u32[]{:S(2)}, u32[]{:S(2)}) collective-permute-start(bf16[2,192,384]{2,1,0:T(8,128)(2,1)S(1)} %get-tuple-element.88), channel_id=1, source_target_pairs={{0,4},{4,8},{8,12},{1,5},{5,9},{9,13},{2,6},{6,10},{10,14},{3,7},{... | collective-permute-start | bytes 884744 | tf_op jit(solution)/shard_map/ppermute | solution.py:526
  38.1 2.3 %collective-permute-start.8 = (bf16[2,192,128]{2,1,0:T(8,128)(2,1)S(1)}, bf16[2,192,128]{2,1,0:T(8,128)(2,1)S(1)}, u32[]{:S(2)}, u32[]{:S(2)}) collective-permute-start(bf16[2,192,128]{2,1,0:T(8,128)(2,1)S(1)} %get-tuple-element.94), channel_id=1, source_target_pairs={{0,1},{1,0},{2,3},{3,2},{4,5},{5,4},{6,7},{7,6},{8,9},{9,8},{10,11... | collective-permute-start | bytes 294920 | tf_op jit(solution)/shard_map/ppermute | solution.py:523
  39.8 1.5 %collective-permute-start.7 = (bf16[2,192,128]{2,1,0:T(8,128)(2,1)S(1)}, bf16[2,192,128]{2,1,0:T(8,128)(2,1)S(1)}, u32[]{:S(2)}, u32[]{:S(2)}) collective-permute-start(bf16[2,192,128]{2,1,0:T(8,128)(2,1)S(1)} %get-tuple-element.90), channel_id=1, source_target_pairs={{0,1},{1,0},{2,3},{3,2},{4,5},{5,4},{6,7},{7,6},{8,9},{9,8},{10,11... | collective-permute-start | bytes 294920 | tf_op jit(solution)/shard_map/ppermute | solution.py:523

commit v13 on v12

--- a/solution.py
+++ b/solution.py
@@ -128,7 +128,7 @@
     lane = lane_of(LANES)
     block, low = divmod(row * pitch, LANES)
     shift = lax.rem(low + LANES - core * (width - window), LANES)
-    turned = pltpu.roll(line, shift, 1)
+    turned = moved(line, shift)
     here = (lane >= low) & (lane < low + window)
     blocks[block] = blocks.get(block, 0.0) + jnp.where(here, turned, 0.0)
     if low + window > LANES:
@@ -152,7 +152,7 @@
             index = at + group * (rows - 1 - 2 * at)
             own, mate = own_refs[p][t, index], mate_ref[f, index]
             one, two = (own, mate) if row < rows else (mate, own)
-            line = jnp.where(outer, one, two).astype(jnp.float32)
+            line = jnp.where(outer, one, two)
             placed(blocks, core, row, window, line)
             there = 4 * rows - 1 - row
             if p < pairs - 1 and there < 2 * rows + halo:
@@ -195,7 +195,7 @@
         at = local % rows
         index = at + (1 - group) * (rows - 1 - 2 * at)
         one, two = (mate_ref, far_ref) if local < rows else (far_ref, mate_ref)
-        line = jnp.where(outer, one[t, index], two[t, index]).astype(jnp.float32)
+        line = jnp.where(outer, one[t, index], two[t, index])
         placed(blocks, core, row, width // 2 + halo, line)
 
 
@@ -251,6 +251,10 @@
         [sums[tap * channels : (tap + 1) * channels, at : at + LANES] for at in range(0, lanes, LANES)]
         for tap in range(3)
     ]
+
+
+def moved(block, shift):
+    return pltpu.roll(block, shift, 1).astype(jnp.float32)
 
 
 def column_sums(taps):
@@ -395,11 +399,11 @@
             if begun_ref is not None:
                 conv = conv + begun_ref[t, :, at]
             total = (values_ref[t, :, at].astype(jnp.float32) + conv + bias).astype(jnp.bfloat16)
-            totals.append(total.astype(jnp.float32))
+            totals.append(total)
             if last:
                 continue
             outs[0][t, :, at] = total
-            acts.append(activated(totals[-1], gain, mask[:, at]))
+            acts.append(activated(total.astype(jnp.float32), gain, mask[:, at]))
             if not sends:
                 continue
             if not rest_sent:
@@ -418,10 +422,10 @@
         def columns_of(row, to):
             b, low = divmod(row * pitch, LANES)
             shift = lax.rem(to + 2 * LANES - low - skipped, LANES)
-            turned = pltpu.roll(totals[b], shift, 1)
+            turned = moved(totals[b], shift)
             if low + pitch - 1 <= LANES:
                 return turned
-            return jnp.where(lane < to + LANES - low - skipped, turned, pltpu.roll(totals[b + 1], shift, 1))
+            return jnp.where(lane < to + LANES - low - skipped, turned, moved(totals[b + 1], shift))
 
         def rows_of(row):
             return jnp.where(lane < half, columns_of(row, 0), columns_of(row + 1, half))

time: 42.5 us -> 42.5 us (level)
  no operation moved by 1% of the time
where the time goes in v13:
time: 42.5 us; the launch traced here: 42.2 us
  Pallas kernels  22.6 us (53%)
  starting transfers between devices  16.6 us (39%)
  waiting for transfers between devices  1.06 us (2%)
  local copies, waits for them, and re-layouts  1 us (2%)
  other arithmetic  0.71 us (2%)
    pallas_call x6, Pallas kernels, conv(): pl.pallas_call(functools.partial(conv_kernel, plan), out_shape=out_shape,...  11.7 us
    ppermute x3, starting transfers between devices, earlier_of(): return lax.ppermute(block, 'tm', [(i, i + 1) for i in range(blocks - 1)])  11.2 us
    pallas_call x4, Pallas kernels, begin(): pl.pallas_call(begin_kernel, out_shape=jax.ShapeDtypeStruct((PAIR, channe...  4.54 us
    ppermute x2, starting transfers between devices, beyond_of(): return lax.ppermute(block, 'rows', [(i, i ^ 2) for i in range(strips)])  4.29 us
    pallas_call x1, Pallas kernels, weights(): pl.pallas_call(weights_kernel, out_shape=(one,) * layers + (jax.ShapeDtyp...  3.54 us
    pallas_call x2, Pallas kernels, join(): pl.pallas_call(functools.partial(join_kernel, pair), out_shape=jax.ShapeD...  1.58 us
    ppermute x4, starting transfers between devices, mate_of(): return lax.ppermute(block, 'rows', [(i, i ^ 1) for i in range(strips)])  1.08 us
    unnamed x2, local copies, waits for them, and re-layouts  1 us
  transfers between devices with their start and end apart: 9, of which 3 were waited for; matrix products, arithmetic and copies ran while one was open for 2% of the time, Pallas kernels for 52%

profile of v13, /device:TPU:0, one launch (start us, length us, event | category | flops | bytes accessed | tf_op | source)
XLA Modules:
  0.0 42.2 jit_solution(5672700911835798164)
XLA Ops:
  0.0 0.5 %collective-permute-start.1 = (bf16[4,2,192,128]{3,2,1,0:T(8,128)(2,1)}, bf16[4,2,192,128]{3,2,1,0:T(8,128)(2,1)S(1)}, u32[]{:S(2)}, u32[]{:S(2)}) collective-permute-start(bf16[4,2,192,128]{3,2,1,0:T(8,128)(2,1)} %in_ref.1), channel_id=1, source_target_pairs={{0,1},{1,0},{2,3},{3,2},{4,5},{5,4},{6,7},{7,6},{8,9},{9,8},{10,11... | collective-permute-start | bytes 1179656 | tf_op jit(solution)/shard_map/ppermute | solution.py:527
  0.5 1.0 %copy-done = bf16[4,2,192,128]{3,2,1,0:T(8,128)(2,1)S(1)} copy-done((bf16[4,2,192,128]{3,2,1,0:T(8,128)(2,1)S(1)}, bf16[4,2,192,128]{3,2,1,0:T(8,128)(2,1)}, u32[]{:S(2)}) %copy-start) | copy-done | bytes 393240
  1.5 2.6 %collective-permute-start = (bf16[2,2,192,128]{3,2,1,0:T(8,128)(2,1)S(1)}, bf16[2,2,192,128]{3,2,1,0:T(8,128)(2,1)S(1)}, u32[]{:S(2)}, u32[]{:S(2)}) collective-permute-start(bf16[2,2,192,128]{3,2,1,0:T(8,128)(2,1)S(1)} %get-tuple-element.50.refs_1_), channel_id=1, source_target_pairs={{0,2},{1,3},{2,0},{3,1},{4,6},{5,7},{6,4},{7,5},{8,10},{9,11},{10,... | collective-permute-start | bytes 589832 | tf_op jit(solution)/shard_map/ppermute | solution.py:533
  4.0 0.7 %pad_maximum_fusion.rows_ref.gains_ref = f32[6,192]{1,0:T(8,128)S(1)} fusion(f32[3,192]{1,0:T(4,128)} %param.7, f32[3,192]{1,0:T(4,128)} %param.6), kind=kLoop, calls=%fused_computation | loop fusion | flops 1152 | bytes 9216 | tf_op jit(solution)/shard_map/concatenate | solution.py:539
  4.7 3.5 %weights.1 = (bf16[576,1728]{1,0:T(8,128)(2,1)S(1)}, bf16[576,1728]{1,0:T(8,128)(2,1)S(1)}, bf16[576,1728]{1,0:T(8,128)(2,1)S(1)}, f32[3,2,192,128]{3,2,1,0:T(8,128)S(1)}) custom-call(bf16[3,27,192,192]{3,2,1,0:T(8,128)(2,1)} %w_ref.1, f32[6,192]{1,0:T(8,128)S(1)} %pad_maximum_fusion.rows_ref.gains_ref), custom_call_target="tpu_custom_call" | custom-call | bytes 11943936 | tf_op jit(solution)/shard_map/weights/pallas_call | solution.py:77
  8.3 0.0 collective-permute-done.1.mate_ref
  8.3 0.7 %near.1 = (bf16[2,192,384]{2,1,0:T(8,128)(2,1)S(1)}, bf16[2,192,384]{2,1,0:T(8,128)(2,1)S(1)}, bf16[2,192,256]{2,1,0:T(8,128)(2,1)S(1)}, bf16[2,192,256]{2,1,0:T(8,128)(2,1)S(1)}, bf16[2,192,256]{2,1,0:T(8,128)(2,1)S(1)}) custom-call(bf16[4,2,192,128]{3,2,1,0:T(8,128)(2,1)S(1)} %collective-permute-done.1.mate_ref, ...), custom_call_target="tpu_custom_call" | custom-call | flops 7864320 | bytes 1572864 | tf_op jit(solution)/shard_map/near/pallas_call | solution.py:176
  9.0 0.6 %collective-permute-done.far_ref = bf16[2,2,192,128]{3,2,1,0:T(8,128)(2,1)S(1)} collective-permute-done((bf16[2,2,192,128]{3,2,1,0:T(8,128)(2,1)S(1)}, bf16[2,2,192,128]{3,2,1,0:T(8,128)(2,1)S(1)}, u32[]{:S(2)}, u32[]{:S(2)}) %collective-permute-start) | collective-permute-done | bytes 196640 | tf_op jit(solution)/shard_map/ppermute | solution.py:533
  9.6 0.0 collective-permute-start.2
  9.6 1.7 %collective-permute-start.3 = (bf16[2,192,256]{2,1,0:T(8,128)(2,1)S(1)}, bf16[2,192,256]{2,1,0:T(8,128)(2,1)S(1)}, u32[]{:S(2)}, u32[]{:S(2)}) collective-permute-start(bf16[2,192,256]{2,1,0:T(8,128)(2,1)S(1)} %get-tuple-element.67), channel_id=1, source_target_pairs={{0,2},{1,3},{2,0},{3,1},{4,6},{5,7},{6,4},{7,5},{8,10},{9,11},{10,... | collective-permute-start | bytes 589832 | tf_op jit(solution)/shard_map/ppermute | solution.py:533
  11.4 0.0 collective-permute-done.2.mate_ref
  11.4 0.5 %beyond.1 = (bf16[2,192,512]{2,1,0:T(8,128)(2,1)S(1)}, bf16[2,3,192,512]{3,2,1,0:T(8,128)(2,1)S(1)}, bf16[2,192,512]{2,1,0:T(8,128)(2,1)S(1)}) custom-call(f32[3,2,192,128]{3,2,1,0:T(8,128)S(1)} %get-tuple-element.60.columns_ref, bf16[2,2,192,128]{3,2,1,0:T(8,128)(2,1)S(1)} %collective-permute-done.far_ref, ...), custom_call_target="tpu_custom_call" | custom-call | flops 3932160 | bytes 786432 | tf_op jit(solution)/shard_map/beyond/pallas_call | solution.py:237
  11.9 3.5 %collective-permute-start.4 = (bf16[2,192,512]{2,1,0:T(8,128)(2,1)S(1)}, bf16[2,192,512]{2,1,0:T(8,128)(2,1)S(1)}, u32[]{:S(2)}, u32[]{:S(2)}) collective-permute-start(bf16[2,192,512]{2,1,0:T(8,128)(2,1)S(1)} %get-tuple-element.76), channel_id=1, source_target_pairs={{0,4},{4,8},{8,12},{1,5},{5,9},{9,13},{2,6},{6,10},{10,14},{3,7},{... | collective-permute-start | bytes 1179656 | tf_op jit(solution)/shard_map/ppermute | solution.py:530
  15.4 1.2 %begin.4.refs_0_ = f32[2,192,512]{2,1,0:T(8,128)S(1)} custom-call(bf16[2,3,192,512]{3,2,1,0:T(8,128)(2,1)S(1)} %get-tuple-element.64.shifted_ref, bf16[576,1728]{1,0:T(8,128)(2,1)S(1)} %get-tuple-element.66.w_ref), custom_call_target="tpu_custom_call" | custom-call | tf_op jit(solution)/shard_map/begin/pallas_call | solution.py:344
  16.6 0.3 collective-permute-done.3.refs_1_
  16.9 2.1 %conv_0.2 = (bf16[2,192,512]{2,1,0:T(8,128)(2,1)S(1)}, bf16[2,3,192,384]{3,2,1,0:T(8,128)(2,1)S(1)}, bf16[192,896]{1,0:T(8,128)(2,1)S(1)}, bf16[2,192,512]{2,1,0:T(8,128)(2,1)S(1)}, bf16[2,3,192,512]{3,2,1,0:T(8,128)(2,1)S(1)}) custom-call(bf16[2,3,192,512]{3,2,1,0:T(8,128)(2,1)S(1)} %get-tuple-element.64.shifted_ref, ...), custom_call_target="tpu_custom_call" | custom-call | flops 4076863488 | bytes 1990656 | tf_op jit(solution)/shard_map/conv_0/pallas_call | solution.py:468
  19.0 1.2 %begin.5.refs_0_ = f32[2,192,512]{2,1,0:T(8,128)S(1)} custom-call(bf16[2,3,192,512]{3,2,1,0:T(8,128)(2,1)S(1)} %get-tuple-element.72.shifted_ref, bf16[576,1728]{1,0:T(8,128)(2,1)S(1)} %get-tuple-element.66.w_ref), custom_call_target="tpu_custom_call" | custom-call | tf_op jit(solution)/shard_map/begin/pallas_call | solution.py:344
  20.2 3.8 %collective-permute-start.5 = (bf16[192,896]{1,0:T(8,128)(2,1)S(1)}, bf16[192,896]{1,0:T(8,128)(2,1)S(1)}, u32[]{:S(2)}, u32[]{:S(2)}) collective-permute-start(bf16[192,896]{1,0:T(8,128)(2,1)S(1)} %get-tuple-element.82), channel_id=1, source_target_pairs={{0,4},{4,8},{8,12},{1,5},{5,9},{9,13},{2,6},{6,10},{10,14},{3,7},{... | collective-permute-start | bytes 1032200 | tf_op jit(solution)/shard_map/ppermute | solution.py:530
  24.0 1.1 %begin.6.refs_0_ = f32[2,192,384]{2,1,0:T(8,128)S(1)} custom-call(bf16[2,3,192,384]{3,2,1,0:T(8,128)(2,1)S(1)} %get-tuple-element.77.shifted_ref, bf16[576,1728]{1,0:T(8,128)(2,1)S(1)} %get-tuple-element.78.w_ref), custom_call_target="tpu_custom_call" | custom-call | tf_op jit(solution)/shard_map/begin/pallas_call | solution.py:344
  25.1 2.0 %conv_0.3 = (bf16[2,192,512]{2,1,0:T(8,128)(2,1)S(1)}, bf16[2,3,192,384]{3,2,1,0:T(8,128)(2,1)S(1)}) custom-call(bf16[2,3,192,512]{3,2,1,0:T(8,128)(2,1)S(1)} %get-tuple-element.72.shifted_ref, bf16[2,192,512]{2,1,0:T(8,128)(2,1)S(1)} %get-tuple-element.73.values_ref, bf16[576,1728]{1,0:T(8,128)(2,1)S(1)} %get-tuple-element.66.w_ref, ...), custom_call_target="tpu_custom_call" | custom-call | flops 2038431744 | bytes 1990656 | tf_op jit(solution)/shard_map/conv_0/pallas_call | solution.py:468
  27.0 1.7 %conv_1.3 = (bf16[2,192,384]{2,1,0:T(8,128)(2,1)S(1)}, bf16[2,3,192,384]{3,2,1,0:T(8,128)(2,1)S(1)}, bf16[2,192,384]{2,1,0:T(8,128)(2,1)S(1)}) custom-call(bf16[2,3,192,384]{3,2,1,0:T(8,128)(2,1)S(1)} %get-tuple-element.77.shifted_ref, bf16[2,192,512]{2,1,0:T(8,128)(2,1)S(1)} %get-tuple-element.86.values_ref, bf16[576,1728]{1,0:T(8,128)(2,1)S(1)} %get-tuple-element.78.w_ref, ...), custom_call_target="tpu_custom_call" | custom-call | flops 1528823808 | bytes 1990656 | tf_op jit(solution)/shard_map/conv_1/pallas_call | solution.py:468
  28.7 3.9 %collective-permute-start.6 = (bf16[2,192,384]{2,1,0:T(8,128)(2,1)S(1)}, bf16[2,192,384]{2,1,0:T(8,128)(2,1)S(1)}, u32[]{:S(2)}, u32[]{:S(2)}) collective-permute-start(bf16[2,192,384]{2,1,0:T(8,128)(2,1)S(1)} %get-tuple-element.88), channel_id=1, source_target_pairs={{0,4},{4,8},{8,12},{1,5},{5,9},{9,13},{2,6},{6,10},{10,14},{3,7},{... | collective-permute-start | bytes 884744 | tf_op jit(solution)/shard_map/ppermute | solution.py:530
  32.6 2.3 %conv_1.2 = (bf16[2,192,384]{2,1,0:T(8,128)(2,1)S(1)}, bf16[2,3,192,384]{3,2,1,0:T(8,128)(2,1)S(1)}) custom-call(bf16[2,3,192,384]{3,2,1,0:T(8,128)(2,1)S(1)} %get-tuple-element.80.shifted_ref.refs_1_, bf16[2,192,512]{2,1,0:T(8,128)(2,1)S(1)} %get-tuple-element.81.values_ref, bf16[576,1728]{1,0:T(8,128)(2,1)S(1)} %get-tuple-element.78.w_ref, ...), custom_call_target="tpu_custom_call" | custom-call | flops 1528823808 | bytes 1990656 | tf_op jit(solution)/shard_map/conv_1/pallas_call | solution.py:468
  34.9 1.1 %begin.7.refs_0_ = f32[2,192,384]{2,1,0:T(8,128)S(1)} custom-call(bf16[2,3,192,384]{3,2,1,0:T(8,128)(2,1)S(1)} %get-tuple-element.83.shifted_ref.refs_0_, bf16[576,1728]{1,0:T(8,128)(2,1)S(1)} %get-tuple-element.85.w_ref), custom_call_target="tpu_custom_call" | custom-call | tf_op jit(solution)/shard_map/begin/pallas_call | solution.py:344
  36.0 2.1 %conv_2.3 = (bf16[2,192,128]{2,1,0:T(8,128)(2,1)S(1)}, bf16[2,192,128]{2,1,0:T(8,128)(2,1)S(1)}) custom-call(bf16[2,3,192,384]{3,2,1,0:T(8,128)(2,1)S(1)} %get-tuple-element.91.shifted_ref, bf16[2,192,384]{2,1,0:T(8,128)(2,1)S(1)} %get-tuple-element.92.values_ref, bf16[576,1728]{1,0:T(8,128)(2,1)S(1)} %get-tuple-element.85.w_ref, ...), custom_call_target="tpu_custom_call" | custom-call | flops 1528823808 | bytes 1990656 | tf_op jit(solution)/shard_map/conv_2/pallas_call | solution.py:468
  38.1 0.1 collective-permute-start.8
  38.1 0.0 collective-permute-done.6.refs_1_
  38.2 1.6 %conv_2.2 = (bf16[2,192,128]{2,1,0:T(8,128)(2,1)S(1)}, bf16[2,192,128]{2,1,0:T(8,128)(2,1)S(1)}) custom-call(bf16[2,3,192,384]{3,2,1,0:T(8,128)(2,1)S(1)} %get-tuple-element.83.shifted_ref.refs_0_, bf16[2,192,384]{2,1,0:T(8,128)(2,1)S(1)} %get-tuple-element.84.values_ref, bf16[576,1728]{1,0:T(8,128)(2,1)S(1)} %get-tuple-element.85.w_ref, ...), custom_call_target="tpu_custom_call" | custom-call | flops 1528823808 | bytes 1990656 | tf_op jit(solution)/shard_map/conv_2/pallas_call | solution.py:468
  39.8 0.6 %collective-permute-start.7 = (bf16[2,192,128]{2,1,0:T(8,128)(2,1)S(1)}, bf16[2,192,128]{2,1,0:T(8,128)(2,1)S(1)}, u32[]{:S(2)}, u32[]{:S(2)}) collective-permute-start(bf16[2,192,128]{2,1,0:T(8,128)(2,1)S(1)} %get-tuple-element.90), channel_id=1, source_target_pairs={{0,1},{1,0},{2,3},{3,2},{4,5},{5,4},{6,7},{7,6},{8,9},{9,8},{10,11... | collective-permute-start | bytes 294920 | tf_op jit(solution)/shard_map/ppermute | solution.py:527
  40.3 0.8 %join.2.refs_0_ = bf16[4,2,192,128]{3,2,1,0:T(8,128)(2,1)} custom-call(bf16[2,192,128]{2,1,0:T(8,128)(2,1)S(1)} %get-tuple-element.93.kept_ref, bf16[2,192,128]{2,1,0:T(8,128)(2,1)S(1)} %collective-permute-done.8.got_ref), custom_call_target="tpu_custom_call" | custom-call | tf_op jit(solution)/shard_map/join/pallas_call | solution.py:508
  41.1 0.1 collective-permute-done.7.got_ref
  41.3 0.8 %join.3 = bf16[4,2,192,128]{3,2,1,0:T(8,128)(2,1)} custom-call(bf16[2,192,128]{2,1,0:T(8,128)(2,1)S(1)} %get-tuple-element.89.kept_ref, bf16[2,192,128]{2,1,0:T(8,128)(2,1)S(1)} %collective-permute-done.7.got_ref, bf16[4,2,192,128]{3,2,1,0:T(8,128)(2,1)} %join.2.refs_0_), custom_call_target="tpu_custom_call", output_to_operand_aliasing={{}: (2, {})} | custom-call | tf_op jit(solution)/shard_map/join/pallas_call | solution.py:508
  (5 shorter events, 0.0 us)
Async XLA Ops:
  0.0 8.3 %collective-permute-start.1 = (bf16[4,2,192,128]{3,2,1,0:T(8,128)(2,1)}, bf16[4,2,192,128]{3,2,1,0:T(8,128)(2,1)S(1)}, u32[]{:S(2)}, u32[]{:S(2)}) collective-permute-start(bf16[4,2,192,128]{3,2,1,0:T(8,128)(2,1)} %in_ref.1), channel_id=1, source_target_pairs={{0,1},{1,0},{2,3},{3,2},{4,5},{5,4},{6,7},{7,6},{8,9},{9,8},{10,11... | collective-permute-start | bytes 1179656 | tf_op jit(solution)/shard_map/ppermute | solution.py:527
  0.5 1.0 %copy-start = (bf16[4,2,192,128]{3,2,1,0:T(8,128)(2,1)S(1)}, bf16[4,2,192,128]{3,2,1,0:T(8,128)(2,1)}, u32[]{:S(2)}) copy-start(bf16[4,2,192,128]{3,2,1,0:T(8,128)(2,1)} %in_ref.1) | copy-start | bytes 1179652
  1.5 8.1 %collective-permute-start = (bf16[2,2,192,128]{3,2,1,0:T(8,128)(2,1)S(1)}, bf16[2,2,192,128]{3,2,1,0:T(8,128)(2,1)S(1)}, u32[]{:S(2)}, u32[]{:S(2)}) collective-permute-start(bf16[2,2,192,128]{3,2,1,0:T(8,128)(2,1)S(1)} %get-tuple-element.50.refs_1_), channel_id=1, source_target_pairs={{0,2},{1,3},{2,0},{3,1},{4,6},{5,7},{6,4},{7,5},{8,10},{9,11},{10,... | collective-permute-start | bytes 589832 | tf_op jit(solution)/shard_map/ppermute | solution.py:533
  9.6 1.7 %collective-permute-start.2 = (bf16[2,2,192,128]{3,2,1,0:T(8,128)(2,1)S(1)}, bf16[2,2,192,128]{3,2,1,0:T(8,128)(2,1)S(1)}, u32[]{:S(2)}, u32[]{:S(2)}) collective-permute-start(bf16[2,2,192,128]{3,2,1,0:T(8,128)(2,1)S(1)} %collective-permute-done.far_ref), channel_id=1, source_target_pairs={{0,1},{1,0},{2,3},{3,2},{4,5},{5,4},{6,7},{7,6},{8,9},{9,8},{10,11... | collective-permute-start | bytes 589832 | tf_op jit(solution)/shard_map/ppermute | solution.py:527
  9.6 7.3 %collective-permute-start.3 = (bf16[2,192,256]{2,1,0:T(8,128)(2,1)S(1)}, bf16[2,192,256]{2,1,0:T(8,128)(2,1)S(1)}, u32[]{:S(2)}, u32[]{:S(2)}) collective-permute-start(bf16[2,192,256]{2,1,0:T(8,128)(2,1)S(1)} %get-tuple-element.67), channel_id=1, source_target_pairs={{0,2},{1,3},{2,0},{3,1},{4,6},{5,7},{6,4},{7,5},{8,10},{9,11},{10,... | collective-permute-start | bytes 589832 | tf_op jit(solution)/shard_map/ppermute | solution.py:533
  11.9 13.2 %collective-permute-start.4 = (bf16[2,192,512]{2,1,0:T(8,128)(2,1)S(1)}, bf16[2,192,512]{2,1,0:T(8,128)(2,1)S(1)}, u32[]{:S(2)}, u32[]{:S(2)}) collective-permute-start(bf16[2,192,512]{2,1,0:T(8,128)(2,1)S(1)} %get-tuple-element.76), channel_id=1, source_target_pairs={{0,4},{4,8},{8,12},{1,5},{5,9},{9,13},{2,6},{6,10},{10,14},{3,7},{... | collective-permute-start | bytes 1179656 | tf_op jit(solution)/shard_map/ppermute | solution.py:530
  20.2 12.4 %collective-permute-start.5 = (bf16[192,896]{1,0:T(8,128)(2,1)S(1)}, bf16[192,896]{1,0:T(8,128)(2,1)S(1)}, u32[]{:S(2)}, u32[]{:S(2)}) collective-permute-start(bf16[192,896]{1,0:T(8,128)(2,1)S(1)} %get-tuple-element.82), channel_id=1, source_target_pairs={{0,4},{4,8},{8,12},{1,5},{5,9},{9,13},{2,6},{6,10},{10,14},{3,7},{... | collective-permute-start | bytes 1032200 | tf_op jit(solution)/shard_map/ppermute | solution.py:530
  28.7 9.4 %collective-permute-start.6 = (bf16[2,192,384]{2,1,0:T(8,128)(2,1)S(1)}, bf16[2,192,384]{2,1,0:T(8,128)(2,1)S(1)}, u32[]{:S(2)}, u32[]{:S(2)}) collective-permute-start(bf16[2,192,384]{2,1,0:T(8,128)(2,1)S(1)} %get-tuple-element.88), channel_id=1, source_target_pairs={{0,4},{4,8},{8,12},{1,5},{5,9},{9,13},{2,6},{6,10},{10,14},{3,7},{... | collective-permute-start | bytes 884744 | tf_op jit(solution)/shard_map/ppermute | solution.py:530
  38.1 2.3 %collective-permute-start.8 = (bf16[2,192,128]{2,1,0:T(8,128)(2,1)S(1)}, bf16[2,192,128]{2,1,0:T(8,128)(2,1)S(1)}, u32[]{:S(2)}, u32[]{:S(2)}) collective-permute-start(bf16[2,192,128]{2,1,0:T(8,128)(2,1)S(1)} %get-tuple-element.94), channel_id=1, source_target_pairs={{0,1},{1,0},{2,3},{3,2},{4,5},{5,4},{6,7},{7,6},{8,9},{9,8},{10,11... | collective-permute-start | bytes 294920 | tf_op jit(solution)/shard_map/ppermute | solution.py:527
  39.8 1.5 %collective-permute-start.7 = (bf16[2,192,128]{2,1,0:T(8,128)(2,1)S(1)}, bf16[2,192,128]{2,1,0:T(8,128)(2,1)S(1)}, u32[]{:S(2)}, u32[]{:S(2)}) collective-permute-start(bf16[2,192,128]{2,1,0:T(8,128)(2,1)S(1)} %get-tuple-element.90), channel_id=1, source_target_pairs={{0,1},{1,0},{2,3},{3,2},{4,5},{5,4},{6,7},{7,6},{8,9},{9,8},{10,11... | collective-permute-start | bytes 294920 | tf_op jit(solution)/shard_map/ppermute | solution.py:527

commit v14 on v13

--- a/solution.py
+++ b/solution.py
@@ -339,17 +339,62 @@
     by_frames(lanes, tile_sums, finish)
 
 
-def begin(shifted, weight):
+class Later:
+    def __init__(self, shape):
+        self.shape, self.dtype, self.value = shape.shape, shape.dtype, None
+
+
+def now(x):
+    return x.value if isinstance(x, Later) else x
+
+
+class Chain:
+    def __init__(self):
+        self.steps = []
+
+    def add(self, kernel, inputs, out_shape, scratch, flops):
+        outs = [Later(shape) for shape in out_shape]
+        self.steps.append((kernel, inputs, outs, out_shape, scratch, flops))
+        return outs
+
+    def run(self, name):
+        steps, self.steps = self.steps, []
+        made = {id(out): n for n, out in enumerate(out for step in steps for out in step[2])}
+        arrays = []
+        for step in steps:
+            for x in step[1]:
+                if id(x) not in made and not any(now(x) is y for y in arrays):
+                    arrays.append(now(x))
+        at = [[("out", made[id(x)]) if id(x) in made else ("in", next(i for i, y in enumerate(arrays) if y is now(x))) for x in step[1]] for step in steps]
+        out_shape = [shape for step in steps for shape in step[3]]
+        scratch = [shape for step in steps for shape in step[4]]
+
+        def kernel(*refs):
+            ins, outs, rest = refs[: len(arrays)], refs[len(arrays) : len(arrays) + len(out_shape)], refs[len(arrays) + len(out_shape) :]
+            first, held = 0, 0
+            for step, places in zip(steps, at):
+                own, kept = outs[first : first + len(step[3])], rest[held : held + len(step[4])]
+                first, held = first + len(own), held + len(kept)
+                step[0](*[(outs if kind == "out" else ins)[n] for kind, n in places], *own, *kept)
+
+        results = pl.pallas_call(
+            kernel,
+            out_shape=tuple(out_shape),
+            in_specs=[VMEM] * len(arrays),
+            out_specs=(VMEM,) * len(out_shape),
+            scratch_shapes=scratch,
+            compiler_params=pltpu.CompilerParams(vmem_limit_bytes=LIMIT),
+            cost_estimate=pl.CostEstimate(flops=sum(step[5] for step in steps), bytes_accessed=0, transcendentals=0),
+            name=name,
+        )(*arrays)
+        for out, value in zip((out for step in steps for out in step[2]), results):
+            out.value = value
+
+
+def begin(chain, shifted, weight):
     _, _, channels, lanes = shifted.shape
-    return pl.pallas_call(
-        begin_kernel,
-        out_shape=jax.ShapeDtypeStruct((PAIR, channels, lanes), jnp.float32),
-        in_specs=[VMEM] * 2,
-        out_specs=VMEM,
-        compiler_params=pltpu.CompilerParams(vmem_limit_bytes=LIMIT),
-        cost_estimate=pl.CostEstimate(flops=0, bytes_accessed=0, transcendentals=0),
-        name="begin",
-    )(shifted, weight)
+    out = jax.ShapeDtypeStruct((PAIR, channels, lanes), jnp.float32)
+    return chain.add(begin_kernel, [shifted, weight], [out], [], 0)[0]
 
 
 def conv_kernel(plan, shifted_ref, values_ref, w_ref, columns_ref, *refs):
@@ -448,7 +493,7 @@
         outs[2][:, PAIR * (chunks - 1) * LANES :] = sum(tails).astype(jnp.bfloat16)
 
 
-def conv(plan, begun, earlier, shifted, values, weight, columns):
+def conv(chain, plan, begun, earlier, shifted, values, weight, columns):
     _, _, channels, lanes = shifted.shape
     pitch, half, received = plan["pitch"], plan["half"], plan["received"]
     if plan["last"]:
@@ -462,23 +507,15 @@
             out_shape += (jax.ShapeDtypeStruct((channels, PAIR * (lanes - LANES) + LANES), jnp.bfloat16),)
         elif plan["sends"]:
             out_shape += out_shape[:1]
-    scratch = [pltpu.VMEM((PAIR, 3, channels, lanes), jnp.bfloat16)] * received
     if plan["builds"]:
         out_shape += far_shapes(plan["rows_near"] // 2, pitch - 1 - half, channels, half)
-    return pl.pallas_call(
+    return chain.add(
         functools.partial(conv_kernel, plan),
-        out_shape=out_shape,
-        in_specs=[VMEM] * (4 + len(begun) + len(earlier)),
-        out_specs=(VMEM,) * len(out_shape),
-        scratch_shapes=scratch,
-        compiler_params=pltpu.CompilerParams(vmem_limit_bytes=LIMIT),
-        cost_estimate=pl.CostEstimate(
-            flops=54 * channels * channels * PAIR * lanes * (1 + plan["builds"]),
-            bytes_accessed=2 * weight.size,
-            transcendentals=PAIR * channels * lanes,
-        ),
-        name=f"conv_{plan['layer']}",
-    )(shifted, values, weight, columns, *begun, *earlier)
+        [shifted, values, weight, columns, *begun, *earlier],
+        out_shape,
+        [pltpu.VMEM((PAIR, 3, channels, lanes), jnp.bfloat16)] * received,
+        54 * channels * channels * PAIR * lanes * (1 + plan["builds"]),
+    )
 
 
 def join_kernel(pair, kept_ref, got_ref, *refs):
@@ -547,7 +584,10 @@
     values[-1], shifted[-1], send = beyond(layers, columns, far, mate_of(far), near_values[-1], near_act[-1])
     halo, rest = earlier_of(send), 0
     next_begun = layer_begun = None
-    first_begun = begin(shifted[-1], weight[0])
+    chain = Chain()
+    first_begun = begin(chain, shifted[-1], weight[0])
+    chain.run("begin")
+    first_begun = now(first_begun)
     *came, first_begun = lax.optimization_barrier((*came, first_begun))
     parts = [(came[p], near_values[p], near_act[p]) for p in range(pairs - 1)]
     half = width // 2
@@ -559,18 +599,20 @@
         for p in reversed(range(pairs)):
             builds = layer == 0 and p > 0
             earlier = (halo,) if p == 0 else parts[p - 1] if builds else (shifted[p - 1],)
-            waits = builds or (p == 0 and (last or layer == 0)) or (layer == 1 and layer_begun is not None and p == pairs - 1)
+            begun = ()
             if builds and p == pairs - 1:
                 begun = (first_begun,)
             elif layer == 0 and p == 0 and next_begun is not None:
                 begun = (next_begun,)
             elif layer == 1 and p == pairs - 1 and layer_begun is not None:
                 begun = (layer_begun,)
-            else:
-                begun = (begin(shifted[p], weight[layer]),) if waits else ()
+            elif builds or (p == 0 and (last or layer == 0)):
+                begun = (begin(chain, shifted[p], weight[layer]),)
+            if last and p == 0:
+                chain.run("convs")
             plan = {
                 "layer": layer,
-                "begun": waits,
+                "begun": len(begun) > 0,
                 "rows_near": 2 * rows,
                 "last": last,
                 "sends": p == pairs - 1 and not last,
@@ -583,25 +625,26 @@
                 "half": half,
                 "rows": rows_left,
             }
-            outs = list(conv(plan, begun, earlier, shifted[p], values[p], weight[layer], columns))
+            outs = list(conv(chain, plan, begun, earlier, shifted[p], values[p], weight[layer], columns))
             if builds:
                 shifted[p - 1], values[p - 1] = outs.pop(), outs.pop()
             results[p] = outs
             if plan["sends"]:
-                message = outs[2]
                 if layer == 0 and p == 1:
-                    next_begun = begin(shifted[0], weight[0])
-                    message, next_begun = lax.optimization_barrier((message, next_begun))
-                arriving = earlier_of(message)
-                if layer == 0 and p == 1 and not last:
-                    layer_begun = begin(outs[1], weight[1])
-                    halo, layer_begun = lax.optimization_barrier((halo, layer_begun))
+                    next_begun = begin(chain, shifted[0], weight[0])
+                chain.run("convs")
+                arriving = earlier_of(now(outs[2]))
+                if layer == 0 and p == 1:
+                    layer_begun = begin(chain, outs[1], weight[1])
+                    chain.run("begin")
+                    halo, layer_begun = lax.optimization_barrier((halo, now(layer_begun)))
         values, shifted = [r[0] for r in results], [r[1] for r in results]
         if not last:
             halo, rest = arriving, joined(rows_left * pitch)
+    chain.run("convs")
     result = ()
     for p in reversed(range(pairs)):
-        result = (join(p, values[p], mate_of(shifted[p]), latents.shape, *result),)
+        result = (join(p, now(values[p]), mate_of(now(shifted[p])), latents.shape, *result),)
     return result[0]
 
 

time: 42.5 us -> 43.2 us (1.016)
  starting transfers between devices: 16.6 us -> 17.2 us
    ppermute x3, starting transfers between devices: 11.2 us -> 11.8 us  [earlier_of(): return lax.ppermute(block, 'tm', [(i, i + 1) for i in range(blocks - 1)])]
    pallas_call x10 -> x6, Pallas kernels: 16.2 us -> 16 us  [run(): pl.pallas_call(kernel, out_shape=tuple(out_shape), in_specs=[VMEM] * len(...]
  transfers between devices with their start and end apart: 9 -> 9, of which waited for: 3 -> 4; matrix products, arithmetic and copies ran while one was open for 2% -> 2% of each run, Pallas kernels for 52% -> 50%
where the time goes in v14:
time: 43.2 us; the launch traced here: 42.9 us
  Pallas kernels  22.4 us (52%)
  starting transfers between devices  17.2 us (40%)
  waiting for transfers between devices  1.32 us (3%)
  local copies, waits for them, and re-layouts  1 us (2%)
  other arithmetic  0.71 us (2%)
    pallas_call x6, Pallas kernels, run(): pl.pallas_call(kernel, out_shape=tuple(out_shape), in_specs=[VMEM] * len(...  16 us
    ppermute x3, starting transfers between devices, earlier_of(): return lax.ppermute(block, 'tm', [(i, i + 1) for i in range(blocks - 1)])  11.8 us
    ppermute x2, starting transfers between devices, beyond_of(): return lax.ppermute(block, 'rows', [(i, i ^ 2) for i in range(strips)])  4.29 us
    pallas_call x1, Pallas kernels, weights(): pl.pallas_call(weights_kernel, out_shape=(one,) * layers + (jax.ShapeDtyp...  3.54 us
    pallas_call x2, Pallas kernels, join(): pl.pallas_call(functools.partial(join_kernel, pair), out_shape=jax.ShapeD...  1.58 us
    ppermute x4, starting transfers between devices, mate_of(): return lax.ppermute(block, 'rows', [(i, i ^ 1) for i in range(strips)])  1.08 us
    unnamed x2, local copies, waits for them, and re-layouts  1 us
    ppermute x2, waiting for transfers between devices, beyond_of(): return lax.ppermute(block, 'rows', [(i, i ^ 2) for i in range(strips)])  0.9 us
  transfers between devices with their start and end apart: 9, of which 4 were waited for; matrix products, arithmetic and copies ran while one was open for 2% of the time, Pallas kernels for 50%

profile of v14, /device:TPU:0, one launch (start us, length us, event | category | flops | bytes accessed | tf_op | source)
XLA Modules:
  0.0 42.9 jit_solution(18274393879303261348)
XLA Ops:
  0.0 0.5 %collective-permute-start.1 = (bf16[4,2,192,128]{3,2,1,0:T(8,128)(2,1)}, bf16[4,2,192,128]{3,2,1,0:T(8,128)(2,1)S(1)}, u32[]{:S(2)}, u32[]{:S(2)}) collective-permute-start(bf16[4,2,192,128]{3,2,1,0:T(8,128)(2,1)} %in_ref.1), channel_id=1, source_target_pairs={{0,1},{1,0},{2,3},{3,2},{4,5},{5,4},{6,7},{7,6},{8,9},{9,8},{10,11... | collective-permute-start | bytes 1179656 | tf_op jit(solution)/shard_map/ppermute | solution.py:564
  0.5 0.0 copy-start
  0.5 1.0 %copy-done = bf16[4,2,192,128]{3,2,1,0:T(8,128)(2,1)S(1)} copy-done((bf16[4,2,192,128]{3,2,1,0:T(8,128)(2,1)S(1)}, bf16[4,2,192,128]{3,2,1,0:T(8,128)(2,1)}, u32[]{:S(2)}) %copy-start) | copy-done | bytes 393240
  1.5 2.6 %collective-permute-start = (bf16[2,2,192,128]{3,2,1,0:T(8,128)(2,1)S(1)}, bf16[2,2,192,128]{3,2,1,0:T(8,128)(2,1)S(1)}, u32[]{:S(2)}, u32[]{:S(2)}) collective-permute-start(bf16[2,2,192,128]{3,2,1,0:T(8,128)(2,1)S(1)} %get-tuple-element.50.refs_1_), channel_id=1, source_target_pairs={{0,2},{1,3},{2,0},{3,1},{4,6},{5,7},{6,4},{7,5},{8,10},{9,11},{10,... | collective-permute-start | bytes 589832 | tf_op jit(solution)/shard_map/ppermute | solution.py:570
  4.0 0.7 %pad_maximum_fusion.rows_ref.gains_ref = f32[6,192]{1,0:T(8,128)S(1)} fusion(f32[3,192]{1,0:T(4,128)} %param.7, f32[3,192]{1,0:T(4,128)} %param.6), kind=kLoop, calls=%fused_computation | loop fusion | flops 1152 | bytes 9216 | tf_op jit(solution)/shard_map/concatenate | solution.py:576
  4.7 3.5 %weights.1 = (bf16[576,1728]{1,0:T(8,128)(2,1)S(1)}, bf16[576,1728]{1,0:T(8,128)(2,1)S(1)}, bf16[576,1728]{1,0:T(8,128)(2,1)S(1)}, f32[3,2,192,128]{3,2,1,0:T(8,128)S(1)}) custom-call(bf16[3,27,192,192]{3,2,1,0:T(8,128)(2,1)} %w_ref.1, f32[6,192]{1,0:T(8,128)S(1)} %pad_maximum_fusion.rows_ref.gains_ref), custom_call_target="tpu_custom_call" | custom-call | bytes 11943936 | tf_op jit(solution)/shard_map/weights/pallas_call | solution.py:77
  8.3 0.0 collective-permute-done.1.mate_ref
  8.3 0.7 %near.1 = (bf16[2,192,384]{2,1,0:T(8,128)(2,1)S(1)}, bf16[2,192,384]{2,1,0:T(8,128)(2,1)S(1)}, bf16[2,192,256]{2,1,0:T(8,128)(2,1)S(1)}, bf16[2,192,256]{2,1,0:T(8,128)(2,1)S(1)}, bf16[2,192,256]{2,1,0:T(8,128)(2,1)S(1)}) custom-call(bf16[4,2,192,128]{3,2,1,0:T(8,128)(2,1)S(1)} %collective-permute-done.1.mate_ref, ...), custom_call_target="tpu_custom_call" | custom-call | flops 7864320 | bytes 1572864 | tf_op jit(solution)/shard_map/near/pallas_call | solution.py:176
  9.0 0.6 %collective-permute-done.far_ref = bf16[2,2,192,128]{3,2,1,0:T(8,128)(2,1)S(1)} collective-permute-done((bf16[2,2,192,128]{3,2,1,0:T(8,128)(2,1)S(1)}, bf16[2,2,192,128]{3,2,1,0:T(8,128)(2,1)S(1)}, u32[]{:S(2)}, u32[]{:S(2)}) %collective-permute-start) | collective-permute-done | bytes 196640 | tf_op jit(solution)/shard_map/ppermute | solution.py:570
  9.6 0.0 collective-permute-start.2
  9.6 1.7 %collective-permute-start.3 = (bf16[2,192,256]{2,1,0:T(8,128)(2,1)S(1)}, bf16[2,192,256]{2,1,0:T(8,128)(2,1)S(1)}, u32[]{:S(2)}, u32[]{:S(2)}) collective-permute-start(bf16[2,192,256]{2,1,0:T(8,128)(2,1)S(1)} %get-tuple-element.67), channel_id=1, source_target_pairs={{0,2},{1,3},{2,0},{3,1},{4,6},{5,7},{6,4},{7,5},{8,10},{9,11},{10,... | collective-permute-start | bytes 589832 | tf_op jit(solution)/shard_map/ppermute | solution.py:570
  11.4 0.0 collective-permute-done.2.mate_ref
  11.4 0.5 %beyond.1 = (bf16[2,192,512]{2,1,0:T(8,128)(2,1)S(1)}, bf16[2,3,192,512]{3,2,1,0:T(8,128)(2,1)S(1)}, bf16[2,192,512]{2,1,0:T(8,128)(2,1)S(1)}) custom-call(f32[3,2,192,128]{3,2,1,0:T(8,128)S(1)} %get-tuple-element.60.columns_ref.refs_3_, bf16[2,2,192,128]{3,2,1,0:T(8,128)(2,1)S(1)} %collective-permute-done.far_ref, ...), custom_call_target="tpu_custom_call" | custom-call | flops 3932160 | bytes 786432 | tf_op jit(solution)/shard_map/beyond/pallas_call | solution.py:237
  11.9 3.5 %collective-permute-start.4 = (bf16[2,192,512]{2,1,0:T(8,128)(2,1)S(1)}, bf16[2,192,512]{2,1,0:T(8,128)(2,1)S(1)}, u32[]{:S(2)}, u32[]{:S(2)}) collective-permute-start(bf16[2,192,512]{2,1,0:T(8,128)(2,1)S(1)} %get-tuple-element.75), channel_id=1, source_target_pairs={{0,4},{4,8},{8,12},{1,5},{5,9},{9,13},{2,6},{6,10},{10,14},{3,7},{... | collective-permute-start | bytes 1179656 | tf_op jit(solution)/shard_map/ppermute | solution.py:567
  15.4 1.2 %begin.2.refs_4_ = f32[2,192,512]{2,1,0:T(8,128)S(1)} custom-call(bf16[2,3,192,512]{3,2,1,0:T(8,128)(2,1)S(1)} %get-tuple-element.64.refs_0_, bf16[576,1728]{1,0:T(8,128)(2,1)S(1)} %get-tuple-element.66.refs_1_.refs_2_), custom_call_target="tpu_custom_call" | custom-call | tf_op jit(solution)/shard_map/begin/pallas_call | solution.py:380
  16.6 0.3 collective-permute-done.3.refs_5_
  16.9 2.8 %convs.4 = (bf16[2,192,512]{2,1,0:T(8,128)(2,1)S(1)}, bf16[2,3,192,384]{3,2,1,0:T(8,128)(2,1)S(1)}, bf16[192,896]{1,0:T(8,128)(2,1)S(1)}, bf16[2,192,512]{2,1,0:...) custom-call(bf16[2,3,192,512]{3,2,1,0:T(8,128)(2,1)S(1)} %get-tuple-element.64.refs_0_, ...), custom_call_target="tpu_custom_call" | custom-call | flops 4076863488 | tf_op jit(solution)/shard_map/convs/pallas_call | solution.py:380
  19.8 3.7 %collective-permute-start.5 = (bf16[192,896]{1,0:T(8,128)(2,1)S(1)}, bf16[192,896]{1,0:T(8,128)(2,1)S(1)}, u32[]{:S(2)}, u32[]{:S(2)}) collective-permute-start(bf16[192,896]{1,0:T(8,128)(2,1)S(1)} %get-tuple-element.83), channel_id=1, source_target_pairs={{0,4},{4,8},{8,12},{1,5},{5,9},{9,13},{2,6},{6,10},{10,14},{3,7},{... | collective-permute-start | bytes 1032200 | tf_op jit(solution)/shard_map/ppermute | solution.py:567
  23.5 1.1 %begin.3.refs_9_ = f32[2,192,384]{2,1,0:T(8,128)S(1)} custom-call(bf16[2,3,192,384]{3,2,1,0:T(8,128)(2,1)S(1)} %get-tuple-element.76.refs_0_.refs_6_, bf16[576,1728]{1,0:T(8,128)(2,1)S(1)} %get-tuple-element.77.refs_1_.refs_8_.refs_2_), custom_call_target="tpu_custom_call" | custom-call | tf_op jit(solution)/shard_map/begin/pallas_call | solution.py:380
  24.6 0.3 collective-permute-done.4.refs_5_
  24.8 4.0 %convs.5 = (bf16[2,192,512]{2,1,0:T(8,128)(2,1)S(1)}, bf16[2,3,192,384]{3,2,1,0:T(8,128)(2,1)S(1)}, bf16[2,192,384]{2,1,0:T(8,128)(2,1)S(1)}, bf16[2,3,192,384]{...) custom-call(bf16[2,3,192,512]{3,2,1,0:T(8,128)(2,1)S(1)} %get-tuple-element.72.refs_0_, ...), custom_call_target="tpu_custom_call" | custom-call | flops 3567255552 | tf_op jit(solution)/shard_map/convs/pallas_call | solution.py:380
  28.8 4.6 %collective-permute-start.6 = (bf16[2,192,384]{2,1,0:T(8,128)(2,1)S(1)}, bf16[2,192,384]{2,1,0:T(8,128)(2,1)S(1)}, u32[]{:S(2)}, u32[]{:S(2)}) collective-permute-start(bf16[2,192,384]{2,1,0:T(8,128)(2,1)S(1)} %get-tuple-element.90), channel_id=1, source_target_pairs={{0,4},{4,8},{8,12},{1,5},{5,9},{9,13},{2,6},{6,10},{10,14},{3,7},{... | collective-permute-start | bytes 884744 | tf_op jit(solution)/shard_map/ppermute | solution.py:567
  33.4 0.0 collective-permute-done.5.refs_4_
  33.4 5.3 %convs.6 = (bf16[2,192,384]{2,1,0:T(8,128)(2,1)S(1)}, bf16[2,3,192,384]{3,2,1,0:T(8,128)(2,1)S(1)}, bf16[2,192,128]{2,1,0:T(8,128)(2,1)S(1)}, bf16[2,192,128]{2,1,0:T(8,128)(2,1)S(1)}, f32[2,192,384]{2,1,0:T(8,128)S(1)}) custom-call(bf16[2,3,192,384]{3,2,1,0:T(8,128)(2,1)S(1)} %get-tuple-element.81.refs_0_, ...), custom_call_target="tpu_custom_call" | custom-call | flops 3057647616 | tf_op jit(solution)/shard_map/convs/pallas_call | solution.py:380
  38.8 0.1 collective-permute-start.8
  38.8 0.0 collective-permute-done.6.refs_5_
  38.9 1.6 %convs.7 = (bf16[2,192,128]{2,1,0:T(8,128)(2,1)S(1)}, bf16[2,192,128]{2,1,0:T(8,128)(2,1)S(1)}) custom-call(bf16[2,3,192,384]{3,2,1,0:T(8,128)(2,1)S(1)} %get-tuple-element.87.refs_0_, bf16[2,192,384]{2,1,0:T(8,128)(2,1)S(1)} %get-tuple-element.88.refs_1_, bf16[576,1728]{1,0:T(8,128)(2,1)S(1)} %get-tuple-element.86.refs_7_.refs_2_, ...), custom_call_target="tpu_custom_call" | custom-call | flops 1528823808 | tf_op jit(solution)/shard_map/convs/pallas_call | solution.py:380
  40.5 0.6 %collective-permute-start.7 = (bf16[2,192,128]{2,1,0:T(8,128)(2,1)S(1)}, bf16[2,192,128]{2,1,0:T(8,128)(2,1)S(1)}, u32[]{:S(2)}, u32[]{:S(2)}) collective-permute-start(bf16[2,192,128]{2,1,0:T(8,128)(2,1)S(1)} %get-tuple-element.92), channel_id=1, source_target_pairs={{0,1},{1,0},{2,3},{3,2},{4,5},{5,4},{6,7},{7,6},{8,9},{9,8},{10,11... | collective-permute-start | bytes 294920 | tf_op jit(solution)/shard_map/ppermute | solution.py:564
  41.0 0.0 collective-permute-done.8.got_ref
  41.0 0.8 %join.2.refs_0_ = bf16[4,2,192,128]{3,2,1,0:T(8,128)(2,1)} custom-call(bf16[2,192,128]{2,1,0:T(8,128)(2,1)S(1)} %get-tuple-element.93.kept_ref, bf16[2,192,128]{2,1,0:T(8,128)(2,1)S(1)} %collective-permute-done.8.got_ref), custom_call_target="tpu_custom_call" | custom-call | tf_op jit(solution)/shard_map/join/pallas_call | solution.py:545
  41.8 0.1 collective-permute-done.7.got_ref
  42.0 0.8 %join.3 = bf16[4,2,192,128]{3,2,1,0:T(8,128)(2,1)} custom-call(bf16[2,192,128]{2,1,0:T(8,128)(2,1)S(1)} %get-tuple-element.91.kept_ref, bf16[2,192,128]{2,1,0:T(8,128)(2,1)S(1)} %collective-permute-done.7.got_ref, bf16[4,2,192,128]{3,2,1,0:T(8,128)(2,1)} %join.2.refs_0_), custom_call_target="tpu_custom_call", output_to_operand_aliasing={{}: (2, {})} | custom-call | tf_op jit(solution)/shard_map/join/pallas_call | solution.py:545
  (1 shorter events, 0.0 us)
Async XLA Ops:
  0.0 8.3 %collective-permute-start.1 = (bf16[4,2,192,128]{3,2,1,0:T(8,128)(2,1)}, bf16[4,2,192,128]{3,2,1,0:T(8,128)(2,1)S(1)}, u32[]{:S(2)}, u32[]{:S(2)}) collective-permute-start(bf16[4,2,192,128]{3,2,1,0:T(8,128)(2,1)} %in_ref.1), channel_id=1, source_target_pairs={{0,1},{1,0},{2,3},{3,2},{4,5},{5,4},{6,7},{7,6},{8,9},{9,8},{10,11... | collective-permute-start | bytes 1179656 | tf_op jit(solution)/shard_map/ppermute | solution.py:564
  0.5 1.0 %copy-start = (bf16[4,2,192,128]{3,2,1,0:T(8,128)(2,1)S(1)}, bf16[4,2,192,128]{3,2,1,0:T(8,128)(2,1)}, u32[]{:S(2)}) copy-start(bf16[4,2,192,128]{3,2,1,0:T(8,128)(2,1)} %in_ref.1) | copy-start | bytes 1179652
  1.5 8.1 %collective-permute-start = (bf16[2,2,192,128]{3,2,1,0:T(8,128)(2,1)S(1)}, bf16[2,2,192,128]{3,2,1,0:T(8,128)(2,1)S(1)}, u32[]{:S(2)}, u32[]{:S(2)}) collective-permute-start(bf16[2,2,192,128]{3,2,1,0:T(8,128)(2,1)S(1)} %get-tuple-element.50.refs_1_), channel_id=1, source_target_pairs={{0,2},{1,3},{2,0},{3,1},{4,6},{5,7},{6,4},{7,5},{8,10},{9,11},{10,... | collective-permute-start | bytes 589832 | tf_op jit(solution)/shard_map/ppermute | solution.py:570
  9.6 1.7 %collective-permute-start.2 = (bf16[2,2,192,128]{3,2,1,0:T(8,128)(2,1)S(1)}, bf16[2,2,192,128]{3,2,1,0:T(8,128)(2,1)S(1)}, u32[]{:S(2)}, u32[]{:S(2)}) collective-permute-start(bf16[2,2,192,128]{3,2,1,0:T(8,128)(2,1)S(1)} %collective-permute-done.far_ref), channel_id=1, source_target_pairs={{0,1},{1,0},{2,3},{3,2},{4,5},{5,4},{6,7},{7,6},{8,9},{9,8},{10,11... | collective-permute-start | bytes 589832 | tf_op jit(solution)/shard_map/ppermute | solution.py:564
  9.6 7.3 %collective-permute-start.3 = (bf16[2,192,256]{2,1,0:T(8,128)(2,1)S(1)}, bf16[2,192,256]{2,1,0:T(8,128)(2,1)S(1)}, u32[]{:S(2)}, u32[]{:S(2)}) collective-permute-start(bf16[2,192,256]{2,1,0:T(8,128)(2,1)S(1)} %get-tuple-element.67), channel_id=1, source_target_pairs={{0,2},{1,3},{2,0},{3,1},{4,6},{5,7},{6,4},{7,5},{8,10},{9,11},{10,... | collective-permute-start | bytes 589832 | tf_op jit(solution)/shard_map/ppermute | solution.py:570
  11.9 12.9 %collective-permute-start.4 = (bf16[2,192,512]{2,1,0:T(8,128)(2,1)S(1)}, bf16[2,192,512]{2,1,0:T(8,128)(2,1)S(1)}, u32[]{:S(2)}, u32[]{:S(2)}) collective-permute-start(bf16[2,192,512]{2,1,0:T(8,128)(2,1)S(1)} %get-tuple-element.75), channel_id=1, source_target_pairs={{0,4},{4,8},{8,12},{1,5},{5,9},{9,13},{2,6},{6,10},{10,14},{3,7},{... | collective-permute-start | bytes 1179656 | tf_op jit(solution)/shard_map/ppermute | solution.py:567
  19.8 13.7 %collective-permute-start.5 = (bf16[192,896]{1,0:T(8,128)(2,1)S(1)}, bf16[192,896]{1,0:T(8,128)(2,1)S(1)}, u32[]{:S(2)}, u32[]{:S(2)}) collective-permute-start(bf16[192,896]{1,0:T(8,128)(2,1)S(1)} %get-tuple-element.83), channel_id=1, source_target_pairs={{0,4},{4,8},{8,12},{1,5},{5,9},{9,13},{2,6},{6,10},{10,14},{3,7},{... | collective-permute-start | bytes 1032200 | tf_op jit(solution)/shard_map/ppermute | solution.py:567
  28.8 10.0 %collective-permute-start.6 = (bf16[2,192,384]{2,1,0:T(8,128)(2,1)S(1)}, bf16[2,192,384]{2,1,0:T(8,128)(2,1)S(1)}, u32[]{:S(2)}, u32[]{:S(2)}) collective-permute-start(bf16[2,192,384]{2,1,0:T(8,128)(2,1)S(1)} %get-tuple-element.90), channel_id=1, source_target_pairs={{0,4},{4,8},{8,12},{1,5},{5,9},{9,13},{2,6},{6,10},{10,14},{3,7},{... | collective-permute-start | bytes 884744 | tf_op jit(solution)/shard_map/ppermute | solution.py:567
  38.8 2.3 %collective-permute-start.8 = (bf16[2,192,128]{2,1,0:T(8,128)(2,1)S(1)}, bf16[2,192,128]{2,1,0:T(8,128)(2,1)S(1)}, u32[]{:S(2)}, u32[]{:S(2)}) collective-permute-start(bf16[2,192,128]{2,1,0:T(8,128)(2,1)S(1)} %get-tuple-element.94), channel_id=1, source_target_pairs={{0,1},{1,0},{2,3},{3,2},{4,5},{5,4},{6,7},{7,6},{8,9},{9,8},{10,11... | collective-permute-start | bytes 294920 | tf_op jit(solution)/shard_map/ppermute | solution.py:564
  40.5 1.5 %collective-permute-start.7 = (bf16[2,192,128]{2,1,0:T(8,128)(2,1)S(1)}, bf16[2,192,128]{2,1,0:T(8,128)(2,1)S(1)}, u32[]{:S(2)}, u32[]{:S(2)}) collective-permute-start(bf16[2,192,128]{2,1,0:T(8,128)(2,1)S(1)} %get-tuple-element.92), channel_id=1, source_target_pairs={{0,1},{1,0},{2,3},{3,2},{4,5},{5,4},{6,7},{7,6},{8,9},{9,8},{10,11... | collective-permute-start | bytes 294920 | tf_op jit(solution)/shard_map/ppermute | solution.py:564

commit v15 on v13

--- a/solution.py
+++ b/solution.py
@@ -107,9 +107,53 @@
     )(latents)
 
 
-def joined(valid):
-    rest = valid % LANES
-    return rest if 0 < PAIR * rest <= LANES else 0
+def folds(channels, rest):
+    fits = [n for n in (4, 3, 2) if n * rest <= LANES and channels % (16 * n) == 0]
+    return fits[0] if fits else 1
+
+
+def message_shape(channels, valid):
+    whole, rest = divmod(PAIR * valid, LANES)
+    lines = whole * channels + (channels // folds(channels, rest) if rest else 0)
+    return jax.ShapeDtypeStruct((lines, LANES), jnp.bfloat16)
+
+
+def write_message(ref, acts, valid):
+    channels, width = acts[0].shape
+    whole, rest = divmod(PAIR * valid, LANES)
+    total = rounded(PAIR * valid)
+    if total > width:
+        acts = [jnp.concatenate([act, jnp.zeros((channels, total - width), jnp.bfloat16)], axis=1) for act in acts]
+    first, second = acts[0], pltpu.roll(acts[1], valid, 1)
+    lane = lane_of(LANES)
+    for n in range(total // LANES):
+        at = slice(n * LANES, (n + 1) * LANES)
+        block = first[:, at] if at.stop <= valid else second[:, at]
+        if at.start < valid < at.stop:
+            mixed = jnp.where(lane < valid - at.start, first[:, at].astype(jnp.float32), second[:, at].astype(jnp.float32))
+            block = mixed.astype(jnp.bfloat16)
+        if n < whole:
+            ref[n * channels : (n + 1) * channels] = block
+            continue
+        parts = folds(channels, rest)
+        size, step = channels // parts, LANES // parts
+        kept = jnp.where(lane < rest, block.astype(jnp.float32), 0.0)
+        pieces = [kept[i * size : (i + 1) * size] for i in range(parts)]
+        ref[n * channels :] = sum(
+            piece if i == 0 else pltpu.roll(piece, i * step, 1) for i, piece in enumerate(pieces)
+        ).astype(jnp.bfloat16)
+
+
+def read_message(ref, channels, width, valid):
+    whole, rest = divmod(PAIR * valid, LANES)
+    blocks = [ref[n * channels : (n + 1) * channels] for n in range(whole)]
+    if rest:
+        parts = folds(channels, rest)
+        folded = ref[whole * channels :]
+        pieces = [folded if i == 0 else pltpu.roll(folded, LANES - i * (LANES // parts), 1) for i in range(parts)]
+        blocks.append(pieces[0] if parts == 1 else jnp.concatenate(pieces, axis=0))
+    both = jnp.concatenate(blocks, axis=1)
+    return both[:, :width], pltpu.roll(both, both.shape[1] - valid, 1)[:, :width]
 
 
 def spread(out_ref, index, act, pitch):
@@ -199,9 +243,10 @@
         placed(blocks, core, row, width // 2 + halo, line)
 
 
-def add_far(pitch, add, near_ref, act_ref, columns_ref, values_ref, shifted_ref, send_ref=None):
+def add_far(pitch, valid, add, near_ref, act_ref, columns_ref, values_ref, shifted_ref, send_ref=None):
     lanes, done = values_ref.shape[2], act_ref.shape[2]
     mask = filled(lanes, pitch)
+    whole_acts = []
     for t in range(PAIR):
         values_ref[t, :, :done] = near_ref[t, :, :done]
         acts = [act_ref[t]]
@@ -213,8 +258,9 @@
             acts.append(activated(blocks[b], columns_ref[0, 0], mask[:, part]))
         act = jnp.concatenate(acts, axis=1)
         spread(shifted_ref, t, act, pitch)
-        if send_ref is not None:
-            send_ref[t] = act
+        whole_acts.append(act)
+    if send_ref is not None:
+        write_message(send_ref, whole_acts, valid)
 
 
 def far_shapes(rows, halo, channels, half):
@@ -229,14 +275,16 @@
     far = parts[0]
     _, rows, channels, width = far.shape
     values, shifted = far_shapes(rows, halo, channels, width // 2)
+    pitch = width // 2 + halo + 1
+    valid = (2 * rows + halo) * pitch
 
     def kernel(columns_ref, far_ref, mate_ref, near_ref, act_ref, *outs):
         add = functools.partial(far_blocks, halo, far_ref, mate_ref)
-        add_far(width // 2 + halo + 1, add, near_ref, act_ref, columns_ref, *outs)
+        add_far(pitch, valid, add, near_ref, act_ref, columns_ref, *outs)
 
     return pl.pallas_call(
         kernel,
-        out_shape=(values, shifted, values),
+        out_shape=(values, shifted, message_shape(channels, valid)),
         in_specs=[VMEM] * 5,
         out_specs=(VMEM,) * 3,
         compiler_params=pltpu.CompilerParams(vmem_limit_bytes=LIMIT),
@@ -354,22 +402,15 @@
 
 def conv_kernel(plan, shifted_ref, values_ref, w_ref, columns_ref, *refs):
     layer, pitch, half, received = plan["layer"], plan["pitch"], plan["half"], plan["received"]
-    last, sends, rest, rest_sent = plan["last"], plan["sends"], plan["rest"], plan["rest_sent"]
+    last, sends = plan["last"], plan["sends"]
     refs = list(refs)
     begun_ref = refs.pop(0) if plan["begun"] else None
     earlier_refs = [refs.pop(0) for _ in range(plan["inputs"])]
     earlier_ref = refs.pop() if received else earlier_refs[0]
     if received:
+        frames = read_message(earlier_refs[0], values_ref.shape[1], values_ref.shape[2], (plan["rows"] + 1) * pitch)
         for t in range(PAIR):
-            if rest:
-                whole = (earlier_refs[0].shape[1] - LANES) // PAIR
-                tail = earlier_refs[0][:, PAIR * whole :].astype(jnp.float32)
-                tail = tail if t == 0 else pltpu.roll(tail, LANES - t * (LANES // PAIR), 1)
-                tail = jnp.where(lane_of(LANES) < rest, tail, 0.0).astype(jnp.bfloat16)
-                act = jnp.concatenate([earlier_refs[0][:, t * whole : (t + 1) * whole], tail], axis=1)
-            else:
-                act = earlier_refs[0][t]
-            spread(earlier_ref, t, act, pitch)
+            spread(earlier_ref, t, frames[t], pitch)
     outs = refs
     if plan["builds"]:
         earlier_ref = outs.pop()
@@ -381,13 +422,13 @@
                 b = (done + at) // LANES
                 blocks[b] = blocks.get(b, 0.0) + came_ref[t, :, at : at + LANES].astype(jnp.float32)
 
-        add_far(pitch, add, near_ref, act_ref, columns_ref, outs.pop(), earlier_ref)
+        add_far(pitch, 0, add, near_ref, act_ref, columns_ref, outs.pop(), earlier_ref)
     _, _, channels, lanes = shifted_ref.shape
     chunks = lanes // LANES
     lane = lane_of(LANES)
 
     bias = columns_ref[layer, 1]
-    tails = []
+    whole_acts = []
     if not last:
         mask = filled(lanes, pitch)
         gain = columns_ref[layer + 1, 0]
@@ -404,17 +445,9 @@
                 continue
             outs[0][t, :, at] = total
             acts.append(activated(total.astype(jnp.float32), gain, mask[:, at]))
-            if not sends:
-                continue
-            if not rest_sent:
-                outs[2][t, :, at] = acts[-1]
-            elif b < chunks - 1:
-                outs[2][:, (t * (chunks - 1) + b) * LANES : (t * (chunks - 1) + b + 1) * LANES] = acts[-1]
-            else:
-                tail = jnp.where(lane < rest_sent, acts[-1].astype(jnp.float32), 0.0)
-                tails.append(tail if t == 0 else pltpu.roll(tail, t * (LANES // PAIR), 1))
         if not last:
-            spread(outs[1], t, jnp.concatenate(acts, axis=1), pitch)
+            whole_acts.append(jnp.concatenate(acts, axis=1))
+            spread(outs[1], t, whole_acts[-1], pitch)
             return
         core, _, outer = place()
         skipped = core * (pitch - 1 - half)
@@ -444,8 +477,8 @@
         return jnp.dot(w_ref[:, start:], jnp.concatenate(rhs, axis=1), preferred_element_type=jnp.float32)
 
     by_frames(lanes, tile_sums, finish)
-    if sends and rest_sent:
-        outs[2][:, PAIR * (chunks - 1) * LANES :] = sum(tails).astype(jnp.bfloat16)
+    if sends:
+        write_message(outs[2], whole_acts, plan["rows"] * pitch)
 
 
 def conv(plan, begun, earlier, shifted, values, weight, columns):
@@ -458,10 +491,8 @@
             jax.ShapeDtypeStruct((PAIR, channels, lanes), jnp.bfloat16),
             jax.ShapeDtypeStruct((PAIR, 3, channels, rounded((plan["rows"] - 1) * pitch)), jnp.bfloat16),
         )
-        if plan["sends"] and plan["rest_sent"]:
-            out_shape += (jax.ShapeDtypeStruct((channels, PAIR * (lanes - LANES) + LANES), jnp.bfloat16),)
-        elif plan["sends"]:
-            out_shape += out_shape[:1]
+        if plan["sends"]:
+            out_shape += (message_shape(channels, plan["rows"] * pitch),)
     scratch = [pltpu.VMEM((PAIR, 3, channels, lanes), jnp.bfloat16)] * received
     if plan["builds"]:
         out_shape += far_shapes(plan["rows_near"] // 2, pitch - 1 - half, channels, half)
@@ -545,7 +576,7 @@
     )
     values, shifted = [None] * pairs, [None] * pairs
     values[-1], shifted[-1], send = beyond(layers, columns, far, mate_of(far), near_values[-1], near_act[-1])
-    halo, rest = earlier_of(send), 0
+    halo = earlier_of(send)
     next_begun = layer_begun = None
     first_begun = begin(shifted[-1], weight[0])
     *came, first_begun = lax.optimization_barrier((*came, first_begun))
@@ -574,9 +605,7 @@
                 "rows_near": 2 * rows,
                 "last": last,
                 "sends": p == pairs - 1 and not last,
-                "rest_sent": joined(rows_left * pitch),
                 "received": p == 0,
-                "rest": 0 if p else rest,
                 "builds": builds,
                 "inputs": len(earlier),
                 "pitch": pitch,
@@ -598,7 +627,7 @@
                     halo, layer_begun = lax.optimization_barrier((halo, layer_begun))
         values, shifted = [r[0] for r in results], [r[1] for r in results]
         if not last:
-            halo, rest = arriving, joined(rows_left * pitch)
+            halo = arriving
     result = ()
     for p in reversed(range(pairs)):
         result = (join(p, values[p], mate_of(shifted[p]), latents.shape, *result),)

time: 42.5 us -> 42.8 us (level)
  Pallas kernels: 22.6 us -> 23.2 us
    pallas_call x6, Pallas kernels: 11.7 us -> 12.2 us  [conv(): pl.pallas_call(functools.partial(conv_kernel, plan), out_shape=out_shape,...]
  transfers between devices with their start and end apart: 9 -> 9, of which waited for: 3 -> 3; matrix products, arithmetic and copies ran while one was open for 2% -> 2% of each run, Pallas kernels for 52% -> 53%
where the time goes in v15:
time: 42.8 us; the launch traced here: 42.5 us
  Pallas kernels  23.2 us (54%)
  starting transfers between devices  16.3 us (38%)
  local copies, waits for them, and re-layouts  1 us (2%)
  waiting for transfers between devices  0.98 us (2%)
  other arithmetic  0.71 us (2%)
    pallas_call x6, Pallas kernels, conv(): pl.pallas_call(functools.partial(conv_kernel, plan), out_shape=out_shape,...  12.2 us
    ppermute x3, starting transfers between devices, earlier_of(): return lax.ppermute(block, 'tm', [(i, i + 1) for i in range(blocks - 1)])  10.9 us
    pallas_call x4, Pallas kernels, begin(): pl.pallas_call(begin_kernel, out_shape=jax.ShapeDtypeStruct((PAIR, channe...  4.54 us
    ppermute x2, starting transfers between devices, beyond_of(): return lax.ppermute(block, 'rows', [(i, i ^ 2) for i in range(strips)])  4.29 us
    pallas_call x1, Pallas kernels, weights(): pl.pallas_call(weights_kernel, out_shape=(one,) * layers + (jax.ShapeDtyp...  3.54 us
    pallas_call x2, Pallas kernels, join(): pl.pallas_call(functools.partial(join_kernel, pair), out_shape=jax.ShapeD...  1.58 us
    ppermute x4, starting transfers between devices, mate_of(): return lax.ppermute(block, 'rows', [(i, i ^ 1) for i in range(strips)])  1.08 us
    unnamed x2, local copies, waits for them, and re-layouts  1 us
  transfers between devices with their start and end apart: 9, of which 3 were waited for; matrix products, arithmetic and copies ran while one was open for 2% of the time, Pallas kernels for 53%

profile of v15, /device:TPU:0, one launch (start us, length us, event | category | flops | bytes accessed | tf_op | source)
XLA Modules:
  0.0 42.5 jit_solution(10983078931973579682)
XLA Ops:
  0.0 0.5 %collective-permute-start.1 = (bf16[4,2,192,128]{3,2,1,0:T(8,128)(2,1)}, bf16[4,2,192,128]{3,2,1,0:T(8,128)(2,1)S(1)}, u32[]{:S(2)}, u32[]{:S(2)}) collective-permute-start(bf16[4,2,192,128]{3,2,1,0:T(8,128)(2,1)} %in_ref.1), channel_id=1, source_target_pairs={{0,1},{1,0},{2,3},{3,2},{4,5},{5,4},{6,7},{7,6},{8,9},{9,8},{10,11... | collective-permute-start | bytes 1179656 | tf_op jit(solution)/shard_map/ppermute | solution.py:558
  0.5 1.0 %copy-done = bf16[4,2,192,128]{3,2,1,0:T(8,128)(2,1)S(1)} copy-done((bf16[4,2,192,128]{3,2,1,0:T(8,128)(2,1)S(1)}, bf16[4,2,192,128]{3,2,1,0:T(8,128)(2,1)}, u32[]{:S(2)}) %copy-start) | copy-done | bytes 393240
  1.5 2.6 %collective-permute-start = (bf16[2,2,192,128]{3,2,1,0:T(8,128)(2,1)S(1)}, bf16[2,2,192,128]{3,2,1,0:T(8,128)(2,1)S(1)}, u32[]{:S(2)}, u32[]{:S(2)}) collective-permute-start(bf16[2,2,192,128]{3,2,1,0:T(8,128)(2,1)S(1)} %get-tuple-element.50.refs_1_), channel_id=1, source_target_pairs={{0,2},{1,3},{2,0},{3,1},{4,6},{5,7},{6,4},{7,5},{8,10},{9,11},{10,... | collective-permute-start | bytes 589832 | tf_op jit(solution)/shard_map/ppermute | solution.py:564
  4.0 0.7 %pad_maximum_fusion.rows_ref.gains_ref = f32[6,192]{1,0:T(8,128)S(1)} fusion(f32[3,192]{1,0:T(4,128)} %param.7, f32[3,192]{1,0:T(4,128)} %param.6), kind=kLoop, calls=%fused_computation | loop fusion | flops 1152 | bytes 9216 | tf_op jit(solution)/shard_map/concatenate | solution.py:570
  4.7 3.5 %weights.1 = (bf16[576,1728]{1,0:T(8,128)(2,1)S(1)}, bf16[576,1728]{1,0:T(8,128)(2,1)S(1)}, bf16[576,1728]{1,0:T(8,128)(2,1)S(1)}, f32[3,2,192,128]{3,2,1,0:T(8,128)S(1)}) custom-call(bf16[3,27,192,192]{3,2,1,0:T(8,128)(2,1)} %w_ref.1, f32[6,192]{1,0:T(8,128)S(1)} %pad_maximum_fusion.rows_ref.gains_ref), custom_call_target="tpu_custom_call" | custom-call | bytes 11943936 | tf_op jit(solution)/shard_map/weights/pallas_call | solution.py:77
  8.3 0.0 collective-permute-done.1.mate_ref
  8.3 0.7 %near.1 = (bf16[2,192,384]{2,1,0:T(8,128)(2,1)S(1)}, bf16[2,192,384]{2,1,0:T(8,128)(2,1)S(1)}, bf16[2,192,256]{2,1,0:T(8,128)(2,1)S(1)}, bf16[2,192,256]{2,1,0:T(8,128)(2,1)S(1)}, bf16[2,192,256]{2,1,0:T(8,128)(2,1)S(1)}) custom-call(bf16[4,2,192,128]{3,2,1,0:T(8,128)(2,1)S(1)} %collective-permute-done.1.mate_ref, ...), custom_call_target="tpu_custom_call" | custom-call | flops 7864320 | bytes 1572864 | tf_op jit(solution)/shard_map/near/pallas_call | solution.py:220
  9.0 0.6 %collective-permute-done.far_ref = bf16[2,2,192,128]{3,2,1,0:T(8,128)(2,1)S(1)} collective-permute-done((bf16[2,2,192,128]{3,2,1,0:T(8,128)(2,1)S(1)}, bf16[2,2,192,128]{3,2,1,0:T(8,128)(2,1)S(1)}, u32[]{:S(2)}, u32[]{:S(2)}) %collective-permute-start) | collective-permute-done | bytes 196640 | tf_op jit(solution)/shard_map/ppermute | solution.py:564
  9.6 1.7 %collective-permute-start.3 = (bf16[2,192,256]{2,1,0:T(8,128)(2,1)S(1)}, bf16[2,192,256]{2,1,0:T(8,128)(2,1)S(1)}, u32[]{:S(2)}, u32[]{:S(2)}) collective-permute-start(bf16[2,192,256]{2,1,0:T(8,128)(2,1)S(1)} %get-tuple-element.67), channel_id=1, source_target_pairs={{0,2},{1,3},{2,0},{3,1},{4,6},{5,7},{6,4},{7,5},{8,10},{9,11},{10,... | collective-permute-start | bytes 589832 | tf_op jit(solution)/shard_map/ppermute | solution.py:564
  11.4 0.0 collective-permute-done.2.mate_ref
  11.4 0.6 %beyond.1 = (bf16[2,192,512]{2,1,0:T(8,128)(2,1)S(1)}, bf16[2,3,192,512]{3,2,1,0:T(8,128)(2,1)S(1)}, bf16[1440,128]{1,0:T(8,128)(2,1)S(1)}) custom-call(f32[3,2,192,128]{3,2,1,0:T(8,128)S(1)} %get-tuple-element.60.columns_ref, bf16[2,2,192,128]{3,2,1,0:T(8,128)(2,1)S(1)} %collective-permute-done.far_ref, ...), custom_call_target="tpu_custom_call" | custom-call | flops 3932160 | bytes 786432 | tf_op jit(solution)/shard_map/beyond/pallas_call | solution.py:285
  12.0 3.5 %collective-permute-start.4 = (bf16[1440,128]{1,0:T(8,128)(2,1)S(1)}, bf16[1440,128]{1,0:T(8,128)(2,1)S(1)}, u32[]{:S(2)}, u32[]{:S(2)}) collective-permute-start(bf16[1440,128]{1,0:T(8,128)(2,1)S(1)} %get-tuple-element.76), channel_id=1, source_target_pairs={{0,4},{4,8},{8,12},{1,5},{5,9},{9,13},{2,6},{6,10},{10,14},{3,7},{... | collective-permute-start | bytes 1105928 | tf_op jit(solution)/shard_map/ppermute | solution.py:561
  15.5 1.2 %begin.4.refs_0_ = f32[2,192,512]{2,1,0:T(8,128)S(1)} custom-call(bf16[2,3,192,512]{3,2,1,0:T(8,128)(2,1)S(1)} %get-tuple-element.64.shifted_ref, bf16[576,1728]{1,0:T(8,128)(2,1)S(1)} %get-tuple-element.66.w_ref), custom_call_target="tpu_custom_call" | custom-call | tf_op jit(solution)/shard_map/begin/pallas_call | solution.py:392
  16.7 0.2 collective-permute-done.3.refs_1_
  16.9 2.1 %conv_0.2 = (bf16[2,192,512]{2,1,0:T(8,128)(2,1)S(1)}, bf16[2,3,192,384]{3,2,1,0:T(8,128)(2,1)S(1)}, bf16[1248,128]{1,0:T(8,128)(2,1)S(1)}, bf16[2,192,512]{2,1,0:T(8,128)(2,1)S(1)}, bf16[2,3,192,512]{3,2,1,0:T(8,128)(2,1)S(1)}) custom-call(bf16[2,3,192,512]{3,2,1,0:T(8,128)(2,1)S(1)} %get-tuple-element.64.shifted_ref, ...), custom_call_target="tpu_custom_call" | custom-call | flops 4076863488 | bytes 1990656 | tf_op jit(solution)/shard_map/conv_0/pallas_call | solution.py:499
  19.1 1.2 %begin.5.refs_0_ = f32[2,192,512]{2,1,0:T(8,128)S(1)} custom-call(bf16[2,3,192,512]{3,2,1,0:T(8,128)(2,1)S(1)} %get-tuple-element.72.shifted_ref, bf16[576,1728]{1,0:T(8,128)(2,1)S(1)} %get-tuple-element.66.w_ref), custom_call_target="tpu_custom_call" | custom-call | tf_op jit(solution)/shard_map/begin/pallas_call | solution.py:392
  20.3 3.8 %collective-permute-start.5 = (bf16[1248,128]{1,0:T(8,128)(2,1)S(1)}, bf16[1248,128]{1,0:T(8,128)(2,1)S(1)}, u32[]{:S(2)}, u32[]{:S(2)}) collective-permute-start(bf16[1248,128]{1,0:T(8,128)(2,1)S(1)} %get-tuple-element.82), channel_id=1, source_target_pairs={{0,4},{4,8},{8,12},{1,5},{5,9},{9,13},{2,6},{6,10},{10,14},{3,7},{... | collective-permute-start | bytes 958472 | tf_op jit(solution)/shard_map/ppermute | solution.py:561
  24.0 1.1 %begin.6.refs_0_ = f32[2,192,384]{2,1,0:T(8,128)S(1)} custom-call(bf16[2,3,192,384]{3,2,1,0:T(8,128)(2,1)S(1)} %get-tuple-element.77.shifted_ref, bf16[576,1728]{1,0:T(8,128)(2,1)S(1)} %get-tuple-element.78.w_ref), custom_call_target="tpu_custom_call" | custom-call | tf_op jit(solution)/shard_map/begin/pallas_call | solution.py:392
  25.1 2.1 %conv_0.3 = (bf16[2,192,512]{2,1,0:T(8,128)(2,1)S(1)}, bf16[2,3,192,384]{3,2,1,0:T(8,128)(2,1)S(1)}) custom-call(bf16[2,3,192,512]{3,2,1,0:T(8,128)(2,1)S(1)} %get-tuple-element.72.shifted_ref, bf16[2,192,512]{2,1,0:T(8,128)(2,1)S(1)} %get-tuple-element.73.values_ref, bf16[576,1728]{1,0:T(8,128)(2,1)S(1)} %get-tuple-element.66.w_ref, ...), custom_call_target="tpu_custom_call" | custom-call | flops 2038431744 | bytes 1990656 | tf_op jit(solution)/shard_map/conv_0/pallas_call | solution.py:499
  27.2 1.7 %conv_1.3 = (bf16[2,192,384]{2,1,0:T(8,128)(2,1)S(1)}, bf16[2,3,192,384]{3,2,1,0:T(8,128)(2,1)S(1)}, bf16[1024,128]{1,0:T(8,128)(2,1)S(1)}) custom-call(bf16[2,3,192,384]{3,2,1,0:T(8,128)(2,1)S(1)} %get-tuple-element.77.shifted_ref, bf16[2,192,512]{2,1,0:T(8,128)(2,1)S(1)} %get-tuple-element.86.values_ref, bf16[576,1728]{1,0:T(8,128)(2,1)S(1)} %get-tuple-element.78.w_ref, ...), custom_call_target="tpu_custom_call" | custom-call | flops 1528823808 | bytes 1990656 | tf_op jit(solution)/shard_map/conv_1/pallas_call | solution.py:499
  28.9 3.7 %collective-permute-start.6 = (bf16[1024,128]{1,0:T(8,128)(2,1)S(1)}, bf16[1024,128]{1,0:T(8,128)(2,1)S(1)}, u32[]{:S(2)}, u32[]{:S(2)}) collective-permute-start(bf16[1024,128]{1,0:T(8,128)(2,1)S(1)} %get-tuple-element.88), channel_id=1, source_target_pairs={{0,4},{4,8},{8,12},{1,5},{5,9},{9,13},{2,6},{6,10},{10,14},{3,7},{... | collective-permute-start | bytes 786440 | tf_op jit(solution)/shard_map/ppermute | solution.py:561
  32.6 0.0 collective-permute-done.5.refs_0_
  32.6 2.5 %conv_1.2 = (bf16[2,192,384]{2,1,0:T(8,128)(2,1)S(1)}, bf16[2,3,192,384]{3,2,1,0:T(8,128)(2,1)S(1)}) custom-call(bf16[2,3,192,384]{3,2,1,0:T(8,128)(2,1)S(1)} %get-tuple-element.80.shifted_ref.refs_1_, bf16[2,192,512]{2,1,0:T(8,128)(2,1)S(1)} %get-tuple-element.81.values_ref, bf16[576,1728]{1,0:T(8,128)(2,1)S(1)} %get-tuple-element.78.w_ref, ...), custom_call_target="tpu_custom_call" | custom-call | flops 1528823808 | bytes 1990656 | tf_op jit(solution)/shard_map/conv_1/pallas_call | solution.py:499
  35.1 1.1 %begin.7.refs_0_ = f32[2,192,384]{2,1,0:T(8,128)S(1)} custom-call(bf16[2,3,192,384]{3,2,1,0:T(8,128)(2,1)S(1)} %get-tuple-element.83.shifted_ref.refs_0_, bf16[576,1728]{1,0:T(8,128)(2,1)S(1)} %get-tuple-element.85.w_ref), custom_call_target="tpu_custom_call" | custom-call | tf_op jit(solution)/shard_map/begin/pallas_call | solution.py:392
  36.2 2.1 %conv_2.3 = (bf16[2,192,128]{2,1,0:T(8,128)(2,1)S(1)}, bf16[2,192,128]{2,1,0:T(8,128)(2,1)S(1)}) custom-call(bf16[2,3,192,384]{3,2,1,0:T(8,128)(2,1)S(1)} %get-tuple-element.91.shifted_ref, bf16[2,192,384]{2,1,0:T(8,128)(2,1)S(1)} %get-tuple-element.92.values_ref, bf16[576,1728]{1,0:T(8,128)(2,1)S(1)} %get-tuple-element.85.w_ref, ...), custom_call_target="tpu_custom_call" | custom-call | flops 1528823808 | bytes 1990656 | tf_op jit(solution)/shard_map/conv_2/pallas_call | solution.py:499
  38.2 0.1 collective-permute-start.8
  38.3 1.7 %conv_2.2 = (bf16[2,192,128]{2,1,0:T(8,128)(2,1)S(1)}, bf16[2,192,128]{2,1,0:T(8,128)(2,1)S(1)}) custom-call(bf16[2,3,192,384]{3,2,1,0:T(8,128)(2,1)S(1)} %get-tuple-element.83.shifted_ref.refs_0_, bf16[2,192,384]{2,1,0:T(8,128)(2,1)S(1)} %get-tuple-element.84.values_ref, bf16[576,1728]{1,0:T(8,128)(2,1)S(1)} %get-tuple-element.85.w_ref, ...), custom_call_target="tpu_custom_call" | custom-call | flops 1528823808 | bytes 1990656 | tf_op jit(solution)/shard_map/conv_2/pallas_call | solution.py:499
  40.1 0.6 %collective-permute-start.7 = (bf16[2,192,128]{2,1,0:T(8,128)(2,1)S(1)}, bf16[2,192,128]{2,1,0:T(8,128)(2,1)S(1)}, u32[]{:S(2)}, u32[]{:S(2)}) collective-permute-start(bf16[2,192,128]{2,1,0:T(8,128)(2,1)S(1)} %get-tuple-element.90), channel_id=1, source_target_pairs={{0,1},{1,0},{2,3},{3,2},{4,5},{5,4},{6,7},{7,6},{8,9},{9,8},{10,11... | collective-permute-start | bytes 294920 | tf_op jit(solution)/shard_map/ppermute | solution.py:558
  40.6 0.0 collective-permute-done.8.got_ref
  40.6 0.8 %join.2.refs_0_ = bf16[4,2,192,128]{3,2,1,0:T(8,128)(2,1)} custom-call(bf16[2,192,128]{2,1,0:T(8,128)(2,1)S(1)} %get-tuple-element.93.kept_ref, bf16[2,192,128]{2,1,0:T(8,128)(2,1)S(1)} %collective-permute-done.8.got_ref), custom_call_target="tpu_custom_call" | custom-call | tf_op jit(solution)/shard_map/join/pallas_call | solution.py:539
  41.4 0.1 collective-permute-done.7.got_ref
  41.6 0.8 %join.3 = bf16[4,2,192,128]{3,2,1,0:T(8,128)(2,1)} custom-call(bf16[2,192,128]{2,1,0:T(8,128)(2,1)S(1)} %get-tuple-element.89.kept_ref, bf16[2,192,128]{2,1,0:T(8,128)(2,1)S(1)} %collective-permute-done.7.got_ref, bf16[4,2,192,128]{3,2,1,0:T(8,128)(2,1)} %join.2.refs_0_), custom_call_target="tpu_custom_call", output_to_operand_aliasing={{}: (2, {})} | custom-call | tf_op jit(solution)/shard_map/join/pallas_call | solution.py:539
  (5 shorter events, 0.0 us)
Async XLA Ops:
  0.0 8.3 %collective-permute-start.1 = (bf16[4,2,192,128]{3,2,1,0:T(8,128)(2,1)}, bf16[4,2,192,128]{3,2,1,0:T(8,128)(2,1)S(1)}, u32[]{:S(2)}, u32[]{:S(2)}) collective-permute-start(bf16[4,2,192,128]{3,2,1,0:T(8,128)(2,1)} %in_ref.1), channel_id=1, source_target_pairs={{0,1},{1,0},{2,3},{3,2},{4,5},{5,4},{6,7},{7,6},{8,9},{9,8},{10,11... | collective-permute-start | bytes 1179656 | tf_op jit(solution)/shard_map/ppermute | solution.py:558
  0.5 1.0 %copy-start = (bf16[4,2,192,128]{3,2,1,0:T(8,128)(2,1)S(1)}, bf16[4,2,192,128]{3,2,1,0:T(8,128)(2,1)}, u32[]{:S(2)}) copy-start(bf16[4,2,192,128]{3,2,1,0:T(8,128)(2,1)} %in_ref.1) | copy-start | bytes 1179652
  1.5 8.1 %collective-permute-start = (bf16[2,2,192,128]{3,2,1,0:T(8,128)(2,1)S(1)}, bf16[2,2,192,128]{3,2,1,0:T(8,128)(2,1)S(1)}, u32[]{:S(2)}, u32[]{:S(2)}) collective-permute-start(bf16[2,2,192,128]{3,2,1,0:T(8,128)(2,1)S(1)} %get-tuple-element.50.refs_1_), channel_id=1, source_target_pairs={{0,2},{1,3},{2,0},{3,1},{4,6},{5,7},{6,4},{7,5},{8,10},{9,11},{10,... | collective-permute-start | bytes 589832 | tf_op jit(solution)/shard_map/ppermute | solution.py:564
  9.6 1.7 %collective-permute-start.2 = (bf16[2,2,192,128]{3,2,1,0:T(8,128)(2,1)S(1)}, bf16[2,2,192,128]{3,2,1,0:T(8,128)(2,1)S(1)}, u32[]{:S(2)}, u32[]{:S(2)}) collective-permute-start(bf16[2,2,192,128]{3,2,1,0:T(8,128)(2,1)S(1)} %collective-permute-done.far_ref), channel_id=1, source_target_pairs={{0,1},{1,0},{2,3},{3,2},{4,5},{5,4},{6,7},{7,6},{8,9},{9,8},{10,11... | collective-permute-start | bytes 589832 | tf_op jit(solution)/shard_map/ppermute | solution.py:558
  9.6 7.3 %collective-permute-start.3 = (bf16[2,192,256]{2,1,0:T(8,128)(2,1)S(1)}, bf16[2,192,256]{2,1,0:T(8,128)(2,1)S(1)}, u32[]{:S(2)}, u32[]{:S(2)}) collective-permute-start(bf16[2,192,256]{2,1,0:T(8,128)(2,1)S(1)} %get-tuple-element.67), channel_id=1, source_target_pairs={{0,2},{1,3},{2,0},{3,1},{4,6},{5,7},{6,4},{7,5},{8,10},{9,11},{10,... | collective-permute-start | bytes 589832 | tf_op jit(solution)/shard_map/ppermute | solution.py:564
  12.0 13.1 %collective-permute-start.4 = (bf16[1440,128]{1,0:T(8,128)(2,1)S(1)}, bf16[1440,128]{1,0:T(8,128)(2,1)S(1)}, u32[]{:S(2)}, u32[]{:S(2)}) collective-permute-start(bf16[1440,128]{1,0:T(8,128)(2,1)S(1)} %get-tuple-element.76), channel_id=1, source_target_pairs={{0,4},{4,8},{8,12},{1,5},{5,9},{9,13},{2,6},{6,10},{10,14},{3,7},{... | collective-permute-start | bytes 1105928 | tf_op jit(solution)/shard_map/ppermute | solution.py:561
  20.3 12.3 %collective-permute-start.5 = (bf16[1248,128]{1,0:T(8,128)(2,1)S(1)}, bf16[1248,128]{1,0:T(8,128)(2,1)S(1)}, u32[]{:S(2)}, u32[]{:S(2)}) collective-permute-start(bf16[1248,128]{1,0:T(8,128)(2,1)S(1)} %get-tuple-element.82), channel_id=1, source_target_pairs={{0,4},{4,8},{8,12},{1,5},{5,9},{9,13},{2,6},{6,10},{10,14},{3,7},{... | collective-permute-start | bytes 958472 | tf_op jit(solution)/shard_map/ppermute | solution.py:561
  28.9 9.4 %collective-permute-start.6 = (bf16[1024,128]{1,0:T(8,128)(2,1)S(1)}, bf16[1024,128]{1,0:T(8,128)(2,1)S(1)}, u32[]{:S(2)}, u32[]{:S(2)}) collective-permute-start(bf16[1024,128]{1,0:T(8,128)(2,1)S(1)} %get-tuple-element.88), channel_id=1, source_target_pairs={{0,4},{4,8},{8,12},{1,5},{5,9},{9,13},{2,6},{6,10},{10,14},{3,7},{... | collective-permute-start | bytes 786440 | tf_op jit(solution)/shard_map/ppermute | solution.py:561
  38.2 2.4 %collective-permute-start.8 = (bf16[2,192,128]{2,1,0:T(8,128)(2,1)S(1)}, bf16[2,192,128]{2,1,0:T(8,128)(2,1)S(1)}, u32[]{:S(2)}, u32[]{:S(2)}) collective-permute-start(bf16[2,192,128]{2,1,0:T(8,128)(2,1)S(1)} %get-tuple-element.94), channel_id=1, source_target_pairs={{0,1},{1,0},{2,3},{3,2},{4,5},{5,4},{6,7},{7,6},{8,9},{9,8},{10,11... | collective-permute-start | bytes 294920 | tf_op jit(solution)/shard_map/ppermute | solution.py:558
  40.1 1.5 %collective-permute-start.7 = (bf16[2,192,128]{2,1,0:T(8,128)(2,1)S(1)}, bf16[2,192,128]{2,1,0:T(8,128)(2,1)S(1)}, u32[]{:S(2)}, u32[]{:S(2)}) collective-permute-start(bf16[2,192,128]{2,1,0:T(8,128)(2,1)S(1)} %get-tuple-element.90), channel_id=1, source_target_pairs={{0,1},{1,0},{2,3},{3,2},{4,5},{5,4},{6,7},{7,6},{8,9},{9,8},{10,11... | collective-permute-start | bytes 294920 | tf_op jit(solution)/shard_map/ppermute | solution.py:558

commit v16 on v14

--- a/solution.py
+++ b/solution.py
@@ -107,9 +107,53 @@
     )(latents)
 
 
-def joined(valid):
-    rest = valid % LANES
-    return rest if 0 < PAIR * rest <= LANES else 0
+def folds(channels, rest):
+    fits = [n for n in (4, 3, 2) if n * rest <= LANES and channels % (16 * n) == 0]
+    return fits[0] if fits else 1
+
+
+def message_shape(channels, valid):
+    whole, rest = divmod(PAIR * valid, LANES)
+    lines = whole * channels + (channels // folds(channels, rest) if rest else 0)
+    return jax.ShapeDtypeStruct((lines, LANES), jnp.bfloat16)
+
+
+def write_message(ref, acts, valid):
+    channels, width = acts[0].shape
+    whole, rest = divmod(PAIR * valid, LANES)
+    total = rounded(PAIR * valid)
+    if total > width:
+        acts = [jnp.concatenate([act, jnp.zeros((channels, total - width), jnp.bfloat16)], axis=1) for act in acts]
+    first, second = acts[0], pltpu.roll(acts[1], valid, 1)
+    lane = lane_of(LANES)
+    for n in range(total // LANES):
+        at = slice(n * LANES, (n + 1) * LANES)
+        block = first[:, at] if at.stop <= valid else second[:, at]
+        if at.start < valid < at.stop:
+            mixed = jnp.where(lane < valid - at.start, first[:, at].astype(jnp.float32), second[:, at].astype(jnp.float32))
+            block = mixed.astype(jnp.bfloat16)
+        if n < whole:
+            ref[n * channels : (n + 1) * channels] = block
+            continue
+        parts = folds(channels, rest)
+        size, step = channels // parts, LANES // parts
+        kept = jnp.where(lane < rest, block.astype(jnp.float32), 0.0)
+        pieces = [kept[i * size : (i + 1) * size] for i in range(parts)]
+        ref[n * channels :] = sum(
+            piece if i == 0 else pltpu.roll(piece, i * step, 1) for i, piece in enumerate(pieces)
+        ).astype(jnp.bfloat16)
+
+
+def read_message(ref, channels, width, valid):
+    whole, rest = divmod(PAIR * valid, LANES)
+    blocks = [ref[n * channels : (n + 1) * channels] for n in range(whole)]
+    if rest:
+        parts = folds(channels, rest)
+        folded = ref[whole * channels :]
+        pieces = [folded if i == 0 else pltpu.roll(folded, LANES - i * (LANES // parts), 1) for i in range(parts)]
+        blocks.append(pieces[0] if parts == 1 else jnp.concatenate(pieces, axis=0))
+    both = jnp.concatenate(blocks, axis=1)
+    return both[:, :width], pltpu.roll(both, both.shape[1] - valid, 1)[:, :width]
 
 
 def spread(out_ref, index, act, pitch):
@@ -199,9 +243,10 @@
         placed(blocks, core, row, width // 2 + halo, line)
 
 
-def add_far(pitch, add, near_ref, act_ref, columns_ref, values_ref, shifted_ref, send_ref=None):
+def add_far(pitch, valid, add, near_ref, act_ref, columns_ref, values_ref, shifted_ref, send_ref=None):
     lanes, done = values_ref.shape[2], act_ref.shape[2]
     mask = filled(lanes, pitch)
+    whole_acts = []
     for t in range(PAIR):
         values_ref[t, :, :done] = near_ref[t, :, :done]
         acts = [act_ref[t]]
@@ -213,8 +258,9 @@
             acts.append(activated(blocks[b], columns_ref[0, 0], mask[:, part]))
         act = jnp.concatenate(acts, axis=1)
         spread(shifted_ref, t, act, pitch)
-        if send_ref is not None:
-            send_ref[t] = act
+        whole_acts.append(act)
+    if send_ref is not None:
+        write_message(send_ref, whole_acts, valid)
 
 
 def far_shapes(rows, halo, channels, half):
@@ -229,14 +275,16 @@
     far = parts[0]
     _, rows, channels, width = far.shape
     values, shifted = far_shapes(rows, halo, channels, width // 2)
+    pitch = width // 2 + halo + 1
+    valid = (2 * rows + halo) * pitch
 
     def kernel(columns_ref, far_ref, mate_ref, near_ref, act_ref, *outs):
         add = functools.partial(far_blocks, halo, far_ref, mate_ref)
-        add_far(width // 2 + halo + 1, add, near_ref, act_ref, columns_ref, *outs)
+        add_far(pitch, valid, add, near_ref, act_ref, columns_ref, *outs)
 
     return pl.pallas_call(
         kernel,
-        out_shape=(values, shifted, values),
+        out_shape=(values, shifted, message_shape(channels, valid)),
         in_specs=[VMEM] * 5,
         out_specs=(VMEM,) * 3,
         compiler_params=pltpu.CompilerParams(vmem_limit_bytes=LIMIT),
@@ -399,22 +447,15 @@
 
 def conv_kernel(plan, shifted_ref, values_ref, w_ref, columns_ref, *refs):
     layer, pitch, half, received = plan["layer"], plan["pitch"], plan["half"], plan["received"]
-    last, sends, rest, rest_sent = plan["last"], plan["sends"], plan["rest"], plan["rest_sent"]
+    last, sends = plan["last"], plan["sends"]
     refs = list(refs)
     begun_ref = refs.pop(0) if plan["begun"] else None
     earlier_refs = [refs.pop(0) for _ in range(plan["inputs"])]
     earlier_ref = refs.pop() if received else earlier_refs[0]
     if received:
+        frames = read_message(earlier_refs[0], values_ref.shape[1], values_ref.shape[2], (plan["rows"] + 1) * pitch)
         for t in range(PAIR):
-            if rest:
-                whole = (earlier_refs[0].shape[1] - LANES) // PAIR
-                tail = earlier_refs[0][:, PAIR * whole :].astype(jnp.float32)
-                tail = tail if t == 0 else pltpu.roll(tail, LANES - t * (LANES // PAIR), 1)
-                tail = jnp.where(lane_of(LANES) < rest, tail, 0.0).astype(jnp.bfloat16)
-                act = jnp.concatenate([earlier_refs[0][:, t * whole : (t + 1) * whole], tail], axis=1)
-            else:
-                act = earlier_refs[0][t]
-            spread(earlier_ref, t, act, pitch)
+            spread(earlier_ref, t, frames[t], pitch)
     outs = refs
     if plan["builds"]:
         earlier_ref = outs.pop()
@@ -426,13 +467,13 @@
                 b = (done + at) // LANES
                 blocks[b] = blocks.get(b, 0.0) + came_ref[t, :, at : at + LANES].astype(jnp.float32)
 
-        add_far(pitch, add, near_ref, act_ref, columns_ref, outs.pop(), earlier_ref)
+        add_far(pitch, 0, add, near_ref, act_ref, columns_ref, outs.pop(), earlier_ref)
     _, _, channels, lanes = shifted_ref.shape
     chunks = lanes // LANES
     lane = lane_of(LANES)
 
     bias = columns_ref[layer, 1]
-    tails = []
+    whole_acts = []
     if not last:
         mask = filled(lanes, pitch)
         gain = columns_ref[layer + 1, 0]
@@ -449,17 +490,9 @@
                 continue
             outs[0][t, :, at] = total
             acts.append(activated(total.astype(jnp.float32), gain, mask[:, at]))
-            if not sends:
-                continue
-            if not rest_sent:
-                outs[2][t, :, at] = acts[-1]
-            elif b < chunks - 1:
-                outs[2][:, (t * (chunks - 1) + b) * LANES : (t * (chunks - 1) + b + 1) * LANES] = acts[-1]
-            else:
-                tail = jnp.where(lane < rest_sent, acts[-1].astype(jnp.float32), 0.0)
-                tails.append(tail if t == 0 else pltpu.roll(tail, t * (LANES // PAIR), 1))
         if not last:
-            spread(outs[1], t, jnp.concatenate(acts, axis=1), pitch)
+            whole_acts.append(jnp.concatenate(acts, axis=1))
+            spread(outs[1], t, whole_acts[-1], pitch)
             return
         core, _, outer = place()
         skipped = core * (pitch - 1 - half)
@@ -489,8 +522,8 @@
         return jnp.dot(w_ref[:, start:], jnp.concatenate(rhs, axis=1), preferred_element_type=jnp.float32)
 
     by_frames(lanes, tile_sums, finish)
-    if sends and rest_sent:
-        outs[2][:, PAIR * (chunks - 1) * LANES :] = sum(tails).astype(jnp.bfloat16)
+    if sends:
+        write_message(outs[2], whole_acts, plan["rows"] * pitch)
 
 
 def conv(chain, plan, begun, earlier, shifted, values, weight, columns):
@@ -503,10 +536,8 @@
             jax.ShapeDtypeStruct((PAIR, channels, lanes), jnp.bfloat16),
             jax.ShapeDtypeStruct((PAIR, 3, channels, rounded((plan["rows"] - 1) * pitch)), jnp.bfloat16),
         )
-        if plan["sends"] and plan["rest_sent"]:
-            out_shape += (jax.ShapeDtypeStruct((channels, PAIR * (lanes - LANES) + LANES), jnp.bfloat16),)
-        elif plan["sends"]:
-            out_shape += out_shape[:1]
+        if plan["sends"]:
+            out_shape += (message_shape(channels, plan["rows"] * pitch),)
     if plan["builds"]:
         out_shape += far_shapes(plan["rows_near"] // 2, pitch - 1 - half, channels, half)
     return chain.add(
@@ -582,7 +613,7 @@
     )
     values, shifted = [None] * pairs, [None] * pairs
     values[-1], shifted[-1], send = beyond(layers, columns, far, mate_of(far), near_values[-1], near_act[-1])
-    halo, rest = earlier_of(send), 0
+    halo = earlier_of(send)
     next_begun = layer_begun = None
     chain = Chain()
     first_begun = begin(chain, shifted[-1], weight[0])
@@ -616,9 +647,7 @@
                 "rows_near": 2 * rows,
                 "last": last,
                 "sends": p == pairs - 1 and not last,
-                "rest_sent": joined(rows_left * pitch),
                 "received": p == 0,
-                "rest": 0 if p else rest,
                 "builds": builds,
                 "inputs": len(earlier),
                 "pitch": pitch,
@@ -629,6 +658,8 @@
             if builds:
                 shifted[p - 1], values[p - 1] = outs.pop(), outs.pop()
             results[p] = outs
+            if layer == 0 and p == 0:
+                chain.run("convs")
             if plan["sends"]:
                 if layer == 0 and p == 1:
                     next_begun = begin(chain, shifted[0], weight[0])
@@ -640,7 +671,7 @@
                     halo, layer_begun = lax.optimization_barrier((halo, now(layer_begun)))
         values, shifted = [r[0] for r in results], [r[1] for r in results]
         if not last:
-            halo, rest = arriving, joined(rows_left * pitch)
+            halo = arriving
     chain.run("convs")
     result = ()
     for p in reversed(range(pairs)):

time: 43.2 us -> 42.3 us (0.979)
  starting transfers between devices: 17.2 us -> 16.6 us
    ppermute x3, starting transfers between devices: 11.8 us -> 11.2 us  [earlier_of(): return lax.ppermute(block, 'tm', [(i, i + 1) for i in range(blocks - 1)])]
    pallas_call x6 -> x7, Pallas kernels: 16 us -> 16 us  [run(): pl.pallas_call(kernel, out_shape=tuple(out_shape), in_specs=[VMEM] * len(...]
  transfers between devices with their start and end apart: 9 -> 9, of which waited for: 4 -> 3; matrix products, arithmetic and copies ran while one was open for 2% -> 2% of each run, Pallas kernels for 50% -> 52%
where the time goes in v16:
time: 42.3 us; the launch traced here: 42 us
  Pallas kernels  22.4 us (53%)
  starting transfers between devices  16.6 us (39%)
  local copies, waits for them, and re-layouts  1 us (2%)
  waiting for transfers between devices  0.98 us (2%)
  other arithmetic  0.71 us (2%)
    pallas_call x7, Pallas kernels, run(): pl.pallas_call(kernel, out_shape=tuple(out_shape), in_specs=[VMEM] * len(...  16 us
    ppermute x3, starting transfers between devices, earlier_of(): return lax.ppermute(block, 'tm', [(i, i + 1) for i in range(blocks - 1)])  11.2 us
    ppermute x2, starting transfers between devices, beyond_of(): return lax.ppermute(block, 'rows', [(i, i ^ 2) for i in range(strips)])  4.29 us
    pallas_call x1, Pallas kernels, weights(): pl.pallas_call(weights_kernel, out_shape=(one,) * layers + (jax.ShapeDtyp...  3.54 us
    pallas_call x2, Pallas kernels, join(): pl.pallas_call(functools.partial(join_kernel, pair), out_shape=jax.ShapeD...  1.58 us
    ppermute x4, starting transfers between devices, mate_of(): return lax.ppermute(block, 'rows', [(i, i ^ 1) for i in range(strips)])  1.08 us
    unnamed x2, local copies, waits for them, and re-layouts  1 us
  transfers between devices with their start and end apart: 9, of which 3 were waited for; matrix products, arithmetic and copies ran while one was open for 2% of the time, Pallas kernels for 52%

profile of v16, /device:TPU:0, one launch (start us, length us, event | category | flops | bytes accessed | tf_op | source)
XLA Modules:
  0.0 42.0 jit_solution(14586660125214891557)
XLA Ops:
  0.0 0.5 %collective-permute-start.1 = (bf16[4,2,192,128]{3,2,1,0:T(8,128)(2,1)}, bf16[4,2,192,128]{3,2,1,0:T(8,128)(2,1)S(1)}, u32[]{:S(2)}, u32[]{:S(2)}) collective-permute-start(bf16[4,2,192,128]{3,2,1,0:T(8,128)(2,1)} %in_ref.1), channel_id=1, source_target_pairs={{0,1},{1,0},{2,3},{3,2},{4,5},{5,4},{6,7},{7,6},{8,9},{9,8},{10,11... | collective-permute-start | bytes 1179656 | tf_op jit(solution)/shard_map/ppermute | solution.py:595
  0.5 1.0 %copy-done = bf16[4,2,192,128]{3,2,1,0:T(8,128)(2,1)S(1)} copy-done((bf16[4,2,192,128]{3,2,1,0:T(8,128)(2,1)S(1)}, bf16[4,2,192,128]{3,2,1,0:T(8,128)(2,1)}, u32[]{:S(2)}) %copy-start) | copy-done | bytes 393240
  1.5 2.6 %collective-permute-start = (bf16[2,2,192,128]{3,2,1,0:T(8,128)(2,1)S(1)}, bf16[2,2,192,128]{3,2,1,0:T(8,128)(2,1)S(1)}, u32[]{:S(2)}, u32[]{:S(2)}) collective-permute-start(bf16[2,2,192,128]{3,2,1,0:T(8,128)(2,1)S(1)} %get-tuple-element.50.refs_1_), channel_id=1, source_target_pairs={{0,2},{1,3},{2,0},{3,1},{4,6},{5,7},{6,4},{7,5},{8,10},{9,11},{10,... | collective-permute-start | bytes 589832 | tf_op jit(solution)/shard_map/ppermute | solution.py:601
  4.0 0.7 %pad_maximum_fusion.rows_ref.gains_ref = f32[6,192]{1,0:T(8,128)S(1)} fusion(f32[3,192]{1,0:T(4,128)} %param.7, f32[3,192]{1,0:T(4,128)} %param.6), kind=kLoop, calls=%fused_computation | loop fusion | flops 1152 | bytes 9216 | tf_op jit(solution)/shard_map/concatenate | solution.py:607
  4.7 3.5 %weights.1 = (bf16[576,1728]{1,0:T(8,128)(2,1)S(1)}, bf16[576,1728]{1,0:T(8,128)(2,1)S(1)}, bf16[576,1728]{1,0:T(8,128)(2,1)S(1)}, f32[3,2,192,128]{3,2,1,0:T(8,128)S(1)}) custom-call(bf16[3,27,192,192]{3,2,1,0:T(8,128)(2,1)} %w_ref.1, f32[6,192]{1,0:T(8,128)S(1)} %pad_maximum_fusion.rows_ref.gains_ref), custom_call_target="tpu_custom_call" | custom-call | bytes 11943936 | tf_op jit(solution)/shard_map/weights/pallas_call | solution.py:77
  8.3 0.0 collective-permute-done.1.mate_ref
  8.3 0.7 %near.1 = (bf16[2,192,384]{2,1,0:T(8,128)(2,1)S(1)}, bf16[2,192,384]{2,1,0:T(8,128)(2,1)S(1)}, bf16[2,192,256]{2,1,0:T(8,128)(2,1)S(1)}, bf16[2,192,256]{2,1,0:T(8,128)(2,1)S(1)}, bf16[2,192,256]{2,1,0:T(8,128)(2,1)S(1)}) custom-call(bf16[4,2,192,128]{3,2,1,0:T(8,128)(2,1)S(1)} %collective-permute-done.1.mate_ref, ...), custom_call_target="tpu_custom_call" | custom-call | flops 7864320 | bytes 1572864 | tf_op jit(solution)/shard_map/near/pallas_call | solution.py:220
  9.0 0.6 %collective-permute-done.far_ref = bf16[2,2,192,128]{3,2,1,0:T(8,128)(2,1)S(1)} collective-permute-done((bf16[2,2,192,128]{3,2,1,0:T(8,128)(2,1)S(1)}, bf16[2,2,192,128]{3,2,1,0:T(8,128)(2,1)S(1)}, u32[]{:S(2)}, u32[]{:S(2)}) %collective-permute-start) | collective-permute-done | bytes 196640 | tf_op jit(solution)/shard_map/ppermute | solution.py:601
  9.6 0.0 collective-permute-start.2
  9.6 1.7 %collective-permute-start.3 = (bf16[2,192,256]{2,1,0:T(8,128)(2,1)S(1)}, bf16[2,192,256]{2,1,0:T(8,128)(2,1)S(1)}, u32[]{:S(2)}, u32[]{:S(2)}) collective-permute-start(bf16[2,192,256]{2,1,0:T(8,128)(2,1)S(1)} %get-tuple-element.67), channel_id=1, source_target_pairs={{0,2},{1,3},{2,0},{3,1},{4,6},{5,7},{6,4},{7,5},{8,10},{9,11},{10,... | collective-permute-start | bytes 589832 | tf_op jit(solution)/shard_map/ppermute | solution.py:601
  11.4 0.0 collective-permute-done.2.mate_ref
  11.4 0.6 %beyond.1 = (bf16[2,192,512]{2,1,0:T(8,128)(2,1)S(1)}, bf16[2,3,192,512]{3,2,1,0:T(8,128)(2,1)S(1)}, bf16[1440,128]{1,0:T(8,128)(2,1)S(1)}) custom-call(f32[3,2,192,128]{3,2,1,0:T(8,128)S(1)} %get-tuple-element.60.columns_ref.refs_3_, bf16[2,2,192,128]{3,2,1,0:T(8,128)(2,1)S(1)} %collective-permute-done.far_ref, ...), custom_call_target="tpu_custom_call" | custom-call | flops 3932160 | bytes 786432 | tf_op jit(solution)/shard_map/beyond/pallas_call | solution.py:285
  12.0 3.5 %collective-permute-start.4 = (bf16[1440,128]{1,0:T(8,128)(2,1)S(1)}, bf16[1440,128]{1,0:T(8,128)(2,1)S(1)}, u32[]{:S(2)}, u32[]{:S(2)}) collective-permute-start(bf16[1440,128]{1,0:T(8,128)(2,1)S(1)} %get-tuple-element.75), channel_id=1, source_target_pairs={{0,4},{4,8},{8,12},{1,5},{5,9},{9,13},{2,6},{6,10},{10,14},{3,7},{... | collective-permute-start | bytes 1105928 | tf_op jit(solution)/shard_map/ppermute | solution.py:598
  15.5 1.2 %begin.2.refs_4_ = f32[2,192,512]{2,1,0:T(8,128)S(1)} custom-call(bf16[2,3,192,512]{3,2,1,0:T(8,128)(2,1)S(1)} %get-tuple-element.64.refs_0_, bf16[576,1728]{1,0:T(8,128)(2,1)S(1)} %get-tuple-element.66.refs_1_.refs_2_), custom_call_target="tpu_custom_call" | custom-call | tf_op jit(solution)/shard_map/begin/pallas_call | solution.py:428
  16.7 0.2 collective-permute-done.3.refs_5_
  16.9 2.8 %convs.5 = (bf16[2,192,512]{2,1,0:T(8,128)(2,1)S(1)}, bf16[2,3,192,384]{3,2,1,0:T(8,128)(2,1)S(1)}, bf16[1248,128]{1,0:T(8,128)(2,1)S(1)}, bf16[2,192,512]{2,1,0...) custom-call(bf16[2,3,192,512]{3,2,1,0:T(8,128)(2,1)S(1)} %get-tuple-element.64.refs_0_, ...), custom_call_target="tpu_custom_call" | custom-call | flops 4076863488 | tf_op jit(solution)/shard_map/convs/pallas_call | solution.py:428
  19.8 3.8 %collective-permute-start.5 = (bf16[1248,128]{1,0:T(8,128)(2,1)S(1)}, bf16[1248,128]{1,0:T(8,128)(2,1)S(1)}, u32[]{:S(2)}, u32[]{:S(2)}) collective-permute-start(bf16[1248,128]{1,0:T(8,128)(2,1)S(1)} %get-tuple-element.81), channel_id=1, source_target_pairs={{0,4},{4,8},{8,12},{1,5},{5,9},{9,13},{2,6},{6,10},{10,14},{3,7},{... | collective-permute-start | bytes 958472 | tf_op jit(solution)/shard_map/ppermute | solution.py:598
  23.5 1.1 %begin.3.refs_4_ = f32[2,192,384]{2,1,0:T(8,128)S(1)} custom-call(bf16[2,3,192,384]{3,2,1,0:T(8,128)(2,1)S(1)} %get-tuple-element.76.refs_0_, bf16[576,1728]{1,0:T(8,128)(2,1)S(1)} %get-tuple-element.77.refs_1_.refs_2_), custom_call_target="tpu_custom_call" | custom-call | tf_op jit(solution)/shard_map/begin/pallas_call | solution.py:428
  24.6 0.0 collective-permute-done.4.refs_5_
  24.6 2.1 %convs.6 = (bf16[2,192,512]{2,1,0:T(8,128)(2,1)S(1)}, bf16[2,3,192,384]{3,2,1,0:T(8,128)(2,1)S(1)}) custom-call(bf16[2,3,192,512]{3,2,1,0:T(8,128)(2,1)S(1)} %get-tuple-element.72.refs_0_, bf16[2,192,512]{2,1,0:T(8,128)(2,1)S(1)} %get-tuple-element.73.refs_1_, bf16[576,1728]{1,0:T(8,128)(2,1)S(1)} %get-tuple-element.66.refs_1_.refs_2_, ...), custom_call_target="tpu_custom_call" | custom-call | flops 2038431744 | tf_op jit(solution)/shard_map/convs/pallas_call | solution.py:428
  26.7 1.7 %convs.7 = (bf16[2,192,384]{2,1,0:T(8,128)(2,1)S(1)}, bf16[2,3,192,384]{3,2,1,0:T(8,128)(2,1)S(1)}, bf16[1024,128]{1,0:T(8,128)(2,1)S(1)}) custom-call(bf16[2,3,192,384]{3,2,1,0:T(8,128)(2,1)S(1)} %get-tuple-element.76.refs_0_, bf16[2,192,512]{2,1,0:T(8,128)(2,1)S(1)} %get-tuple-element.82.refs_1_, bf16[576,1728]{1,0:T(8,128)(2,1)S(1)} %get-tuple-element.77.refs_1_.refs_2_, ...), custom_call_target="tpu_custom_call" | custom-call | flops 1528823808 | tf_op jit(solution)/shard_map/convs/pallas_call | solution.py:428
  28.4 3.9 %collective-permute-start.6 = (bf16[1024,128]{1,0:T(8,128)(2,1)S(1)}, bf16[1024,128]{1,0:T(8,128)(2,1)S(1)}, u32[]{:S(2)}, u32[]{:S(2)}) collective-permute-start(bf16[1024,128]{1,0:T(8,128)(2,1)S(1)} %get-tuple-element.90), channel_id=1, source_target_pairs={{0,4},{4,8},{8,12},{1,5},{5,9},{9,13},{2,6},{6,10},{10,14},{3,7},{... | collective-permute-start | bytes 786440 | tf_op jit(solution)/shard_map/ppermute | solution.py:598
  32.4 0.0 collective-permute-done.5.refs_4_
  32.4 5.4 %convs.8 = (bf16[2,192,384]{2,1,0:T(8,128)(2,1)S(1)}, bf16[2,3,192,384]{3,2,1,0:T(8,128)(2,1)S(1)}, bf16[2,192,128]{2,1,0:T(8,128)(2,1)S(1)}, bf16[2,192,128]{2,1,0:T(8,128)(2,1)S(1)}, f32[2,192,384]{2,1,0:T(8,128)S(1)}) custom-call(bf16[2,3,192,384]{3,2,1,0:T(8,128)(2,1)S(1)} %get-tuple-element.79.refs_5_.refs_0_, ...), custom_call_target="tpu_custom_call" | custom-call | flops 3057647616 | tf_op jit(solution)/shard_map/convs/pallas_call | solution.py:428
  37.7 0.1 collective-permute-start.8
  37.8 0.0 collective-permute-done.6.refs_5_
  37.8 1.7 %convs.9 = (bf16[2,192,128]{2,1,0:T(8,128)(2,1)S(1)}, bf16[2,192,128]{2,1,0:T(8,128)(2,1)S(1)}) custom-call(bf16[2,3,192,384]{3,2,1,0:T(8,128)(2,1)S(1)} %get-tuple-element.87.refs_0_, bf16[2,192,384]{2,1,0:T(8,128)(2,1)S(1)} %get-tuple-element.88.refs_1_, bf16[576,1728]{1,0:T(8,128)(2,1)S(1)} %get-tuple-element.86.refs_7_.refs_2_, ...), custom_call_target="tpu_custom_call" | custom-call | flops 1528823808 | tf_op jit(solution)/shard_map/convs/pallas_call | solution.py:428
  39.6 0.6 %collective-permute-start.7 = (bf16[2,192,128]{2,1,0:T(8,128)(2,1)S(1)}, bf16[2,192,128]{2,1,0:T(8,128)(2,1)S(1)}, u32[]{:S(2)}, u32[]{:S(2)}) collective-permute-start(bf16[2,192,128]{2,1,0:T(8,128)(2,1)S(1)} %get-tuple-element.92), channel_id=1, source_target_pairs={{0,1},{1,0},{2,3},{3,2},{4,5},{5,4},{6,7},{7,6},{8,9},{9,8},{10,11... | collective-permute-start | bytes 294920 | tf_op jit(solution)/shard_map/ppermute | solution.py:595
  40.1 0.0 collective-permute-done.8.got_ref
  40.1 0.8 %join.2.refs_0_ = bf16[4,2,192,128]{3,2,1,0:T(8,128)(2,1)} custom-call(bf16[2,192,128]{2,1,0:T(8,128)(2,1)S(1)} %get-tuple-element.93.kept_ref, bf16[2,192,128]{2,1,0:T(8,128)(2,1)S(1)} %collective-permute-done.8.got_ref), custom_call_target="tpu_custom_call" | custom-call | tf_op jit(solution)/shard_map/join/pallas_call | solution.py:576
  40.9 0.1 collective-permute-done.7.got_ref
  41.1 0.8 %join.3 = bf16[4,2,192,128]{3,2,1,0:T(8,128)(2,1)} custom-call(bf16[2,192,128]{2,1,0:T(8,128)(2,1)S(1)} %get-tuple-element.91.kept_ref, bf16[2,192,128]{2,1,0:T(8,128)(2,1)S(1)} %collective-permute-done.7.got_ref, bf16[4,2,192,128]{3,2,1,0:T(8,128)(2,1)} %join.2.refs_0_), custom_call_target="tpu_custom_call", output_to_operand_aliasing={{}: (2, {})} | custom-call | tf_op jit(solution)/shard_map/join/pallas_call | solution.py:576
  (2 shorter events, 0.0 us)
Async XLA Ops:
  0.0 8.3 %collective-permute-start.1 = (bf16[4,2,192,128]{3,2,1,0:T(8,128)(2,1)}, bf16[4,2,192,128]{3,2,1,0:T(8,128)(2,1)S(1)}, u32[]{:S(2)}, u32[]{:S(2)}) collective-permute-start(bf16[4,2,192,128]{3,2,1,0:T(8,128)(2,1)} %in_ref.1), channel_id=1, source_target_pairs={{0,1},{1,0},{2,3},{3,2},{4,5},{5,4},{6,7},{7,6},{8,9},{9,8},{10,11... | collective-permute-start | bytes 1179656 | tf_op jit(solution)/shard_map/ppermute | solution.py:595
  0.5 1.0 %copy-start = (bf16[4,2,192,128]{3,2,1,0:T(8,128)(2,1)S(1)}, bf16[4,2,192,128]{3,2,1,0:T(8,128)(2,1)}, u32[]{:S(2)}) copy-start(bf16[4,2,192,128]{3,2,1,0:T(8,128)(2,1)} %in_ref.1) | copy-start | bytes 1179652
  1.5 8.1 %collective-permute-start = (bf16[2,2,192,128]{3,2,1,0:T(8,128)(2,1)S(1)}, bf16[2,2,192,128]{3,2,1,0:T(8,128)(2,1)S(1)}, u32[]{:S(2)}, u32[]{:S(2)}) collective-permute-start(bf16[2,2,192,128]{3,2,1,0:T(8,128)(2,1)S(1)} %get-tuple-element.50.refs_1_), channel_id=1, source_target_pairs={{0,2},{1,3},{2,0},{3,1},{4,6},{5,7},{6,4},{7,5},{8,10},{9,11},{10,... | collective-permute-start | bytes 589832 | tf_op jit(solution)/shard_map/ppermute | solution.py:601
  9.6 1.7 %collective-permute-start.2 = (bf16[2,2,192,128]{3,2,1,0:T(8,128)(2,1)S(1)}, bf16[2,2,192,128]{3,2,1,0:T(8,128)(2,1)S(1)}, u32[]{:S(2)}, u32[]{:S(2)}) collective-permute-start(bf16[2,2,192,128]{3,2,1,0:T(8,128)(2,1)S(1)} %collective-permute-done.far_ref), channel_id=1, source_target_pairs={{0,1},{1,0},{2,3},{3,2},{4,5},{5,4},{6,7},{7,6},{8,9},{9,8},{10,11... | collective-permute-start | bytes 589832 | tf_op jit(solution)/shard_map/ppermute | solution.py:595
  9.6 7.3 %collective-permute-start.3 = (bf16[2,192,256]{2,1,0:T(8,128)(2,1)S(1)}, bf16[2,192,256]{2,1,0:T(8,128)(2,1)S(1)}, u32[]{:S(2)}, u32[]{:S(2)}) collective-permute-start(bf16[2,192,256]{2,1,0:T(8,128)(2,1)S(1)} %get-tuple-element.67), channel_id=1, source_target_pairs={{0,2},{1,3},{2,0},{3,1},{4,6},{5,7},{6,4},{7,5},{8,10},{9,11},{10,... | collective-permute-start | bytes 589832 | tf_op jit(solution)/shard_map/ppermute | solution.py:601
  12.0 12.6 %collective-permute-start.4 = (bf16[1440,128]{1,0:T(8,128)(2,1)S(1)}, bf16[1440,128]{1,0:T(8,128)(2,1)S(1)}, u32[]{:S(2)}, u32[]{:S(2)}) collective-permute-start(bf16[1440,128]{1,0:T(8,128)(2,1)S(1)} %get-tuple-element.75), channel_id=1, source_target_pairs={{0,4},{4,8},{8,12},{1,5},{5,9},{9,13},{2,6},{6,10},{10,14},{3,7},{... | collective-permute-start | bytes 1105928 | tf_op jit(solution)/shard_map/ppermute | solution.py:598
  19.8 12.6 %collective-permute-start.5 = (bf16[1248,128]{1,0:T(8,128)(2,1)S(1)}, bf16[1248,128]{1,0:T(8,128)(2,1)S(1)}, u32[]{:S(2)}, u32[]{:S(2)}) collective-permute-start(bf16[1248,128]{1,0:T(8,128)(2,1)S(1)} %get-tuple-element.81), channel_id=1, source_target_pairs={{0,4},{4,8},{8,12},{1,5},{5,9},{9,13},{2,6},{6,10},{10,14},{3,7},{... | collective-permute-start | bytes 958472 | tf_op jit(solution)/shard_map/ppermute | solution.py:598
  28.4 9.4 %collective-permute-start.6 = (bf16[1024,128]{1,0:T(8,128)(2,1)S(1)}, bf16[1024,128]{1,0:T(8,128)(2,1)S(1)}, u32[]{:S(2)}, u32[]{:S(2)}) collective-permute-start(bf16[1024,128]{1,0:T(8,128)(2,1)S(1)} %get-tuple-element.90), channel_id=1, source_target_pairs={{0,4},{4,8},{8,12},{1,5},{5,9},{9,13},{2,6},{6,10},{10,14},{3,7},{... | collective-permute-start | bytes 786440 | tf_op jit(solution)/shard_map/ppermute | solution.py:598
  37.7 2.4 %collective-permute-start.8 = (bf16[2,192,128]{2,1,0:T(8,128)(2,1)S(1)}, bf16[2,192,128]{2,1,0:T(8,128)(2,1)S(1)}, u32[]{:S(2)}, u32[]{:S(2)}) collective-permute-start(bf16[2,192,128]{2,1,0:T(8,128)(2,1)S(1)} %get-tuple-element.94), channel_id=1, source_target_pairs={{0,1},{1,0},{2,3},{3,2},{4,5},{5,4},{6,7},{7,6},{8,9},{9,8},{10,11... | collective-permute-start | bytes 294920 | tf_op jit(solution)/shard_map/ppermute | solution.py:595
  39.6 1.5 %collective-permute-start.7 = (bf16[2,192,128]{2,1,0:T(8,128)(2,1)S(1)}, bf16[2,192,128]{2,1,0:T(8,128)(2,1)S(1)}, u32[]{:S(2)}, u32[]{:S(2)}) collective-permute-start(bf16[2,192,128]{2,1,0:T(8,128)(2,1)S(1)} %get-tuple-element.92), channel_id=1, source_target_pairs={{0,1},{1,0},{2,3},{3,2},{4,5},{5,4},{6,7},{7,6},{8,9},{9,8},{10,11... | collective-permute-start | bytes 294920 | tf_op jit(solution)/shard_map/ppermute | solution.py:595

commit v17 on v16

--- a/solution.py
+++ b/solution.py
@@ -15,6 +15,7 @@
 ANY = pl.BlockSpec(memory_space=pl.ANY)
 LIMIT = 24 * 1024 * 1024
 LARGE = 44 * 1024 * 1024
+WHOLE = 60 * 1024 * 1024
 
 
 def place():
@@ -90,9 +91,15 @@
     return results[:-1], results[-1]
 
 
-def split_kernel(in_ref, *out_refs):
-    for p, out_ref in enumerate(out_refs):
-        out_ref[...] = in_ref[PAIR * p : PAIR * (p + 1)]
+def split_kernel(in_ref, *refs):
+    out_refs, sems = refs[:-1], refs[-1]
+    copies = [
+        pltpu.make_async_copy(in_ref.at[pl.ds(PAIR * p, PAIR)], out_ref, sems.at[p]) for p, out_ref in enumerate(out_refs)
+    ]
+    for copy in reversed(copies):
+        copy.start()
+    for copy in copies:
+        copy.wait()
 
 
 def split(latents):
@@ -100,9 +107,10 @@
     return pl.pallas_call(
         split_kernel,
         out_shape=(jax.ShapeDtypeStruct((PAIR,) + latents.shape[1:], latents.dtype),) * pairs,
-        in_specs=[VMEM],
+        in_specs=[ANY],
         out_specs=(VMEM,) * pairs,
-        compiler_params=pltpu.CompilerParams(vmem_limit_bytes=LIMIT),
+        scratch_shapes=[pltpu.SemaphoreType.DMA((pairs,))],
+        compiler_params=pltpu.CompilerParams(vmem_limit_bytes=WHOLE),
         name="split",
     )(latents)
 

time: 42.3 us -> 43.3 us (1.024)
  Pallas kernels: 22.4 us -> 24.2 us
  local copies, waits for them, and re-layouts: 1 us -> 0.01 us
    pallas_call x1, Pallas kernels: 0.03 us -> 1.77 us  [split(): pl.pallas_call(split_kernel, out_shape=(jax.ShapeDtypeStruct((PAIR,) + la...]
    unnamed x2 -> x4, local copies, waits for them, and re-layouts: 1 us -> 0.01 us
  transfers between devices with their start and end apart: 9 -> 9, of which waited for: 3 -> 3; matrix products, arithmetic and copies ran while one was open for 2% -> 2% of each run, Pallas kernels for 52% -> 55%
where the time goes in v17:
time: 43.3 us; the launch traced here: 43 us
  Pallas kernels  24.2 us (56%)
  starting transfers between devices  16.6 us (38%)
  waiting for transfers between devices  1.12 us (3%)
  other arithmetic  0.71 us (2%)
    pallas_call x7, Pallas kernels, run(): pl.pallas_call(kernel, out_shape=tuple(out_shape), in_specs=[VMEM] * len(...  16 us
    ppermute x3, starting transfers between devices, earlier_of(): return lax.ppermute(block, 'tm', [(i, i + 1) for i in range(blocks - 1)])  11.2 us
    ppermute x2, starting transfers between devices, beyond_of(): return lax.ppermute(block, 'rows', [(i, i ^ 2) for i in range(strips)])  4.3 us
    pallas_call x1, Pallas kernels, weights(): pl.pallas_call(weights_kernel, out_shape=(one,) * layers + (jax.ShapeDtyp...  3.58 us
    pallas_call x1, Pallas kernels, split(): pl.pallas_call(split_kernel, out_shape=(jax.ShapeDtypeStruct((PAIR,) + la...  1.77 us
    pallas_call x2, Pallas kernels, join(): pl.pallas_call(functools.partial(join_kernel, pair), out_shape=jax.ShapeD...  1.58 us
    ppermute x4, starting transfers between devices, mate_of(): return lax.ppermute(block, 'rows', [(i, i ^ 1) for i in range(strips)])  1.08 us
    ppermute x2, waiting for transfers between devices, beyond_of(): return lax.ppermute(block, 'rows', [(i, i ^ 2) for i in range(strips)])  0.96 us
  transfers between devices with their start and end apart: 9, of which 3 were waited for; matrix products, arithmetic and copies ran while one was open for 2% of the time, Pallas kernels for 55%

profile of v17, /device:TPU:0, one launch (start us, length us, event | category | flops | bytes accessed | tf_op | source)
XLA Modules:
  0.0 43.0 jit_solution(8153142569521035696)
XLA Ops:
  0.0 0.5 %collective-permute-start.1 = (bf16[4,2,192,128]{3,2,1,0:T(8,128)(2,1)}, bf16[4,2,192,128]{3,2,1,0:T(8,128)(2,1)S(1)}, u32[]{:S(2)}, u32[]{:S(2)}) collective-permute-start(bf16[4,2,192,128]{3,2,1,0:T(8,128)(2,1)} %in_ref.1), channel_id=1, source_target_pairs={{0,1},{1,0},{2,3},{3,2},{4,5},{5,4},{6,7},{7,6},{8,9},{9,8},{10,11... | collective-permute-start | bytes 1179656 | tf_op jit(solution)/shard_map/ppermute | solution.py:603
  0.5 1.8 %split.1 = (bf16[2,2,192,128]{3,2,1,0:T(8,128)(2,1)}, bf16[2,2,192,128]{3,2,1,0:T(8,128)(2,1)}) custom-call(bf16[4,2,192,128]{3,2,1,0:T(8,128)(2,1)} %in_ref.1), custom_call_target="tpu_custom_call" | custom-call | tf_op jit(solution)/shard_map/split/pallas_call | solution.py:107
  2.2 2.6 %collective-permute-start = (bf16[2,2,192,128]{3,2,1,0:T(8,128)(2,1)}, bf16[2,2,192,128]{3,2,1,0:T(8,128)(2,1)S(1)}, u32[]{:S(2)}, u32[]{:S(2)}) collective-permute-start(bf16[2,2,192,128]{3,2,1,0:T(8,128)(2,1)} %get-tuple-element.50.refs_1_), channel_id=1, source_target_pairs={{0,2},{1,3},{2,0},{3,1},{4,6},{5,7},{6,4},{7,5},{8,10},{9,11},{10,... | collective-permute-start | bytes 589832 | tf_op jit(solution)/shard_map/ppermute | solution.py:609
  4.8 0.7 %pad_maximum_fusion.rows_ref.gains_ref = f32[6,192]{1,0:T(8,128)S(1)} fusion(f32[3,192]{1,0:T(4,128)} %param.7, f32[3,192]{1,0:T(4,128)} %param.6), kind=kLoop, calls=%fused_computation | loop fusion | flops 1152 | bytes 9216 | tf_op jit(solution)/shard_map/concatenate | solution.py:615
  5.5 0.0 copy-start.1
  5.5 3.6 %weights.1 = (bf16[576,1728]{1,0:T(8,128)(2,1)S(1)}, bf16[576,1728]{1,0:T(8,128)(2,1)S(1)}, bf16[576,1728]{1,0:T(8,128)(2,1)S(1)}, f32[3,2,192,128]{3,2,1,0:T(8,128)S(1)}) custom-call(bf16[3,27,192,192]{3,2,1,0:T(8,128)(2,1)} %w_ref.1, f32[6,192]{1,0:T(8,128)S(1)} %pad_maximum_fusion.rows_ref.gains_ref), custom_call_target="tpu_custom_call" | custom-call | bytes 11943936 | tf_op jit(solution)/shard_map/weights/pallas_call | solution.py:78
  9.1 0.0 collective-permute-done.1.mate_ref
  9.1 0.7 %near.1 = (bf16[2,192,384]{2,1,0:T(8,128)(2,1)S(1)}, bf16[2,192,384]{2,1,0:T(8,128)(2,1)S(1)}, bf16[2,192,256]{2,1,0:T(8,128)(2,1)S(1)}, bf16[2,192,256]{2,1,0:T(8,128)(2,1)S(1)}, bf16[2,192,256]{2,1,0:T(8,128)(2,1)S(1)}) custom-call(bf16[4,2,192,128]{3,2,1,0:T(8,128)(2,1)S(1)} %collective-permute-done.1.mate_ref, ...), custom_call_target="tpu_custom_call" | custom-call | flops 7864320 | bytes 1572864 | tf_op jit(solution)/shard_map/near/pallas_call | solution.py:228
  9.8 0.7 %collective-permute-done.far_ref = bf16[2,2,192,128]{3,2,1,0:T(8,128)(2,1)S(1)} collective-permute-done((bf16[2,2,192,128]{3,2,1,0:T(8,128)(2,1)}, bf16[2,2,192,128]{3,2,1,0:T(8,128)(2,1)S(1)}, u32[]{:S(2)}, u32[]{:S(2)}) %collective-permute-start) | collective-permute-done | bytes 196640 | tf_op jit(solution)/shard_map/ppermute | solution.py:609
  10.6 0.0 collective-permute-start.2
  10.6 1.7 %collective-permute-start.3 = (bf16[2,192,256]{2,1,0:T(8,128)(2,1)S(1)}, bf16[2,192,256]{2,1,0:T(8,128)(2,1)S(1)}, u32[]{:S(2)}, u32[]{:S(2)}) collective-permute-start(bf16[2,192,256]{2,1,0:T(8,128)(2,1)S(1)} %get-tuple-element.67), channel_id=1, source_target_pairs={{0,2},{1,3},{2,0},{3,1},{4,6},{5,7},{6,4},{7,5},{8,10},{9,11},{10,... | collective-permute-start | bytes 589832 | tf_op jit(solution)/shard_map/ppermute | solution.py:609
  12.3 0.0 collective-permute-done.2.mate_ref
  12.3 0.6 %beyond.1 = (bf16[2,192,512]{2,1,0:T(8,128)(2,1)S(1)}, bf16[2,3,192,512]{3,2,1,0:T(8,128)(2,1)S(1)}, bf16[1440,128]{1,0:T(8,128)(2,1)S(1)}) custom-call(f32[3,2,192,128]{3,2,1,0:T(8,128)S(1)} %get-tuple-element.60.columns_ref.refs_3_, bf16[2,2,192,128]{3,2,1,0:T(8,128)(2,1)S(1)} %collective-permute-done.far_ref, ...), custom_call_target="tpu_custom_call" | custom-call | flops 3932160 | bytes 786432 | tf_op jit(solution)/shard_map/beyond/pallas_call | solution.py:293
  12.9 3.5 %collective-permute-start.4 = (bf16[1440,128]{1,0:T(8,128)(2,1)S(1)}, bf16[1440,128]{1,0:T(8,128)(2,1)S(1)}, u32[]{:S(2)}, u32[]{:S(2)}) collective-permute-start(bf16[1440,128]{1,0:T(8,128)(2,1)S(1)} %get-tuple-element.75), channel_id=1, source_target_pairs={{0,4},{4,8},{8,12},{1,5},{5,9},{9,13},{2,6},{6,10},{10,14},{3,7},{... | collective-permute-start | bytes 1105928 | tf_op jit(solution)/shard_map/ppermute | solution.py:606
  16.5 1.2 %begin.2.refs_4_ = f32[2,192,512]{2,1,0:T(8,128)S(1)} custom-call(bf16[2,3,192,512]{3,2,1,0:T(8,128)(2,1)S(1)} %get-tuple-element.64.refs_0_, bf16[576,1728]{1,0:T(8,128)(2,1)S(1)} %get-tuple-element.66.refs_1_.refs_2_), custom_call_target="tpu_custom_call" | custom-call | tf_op jit(solution)/shard_map/begin/pallas_call | solution.py:436
  17.7 0.2 collective-permute-done.3.refs_5_
  17.9 2.8 %convs.5 = (bf16[2,192,512]{2,1,0:T(8,128)(2,1)S(1)}, bf16[2,3,192,384]{3,2,1,0:T(8,128)(2,1)S(1)}, bf16[1248,128]{1,0:T(8,128)(2,1)S(1)}, bf16[2,192,512]{2,1,0...) custom-call(bf16[2,3,192,512]{3,2,1,0:T(8,128)(2,1)S(1)} %get-tuple-element.64.refs_0_, ...), custom_call_target="tpu_custom_call" | custom-call | flops 4076863488 | tf_op jit(solution)/shard_map/convs/pallas_call | solution.py:436
  20.7 3.7 %collective-permute-start.5 = (bf16[1248,128]{1,0:T(8,128)(2,1)S(1)}, bf16[1248,128]{1,0:T(8,128)(2,1)S(1)}, u32[]{:S(2)}, u32[]{:S(2)}) collective-permute-start(bf16[1248,128]{1,0:T(8,128)(2,1)S(1)} %get-tuple-element.81), channel_id=1, source_target_pairs={{0,4},{4,8},{8,12},{1,5},{5,9},{9,13},{2,6},{6,10},{10,14},{3,7},{... | collective-permute-start | bytes 958472 | tf_op jit(solution)/shard_map/ppermute | solution.py:606
  24.5 1.1 %begin.3.refs_4_ = f32[2,192,384]{2,1,0:T(8,128)S(1)} custom-call(bf16[2,3,192,384]{3,2,1,0:T(8,128)(2,1)S(1)} %get-tuple-element.76.refs_0_, bf16[576,1728]{1,0:T(8,128)(2,1)S(1)} %get-tuple-element.77.refs_1_.refs_2_), custom_call_target="tpu_custom_call" | custom-call | tf_op jit(solution)/shard_map/begin/pallas_call | solution.py:436
  25.6 2.1 %convs.6 = (bf16[2,192,512]{2,1,0:T(8,128)(2,1)S(1)}, bf16[2,3,192,384]{3,2,1,0:T(8,128)(2,1)S(1)}) custom-call(bf16[2,3,192,512]{3,2,1,0:T(8,128)(2,1)S(1)} %get-tuple-element.72.refs_0_, bf16[2,192,512]{2,1,0:T(8,128)(2,1)S(1)} %get-tuple-element.73.refs_1_, bf16[576,1728]{1,0:T(8,128)(2,1)S(1)} %get-tuple-element.66.refs_1_.refs_2_, ...), custom_call_target="tpu_custom_call" | custom-call | flops 2038431744 | tf_op jit(solution)/shard_map/convs/pallas_call | solution.py:436
  27.7 1.7 %convs.7 = (bf16[2,192,384]{2,1,0:T(8,128)(2,1)S(1)}, bf16[2,3,192,384]{3,2,1,0:T(8,128)(2,1)S(1)}, bf16[1024,128]{1,0:T(8,128)(2,1)S(1)}) custom-call(bf16[2,3,192,384]{3,2,1,0:T(8,128)(2,1)S(1)} %get-tuple-element.76.refs_0_, bf16[2,192,512]{2,1,0:T(8,128)(2,1)S(1)} %get-tuple-element.82.refs_1_, bf16[576,1728]{1,0:T(8,128)(2,1)S(1)} %get-tuple-element.77.refs_1_.refs_2_, ...), custom_call_target="tpu_custom_call" | custom-call | flops 1528823808 | tf_op jit(solution)/shard_map/convs/pallas_call | solution.py:436
  29.4 3.9 %collective-permute-start.6 = (bf16[1024,128]{1,0:T(8,128)(2,1)S(1)}, bf16[1024,128]{1,0:T(8,128)(2,1)S(1)}, u32[]{:S(2)}, u32[]{:S(2)}) collective-permute-start(bf16[1024,128]{1,0:T(8,128)(2,1)S(1)} %get-tuple-element.90), channel_id=1, source_target_pairs={{0,4},{4,8},{8,12},{1,5},{5,9},{9,13},{2,6},{6,10},{10,14},{3,7},{... | collective-permute-start | bytes 786440 | tf_op jit(solution)/shard_map/ppermute | solution.py:606
  33.3 0.0 collective-permute-done.5.refs_4_
  33.3 5.4 %convs.8 = (bf16[2,192,384]{2,1,0:T(8,128)(2,1)S(1)}, bf16[2,3,192,384]{3,2,1,0:T(8,128)(2,1)S(1)}, bf16[2,192,128]{2,1,0:T(8,128)(2,1)S(1)}, bf16[2,192,128]{2,1,0:T(8,128)(2,1)S(1)}, f32[2,192,384]{2,1,0:T(8,128)S(1)}) custom-call(bf16[2,3,192,384]{3,2,1,0:T(8,128)(2,1)S(1)} %get-tuple-element.79.refs_5_.refs_0_, ...), custom_call_target="tpu_custom_call" | custom-call | flops 3057647616 | tf_op jit(solution)/shard_map/convs/pallas_call | solution.py:436
  38.7 0.1 collective-permute-start.8
  38.8 0.0 collective-permute-done.6.refs_5_
  38.8 1.7 %convs.9 = (bf16[2,192,128]{2,1,0:T(8,128)(2,1)S(1)}, bf16[2,192,128]{2,1,0:T(8,128)(2,1)S(1)}) custom-call(bf16[2,3,192,384]{3,2,1,0:T(8,128)(2,1)S(1)} %get-tuple-element.87.refs_0_, bf16[2,192,384]{2,1,0:T(8,128)(2,1)S(1)} %get-tuple-element.88.refs_1_, bf16[576,1728]{1,0:T(8,128)(2,1)S(1)} %get-tuple-element.86.refs_7_.refs_2_, ...), custom_call_target="tpu_custom_call" | custom-call | flops 1528823808 | tf_op jit(solution)/shard_map/convs/pallas_call | solution.py:436
  40.5 0.6 %collective-permute-start.7 = (bf16[2,192,128]{2,1,0:T(8,128)(2,1)S(1)}, bf16[2,192,128]{2,1,0:T(8,128)(2,1)S(1)}, u32[]{:S(2)}, u32[]{:S(2)}) collective-permute-start(bf16[2,192,128]{2,1,0:T(8,128)(2,1)S(1)} %get-tuple-element.92), channel_id=1, source_target_pairs={{0,1},{1,0},{2,3},{3,2},{4,5},{5,4},{6,7},{7,6},{8,9},{9,8},{10,11... | collective-permute-start | bytes 294920 | tf_op jit(solution)/shard_map/ppermute | solution.py:603
  41.1 0.0 collective-permute-done.8.got_ref
  41.1 0.8 %join.2.refs_0_ = bf16[4,2,192,128]{3,2,1,0:T(8,128)(2,1)} custom-call(bf16[2,192,128]{2,1,0:T(8,128)(2,1)S(1)} %get-tuple-element.93.kept_ref, bf16[2,192,128]{2,1,0:T(8,128)(2,1)S(1)} %collective-permute-done.8.got_ref), custom_call_target="tpu_custom_call" | custom-call | tf_op jit(solution)/shard_map/join/pallas_call | solution.py:584
  41.9 0.1 collective-permute-done.7.got_ref
  42.0 0.8 %join.3 = bf16[4,2,192,128]{3,2,1,0:T(8,128)(2,1)} custom-call(bf16[2,192,128]{2,1,0:T(8,128)(2,1)S(1)} %get-tuple-element.91.kept_ref, bf16[2,192,128]{2,1,0:T(8,128)(2,1)S(1)} %collective-permute-done.7.got_ref, bf16[4,2,192,128]{3,2,1,0:T(8,128)(2,1)} %join.2.refs_0_), custom_call_target="tpu_custom_call", output_to_operand_aliasing={{}: (2, {})} | custom-call | tf_op jit(solution)/shard_map/join/pallas_call | solution.py:584
  (4 shorter events, 0.0 us)
Async XLA Ops:
  0.0 9.1 %collective-permute-start.1 = (bf16[4,2,192,128]{3,2,1,0:T(8,128)(2,1)}, bf16[4,2,192,128]{3,2,1,0:T(8,128)(2,1)S(1)}, u32[]{:S(2)}, u32[]{:S(2)}) collective-permute-start(bf16[4,2,192,128]{3,2,1,0:T(8,128)(2,1)} %in_ref.1), channel_id=1, source_target_pairs={{0,1},{1,0},{2,3},{3,2},{4,5},{5,4},{6,7},{7,6},{8,9},{9,8},{10,11... | collective-permute-start | bytes 1179656 | tf_op jit(solution)/shard_map/ppermute | solution.py:603
  2.2 8.3 %collective-permute-start = (bf16[2,2,192,128]{3,2,1,0:T(8,128)(2,1)}, bf16[2,2,192,128]{3,2,1,0:T(8,128)(2,1)S(1)}, u32[]{:S(2)}, u32[]{:S(2)}) collective-permute-start(bf16[2,2,192,128]{3,2,1,0:T(8,128)(2,1)} %get-tuple-element.50.refs_1_), channel_id=1, source_target_pairs={{0,2},{1,3},{2,0},{3,1},{4,6},{5,7},{6,4},{7,5},{8,10},{9,11},{10,... | collective-permute-start | bytes 589832 | tf_op jit(solution)/shard_map/ppermute | solution.py:609
  5.5 3.6 %copy-start = (bf16[2,2,192,128]{3,2,1,0:T(8,128)(2,1)S(1)}, bf16[2,2,192,128]{3,2,1,0:T(8,128)(2,1)}, u32[]{:S(2)}) copy-start(bf16[2,2,192,128]{3,2,1,0:T(8,128)(2,1)} %get-tuple-element.50.refs_1_) | copy-start | bytes 589828
  5.5 3.6 %copy-start.1 = (bf16[2,2,192,128]{3,2,1,0:T(8,128)(2,1)S(1)}, bf16[2,2,192,128]{3,2,1,0:T(8,128)(2,1)}, u32[]{:S(2)}) copy-start(bf16[2,2,192,128]{3,2,1,0:T(8,128)(2,1)} %get-tuple-element.55.refs_0_) | copy-start | bytes 589828
  10.6 1.7 %collective-permute-start.2 = (bf16[2,2,192,128]{3,2,1,0:T(8,128)(2,1)S(1)}, bf16[2,2,192,128]{3,2,1,0:T(8,128)(2,1)S(1)}, u32[]{:S(2)}, u32[]{:S(2)}) collective-permute-start(bf16[2,2,192,128]{3,2,1,0:T(8,128)(2,1)S(1)} %collective-permute-done.far_ref), channel_id=1, source_target_pairs={{0,1},{1,0},{2,3},{3,2},{4,5},{5,4},{6,7},{7,6},{8,9},{9,8},{10,11... | collective-permute-start | bytes 589832 | tf_op jit(solution)/shard_map/ppermute | solution.py:603
  10.6 7.3 %collective-permute-start.3 = (bf16[2,192,256]{2,1,0:T(8,128)(2,1)S(1)}, bf16[2,192,256]{2,1,0:T(8,128)(2,1)S(1)}, u32[]{:S(2)}, u32[]{:S(2)}) collective-permute-start(bf16[2,192,256]{2,1,0:T(8,128)(2,1)S(1)} %get-tuple-element.67), channel_id=1, source_target_pairs={{0,2},{1,3},{2,0},{3,1},{4,6},{5,7},{6,4},{7,5},{8,10},{9,11},{10,... | collective-permute-start | bytes 589832 | tf_op jit(solution)/shard_map/ppermute | solution.py:609
  12.9 12.6 %collective-permute-start.4 = (bf16[1440,128]{1,0:T(8,128)(2,1)S(1)}, bf16[1440,128]{1,0:T(8,128)(2,1)S(1)}, u32[]{:S(2)}, u32[]{:S(2)}) collective-permute-start(bf16[1440,128]{1,0:T(8,128)(2,1)S(1)} %get-tuple-element.75), channel_id=1, source_target_pairs={{0,4},{4,8},{8,12},{1,5},{5,9},{9,13},{2,6},{6,10},{10,14},{3,7},{... | collective-permute-start | bytes 1105928 | tf_op jit(solution)/shard_map/ppermute | solution.py:606
  20.7 12.6 %collective-permute-start.5 = (bf16[1248,128]{1,0:T(8,128)(2,1)S(1)}, bf16[1248,128]{1,0:T(8,128)(2,1)S(1)}, u32[]{:S(2)}, u32[]{:S(2)}) collective-permute-start(bf16[1248,128]{1,0:T(8,128)(2,1)S(1)} %get-tuple-element.81), channel_id=1, source_target_pairs={{0,4},{4,8},{8,12},{1,5},{5,9},{9,13},{2,6},{6,10},{10,14},{3,7},{... | collective-permute-start | bytes 958472 | tf_op jit(solution)/shard_map/ppermute | solution.py:606
  29.4 9.4 %collective-permute-start.6 = (bf16[1024,128]{1,0:T(8,128)(2,1)S(1)}, bf16[1024,128]{1,0:T(8,128)(2,1)S(1)}, u32[]{:S(2)}, u32[]{:S(2)}) collective-permute-start(bf16[1024,128]{1,0:T(8,128)(2,1)S(1)} %get-tuple-element.90), channel_id=1, source_target_pairs={{0,4},{4,8},{8,12},{1,5},{5,9},{9,13},{2,6},{6,10},{10,14},{3,7},{... | collective-permute-start | bytes 786440 | tf_op jit(solution)/shard_map/ppermute | solution.py:606
  38.7 2.4 %collective-permute-start.8 = (bf16[2,192,128]{2,1,0:T(8,128)(2,1)S(1)}, bf16[2,192,128]{2,1,0:T(8,128)(2,1)S(1)}, u32[]{:S(2)}, u32[]{:S(2)}) collective-permute-start(bf16[2,192,128]{2,1,0:T(8,128)(2,1)S(1)} %get-tuple-element.94), channel_id=1, source_target_pairs={{0,1},{1,0},{2,3},{3,2},{4,5},{5,4},{6,7},{7,6},{8,9},{9,8},{10,11... | collective-permute-start | bytes 294920 | tf_op jit(solution)/shard_map/ppermute | solution.py:603
  40.5 1.5 %collective-permute-start.7 = (bf16[2,192,128]{2,1,0:T(8,128)(2,1)S(1)}, bf16[2,192,128]{2,1,0:T(8,128)(2,1)S(1)}, u32[]{:S(2)}, u32[]{:S(2)}) collective-permute-start(bf16[2,192,128]{2,1,0:T(8,128)(2,1)S(1)} %get-tuple-element.92), channel_id=1, source_target_pairs={{0,1},{1,0},{2,3},{3,2},{4,5},{5,4},{6,7},{7,6},{8,9},{9,8},{10,11... | collective-permute-start | bytes 294920 | tf_op jit(solution)/shard_map/ppermute | solution.py:603

commit v18 on v16

--- a/solution.py
+++ b/solution.py
@@ -637,7 +637,7 @@
                 begun = (next_begun,)
             elif layer == 1 and p == pairs - 1 and layer_begun is not None:
                 begun = (layer_begun,)
-            elif builds or (p == 0 and (last or layer == 0)):
+            elif builds or (p == 0 and layer == 0):
                 begun = (begin(chain, shifted[p], weight[layer]),)
             if last and p == 0:
                 chain.run("convs")

time: 42.3 us -> 42.3 us (level)
  no operation moved by 1% of the time
where the time goes in v18:
time: 42.3 us; the launch traced here: 42.1 us
  Pallas kernels  22.5 us (53%)
  starting transfers between devices  16.6 us (39%)
  local copies, waits for them, and re-layouts  1 us (2%)
  waiting for transfers between devices  0.98 us (2%)
  other arithmetic  0.71 us (2%)
    pallas_call x7, Pallas kernels, run(): pl.pallas_call(kernel, out_shape=tuple(out_shape), in_specs=[VMEM] * len(...  16.1 us
    ppermute x3, starting transfers between devices, earlier_of(): return lax.ppermute(block, 'tm', [(i, i + 1) for i in range(blocks - 1)])  11.2 us
    ppermute x2, starting transfers between devices, beyond_of(): return lax.ppermute(block, 'rows', [(i, i ^ 2) for i in range(strips)])  4.29 us
    pallas_call x1, Pallas kernels, weights(): pl.pallas_call(weights_kernel, out_shape=(one,) * layers + (jax.ShapeDtyp...  3.54 us
    pallas_call x2, Pallas kernels, join(): pl.pallas_call(functools.partial(join_kernel, pair), out_shape=jax.ShapeD...  1.58 us
    ppermute x4, starting transfers between devices, mate_of(): return lax.ppermute(block, 'rows', [(i, i ^ 1) for i in range(strips)])  1.07 us
    unnamed x2, local copies, waits for them, and re-layouts  1 us
  transfers between devices with their start and end apart: 9, of which 3 were waited for; matrix products, arithmetic and copies ran while one was open for 2% of the time, Pallas kernels for 52%

profile of v18, /device:TPU:0, one launch (start us, length us, event | category | flops | bytes accessed | tf_op | source)
XLA Modules:
  0.0 42.1 jit_solution(5661072063728619118)
XLA Ops:
  0.0 0.5 %collective-permute-start.1 = (bf16[4,2,192,128]{3,2,1,0:T(8,128)(2,1)}, bf16[4,2,192,128]{3,2,1,0:T(8,128)(2,1)S(1)}, u32[]{:S(2)}, u32[]{:S(2)}) collective-permute-start(bf16[4,2,192,128]{3,2,1,0:T(8,128)(2,1)} %in_ref.1), channel_id=1, source_target_pairs={{0,1},{1,0},{2,3},{3,2},{4,5},{5,4},{6,7},{7,6},{8,9},{9,8},{10,11... | collective-permute-start | bytes 1179656 | tf_op jit(solution)/shard_map/ppermute | solution.py:595
  0.5 1.0 %copy-done = bf16[4,2,192,128]{3,2,1,0:T(8,128)(2,1)S(1)} copy-done((bf16[4,2,192,128]{3,2,1,0:T(8,128)(2,1)S(1)}, bf16[4,2,192,128]{3,2,1,0:T(8,128)(2,1)}, u32[]{:S(2)}) %copy-start) | copy-done | bytes 393240
  1.5 2.6 %collective-permute-start = (bf16[2,2,192,128]{3,2,1,0:T(8,128)(2,1)S(1)}, bf16[2,2,192,128]{3,2,1,0:T(8,128)(2,1)S(1)}, u32[]{:S(2)}, u32[]{:S(2)}) collective-permute-start(bf16[2,2,192,128]{3,2,1,0:T(8,128)(2,1)S(1)} %get-tuple-element.49.refs_1_), channel_id=1, source_target_pairs={{0,2},{1,3},{2,0},{3,1},{4,6},{5,7},{6,4},{7,5},{8,10},{9,11},{10,... | collective-permute-start | bytes 589832 | tf_op jit(solution)/shard_map/ppermute | solution.py:601
  4.0 0.7 %pad_maximum_fusion.rows_ref.gains_ref = f32[6,192]{1,0:T(8,128)S(1)} fusion(f32[3,192]{1,0:T(4,128)} %param.7, f32[3,192]{1,0:T(4,128)} %param.6), kind=kLoop, calls=%fused_computation | loop fusion | flops 1152 | bytes 9216 | tf_op jit(solution)/shard_map/concatenate | solution.py:607
  4.7 3.5 %weights.1 = (bf16[576,1728]{1,0:T(8,128)(2,1)S(1)}, bf16[576,1728]{1,0:T(8,128)(2,1)S(1)}, bf16[576,1728]{1,0:T(8,128)(2,1)S(1)}, f32[3,2,192,128]{3,2,1,0:T(8,128)S(1)}) custom-call(bf16[3,27,192,192]{3,2,1,0:T(8,128)(2,1)} %w_ref.1, f32[6,192]{1,0:T(8,128)S(1)} %pad_maximum_fusion.rows_ref.gains_ref), custom_call_target="tpu_custom_call" | custom-call | bytes 11943936 | tf_op jit(solution)/shard_map/weights/pallas_call | solution.py:77
  8.3 0.0 collective-permute-done.1.mate_ref
  8.3 0.7 %near.1 = (bf16[2,192,384]{2,1,0:T(8,128)(2,1)S(1)}, bf16[2,192,384]{2,1,0:T(8,128)(2,1)S(1)}, bf16[2,192,256]{2,1,0:T(8,128)(2,1)S(1)}, bf16[2,192,256]{2,1,0:T(8,128)(2,1)S(1)}, bf16[2,192,256]{2,1,0:T(8,128)(2,1)S(1)}) custom-call(bf16[4,2,192,128]{3,2,1,0:T(8,128)(2,1)S(1)} %collective-permute-done.1.mate_ref, ...), custom_call_target="tpu_custom_call" | custom-call | flops 7864320 | bytes 1572864 | tf_op jit(solution)/shard_map/near/pallas_call | solution.py:220
  9.0 0.6 %collective-permute-done.far_ref = bf16[2,2,192,128]{3,2,1,0:T(8,128)(2,1)S(1)} collective-permute-done((bf16[2,2,192,128]{3,2,1,0:T(8,128)(2,1)S(1)}, bf16[2,2,192,128]{3,2,1,0:T(8,128)(2,1)S(1)}, u32[]{:S(2)}, u32[]{:S(2)}) %collective-permute-start) | collective-permute-done | bytes 196640 | tf_op jit(solution)/shard_map/ppermute | solution.py:601
  9.6 0.0 collective-permute-start.2
  9.6 1.7 %collective-permute-start.3 = (bf16[2,192,256]{2,1,0:T(8,128)(2,1)S(1)}, bf16[2,192,256]{2,1,0:T(8,128)(2,1)S(1)}, u32[]{:S(2)}, u32[]{:S(2)}) collective-permute-start(bf16[2,192,256]{2,1,0:T(8,128)(2,1)S(1)} %get-tuple-element.66), channel_id=1, source_target_pairs={{0,2},{1,3},{2,0},{3,1},{4,6},{5,7},{6,4},{7,5},{8,10},{9,11},{10,... | collective-permute-start | bytes 589832 | tf_op jit(solution)/shard_map/ppermute | solution.py:601
  11.4 0.0 collective-permute-done.2.mate_ref
  11.4 0.6 %beyond.1 = (bf16[2,192,512]{2,1,0:T(8,128)(2,1)S(1)}, bf16[2,3,192,512]{3,2,1,0:T(8,128)(2,1)S(1)}, bf16[1440,128]{1,0:T(8,128)(2,1)S(1)}) custom-call(f32[3,2,192,128]{3,2,1,0:T(8,128)S(1)} %get-tuple-element.59.columns_ref.refs_3_, bf16[2,2,192,128]{3,2,1,0:T(8,128)(2,1)S(1)} %collective-permute-done.far_ref, ...), custom_call_target="tpu_custom_call" | custom-call | flops 3932160 | bytes 786432 | tf_op jit(solution)/shard_map/beyond/pallas_call | solution.py:285
  12.0 3.5 %collective-permute-start.4 = (bf16[1440,128]{1,0:T(8,128)(2,1)S(1)}, bf16[1440,128]{1,0:T(8,128)(2,1)S(1)}, u32[]{:S(2)}, u32[]{:S(2)}) collective-permute-start(bf16[1440,128]{1,0:T(8,128)(2,1)S(1)} %get-tuple-element.74), channel_id=1, source_target_pairs={{0,4},{4,8},{8,12},{1,5},{5,9},{9,13},{2,6},{6,10},{10,14},{3,7},{... | collective-permute-start | bytes 1105928 | tf_op jit(solution)/shard_map/ppermute | solution.py:598
  15.5 1.2 %begin.2.refs_4_ = f32[2,192,512]{2,1,0:T(8,128)S(1)} custom-call(bf16[2,3,192,512]{3,2,1,0:T(8,128)(2,1)S(1)} %get-tuple-element.63.refs_0_, bf16[576,1728]{1,0:T(8,128)(2,1)S(1)} %get-tuple-element.65.refs_1_.refs_2_), custom_call_target="tpu_custom_call" | custom-call | tf_op jit(solution)/shard_map/begin/pallas_call | solution.py:428
  16.7 0.2 collective-permute-done.3.refs_5_
  16.9 2.8 %convs.5 = (bf16[2,192,512]{2,1,0:T(8,128)(2,1)S(1)}, bf16[2,3,192,384]{3,2,1,0:T(8,128)(2,1)S(1)}, bf16[1248,128]{1,0:T(8,128)(2,1)S(1)}, bf16[2,192,512]{2,1,0...) custom-call(bf16[2,3,192,512]{3,2,1,0:T(8,128)(2,1)S(1)} %get-tuple-element.63.refs_0_, ...), custom_call_target="tpu_custom_call" | custom-call | flops 4076863488 | tf_op jit(solution)/shard_map/convs/pallas_call | solution.py:428
  19.8 3.8 %collective-permute-start.5 = (bf16[1248,128]{1,0:T(8,128)(2,1)S(1)}, bf16[1248,128]{1,0:T(8,128)(2,1)S(1)}, u32[]{:S(2)}, u32[]{:S(2)}) collective-permute-start(bf16[1248,128]{1,0:T(8,128)(2,1)S(1)} %get-tuple-element.80), channel_id=1, source_target_pairs={{0,4},{4,8},{8,12},{1,5},{5,9},{9,13},{2,6},{6,10},{10,14},{3,7},{... | collective-permute-start | bytes 958472 | tf_op jit(solution)/shard_map/ppermute | solution.py:598
  23.5 1.1 %begin.3.refs_4_ = f32[2,192,384]{2,1,0:T(8,128)S(1)} custom-call(bf16[2,3,192,384]{3,2,1,0:T(8,128)(2,1)S(1)} %get-tuple-element.75.refs_0_, bf16[576,1728]{1,0:T(8,128)(2,1)S(1)} %get-tuple-element.76.refs_1_.refs_2_), custom_call_target="tpu_custom_call" | custom-call | tf_op jit(solution)/shard_map/begin/pallas_call | solution.py:428
  24.6 0.0 collective-permute-done.4.refs_5_
  24.6 2.1 %convs.6 = (bf16[2,192,512]{2,1,0:T(8,128)(2,1)S(1)}, bf16[2,3,192,384]{3,2,1,0:T(8,128)(2,1)S(1)}) custom-call(bf16[2,3,192,512]{3,2,1,0:T(8,128)(2,1)S(1)} %get-tuple-element.71.refs_0_, bf16[2,192,512]{2,1,0:T(8,128)(2,1)S(1)} %get-tuple-element.72.refs_1_, bf16[576,1728]{1,0:T(8,128)(2,1)S(1)} %get-tuple-element.65.refs_1_.refs_2_, ...), custom_call_target="tpu_custom_call" | custom-call | flops 2038431744 | tf_op jit(solution)/shard_map/convs/pallas_call | solution.py:428
  26.7 1.7 %convs.7 = (bf16[2,192,384]{2,1,0:T(8,128)(2,1)S(1)}, bf16[2,3,192,384]{3,2,1,0:T(8,128)(2,1)S(1)}, bf16[1024,128]{1,0:T(8,128)(2,1)S(1)}) custom-call(bf16[2,3,192,384]{3,2,1,0:T(8,128)(2,1)S(1)} %get-tuple-element.75.refs_0_, bf16[2,192,512]{2,1,0:T(8,128)(2,1)S(1)} %get-tuple-element.81.refs_1_, bf16[576,1728]{1,0:T(8,128)(2,1)S(1)} %get-tuple-element.76.refs_1_.refs_2_, ...), custom_call_target="tpu_custom_call" | custom-call | flops 1528823808 | tf_op jit(solution)/shard_map/convs/pallas_call | solution.py:428
  28.4 3.9 %collective-permute-start.6 = (bf16[1024,128]{1,0:T(8,128)(2,1)S(1)}, bf16[1024,128]{1,0:T(8,128)(2,1)S(1)}, u32[]{:S(2)}, u32[]{:S(2)}) collective-permute-start(bf16[1024,128]{1,0:T(8,128)(2,1)S(1)} %get-tuple-element.88), channel_id=1, source_target_pairs={{0,4},{4,8},{8,12},{1,5},{5,9},{9,13},{2,6},{6,10},{10,14},{3,7},{... | collective-permute-start | bytes 786440 | tf_op jit(solution)/shard_map/ppermute | solution.py:598
  32.4 0.0 collective-permute-done.5.refs_4_
  32.4 4.9 %convs.8 = (bf16[2,192,384]{2,1,0:T(8,128)(2,1)S(1)}, bf16[2,3,192,384]{3,2,1,0:T(8,128)(2,1)S(1)}, bf16[2,192,128]{2,1,0:T(8,128)(2,1)S(1)}, bf16[2,192,128]{2,1,0:T(8,128)(2,1)S(1)}) custom-call(bf16[2,3,192,384]{3,2,1,0:T(8,128)(2,1)S(1)} %get-tuple-element.78.refs_5_.refs_0_, bf16[2,192,512]{2,1,0:T(8,128)(2,1)S(1)} %get-tuple-element.79.refs_1_, ...), custom_call_target="tpu_custom_call" | custom-call | flops 3057647616 | tf_op jit(solution)/shard_map/convs/pallas_call | solution.py:428
  37.3 0.1 collective-permute-start.8
  37.4 0.0 collective-permute-done.6.refs_4_
  37.4 2.2 %convs.9 = (bf16[2,192,128]{2,1,0:T(8,128)(2,1)S(1)}, bf16[2,192,128]{2,1,0:T(8,128)(2,1)S(1)}) custom-call(bf16[2,3,192,384]{3,2,1,0:T(8,128)(2,1)S(1)} %get-tuple-element.86.refs_0_, bf16[2,192,384]{2,1,0:T(8,128)(2,1)S(1)} %get-tuple-element.87.refs_1_, bf16[576,1728]{1,0:T(8,128)(2,1)S(1)} %get-tuple-element.85.refs_7_.refs_2_, ...), custom_call_target="tpu_custom_call" | custom-call | flops 1528823808 | tf_op jit(solution)/shard_map/convs/pallas_call | solution.py:428
  39.6 0.5 %collective-permute-start.7 = (bf16[2,192,128]{2,1,0:T(8,128)(2,1)S(1)}, bf16[2,192,128]{2,1,0:T(8,128)(2,1)S(1)}, u32[]{:S(2)}, u32[]{:S(2)}) collective-permute-start(bf16[2,192,128]{2,1,0:T(8,128)(2,1)S(1)} %get-tuple-element.90), channel_id=1, source_target_pairs={{0,1},{1,0},{2,3},{3,2},{4,5},{5,4},{6,7},{7,6},{8,9},{9,8},{10,11... | collective-permute-start | bytes 294920 | tf_op jit(solution)/shard_map/ppermute | solution.py:595
  40.2 0.0 collective-permute-done.8.got_ref
  40.2 0.8 %join.2.refs_0_ = bf16[4,2,192,128]{3,2,1,0:T(8,128)(2,1)} custom-call(bf16[2,192,128]{2,1,0:T(8,128)(2,1)S(1)} %get-tuple-element.91.kept_ref, bf16[2,192,128]{2,1,0:T(8,128)(2,1)S(1)} %collective-permute-done.8.got_ref), custom_call_target="tpu_custom_call" | custom-call | tf_op jit(solution)/shard_map/join/pallas_call | solution.py:576
  41.0 0.1 collective-permute-done.7.got_ref
  41.1 0.8 %join.3 = bf16[4,2,192,128]{3,2,1,0:T(8,128)(2,1)} custom-call(bf16[2,192,128]{2,1,0:T(8,128)(2,1)S(1)} %get-tuple-element.89.kept_ref, bf16[2,192,128]{2,1,0:T(8,128)(2,1)S(1)} %collective-permute-done.7.got_ref, bf16[4,2,192,128]{3,2,1,0:T(8,128)(2,1)} %join.2.refs_0_), custom_call_target="tpu_custom_call", output_to_operand_aliasing={{}: (2, {})} | custom-call | tf_op jit(solution)/shard_map/join/pallas_call | solution.py:576
  (2 shorter events, 0.0 us)
Async XLA Ops:
  0.0 8.3 %collective-permute-start.1 = (bf16[4,2,192,128]{3,2,1,0:T(8,128)(2,1)}, bf16[4,2,192,128]{3,2,1,0:T(8,128)(2,1)S(1)}, u32[]{:S(2)}, u32[]{:S(2)}) collective-permute-start(bf16[4,2,192,128]{3,2,1,0:T(8,128)(2,1)} %in_ref.1), channel_id=1, source_target_pairs={{0,1},{1,0},{2,3},{3,2},{4,5},{5,4},{6,7},{7,6},{8,9},{9,8},{10,11... | collective-permute-start | bytes 1179656 | tf_op jit(solution)/shard_map/ppermute | solution.py:595
  0.5 1.0 %copy-start = (bf16[4,2,192,128]{3,2,1,0:T(8,128)(2,1)S(1)}, bf16[4,2,192,128]{3,2,1,0:T(8,128)(2,1)}, u32[]{:S(2)}) copy-start(bf16[4,2,192,128]{3,2,1,0:T(8,128)(2,1)} %in_ref.1) | copy-start | bytes 1179652
  1.5 8.1 %collective-permute-start = (bf16[2,2,192,128]{3,2,1,0:T(8,128)(2,1)S(1)}, bf16[2,2,192,128]{3,2,1,0:T(8,128)(2,1)S(1)}, u32[]{:S(2)}, u32[]{:S(2)}) collective-permute-start(bf16[2,2,192,128]{3,2,1,0:T(8,128)(2,1)S(1)} %get-tuple-element.49.refs_1_), channel_id=1, source_target_pairs={{0,2},{1,3},{2,0},{3,1},{4,6},{5,7},{6,4},{7,5},{8,10},{9,11},{10,... | collective-permute-start | bytes 589832 | tf_op jit(solution)/shard_map/ppermute | solution.py:601
  9.6 1.7 %collective-permute-start.2 = (bf16[2,2,192,128]{3,2,1,0:T(8,128)(2,1)S(1)}, bf16[2,2,192,128]{3,2,1,0:T(8,128)(2,1)S(1)}, u32[]{:S(2)}, u32[]{:S(2)}) collective-permute-start(bf16[2,2,192,128]{3,2,1,0:T(8,128)(2,1)S(1)} %collective-permute-done.far_ref), channel_id=1, source_target_pairs={{0,1},{1,0},{2,3},{3,2},{4,5},{5,4},{6,7},{7,6},{8,9},{9,8},{10,11... | collective-permute-start | bytes 589832 | tf_op jit(solution)/shard_map/ppermute | solution.py:595
  9.6 7.3 %collective-permute-start.3 = (bf16[2,192,256]{2,1,0:T(8,128)(2,1)S(1)}, bf16[2,192,256]{2,1,0:T(8,128)(2,1)S(1)}, u32[]{:S(2)}, u32[]{:S(2)}) collective-permute-start(bf16[2,192,256]{2,1,0:T(8,128)(2,1)S(1)} %get-tuple-element.66), channel_id=1, source_target_pairs={{0,2},{1,3},{2,0},{3,1},{4,6},{5,7},{6,4},{7,5},{8,10},{9,11},{10,... | collective-permute-start | bytes 589832 | tf_op jit(solution)/shard_map/ppermute | solution.py:601
  12.0 12.6 %collective-permute-start.4 = (bf16[1440,128]{1,0:T(8,128)(2,1)S(1)}, bf16[1440,128]{1,0:T(8,128)(2,1)S(1)}, u32[]{:S(2)}, u32[]{:S(2)}) collective-permute-start(bf16[1440,128]{1,0:T(8,128)(2,1)S(1)} %get-tuple-element.74), channel_id=1, source_target_pairs={{0,4},{4,8},{8,12},{1,5},{5,9},{9,13},{2,6},{6,10},{10,14},{3,7},{... | collective-permute-start | bytes 1105928 | tf_op jit(solution)/shard_map/ppermute | solution.py:598
  19.8 12.6 %collective-permute-start.5 = (bf16[1248,128]{1,0:T(8,128)(2,1)S(1)}, bf16[1248,128]{1,0:T(8,128)(2,1)S(1)}, u32[]{:S(2)}, u32[]{:S(2)}) collective-permute-start(bf16[1248,128]{1,0:T(8,128)(2,1)S(1)} %get-tuple-element.80), channel_id=1, source_target_pairs={{0,4},{4,8},{8,12},{1,5},{5,9},{9,13},{2,6},{6,10},{10,14},{3,7},{... | collective-permute-start | bytes 958472 | tf_op jit(solution)/shard_map/ppermute | solution.py:598
  28.4 8.9 %collective-permute-start.6 = (bf16[1024,128]{1,0:T(8,128)(2,1)S(1)}, bf16[1024,128]{1,0:T(8,128)(2,1)S(1)}, u32[]{:S(2)}, u32[]{:S(2)}) collective-permute-start(bf16[1024,128]{1,0:T(8,128)(2,1)S(1)} %get-tuple-element.88), channel_id=1, source_target_pairs={{0,4},{4,8},{8,12},{1,5},{5,9},{9,13},{2,6},{6,10},{10,14},{3,7},{... | collective-permute-start | bytes 786440 | tf_op jit(solution)/shard_map/ppermute | solution.py:598
  37.3 2.9 %collective-permute-start.8 = (bf16[2,192,128]{2,1,0:T(8,128)(2,1)S(1)}, bf16[2,192,128]{2,1,0:T(8,128)(2,1)S(1)}, u32[]{:S(2)}, u32[]{:S(2)}) collective-permute-start(bf16[2,192,128]{2,1,0:T(8,128)(2,1)S(1)} %get-tuple-element.92), channel_id=1, source_target_pairs={{0,1},{1,0},{2,3},{3,2},{4,5},{5,4},{6,7},{7,6},{8,9},{9,8},{10,11... | collective-permute-start | bytes 294920 | tf_op jit(solution)/shard_map/ppermute | solution.py:595
  39.6 1.5 %collective-permute-start.7 = (bf16[2,192,128]{2,1,0:T(8,128)(2,1)S(1)}, bf16[2,192,128]{2,1,0:T(8,128)(2,1)S(1)}, u32[]{:S(2)}, u32[]{:S(2)}) collective-permute-start(bf16[2,192,128]{2,1,0:T(8,128)(2,1)S(1)} %get-tuple-element.90), channel_id=1, source_target_pairs={{0,1},{1,0},{2,3},{3,2},{4,5},{5,4},{6,7},{7,6},{8,9},{9,8},{10,11... | collective-permute-start | bytes 294920 | tf_op jit(solution)/shard_map/ppermute | solution.py:595

commit v19 on v16

--- a/solution.py
+++ b/solution.py
@@ -257,7 +257,10 @@
             values_ref[t, :, part] = blocks[b].astype(jnp.bfloat16)
             acts.append(activated(blocks[b], columns_ref[0, 0], mask[:, part]))
         act = jnp.concatenate(acts, axis=1)
-        spread(shifted_ref, t, act, pitch)
+        if send_ref is None:
+            spread(shifted_ref, t, act, pitch)
+        else:
+            shifted_ref[t] = act
         whole_acts.append(act)
     if send_ref is not None:
         write_message(send_ref, whole_acts, valid)
@@ -274,7 +277,7 @@
 def beyond(halo, columns, *parts):
     far = parts[0]
     _, rows, channels, width = far.shape
-    values, shifted = far_shapes(rows, halo, channels, width // 2)
+    values, _ = far_shapes(rows, halo, channels, width // 2)
     pitch = width // 2 + halo + 1
     valid = (2 * rows + halo) * pitch
 
@@ -284,7 +287,7 @@
 
     return pl.pallas_call(
         kernel,
-        out_shape=(values, shifted, message_shape(channels, valid)),
+        out_shape=(values, values, message_shape(channels, valid)),
         in_specs=[VMEM] * 5,
         out_specs=(VMEM,) * 3,
         compiler_params=pltpu.CompilerParams(vmem_limit_bytes=LIMIT),
@@ -437,6 +440,11 @@
         )(*arrays)
         for out, value in zip((out for step in steps for out in step[2]), results):
             out.value = value
+
+
+def spread_kernel(pitch, act_ref, shifted_ref):
+    for t in range(PAIR):
+        spread(shifted_ref, t, act_ref[t], pitch)
 
 
 def begin(chain, shifted, weight):
@@ -612,13 +620,16 @@
         (far, weight, columns, near_values, near_act)
     )
     values, shifted = [None] * pairs, [None] * pairs
-    values[-1], shifted[-1], send = beyond(layers, columns, far, mate_of(far), near_values[-1], near_act[-1])
+    values[-1], last_act, send = beyond(layers, columns, far, mate_of(far), near_values[-1], near_act[-1])
     halo = earlier_of(send)
     next_begun = layer_begun = None
     chain = Chain()
+    shift_shape = far_shapes(rows, layers, channels, width // 2)[1]
+    spread_last = functools.partial(spread_kernel, width // 2 + layers + 1)
+    shifted[-1] = chain.add(spread_last, [last_act], [shift_shape], [], 0)[0]
     first_begun = begin(chain, shifted[-1], weight[0])
     chain.run("begin")
-    first_begun = now(first_begun)
+    shifted[-1], first_begun = now(shifted[-1]), now(first_begun)
     *came, first_begun = lax.optimization_barrier((*came, first_begun))
     parts = [(came[p], near_values[p], near_act[p]) for p in range(pairs - 1)]
     half = width // 2

time: 42.3 us -> 42 us (level)
  no operation moved by 1% of the time
where the time goes in v19:
time: 42 us; the launch traced here: 41.7 us
  Pallas kernels  22.4 us (53%)
  starting transfers between devices  16.3 us (39%)
  waiting for transfers between devices  1.08 us (3%)
  local copies, waits for them, and re-layouts  1 us (2%)
  other arithmetic  0.71 us (2%)
    pallas_call x7, Pallas kernels, run(): pl.pallas_call(kernel, out_shape=tuple(out_shape), in_specs=[VMEM] * len(...  16.2 us
    ppermute x3, starting transfers between devices, earlier_of(): return lax.ppermute(block, 'tm', [(i, i + 1) for i in range(blocks - 1)])  10.9 us
    ppermute x2, starting transfers between devices, beyond_of(): return lax.ppermute(block, 'rows', [(i, i ^ 2) for i in range(strips)])  4.29 us
    pallas_call x1, Pallas kernels, weights(): pl.pallas_call(weights_kernel, out_shape=(one,) * layers + (jax.ShapeDtyp...  3.54 us
    pallas_call x2, Pallas kernels, join(): pl.pallas_call(functools.partial(join_kernel, pair), out_shape=jax.ShapeD...  1.58 us
    ppermute x4, starting transfers between devices, mate_of(): return lax.ppermute(block, 'rows', [(i, i ^ 1) for i in range(strips)])  1.08 us
    unnamed x2, local copies, waits for them, and re-layouts  1 us
    ppermute x2, waiting for transfers between devices, beyond_of(): return lax.ppermute(block, 'rows', [(i, i ^ 2) for i in range(strips)])  0.92 us
  transfers between devices with their start and end apart: 9, of which 3 were waited for; matrix products, arithmetic and copies ran while one was open for 2% of the time, Pallas kernels for 52%

profile of v19, /device:TPU:0, one launch (start us, length us, event | category | flops | bytes accessed | tf_op | source)
XLA Modules:
  0.0 41.7 jit_solution(10653074811011391605)
XLA Ops:
  0.0 0.5 %collective-permute-start.1 = (bf16[4,2,192,128]{3,2,1,0:T(8,128)(2,1)}, bf16[4,2,192,128]{3,2,1,0:T(8,128)(2,1)S(1)}, u32[]{:S(2)}, u32[]{:S(2)}) collective-permute-start(bf16[4,2,192,128]{3,2,1,0:T(8,128)(2,1)} %in_ref.1), channel_id=1, source_target_pairs={{0,1},{1,0},{2,3},{3,2},{4,5},{5,4},{6,7},{7,6},{8,9},{9,8},{10,11... | collective-permute-start | bytes 1179656 | tf_op jit(solution)/shard_map/ppermute | solution.py:603
  0.5 1.0 %copy-done = bf16[4,2,192,128]{3,2,1,0:T(8,128)(2,1)S(1)} copy-done((bf16[4,2,192,128]{3,2,1,0:T(8,128)(2,1)S(1)}, bf16[4,2,192,128]{3,2,1,0:T(8,128)(2,1)}, u32[]{:S(2)}) %copy-start) | copy-done | bytes 393240
  1.5 2.6 %collective-permute-start = (bf16[2,2,192,128]{3,2,1,0:T(8,128)(2,1)S(1)}, bf16[2,2,192,128]{3,2,1,0:T(8,128)(2,1)S(1)}, u32[]{:S(2)}, u32[]{:S(2)}) collective-permute-start(bf16[2,2,192,128]{3,2,1,0:T(8,128)(2,1)S(1)} %get-tuple-element.52.refs_1_), channel_id=1, source_target_pairs={{0,2},{1,3},{2,0},{3,1},{4,6},{5,7},{6,4},{7,5},{8,10},{9,11},{10,... | collective-permute-start | bytes 589832 | tf_op jit(solution)/shard_map/ppermute | solution.py:609
  4.0 0.7 %pad_maximum_fusion.rows_ref.gains_ref = f32[6,192]{1,0:T(8,128)S(1)} fusion(f32[3,192]{1,0:T(4,128)} %param.7, f32[3,192]{1,0:T(4,128)} %param.6), kind=kLoop, calls=%fused_computation | loop fusion | flops 1152 | bytes 9216 | tf_op jit(solution)/shard_map/concatenate | solution.py:615
  4.7 3.5 %weights.1 = (bf16[576,1728]{1,0:T(8,128)(2,1)S(1)}, bf16[576,1728]{1,0:T(8,128)(2,1)S(1)}, bf16[576,1728]{1,0:T(8,128)(2,1)S(1)}, f32[3,2,192,128]{3,2,1,0:T(8,128)S(1)}) custom-call(bf16[3,27,192,192]{3,2,1,0:T(8,128)(2,1)} %w_ref.1, f32[6,192]{1,0:T(8,128)S(1)} %pad_maximum_fusion.rows_ref.gains_ref), custom_call_target="tpu_custom_call" | custom-call | bytes 11943936 | tf_op jit(solution)/shard_map/weights/pallas_call | solution.py:77
  8.3 0.0 collective-permute-done.1.mate_ref
  8.3 0.7 %near.1 = (bf16[2,192,384]{2,1,0:T(8,128)(2,1)S(1)}, bf16[2,192,384]{2,1,0:T(8,128)(2,1)S(1)}, bf16[2,192,256]{2,1,0:T(8,128)(2,1)S(1)}, bf16[2,192,256]{2,1,0:T(8,128)(2,1)S(1)}, bf16[2,192,256]{2,1,0:T(8,128)(2,1)S(1)}) custom-call(bf16[4,2,192,128]{3,2,1,0:T(8,128)(2,1)S(1)} %collective-permute-done.1.mate_ref, ...), custom_call_target="tpu_custom_call" | custom-call | flops 7864320 | bytes 1572864 | tf_op jit(solution)/shard_map/near/pallas_call | solution.py:220
  9.0 0.6 %collective-permute-done.far_ref = bf16[2,2,192,128]{3,2,1,0:T(8,128)(2,1)S(1)} collective-permute-done((bf16[2,2,192,128]{3,2,1,0:T(8,128)(2,1)S(1)}, bf16[2,2,192,128]{3,2,1,0:T(8,128)(2,1)S(1)}, u32[]{:S(2)}, u32[]{:S(2)}) %collective-permute-start) | collective-permute-done | bytes 196640 | tf_op jit(solution)/shard_map/ppermute | solution.py:609
  9.6 0.0 collective-permute-start.2
  9.6 1.7 %collective-permute-start.3 = (bf16[2,192,256]{2,1,0:T(8,128)(2,1)S(1)}, bf16[2,192,256]{2,1,0:T(8,128)(2,1)S(1)}, u32[]{:S(2)}, u32[]{:S(2)}) collective-permute-start(bf16[2,192,256]{2,1,0:T(8,128)(2,1)S(1)} %get-tuple-element.70), channel_id=1, source_target_pairs={{0,2},{1,3},{2,0},{3,1},{4,6},{5,7},{6,4},{7,5},{8,10},{9,11},{10,... | collective-permute-start | bytes 589832 | tf_op jit(solution)/shard_map/ppermute | solution.py:609
  11.4 0.0 collective-permute-done.2.mate_ref
  11.4 0.4 beyond.1
  11.7 3.5 %collective-permute-start.4 = (bf16[1440,128]{1,0:T(8,128)(2,1)S(1)}, bf16[1440,128]{1,0:T(8,128)(2,1)S(1)}, u32[]{:S(2)}, u32[]{:S(2)}) collective-permute-start(bf16[1440,128]{1,0:T(8,128)(2,1)S(1)} %get-tuple-element.79), channel_id=1, source_target_pairs={{0,4},{4,8},{8,12},{1,5},{5,9},{9,13},{2,6},{6,10},{10,14},{3,7},{... | collective-permute-start | bytes 1105928 | tf_op jit(solution)/shard_map/ppermute | solution.py:606
  15.2 1.4 %begin.2 = (bf16[2,3,192,512]{3,2,1,0:T(8,128)(2,1)S(1)}, f32[2,192,512]{2,1,0:T(8,128)S(1)}) custom-call(bf16[2,192,512]{2,1,0:T(8,128)(2,1)S(1)} %get-tuple-element.66.refs_0_, bf16[576,1728]{1,0:T(8,128)(2,1)S(1)} %get-tuple-element.67.refs_1_.refs_2_), custom_call_target="tpu_custom_call" | custom-call | tf_op jit(solution)/shard_map/begin/pallas_call | solution.py:431
  16.6 0.3 collective-permute-done.3.refs_5_
  16.9 2.9 %convs.5 = (bf16[2,192,512]{2,1,0:T(8,128)(2,1)S(1)}, bf16[2,3,192,384]{3,2,1,0:T(8,128)(2,1)S(1)}, bf16[1248,128]{1,0:T(8,128)(2,1)S(1)}, bf16[2,192,512]{2,1,0...) custom-call(bf16[2,3,192,512]{3,2,1,0:T(8,128)(2,1)S(1)} %get-tuple-element.68.refs_0_, ...), custom_call_target="tpu_custom_call" | custom-call | flops 4076863488 | tf_op jit(solution)/shard_map/convs/pallas_call | solution.py:431
  19.8 3.7 %collective-permute-start.5 = (bf16[1248,128]{1,0:T(8,128)(2,1)S(1)}, bf16[1248,128]{1,0:T(8,128)(2,1)S(1)}, u32[]{:S(2)}, u32[]{:S(2)}) collective-permute-start(bf16[1248,128]{1,0:T(8,128)(2,1)S(1)} %get-tuple-element.85), channel_id=1, source_target_pairs={{0,4},{4,8},{8,12},{1,5},{5,9},{9,13},{2,6},{6,10},{10,14},{3,7},{... | collective-permute-start | bytes 958472 | tf_op jit(solution)/shard_map/ppermute | solution.py:606
  23.5 1.1 %begin.3.refs_4_ = f32[2,192,384]{2,1,0:T(8,128)S(1)} custom-call(bf16[2,3,192,384]{3,2,1,0:T(8,128)(2,1)S(1)} %get-tuple-element.80.refs_0_, bf16[576,1728]{1,0:T(8,128)(2,1)S(1)} %get-tuple-element.81.refs_1_.refs_2_), custom_call_target="tpu_custom_call" | custom-call | tf_op jit(solution)/shard_map/begin/pallas_call | solution.py:431
  24.6 0.0 collective-permute-done.4.refs_5_
  24.6 2.1 %convs.6 = (bf16[2,192,512]{2,1,0:T(8,128)(2,1)S(1)}, bf16[2,3,192,384]{3,2,1,0:T(8,128)(2,1)S(1)}) custom-call(bf16[2,3,192,512]{3,2,1,0:T(8,128)(2,1)S(1)} %get-tuple-element.76.refs_0_, bf16[2,192,512]{2,1,0:T(8,128)(2,1)S(1)} %get-tuple-element.77.refs_1_, bf16[576,1728]{1,0:T(8,128)(2,1)S(1)} %get-tuple-element.67.refs_1_.refs_2_, ...), custom_call_target="tpu_custom_call" | custom-call | flops 2038431744 | tf_op jit(solution)/shard_map/convs/pallas_call | solution.py:431
  26.7 1.7 %convs.7 = (bf16[2,192,384]{2,1,0:T(8,128)(2,1)S(1)}, bf16[2,3,192,384]{3,2,1,0:T(8,128)(2,1)S(1)}, bf16[1024,128]{1,0:T(8,128)(2,1)S(1)}) custom-call(bf16[2,3,192,384]{3,2,1,0:T(8,128)(2,1)S(1)} %get-tuple-element.80.refs_0_, bf16[2,192,512]{2,1,0:T(8,128)(2,1)S(1)} %get-tuple-element.86.refs_1_, bf16[576,1728]{1,0:T(8,128)(2,1)S(1)} %get-tuple-element.81.refs_1_.refs_2_, ...), custom_call_target="tpu_custom_call" | custom-call | flops 1528823808 | tf_op jit(solution)/shard_map/convs/pallas_call | solution.py:431
  28.4 3.7 %collective-permute-start.6 = (bf16[1024,128]{1,0:T(8,128)(2,1)S(1)}, bf16[1024,128]{1,0:T(8,128)(2,1)S(1)}, u32[]{:S(2)}, u32[]{:S(2)}) collective-permute-start(bf16[1024,128]{1,0:T(8,128)(2,1)S(1)} %get-tuple-element.94), channel_id=1, source_target_pairs={{0,4},{4,8},{8,12},{1,5},{5,9},{9,13},{2,6},{6,10},{10,14},{3,7},{... | collective-permute-start | bytes 786440 | tf_op jit(solution)/shard_map/ppermute | solution.py:606
  32.1 0.0 collective-permute-done.5.refs_4_
  32.1 5.4 %convs.8 = (bf16[2,192,384]{2,1,0:T(8,128)(2,1)S(1)}, bf16[2,3,192,384]{3,2,1,0:T(8,128)(2,1)S(1)}, bf16[2,192,128]{2,1,0:T(8,128)(2,1)S(1)}, bf16[2,192,128]{2,1,0:T(8,128)(2,1)S(1)}, f32[2,192,384]{2,1,0:T(8,128)S(1)}) custom-call(bf16[2,3,192,384]{3,2,1,0:T(8,128)(2,1)S(1)} %get-tuple-element.83.refs_5_.refs_0_, ...), custom_call_target="tpu_custom_call" | custom-call | flops 3057647616 | tf_op jit(solution)/shard_map/convs/pallas_call | solution.py:431
  37.5 0.1 collective-permute-start.8
  37.5 0.0 collective-permute-done.6.refs_5_
  37.5 1.7 %convs.9 = (bf16[2,192,128]{2,1,0:T(8,128)(2,1)S(1)}, bf16[2,192,128]{2,1,0:T(8,128)(2,1)S(1)}) custom-call(bf16[2,3,192,384]{3,2,1,0:T(8,128)(2,1)S(1)} %get-tuple-element.91.refs_0_, bf16[2,192,384]{2,1,0:T(8,128)(2,1)S(1)} %get-tuple-element.92.refs_1_, bf16[576,1728]{1,0:T(8,128)(2,1)S(1)} %get-tuple-element.90.refs_7_.refs_2_, ...), custom_call_target="tpu_custom_call" | custom-call | flops 1528823808 | tf_op jit(solution)/shard_map/convs/pallas_call | solution.py:431
  39.3 0.6 %collective-permute-start.7 = (bf16[2,192,128]{2,1,0:T(8,128)(2,1)S(1)}, bf16[2,192,128]{2,1,0:T(8,128)(2,1)S(1)}, u32[]{:S(2)}, u32[]{:S(2)}) collective-permute-start(bf16[2,192,128]{2,1,0:T(8,128)(2,1)S(1)} %get-tuple-element.96), channel_id=1, source_target_pairs={{0,1},{1,0},{2,3},{3,2},{4,5},{5,4},{6,7},{7,6},{8,9},{9,8},{10,11... | collective-permute-start | bytes 294920 | tf_op jit(solution)/shard_map/ppermute | solution.py:603
  39.8 0.0 collective-permute-done.8.got_ref
  39.8 0.8 %join.2.refs_0_ = bf16[4,2,192,128]{3,2,1,0:T(8,128)(2,1)} custom-call(bf16[2,192,128]{2,1,0:T(8,128)(2,1)S(1)} %get-tuple-element.97.kept_ref, bf16[2,192,128]{2,1,0:T(8,128)(2,1)S(1)} %collective-permute-done.8.got_ref), custom_call_target="tpu_custom_call" | custom-call | tf_op jit(solution)/shard_map/join/pallas_call | solution.py:584
  40.6 0.1 collective-permute-done.7.got_ref
  40.8 0.8 %join.3 = bf16[4,2,192,128]{3,2,1,0:T(8,128)(2,1)} custom-call(bf16[2,192,128]{2,1,0:T(8,128)(2,1)S(1)} %get-tuple-element.95.kept_ref, bf16[2,192,128]{2,1,0:T(8,128)(2,1)S(1)} %collective-permute-done.7.got_ref, bf16[4,2,192,128]{3,2,1,0:T(8,128)(2,1)} %join.2.refs_0_), custom_call_target="tpu_custom_call", output_to_operand_aliasing={{}: (2, {})} | custom-call | tf_op jit(solution)/shard_map/join/pallas_call | solution.py:584
  (2 shorter events, 0.0 us)
Async XLA Ops:
  0.0 8.3 %collective-permute-start.1 = (bf16[4,2,192,128]{3,2,1,0:T(8,128)(2,1)}, bf16[4,2,192,128]{3,2,1,0:T(8,128)(2,1)S(1)}, u32[]{:S(2)}, u32[]{:S(2)}) collective-permute-start(bf16[4,2,192,128]{3,2,1,0:T(8,128)(2,1)} %in_ref.1), channel_id=1, source_target_pairs={{0,1},{1,0},{2,3},{3,2},{4,5},{5,4},{6,7},{7,6},{8,9},{9,8},{10,11... | collective-permute-start | bytes 1179656 | tf_op jit(solution)/shard_map/ppermute | solution.py:603
  0.5 1.0 %copy-start = (bf16[4,2,192,128]{3,2,1,0:T(8,128)(2,1)S(1)}, bf16[4,2,192,128]{3,2,1,0:T(8,128)(2,1)}, u32[]{:S(2)}) copy-start(bf16[4,2,192,128]{3,2,1,0:T(8,128)(2,1)} %in_ref.1) | copy-start | bytes 1179652
  1.5 8.1 %collective-permute-start = (bf16[2,2,192,128]{3,2,1,0:T(8,128)(2,1)S(1)}, bf16[2,2,192,128]{3,2,1,0:T(8,128)(2,1)S(1)}, u32[]{:S(2)}, u32[]{:S(2)}) collective-permute-start(bf16[2,2,192,128]{3,2,1,0:T(8,128)(2,1)S(1)} %get-tuple-element.52.refs_1_), channel_id=1, source_target_pairs={{0,2},{1,3},{2,0},{3,1},{4,6},{5,7},{6,4},{7,5},{8,10},{9,11},{10,... | collective-permute-start | bytes 589832 | tf_op jit(solution)/shard_map/ppermute | solution.py:609
  9.6 1.7 %collective-permute-start.2 = (bf16[2,2,192,128]{3,2,1,0:T(8,128)(2,1)S(1)}, bf16[2,2,192,128]{3,2,1,0:T(8,128)(2,1)S(1)}, u32[]{:S(2)}, u32[]{:S(2)}) collective-permute-start(bf16[2,2,192,128]{3,2,1,0:T(8,128)(2,1)S(1)} %collective-permute-done.far_ref), channel_id=1, source_target_pairs={{0,1},{1,0},{2,3},{3,2},{4,5},{5,4},{6,7},{7,6},{8,9},{9,8},{10,11... | collective-permute-start | bytes 589832 | tf_op jit(solution)/shard_map/ppermute | solution.py:603
  9.6 7.3 %collective-permute-start.3 = (bf16[2,192,256]{2,1,0:T(8,128)(2,1)S(1)}, bf16[2,192,256]{2,1,0:T(8,128)(2,1)S(1)}, u32[]{:S(2)}, u32[]{:S(2)}) collective-permute-start(bf16[2,192,256]{2,1,0:T(8,128)(2,1)S(1)} %get-tuple-element.70), channel_id=1, source_target_pairs={{0,2},{1,3},{2,0},{3,1},{4,6},{5,7},{6,4},{7,5},{8,10},{9,11},{10,... | collective-permute-start | bytes 589832 | tf_op jit(solution)/shard_map/ppermute | solution.py:609
  11.7 12.9 %collective-permute-start.4 = (bf16[1440,128]{1,0:T(8,128)(2,1)S(1)}, bf16[1440,128]{1,0:T(8,128)(2,1)S(1)}, u32[]{:S(2)}, u32[]{:S(2)}) collective-permute-start(bf16[1440,128]{1,0:T(8,128)(2,1)S(1)} %get-tuple-element.79), channel_id=1, source_target_pairs={{0,4},{4,8},{8,12},{1,5},{5,9},{9,13},{2,6},{6,10},{10,14},{3,7},{... | collective-permute-start | bytes 1105928 | tf_op jit(solution)/shard_map/ppermute | solution.py:606
  19.8 12.3 %collective-permute-start.5 = (bf16[1248,128]{1,0:T(8,128)(2,1)S(1)}, bf16[1248,128]{1,0:T(8,128)(2,1)S(1)}, u32[]{:S(2)}, u32[]{:S(2)}) collective-permute-start(bf16[1248,128]{1,0:T(8,128)(2,1)S(1)} %get-tuple-element.85), channel_id=1, source_target_pairs={{0,4},{4,8},{8,12},{1,5},{5,9},{9,13},{2,6},{6,10},{10,14},{3,7},{... | collective-permute-start | bytes 958472 | tf_op jit(solution)/shard_map/ppermute | solution.py:606
  28.4 9.1 %collective-permute-start.6 = (bf16[1024,128]{1,0:T(8,128)(2,1)S(1)}, bf16[1024,128]{1,0:T(8,128)(2,1)S(1)}, u32[]{:S(2)}, u32[]{:S(2)}) collective-permute-start(bf16[1024,128]{1,0:T(8,128)(2,1)S(1)} %get-tuple-element.94), channel_id=1, source_target_pairs={{0,4},{4,8},{8,12},{1,5},{5,9},{9,13},{2,6},{6,10},{10,14},{3,7},{... | collective-permute-start | bytes 786440 | tf_op jit(solution)/shard_map/ppermute | solution.py:606
  37.5 2.4 %collective-permute-start.8 = (bf16[2,192,128]{2,1,0:T(8,128)(2,1)S(1)}, bf16[2,192,128]{2,1,0:T(8,128)(2,1)S(1)}, u32[]{:S(2)}, u32[]{:S(2)}) collective-permute-start(bf16[2,192,128]{2,1,0:T(8,128)(2,1)S(1)} %get-tuple-element.98), channel_id=1, source_target_pairs={{0,1},{1,0},{2,3},{3,2},{4,5},{5,4},{6,7},{7,6},{8,9},{9,8},{10,11... | collective-permute-start | bytes 294920 | tf_op jit(solution)/shard_map/ppermute | solution.py:603
  39.3 1.5 %collective-permute-start.7 = (bf16[2,192,128]{2,1,0:T(8,128)(2,1)S(1)}, bf16[2,192,128]{2,1,0:T(8,128)(2,1)S(1)}, u32[]{:S(2)}, u32[]{:S(2)}) collective-permute-start(bf16[2,192,128]{2,1,0:T(8,128)(2,1)S(1)} %get-tuple-element.96), channel_id=1, source_target_pairs={{0,1},{1,0},{2,3},{3,2},{4,5},{5,4},{6,7},{7,6},{8,9},{9,8},{10,11... | collective-permute-start | bytes 294920 | tf_op jit(solution)/shard_map/ppermute | solution.py:603

commit v20 on v19

--- a/solution.py
+++ b/solution.py
@@ -608,10 +608,11 @@
     def beyond_of(block):
         return lax.ppermute(block, "rows", [(i, i ^ 2) for i in range(strips)])
 
-    mate = mate_of(latents)
     pairs = frames // PAIR
     own = split(latents)
     far = beyond_of(own[-1])
+    whole, *own = lax.optimization_barrier((latents, *own))
+    mate = mate_of(whole)
     row_values = jnp.concatenate([norm_gains, biases], axis=0)
     weight, columns = weights(conv_weight, row_values)
     near_values, near_act, near_sent = near(layers, mate, row_values, own)

time: 42 us -> 42 us (level)
  local copies, waits for them, and re-layouts: 1 us -> 0 us
  Pallas kernels: 22.4 us -> 23.3 us
    unnamed x2 -> x0, local copies, waits for them, and re-layouts: 1 us -> none
    pallas_call x1, Pallas kernels: 0.03 us -> 1.02 us  [split(): pl.pallas_call(split_kernel, out_shape=(jax.ShapeDtypeStruct((PAIR,) + la...]
where the time goes in v20:
time: 42 us; the launch traced here: 41.7 us
  Pallas kernels  23.3 us (55%)
  starting transfers between devices  16.4 us (39%)
  waiting for transfers between devices  1 us (2%)
  other arithmetic  0.71 us (2%)
    pallas_call x7, Pallas kernels, run(): pl.pallas_call(kernel, out_shape=tuple(out_shape), in_specs=[VMEM] * len(...  16.1 us
    ppermute x3, starting transfers between devices, earlier_of(): return lax.ppermute(block, 'tm', [(i, i + 1) for i in range(blocks - 1)])  10.9 us
    ppermute x2, starting transfers between devices, beyond_of(): return lax.ppermute(block, 'rows', [(i, i ^ 2) for i in range(strips)])  4.32 us
    pallas_call x1, Pallas kernels, weights(): pl.pallas_call(weights_kernel, out_shape=(one,) * layers + (jax.ShapeDtyp...  3.54 us
    pallas_call x2, Pallas kernels, join(): pl.pallas_call(functools.partial(join_kernel, pair), out_shape=jax.ShapeD...  1.58 us
    ppermute x4, starting transfers between devices, mate_of(): return lax.ppermute(block, 'rows', [(i, i ^ 1) for i in range(strips)])  1.14 us
    pallas_call x1, Pallas kernels, split(): pl.pallas_call(split_kernel, out_shape=(jax.ShapeDtypeStruct((PAIR,) + la...  1.02 us
    ppermute x2, waiting for transfers between devices, beyond_of(): return lax.ppermute(block, 'rows', [(i, i ^ 2) for i in range(strips)])  0.84 us
  transfers between devices with their start and end apart: 9, of which 3 were waited for; matrix products, arithmetic and copies ran while one was open for 2% of the time, Pallas kernels for 52%

profile of v20, /device:TPU:0, one launch (start us, length us, event | category | flops | bytes accessed | tf_op | source)
XLA Modules:
  0.0 41.7 jit_solution(4274837915890179267)
XLA Ops:
  0.0 1.0 %split.1 = (bf16[2,2,192,128]{3,2,1,0:T(8,128)(2,1)S(1)}, bf16[2,2,192,128]{3,2,1,0:T(8,128)(2,1)S(1)}) custom-call(bf16[4,2,192,128]{3,2,1,0:T(8,128)(2,1)} %in_ref.1), custom_call_target="tpu_custom_call" | custom-call | tf_op jit(solution)/shard_map/split/pallas_call | solution.py:100
  1.0 0.5 %collective-permute-start.1 = (bf16[4,2,192,128]{3,2,1,0:T(8,128)(2,1)}, bf16[4,2,192,128]{3,2,1,0:T(8,128)(2,1)S(1)}, u32[]{:S(2)}, u32[]{:S(2)}) collective-permute-start(bf16[4,2,192,128]{3,2,1,0:T(8,128)(2,1)} %in_ref.1), channel_id=1, source_target_pairs={{0,1},{1,0},{2,3},{3,2},{4,5},{5,4},{6,7},{7,6},{8,9},{9,8},{10,11... | collective-permute-start | bytes 1179656 | tf_op jit(solution)/shard_map/ppermute | solution.py:603
  1.5 2.6 %collective-permute-start = (bf16[2,2,192,128]{3,2,1,0:T(8,128)(2,1)S(1)}, bf16[2,2,192,128]{3,2,1,0:T(8,128)(2,1)S(1)}, u32[]{:S(2)}, u32[]{:S(2)}) collective-permute-start(bf16[2,2,192,128]{3,2,1,0:T(8,128)(2,1)S(1)} %get-tuple-element.63.refs_1_), channel_id=1, source_target_pairs={{0,2},{1,3},{2,0},{3,1},{4,6},{5,7},{6,4},{7,5},{8,10},{9,11},{10,... | collective-permute-start | bytes 589832 | tf_op jit(solution)/shard_map/ppermute | solution.py:609
  4.1 0.7 %pad_maximum_fusion.rows_ref.gains_ref = f32[6,192]{1,0:T(8,128)S(1)} fusion(f32[3,192]{1,0:T(4,128)} %param.7, f32[3,192]{1,0:T(4,128)} %param.6), kind=kLoop, calls=%fused_computation | loop fusion | flops 1152 | bytes 9216 | tf_op jit(solution)/shard_map/concatenate | solution.py:616
  4.8 3.5 %weights.1 = (bf16[576,1728]{1,0:T(8,128)(2,1)S(1)}, bf16[576,1728]{1,0:T(8,128)(2,1)S(1)}, bf16[576,1728]{1,0:T(8,128)(2,1)S(1)}, f32[3,2,192,128]{3,2,1,0:T(8,128)S(1)}) custom-call(bf16[3,27,192,192]{3,2,1,0:T(8,128)(2,1)} %w_ref.1, f32[6,192]{1,0:T(8,128)S(1)} %pad_maximum_fusion.rows_ref.gains_ref), custom_call_target="tpu_custom_call" | custom-call | bytes 11943936 | tf_op jit(solution)/shard_map/weights/pallas_call | solution.py:77
  8.4 0.0 collective-permute-done.1.mate_ref
  8.4 0.7 %near.1 = (bf16[2,192,384]{2,1,0:T(8,128)(2,1)S(1)}, bf16[2,192,384]{2,1,0:T(8,128)(2,1)S(1)}, bf16[2,192,256]{2,1,0:T(8,128)(2,1)S(1)}, bf16[2,192,256]{2,1,0:T(8,128)(2,1)S(1)}, bf16[2,192,256]{2,1,0:T(8,128)(2,1)S(1)}) custom-call(bf16[4,2,192,128]{3,2,1,0:T(8,128)(2,1)S(1)} %collective-permute-done.1.mate_ref, ...), custom_call_target="tpu_custom_call" | custom-call | flops 7864320 | bytes 1572864 | tf_op jit(solution)/shard_map/near/pallas_call | solution.py:220
  9.1 0.5 %collective-permute-done.far_ref = bf16[2,2,192,128]{3,2,1,0:T(8,128)(2,1)S(1)} collective-permute-done((bf16[2,2,192,128]{3,2,1,0:T(8,128)(2,1)S(1)}, bf16[2,2,192,128]{3,2,1,0:T(8,128)(2,1)S(1)}, u32[]{:S(2)}, u32[]{:S(2)}) %collective-permute-start) | collective-permute-done | bytes 196640 | tf_op jit(solution)/shard_map/ppermute | solution.py:609
  9.6 0.0 collective-permute-start.2
  9.6 1.8 %collective-permute-start.3 = (bf16[2,192,256]{2,1,0:T(8,128)(2,1)S(1)}, bf16[2,192,256]{2,1,0:T(8,128)(2,1)S(1)}, u32[]{:S(2)}, u32[]{:S(2)}) collective-permute-start(bf16[2,192,256]{2,1,0:T(8,128)(2,1)S(1)} %get-tuple-element.76), channel_id=1, source_target_pairs={{0,2},{1,3},{2,0},{3,1},{4,6},{5,7},{6,4},{7,5},{8,10},{9,11},{10,... | collective-permute-start | bytes 589832 | tf_op jit(solution)/shard_map/ppermute | solution.py:609
  11.4 0.0 collective-permute-done.2.mate_ref
  11.4 0.4 beyond.1
  11.7 3.5 %collective-permute-start.4 = (bf16[1440,128]{1,0:T(8,128)(2,1)S(1)}, bf16[1440,128]{1,0:T(8,128)(2,1)S(1)}, u32[]{:S(2)}, u32[]{:S(2)}) collective-permute-start(bf16[1440,128]{1,0:T(8,128)(2,1)S(1)} %get-tuple-element.85), channel_id=1, source_target_pairs={{0,4},{4,8},{8,12},{1,5},{5,9},{9,13},{2,6},{6,10},{10,14},{3,7},{... | collective-permute-start | bytes 1105928 | tf_op jit(solution)/shard_map/ppermute | solution.py:606
  15.3 1.4 %begin.2 = (bf16[2,3,192,512]{3,2,1,0:T(8,128)(2,1)S(1)}, f32[2,192,512]{2,1,0:T(8,128)S(1)}) custom-call(bf16[2,192,512]{2,1,0:T(8,128)(2,1)S(1)} %get-tuple-element.72.refs_0_, bf16[576,1728]{1,0:T(8,128)(2,1)S(1)} %get-tuple-element.73.refs_1_.refs_2_), custom_call_target="tpu_custom_call" | custom-call | tf_op jit(solution)/shard_map/begin/pallas_call | solution.py:431
  16.6 0.3 collective-permute-done.3.refs_5_
  16.9 2.9 %convs.5 = (bf16[2,192,512]{2,1,0:T(8,128)(2,1)S(1)}, bf16[2,3,192,384]{3,2,1,0:T(8,128)(2,1)S(1)}, bf16[1248,128]{1,0:T(8,128)(2,1)S(1)}, bf16[2,192,512]{2,1,0...) custom-call(bf16[2,3,192,512]{3,2,1,0:T(8,128)(2,1)S(1)} %get-tuple-element.74.refs_0_, ...), custom_call_target="tpu_custom_call" | custom-call | flops 4076863488 | tf_op jit(solution)/shard_map/convs/pallas_call | solution.py:431
  19.8 3.8 %collective-permute-start.5 = (bf16[1248,128]{1,0:T(8,128)(2,1)S(1)}, bf16[1248,128]{1,0:T(8,128)(2,1)S(1)}, u32[]{:S(2)}, u32[]{:S(2)}) collective-permute-start(bf16[1248,128]{1,0:T(8,128)(2,1)S(1)} %get-tuple-element.91), channel_id=1, source_target_pairs={{0,4},{4,8},{8,12},{1,5},{5,9},{9,13},{2,6},{6,10},{10,14},{3,7},{... | collective-permute-start | bytes 958472 | tf_op jit(solution)/shard_map/ppermute | solution.py:606
  23.6 1.1 %begin.3.refs_4_ = f32[2,192,384]{2,1,0:T(8,128)S(1)} custom-call(bf16[2,3,192,384]{3,2,1,0:T(8,128)(2,1)S(1)} %get-tuple-element.86.refs_0_, bf16[576,1728]{1,0:T(8,128)(2,1)S(1)} %get-tuple-element.87.refs_1_.refs_2_), custom_call_target="tpu_custom_call" | custom-call | tf_op jit(solution)/shard_map/begin/pallas_call | solution.py:431
  24.6 0.0 collective-permute-done.4.refs_5_
  24.6 2.1 %convs.6 = (bf16[2,192,512]{2,1,0:T(8,128)(2,1)S(1)}, bf16[2,3,192,384]{3,2,1,0:T(8,128)(2,1)S(1)}) custom-call(bf16[2,3,192,512]{3,2,1,0:T(8,128)(2,1)S(1)} %get-tuple-element.82.refs_0_, bf16[2,192,512]{2,1,0:T(8,128)(2,1)S(1)} %get-tuple-element.83.refs_1_, bf16[576,1728]{1,0:T(8,128)(2,1)S(1)} %get-tuple-element.73.refs_1_.refs_2_, ...), custom_call_target="tpu_custom_call" | custom-call | flops 2038431744 | tf_op jit(solution)/shard_map/convs/pallas_call | solution.py:431
  26.7 1.7 %convs.7 = (bf16[2,192,384]{2,1,0:T(8,128)(2,1)S(1)}, bf16[2,3,192,384]{3,2,1,0:T(8,128)(2,1)S(1)}, bf16[1024,128]{1,0:T(8,128)(2,1)S(1)}) custom-call(bf16[2,3,192,384]{3,2,1,0:T(8,128)(2,1)S(1)} %get-tuple-element.86.refs_0_, bf16[2,192,512]{2,1,0:T(8,128)(2,1)S(1)} %get-tuple-element.92.refs_1_, bf16[576,1728]{1,0:T(8,128)(2,1)S(1)} %get-tuple-element.87.refs_1_.refs_2_, ...), custom_call_target="tpu_custom_call" | custom-call | flops 1528823808 | tf_op jit(solution)/shard_map/convs/pallas_call | solution.py:431
  28.4 3.7 %collective-permute-start.6 = (bf16[1024,128]{1,0:T(8,128)(2,1)S(1)}, bf16[1024,128]{1,0:T(8,128)(2,1)S(1)}, u32[]{:S(2)}, u32[]{:S(2)}) collective-permute-start(bf16[1024,128]{1,0:T(8,128)(2,1)S(1)} %get-tuple-element.100), channel_id=1, source_target_pairs={{0,4},{4,8},{8,12},{1,5},{5,9},{9,13},{2,6},{6,10},{10,14},{3,7},{... | collective-permute-start | bytes 786440 | tf_op jit(solution)/shard_map/ppermute | solution.py:606
  32.1 0.0 collective-permute-done.5.refs_4_
  32.1 5.4 %convs.8 = (bf16[2,192,384]{2,1,0:T(8,128)(2,1)S(1)}, bf16[2,3,192,384]{3,2,1,0:T(8,128)(2,1)S(1)}, bf16[2,192,128]{2,1,0:T(8,128)(2,1)S(1)}, bf16[2,192,128]{2,1,0:T(8,128)(2,1)S(1)}, f32[2,192,384]{2,1,0:T(8,128)S(1)}) custom-call(bf16[2,3,192,384]{3,2,1,0:T(8,128)(2,1)S(1)} %get-tuple-element.89.refs_5_.refs_0_, ...), custom_call_target="tpu_custom_call" | custom-call | flops 3057647616 | tf_op jit(solution)/shard_map/convs/pallas_call | solution.py:431
  37.5 0.1 collective-permute-start.8
  37.5 0.0 collective-permute-done.6.refs_5_
  37.5 1.7 %convs.9 = (bf16[2,192,128]{2,1,0:T(8,128)(2,1)S(1)}, bf16[2,192,128]{2,1,0:T(8,128)(2,1)S(1)}) custom-call(bf16[2,3,192,384]{3,2,1,0:T(8,128)(2,1)S(1)} %get-tuple-element.97.refs_0_, bf16[2,192,384]{2,1,0:T(8,128)(2,1)S(1)} %get-tuple-element.98.refs_1_, bf16[576,1728]{1,0:T(8,128)(2,1)S(1)} %get-tuple-element.96.refs_7_.refs_2_, ...), custom_call_target="tpu_custom_call" | custom-call | flops 1528823808 | tf_op jit(solution)/shard_map/convs/pallas_call | solution.py:431
  39.3 0.6 %collective-permute-start.7 = (bf16[2,192,128]{2,1,0:T(8,128)(2,1)S(1)}, bf16[2,192,128]{2,1,0:T(8,128)(2,1)S(1)}, u32[]{:S(2)}, u32[]{:S(2)}) collective-permute-start(bf16[2,192,128]{2,1,0:T(8,128)(2,1)S(1)} %get-tuple-element.102), channel_id=1, source_target_pairs={{0,1},{1,0},{2,3},{3,2},{4,5},{5,4},{6,7},{7,6},{8,9},{9,8},{10,11... | collective-permute-start | bytes 294920 | tf_op jit(solution)/shard_map/ppermute | solution.py:603
  39.8 0.0 collective-permute-done.8.got_ref
  39.9 0.8 %join.2.refs_0_ = bf16[4,2,192,128]{3,2,1,0:T(8,128)(2,1)} custom-call(bf16[2,192,128]{2,1,0:T(8,128)(2,1)S(1)} %get-tuple-element.103.kept_ref, bf16[2,192,128]{2,1,0:T(8,128)(2,1)S(1)} %collective-permute-done.8.got_ref), custom_call_target="tpu_custom_call" | custom-call | tf_op jit(solution)/shard_map/join/pallas_call | solution.py:584
  40.6 0.1 collective-permute-done.7.got_ref
  40.8 0.8 %join.3 = bf16[4,2,192,128]{3,2,1,0:T(8,128)(2,1)} custom-call(bf16[2,192,128]{2,1,0:T(8,128)(2,1)S(1)} %get-tuple-element.101.kept_ref, bf16[2,192,128]{2,1,0:T(8,128)(2,1)S(1)} %collective-permute-done.7.got_ref, bf16[4,2,192,128]{3,2,1,0:T(8,128)(2,1)} %join.2.refs_0_), custom_call_target="tpu_custom_call", output_to_operand_aliasing={{}: (2, {})} | custom-call | tf_op jit(solution)/shard_map/join/pallas_call | solution.py:584
Async XLA Ops:
  1.0 7.3 %collective-permute-start.1 = (bf16[4,2,192,128]{3,2,1,0:T(8,128)(2,1)}, bf16[4,2,192,128]{3,2,1,0:T(8,128)(2,1)S(1)}, u32[]{:S(2)}, u32[]{:S(2)}) collective-permute-start(bf16[4,2,192,128]{3,2,1,0:T(8,128)(2,1)} %in_ref.1), channel_id=1, source_target_pairs={{0,1},{1,0},{2,3},{3,2},{4,5},{5,4},{6,7},{7,6},{8,9},{9,8},{10,11... | collective-permute-start | bytes 1179656 | tf_op jit(solution)/shard_map/ppermute | solution.py:603
  1.5 8.1 %collective-permute-start = (bf16[2,2,192,128]{3,2,1,0:T(8,128)(2,1)S(1)}, bf16[2,2,192,128]{3,2,1,0:T(8,128)(2,1)S(1)}, u32[]{:S(2)}, u32[]{:S(2)}) collective-permute-start(bf16[2,2,192,128]{3,2,1,0:T(8,128)(2,1)S(1)} %get-tuple-element.63.refs_1_), channel_id=1, source_target_pairs={{0,2},{1,3},{2,0},{3,1},{4,6},{5,7},{6,4},{7,5},{8,10},{9,11},{10,... | collective-permute-start | bytes 589832 | tf_op jit(solution)/shard_map/ppermute | solution.py:609
  9.6 1.8 %collective-permute-start.2 = (bf16[2,2,192,128]{3,2,1,0:T(8,128)(2,1)S(1)}, bf16[2,2,192,128]{3,2,1,0:T(8,128)(2,1)S(1)}, u32[]{:S(2)}, u32[]{:S(2)}) collective-permute-start(bf16[2,2,192,128]{3,2,1,0:T(8,128)(2,1)S(1)} %collective-permute-done.far_ref), channel_id=1, source_target_pairs={{0,1},{1,0},{2,3},{3,2},{4,5},{5,4},{6,7},{7,6},{8,9},{9,8},{10,11... | collective-permute-start | bytes 589832 | tf_op jit(solution)/shard_map/ppermute | solution.py:603
  9.6 7.3 %collective-permute-start.3 = (bf16[2,192,256]{2,1,0:T(8,128)(2,1)S(1)}, bf16[2,192,256]{2,1,0:T(8,128)(2,1)S(1)}, u32[]{:S(2)}, u32[]{:S(2)}) collective-permute-start(bf16[2,192,256]{2,1,0:T(8,128)(2,1)S(1)} %get-tuple-element.76), channel_id=1, source_target_pairs={{0,2},{1,3},{2,0},{3,1},{4,6},{5,7},{6,4},{7,5},{8,10},{9,11},{10,... | collective-permute-start | bytes 589832 | tf_op jit(solution)/shard_map/ppermute | solution.py:609
  11.7 12.9 %collective-permute-start.4 = (bf16[1440,128]{1,0:T(8,128)(2,1)S(1)}, bf16[1440,128]{1,0:T(8,128)(2,1)S(1)}, u32[]{:S(2)}, u32[]{:S(2)}) collective-permute-start(bf16[1440,128]{1,0:T(8,128)(2,1)S(1)} %get-tuple-element.85), channel_id=1, source_target_pairs={{0,4},{4,8},{8,12},{1,5},{5,9},{9,13},{2,6},{6,10},{10,14},{3,7},{... | collective-permute-start | bytes 1105928 | tf_op jit(solution)/shard_map/ppermute | solution.py:606
  19.8 12.3 %collective-permute-start.5 = (bf16[1248,128]{1,0:T(8,128)(2,1)S(1)}, bf16[1248,128]{1,0:T(8,128)(2,1)S(1)}, u32[]{:S(2)}, u32[]{:S(2)}) collective-permute-start(bf16[1248,128]{1,0:T(8,128)(2,1)S(1)} %get-tuple-element.91), channel_id=1, source_target_pairs={{0,4},{4,8},{8,12},{1,5},{5,9},{9,13},{2,6},{6,10},{10,14},{3,7},{... | collective-permute-start | bytes 958472 | tf_op jit(solution)/shard_map/ppermute | solution.py:606
  28.4 9.1 %collective-permute-start.6 = (bf16[1024,128]{1,0:T(8,128)(2,1)S(1)}, bf16[1024,128]{1,0:T(8,128)(2,1)S(1)}, u32[]{:S(2)}, u32[]{:S(2)}) collective-permute-start(bf16[1024,128]{1,0:T(8,128)(2,1)S(1)} %get-tuple-element.100), channel_id=1, source_target_pairs={{0,4},{4,8},{8,12},{1,5},{5,9},{9,13},{2,6},{6,10},{10,14},{3,7},{... | collective-permute-start | bytes 786440 | tf_op jit(solution)/shard_map/ppermute | solution.py:606
  37.5 2.4 %collective-permute-start.8 = (bf16[2,192,128]{2,1,0:T(8,128)(2,1)S(1)}, bf16[2,192,128]{2,1,0:T(8,128)(2,1)S(1)}, u32[]{:S(2)}, u32[]{:S(2)}) collective-permute-start(bf16[2,192,128]{2,1,0:T(8,128)(2,1)S(1)} %get-tuple-element.104), channel_id=1, source_target_pairs={{0,1},{1,0},{2,3},{3,2},{4,5},{5,4},{6,7},{7,6},{8,9},{9,8},{10,11... | collective-permute-start | bytes 294920 | tf_op jit(solution)/shard_map/ppermute | solution.py:603
  39.3 1.5 %collective-permute-start.7 = (bf16[2,192,128]{2,1,0:T(8,128)(2,1)S(1)}, bf16[2,192,128]{2,1,0:T(8,128)(2,1)S(1)}, u32[]{:S(2)}, u32[]{:S(2)}) collective-permute-start(bf16[2,192,128]{2,1,0:T(8,128)(2,1)S(1)} %get-tuple-element.102), channel_id=1, source_target_pairs={{0,1},{1,0},{2,3},{3,2},{4,5},{5,4},{6,7},{7,6},{8,9},{9,8},{10,11... | collective-permute-start | bytes 294920 | tf_op jit(solution)/shard_map/ppermute | solution.py:603
